TPU v7x, 32 devices: a whole 2x2x4 slice. The times are simulated.
32 devices in a mesh: win: 2 (over x), row: 16 (over z, y, core).
Axes of the slice: x: 2, y: 2, z: 4, core: 2. Of those that a mesh axis runs over, the one named last changes fastest.
Arguments:
- mask_field: float32 [2, 4096, 128], P(None, ('win', 'row')), parts along dimension 1, may hold values from -6 to 6
- target: int32 [4096, 128], P(('win', 'row')), parts along dimension 0, may hold values 0 or 1
- kernel_taps: float32 [24, 2, 128, 128], replicated, may hold values from -0.046875 to 0.046875
- kernel_radii: int32 [24], replicated, may hold values from 16 to 64, as said below
- kernel_group: int32 [24], replicated, may hold values from 0 to 2, as said below
- kernel_weight: float32 [24], replicated, may hold values from 0.1 to 1
Outputs:
- resist: float32 [3, 4096, 128], P(None, ('win', 'row')), parts along dimension 1
- gradient: float32 [2, 4096, 128], P(None, ('win', 'row')), parts along dimension 1
There are 2 independent parts, one for each index of `win`. A program takes and returns all parts, laid end to end along the dimension named above; an argument that names none is the same for every part. Nothing has to cross between parts.
Inputs may be any that keep to these rules, and one draw needn't show every extreme that they name: `kernel_radii`: every radius lies in 16 to 64; some kernel has radius exactly 64 and some exactly 16. `kernel_group`: every one of the 3 process conditions holds at least one kernel.
All inputs are finite; a program needn't handle non-finite values. No bound on the sum of `target` on one device may be relied on, other than what follows from the above.
Results may differ from a plain program's by a relative error of at most 0.0003.
Values sent between devices are 32-bit elements; how exact they have to be, the bound alone decides.
No kernel may reach another device: no remote copies, remote signals or barrier semaphores. Data moves between devices by JAX's collectives and lax.ppermute only.
A program may use at most 128 MiB of HBM per device.

v0:
```python
import math

import jax
import jax.numpy as jnp
import ml_dtypes
import numpy as np
from jax import lax
from jax.experimental import pallas as pl
from jax.experimental.pallas import tpu as pltpu
from jax.sharding import PartitionSpec as P

RMAX = 64
GROUPS = 3
STEEPNESS = 1.0
THRESHOLD = 2.0

f32 = jnp.float32
bf16 = jnp.bfloat16


def halves(table):
    high = table.astype(ml_dtypes.bfloat16)
    low = (table - high.astype(np.float64)).astype(ml_dtypes.bfloat16)
    return np.concatenate([high, low], axis=1)


def analysis(freqs, points, shift):
    f = np.arange(freqs)[:, None]
    n = np.arange(points)[None, :] - shift
    angle = 2.0 * math.pi * ((f * n) % freqs) / freqs
    cos, sin = np.cos(angle), np.sin(angle)
    return np.block([[cos, sin], [-sin, cos]])


def synthesis(freqs, points, shift, scale=1.0):
    return analysis(freqs, points, shift).T * scale


def split(x):
    high = x.astype(bf16)
    low = (x - high.astype(f32)).astype(bf16)
    return high, low


def apply_rows(table, high, low):
    depth = high.shape[0]
    left = table[...]
    left = jnp.concatenate([left, left[:, :depth]], axis=1)
    right = jnp.concatenate([high, high, low], axis=0)
    return lax.dot_general(left, right, (((1,), (0,)), ((), ())), preferred_element_type=f32)


def apply_lanes(table, high, low):
    depth = high.shape[1]
    left = table[...]
    left = jnp.concatenate([left, left[:, :depth]], axis=1)
    right = jnp.concatenate([high, high, low], axis=1)
    return lax.dot_general(left, right, (((1,), (1,)), ((), ())), preferred_element_type=f32)


def side(x, rows):
    return jnp.concatenate([x[:rows], x[rows:]], axis=1)


def body(
    radii, group, weight,
    own, above, below, target, taps,
    row_tab, col_tab, col_inv, row_inv, mask_row, mask_col, grad_col, grad_row,
    resist, grad_own, grad_up, grad_down,
    spec, field, mask_spec, slopes, grad_spec,
):
    kernels, _, span, _ = taps.shape
    count, width = target.shape
    grid_rows = row_tab.shape[0] // 2
    grid_cols = col_tab.shape[0] // 2
    rim = above.shape[1]

    mask = jnp.concatenate([above[0], own[0], below[0], above[1], own[1], below[1]], axis=0)
    half = apply_rows(mask_row, *split(mask))
    mask_spec[...] = apply_lanes(mask_col, *split(side(half, grid_rows)))

    slopes[...] = jnp.zeros(slopes.shape, f32)
    grad_spec[...] = jnp.zeros(grad_spec.shape, f32)

    def spectra(pair):
        half = apply_rows(row_tab, *split(pair))
        out = []
        for j in range(2):
            mine = side(half[:, j * width:(j + 1) * width], grid_rows)
            out.append(apply_lanes(col_tab, *split(mine)))
        return out

    row_at = lax.broadcasted_iota(jnp.int32, (2 * span, span), 0) % span - span // 2
    col_at = lax.broadcasted_iota(jnp.int32, (2 * span, span), 1) - span // 2

    def forward(i, carry):
        planes = []
        for j in range(2):
            k = 2 * i + j
            r = radii[k]
            inside = (row_at >= -r) & (row_at < r) & (col_at >= -r) & (col_at < r)
            planes.append(jnp.where(inside, taps[k].reshape(2 * span, span), 0.0))
        found = spectra(jnp.concatenate(planes, axis=1))
        backs = []
        for j in range(2):
            spec[2 * i + j] = found[j]
            s_re, s_im = found[j][:grid_cols], found[j][grid_cols:]
            m_re, m_im = mask_spec[:grid_cols], mask_spec[grid_cols:]
            product = jnp.concatenate([s_re * m_re - s_im * m_im, s_re * m_im + s_im * m_re], axis=0)
            back = apply_rows(col_inv, *split(product))
            backs.append(side(back, width))
        pair = apply_lanes(row_inv, *split(jnp.concatenate(backs, axis=0)))
        field[i] = pair
        power = pair[:count] * pair[:count] + pair[count:] * pair[count:]
        for j in range(2):
            k = 2 * i + j
            g = group[k]
            slopes[g] = slopes[g] + weight[k] * power[:, j * width:(j + 1) * width]
        return carry

    lax.fori_loop(0, kernels // 2, forward, 0)

    wanted = target[...].astype(f32)
    for g in range(GROUPS):
        seen = jax.nn.sigmoid(STEEPNESS * (slopes[g] - THRESHOLD))
        resist[g] = seen
        slopes[g] = 2.0 * (seen - wanted) * seen * (1.0 - seen) * STEEPNESS

    def backward(i, carry):
        factors = []
        for j in range(2):
            k = 2 * i + j
            factors.append((2.0 * weight[k]) * slopes[group[k]])
        factor = jnp.concatenate(factors, axis=1)
        cot = field[i] * jnp.concatenate([factor, factor], axis=0)
        found = spectra(cot)
        total_re = grad_spec[:grid_cols]
        total_im = grad_spec[grid_cols:]
        for j in range(2):
            s_re, s_im = spec[2 * i + j, :grid_cols], spec[2 * i + j, grid_cols:]
            c_re, c_im = found[j][:grid_cols], found[j][grid_cols:]
            total_re = total_re + (s_re * c_re + s_im * c_im)
            total_im = total_im + (s_re * c_im - s_im * c_re)
        grad_spec[:grid_cols] = total_re
        grad_spec[grid_cols:] = total_im
        return carry

    lax.fori_loop(0, kernels // 2, backward, 0)

    back = apply_rows(grad_col, *split(grad_spec[...]))
    full = apply_lanes(grad_row, *split(side(back, width)))
    for c in range(2):
        base = c * grid_rows
        grad_up[c] = full[base:base + rim]
        grad_own[c] = full[base + rim:base + rim + count]
        grad_down[c] = full[base + rim + count:base + grid_rows]


def on_device(mask_field, target, kernel_taps, kernel_radii, kernel_group, kernel_weight):
    _, count, width = mask_field.shape
    kernels, _, span, _ = kernel_taps.shape
    rim = span // 2
    grid_rows = count + 2 * rim
    grid_cols = width + rim
    assert count == span and width == span and kernels % 2 == 0

    strips = lax.axis_size("row")
    down = [(i, i + 1) for i in range(strips - 1)]
    up = [(i + 1, i) for i in range(strips - 1)]
    above = lax.ppermute(mask_field[:, count - rim:], "row", down)
    below = lax.ppermute(mask_field[:, :rim], "row", up)

    scale = 1.0 / (grid_rows * grid_cols)
    tables = [
        analysis(grid_rows, span, 0),
        analysis(grid_cols, span, 0),
        synthesis(grid_cols, width, 0),
        synthesis(grid_rows, count, 0, scale),
        analysis(grid_rows, grid_rows, 2 * rim),
        analysis(grid_cols, width, rim),
        synthesis(grid_cols, width, rim),
        synthesis(grid_rows, grid_rows, 2 * rim, scale),
    ]
    tables = [jnp.asarray(halves(t)) for t in tables]

    smem = pl.BlockSpec(memory_space=pltpu.SMEM)
    vmem = pl.BlockSpec(memory_space=pltpu.VMEM)
    resist, own, up_rim, down_rim = pl.pallas_call(
        body,
        out_shape=[
            jax.ShapeDtypeStruct((GROUPS, count, width), f32),
            jax.ShapeDtypeStruct((2, count, width), f32),
            jax.ShapeDtypeStruct((2, rim, width), f32),
            jax.ShapeDtypeStruct((2, rim, width), f32),
        ],
        in_specs=[smem] * 3 + [vmem] * 13,
        out_specs=[vmem] * 4,
        scratch_shapes=[
            pltpu.VMEM((kernels, 2 * grid_cols, grid_rows), f32),
            pltpu.VMEM((kernels // 2, 2 * count, 2 * width), f32),
            pltpu.VMEM((2 * grid_cols, grid_rows), f32),
            pltpu.VMEM((GROUPS, count, width), f32),
            pltpu.VMEM((2 * grid_cols, grid_rows), f32),
        ],
        compiler_params=pltpu.CompilerParams(vmem_limit_bytes=56 * 1024 * 1024),
        name="socs",
    )(kernel_radii, kernel_group, kernel_weight, mask_field, above, below, target, kernel_taps, *tables)

    from_below = lax.ppermute(up_rim, "row", up)
    from_above = lax.ppermute(down_rim, "row", down)
    gradient = jnp.concatenate([own[:, :rim] + from_above, own[:, rim:] + from_below], axis=1)
    return resist, gradient


def solution(mesh):
    in_specs = (P(None, ("win", "row"), None), P(("win", "row"), None), P(), P(), P(), P())
    out_specs = (P(None, ("win", "row"), None), P(None, ("win", "row"), None))
    return jax.shard_map(
        on_device, mesh=mesh, in_specs=in_specs, out_specs=out_specs, check_vma=False
    )
```

profile of v0, /device:TPU:21, one launch (start us, length us, event | category | flops | bytes accessed | tf_op | source)
XLA Modules:
  0.0 71.1 jit_solution(7700448014999594676)
XLA Ops:
  0.6 0.9 %fusion = (f32[2,64,128]{2,1,0:T(8,128)S(1)}, f32[2,64,128]{2,1,0:T(8,128)S(1)}) fusion(f32[2,128,128]{2,1,0:T(8,128)} %own.1), kind=kLoop, calls=%fused_computation.3 | loop fusion | bytes 262144 | tf_op jit(solution)/shard_map/slice | solution.py:171
  1.5 2.6 %collective-permute-start.1 = (f32[2,64,128]{2,1,0:T(8,128)S(1)}, f32[2,64,128]{2,1,0:T(8,128)S(1)}, u32[]{:S(2)}, u32[]{:S(2)}) collective-permute-start(f32[2,64,128]{2,1,0:T(8,128)S(1)} %get-tuple-element.12), channel_id=1, source_target_pairs={{1,0},{2,1},{3,2},{4,3},{5,4},{6,5},{7,6},{8,7},{9,8},{10,9},{11,1... | collective-permute-start | bytes 196616 | tf_op jit(solution)/shard_map/ppermute | solution.py:171
  4.1 3.9 %collective-permute-start = (f32[2,64,128]{2,1,0:T(8,128)S(1)}, f32[2,64,128]{2,1,0:T(8,128)S(1)}, u32[]{:S(2)}, u32[]{:S(2)}) collective-permute-start(f32[2,64,128]{2,1,0:T(8,128)S(1)} %get-tuple-element.13), channel_id=1, source_target_pairs={{0,1},{1,2},{2,3},{3,4},{4,5},{5,6},{6,7},{7,8},{8,9},{9,10},{10,1... | collective-permute-start | bytes 196616 | tf_op jit(solution)/shard_map/ppermute | solution.py:170
  8.0 0.0 collective-permute-done.1.below
  8.0 0.0 copy-start
  8.0 1.3 %collective-permute-done.above = f32[2,64,128]{2,1,0:T(8,128)S(1)} collective-permute-done((f32[2,64,128]{2,1,0:T(8,128)S(1)}, f32[2,64,128]{2,1,0:T(8,128)S(1)}, u32[]{:S(2)}, u32[]{:S(2)}) %collective-permute-start) | collective-permute-done | bytes 65568 | tf_op jit(solution)/shard_map/ppermute | solution.py:170
  9.3 0.0 copy-done
  9.3 0.0 copy-start.1
  9.3 0.6 copy-done.1
  9.9 47.8 %socs.1 = (f32[3,128,128]{2,1,0:T(8,128)}, f32[2,128,128]{2,1,0:T(8,128)}, f32[2,64,128]{2,1,0:T(8,128)}, f32[2,64,128]{2,1,0:T(8,128)}) custom-call(s32[24]{0:T(128)} %radii.1, s32[24]{0:T(128)} %group.1, f32[24]{0:T(128)} %weight.1, f32[2,128,128]{2,1,0:T(8,128)} %own.1, f32[2,64,128]{2,1,0:T(8,128)} %copy-done.1, f32[2,64,128]{2,1,0:T(8,128)} %copy-done, ...), custom_call_target="tpu_custom_call" | custom-call | tf_op jit(solution)/shard_map/socs/pallas_call | solution.py:188
  57.7 5.2 %collective-permute-start.2 = (f32[2,64,128]{2,1,0:T(8,128)}, f32[2,64,128]{2,1,0:T(8,128)S(1)}, u32[]{:S(2)}, u32[]{:S(2)}) collective-permute-start(f32[2,64,128]{2,1,0:T(8,128)} %get-tuple-element.8), channel_id=1, source_target_pairs={{0,1},{1,2},{2,3},{3,4},{4,5},{5,6},{6,7},{7,8},{8,9},{9,10},{10,1... | collective-permute-start | bytes 196616 | tf_op jit(solution)/shard_map/ppermute | solution.py:210
  62.9 1.9 %collective-permute-start.3 = (f32[2,64,128]{2,1,0:T(8,128)}, f32[2,64,128]{2,1,0:T(8,128)S(1)}, u32[]{:S(2)}, u32[]{:S(2)}) collective-permute-start(f32[2,64,128]{2,1,0:T(8,128)} %get-tuple-element.9), channel_id=1, source_target_pairs={{1,0},{2,1},{3,2},{4,3},{5,4},{6,5},{7,6},{8,7},{9,8},{10,9},{11,1... | collective-permute-start | bytes 196616 | tf_op jit(solution)/shard_map/ppermute | solution.py:209
  64.8 0.0 collective-permute-done.2
  64.8 4.8 %collective-permute-done.3 = f32[2,64,128]{2,1,0:T(8,128)S(1)} collective-permute-done((f32[2,64,128]{2,1,0:T(8,128)}, f32[2,64,128]{2,1,0:T(8,128)S(1)}, u32[]{:S(2)}, u32[]{:S(2)}) %collective-permute-start.3) | collective-permute-done | bytes 65568 | tf_op jit(solution)/shard_map/ppermute | solution.py:209
  69.5 0.9 %slice_add_fusion.1 = (f32[2,64,128]{2,1,0:T(8,128)S(1)}, f32[2,64,128]{2,1,0:T(8,128)S(1)}) fusion(f32[2,64,128]{2,1,0:T(8,128)S(1)} %collective-permute-done.2, f32[2,128,128]{2,1,0:T(8,128)} %get-tuple-element.7, f32[2,64,128]{2,1,0:T(8,128)S(1)} %collective-permute-done.3), kind=kLoop, calls=%fused_computation.2 | loop fusion | flops 32768 | bytes 393216 | tf_op jit(solution)/shard_map/add | solution.py:211
  70.4 0.7 pad_maximum_fusion
Async XLA Ops:
  1.5 6.5 %collective-permute-start.1 = (f32[2,64,128]{2,1,0:T(8,128)S(1)}, f32[2,64,128]{2,1,0:T(8,128)S(1)}, u32[]{:S(2)}, u32[]{:S(2)}) collective-permute-start(f32[2,64,128]{2,1,0:T(8,128)S(1)} %get-tuple-element.12), channel_id=1, source_target_pairs={{1,0},{2,1},{3,2},{4,3},{5,4},{6,5},{7,6},{8,7},{9,8},{10,9},{11,1... | collective-permute-start | bytes 196616 | tf_op jit(solution)/shard_map/ppermute | solution.py:171
  4.1 5.2 %collective-permute-start = (f32[2,64,128]{2,1,0:T(8,128)S(1)}, f32[2,64,128]{2,1,0:T(8,128)S(1)}, u32[]{:S(2)}, u32[]{:S(2)}) collective-permute-start(f32[2,64,128]{2,1,0:T(8,128)S(1)} %get-tuple-element.13), channel_id=1, source_target_pairs={{0,1},{1,2},{2,3},{3,4},{4,5},{5,6},{6,7},{7,8},{8,9},{9,10},{10,1... | collective-permute-start | bytes 196616 | tf_op jit(solution)/shard_map/ppermute | solution.py:170
  8.0 1.3 %copy-start = (f32[2,64,128]{2,1,0:T(8,128)}, f32[2,64,128]{2,1,0:T(8,128)S(1)}, u32[]{:S(2)}) copy-start(f32[2,64,128]{2,1,0:T(8,128)S(1)} %collective-permute-done.1.below) | copy-start | bytes 196612
  9.3 0.6 copy-start.1
  57.7 7.1 %collective-permute-start.2 = (f32[2,64,128]{2,1,0:T(8,128)}, f32[2,64,128]{2,1,0:T(8,128)S(1)}, u32[]{:S(2)}, u32[]{:S(2)}) collective-permute-start(f32[2,64,128]{2,1,0:T(8,128)} %get-tuple-element.8), channel_id=1, source_target_pairs={{0,1},{1,2},{2,3},{3,4},{4,5},{5,6},{6,7},{7,8},{8,9},{9,10},{10,1... | collective-permute-start | bytes 196616 | tf_op jit(solution)/shard_map/ppermute | solution.py:210
  62.9 6.7 %collective-permute-start.3 = (f32[2,64,128]{2,1,0:T(8,128)}, f32[2,64,128]{2,1,0:T(8,128)S(1)}, u32[]{:S(2)}, u32[]{:S(2)}) collective-permute-start(f32[2,64,128]{2,1,0:T(8,128)} %get-tuple-element.9), channel_id=1, source_target_pairs={{1,0},{2,1},{3,2},{4,3},{5,4},{6,5},{7,6},{8,7},{9,8},{10,9},{11,1... | collective-permute-start | bytes 196616 | tf_op jit(solution)/shard_map/ppermute | solution.py:209
where the time goes:
time: 71.4 us; the launch traced here: 71.1 us
  Pallas kernels  47.8 us (67%)
  starting transfers between devices  13.5 us (19%)
  waiting for transfers between devices  6.05 us (8%)
  other arithmetic  1.56 us (2%)
  local copies, waits for them, and re-layouts  1.52 us (2%)
    pallas_call x1, Pallas kernels, on_device(): pl.pallas_call(body, out_shape=[jax.ShapeDtypeStruct((GROUPS, count, widt...  47.8 us
    ppermute x1, starting transfers between devices, on_device(): from_above = lax.ppermute(down_rim, 'row', down)  5.15 us
    ppermute x1, waiting for transfers between devices, on_device(): from_below = lax.ppermute(up_rim, 'row', up)  4.76 us
    ppermute x1, starting transfers between devices, on_device(): above = lax.ppermute(mask_field[:, count - rim:], 'row', down)  3.88 us
    ppermute x1, starting transfers between devices, on_device(): below = lax.ppermute(mask_field[:, :rim], 'row', up)  2.58 us
    ppermute x1, starting transfers between devices, on_device(): from_below = lax.ppermute(up_rim, 'row', up)  1.92 us
  transfers between devices with their start and end apart: 4, of which 2 were waited for; matrix products, arithmetic and copies ran while one was open for 0% of the time, Pallas kernels for 0%

commit v1 on v0

v1 whole, which is shorter than its diff:
```python
import math

import jax
import jax.numpy as jnp
import ml_dtypes
import numpy as np
from jax import lax
from jax.experimental import pallas as pl
from jax.experimental.pallas import tpu as pltpu
from jax.sharding import PartitionSpec as P

RMAX = 64
GROUPS = 3
STEEPNESS = 1.0
THRESHOLD = 2.0
BATCH = 4

f32 = jnp.float32
bf16 = jnp.bfloat16


def halves(table):
    high = table.astype(ml_dtypes.bfloat16)
    low = (table - high.astype(np.float64)).astype(ml_dtypes.bfloat16)
    return np.concatenate([high, low], axis=1)


def analysis(freqs, points, shift):
    f = np.arange(freqs)[:, None]
    n = np.arange(points)[None, :] - shift
    angle = 2.0 * math.pi * ((f * n) % freqs) / freqs
    cos, sin = np.cos(angle), np.sin(angle)
    return np.block([[cos, sin], [-sin, cos]])


def synthesis(freqs, points, shift, scale=1.0):
    return analysis(freqs, points, shift).T * scale


def split(x):
    high = x.astype(bf16)
    low = (x - high.astype(f32)).astype(bf16)
    return high, low


def apply_rows(table, high, low):
    depth = high.shape[0]
    left = table[...]
    left = jnp.concatenate([left, left[:, :depth]], axis=1)
    right = jnp.concatenate([high, high, low], axis=0)
    return lax.dot_general(left, right, (((1,), (0,)), ((), ())), preferred_element_type=f32)


def apply_lanes(table, high, low):
    depth = high.shape[1]
    left = table[...]
    left = jnp.concatenate([left, left[:, :depth]], axis=1)
    right = jnp.concatenate([high, high, low], axis=1)
    return lax.dot_general(left, right, (((1,), (1,)), ((), ())), preferred_element_type=f32)


def side(x, rows):
    return jnp.concatenate([x[:rows], x[rows:]], axis=1)


def dft_pair(pair, row_tab, col_tab):
    width = pair.shape[1] // 2
    grid_rows = row_tab.shape[0] // 2
    half = apply_rows(row_tab, *split(pair))
    out = []
    for j in range(2):
        mine = side(half[:, j * width:(j + 1) * width], grid_rows)
        out.append(apply_lanes(col_tab, *split(mine)))
    return out


def spectra_body(radii, taps, row_tab, col_tab, spec):
    batch, _, span, _ = taps.shape
    first = pl.program_id(0) * batch
    row_at = lax.broadcasted_iota(jnp.int32, (span, span), 0) - span // 2
    col_at = lax.broadcasted_iota(jnp.int32, (span, span), 1) - span // 2
    reach = jnp.maximum(jnp.maximum(row_at, -1 - row_at), jnp.maximum(col_at, -1 - col_at))
    for i in range(batch // 2):
        planes = []
        for j in range(2):
            k = 2 * i + j
            inside = reach < radii[first + k]
            parts = [jnp.where(inside, taps[k, c], 0.0) for c in range(2)]
            planes.append(jnp.concatenate(parts, axis=0))
        found = dft_pair(jnp.concatenate(planes, axis=1), row_tab, col_tab)
        for j in range(2):
            spec[2 * i + j] = found[j]


def main_body(
    group, weight,
    own, above, below, target, spec_far,
    row_tab, col_tab, col_inv, row_inv, mask_row, mask_col, grad_col, grad_row,
    resist, grad_own, grad_up, grad_down,
    spec, field, mask_spec, slopes, grad_spec, sems,
):
    kernels = spec.shape[0]
    count, width = target.shape
    grid_rows = row_tab.shape[0] // 2
    grid_cols = col_tab.shape[0] // 2
    rim = (grid_rows - count) // 2
    steps = sems.shape[0]
    batch = kernels // steps

    def fetch(i):
        here = pl.ds(i * batch, batch)
        return pltpu.make_async_copy(spec_far.at[here], spec.at[here], sems.at[i])

    for i in range(steps):
        fetch(i).start()

    mask = jnp.concatenate(
        [part for c in range(2) for part in (above[c, count - rim:], own[c], below[c, :rim])], axis=0
    )
    half = apply_rows(mask_row, *split(mask))
    mask_spec[...] = apply_lanes(mask_col, *split(side(half, grid_rows)))

    slopes[...] = jnp.zeros(slopes.shape, f32)
    grad_spec[...] = jnp.zeros(grad_spec.shape, f32)

    def forward(i, carry):
        fetch(i).wait()
        powers = []
        for p in range(batch // 2):
            backs = []
            for j in range(2):
                k = i * batch + 2 * p + j
                s_re, s_im = spec[k, :grid_cols], spec[k, grid_cols:]
                m_re, m_im = mask_spec[:grid_cols], mask_spec[grid_cols:]
                product = jnp.concatenate([s_re * m_re - s_im * m_im, s_re * m_im + s_im * m_re], axis=0)
                back = apply_rows(col_inv, *split(product))
                backs.append(side(back, width))
            pair = apply_lanes(row_inv, *split(jnp.concatenate(backs, axis=0)))
            field[i * (batch // 2) + p] = pair
            powers.append(pair[:count] * pair[:count] + pair[count:] * pair[count:])
        for p in range(batch // 2):
            for j in range(2):
                k = i * batch + 2 * p + j
                g = group[k]
                slopes[g] = slopes[g] + weight[k] * powers[p][:, j * width:(j + 1) * width]
        return carry

    lax.fori_loop(0, steps, forward, 0)

    wanted = target[...].astype(f32)
    for g in range(GROUPS):
        seen = jax.nn.sigmoid(STEEPNESS * (slopes[g] - THRESHOLD))
        resist[g] = seen
        slopes[g] = 2.0 * (seen - wanted) * seen * (1.0 - seen) * STEEPNESS

    def backward(i, carry):
        total_re = grad_spec[:grid_cols]
        total_im = grad_spec[grid_cols:]
        for p in range(batch // 2):
            factors = []
            for j in range(2):
                k = i * batch + 2 * p + j
                factors.append((2.0 * weight[k]) * slopes[group[k]])
            factor = jnp.concatenate(factors, axis=1)
            cot = field[i * (batch // 2) + p] * jnp.concatenate([factor, factor], axis=0)
            found = dft_pair(cot, row_tab, col_tab)
            for j in range(2):
                k = i * batch + 2 * p + j
                s_re, s_im = spec[k, :grid_cols], spec[k, grid_cols:]
                c_re, c_im = found[j][:grid_cols], found[j][grid_cols:]
                total_re = total_re + (s_re * c_re + s_im * c_im)
                total_im = total_im + (s_re * c_im - s_im * c_re)
        grad_spec[:grid_cols] = total_re
        grad_spec[grid_cols:] = total_im
        return carry

    lax.fori_loop(0, steps, backward, 0)

    back = apply_rows(grad_col, *split(grad_spec[...]))
    full = apply_lanes(grad_row, *split(side(back, width)))
    for c in range(2):
        base = c * grid_rows
        grad_up[c] = full[base:base + rim]
        grad_own[c] = full[base + rim:base + rim + count]
        grad_down[c] = full[base + rim + count:base + grid_rows]


def on_device(mask_field, target, kernel_taps, kernel_radii, kernel_group, kernel_weight):
    _, count, width = mask_field.shape
    kernels, _, span, _ = kernel_taps.shape
    rim = span // 2
    grid_rows = count + 2 * rim
    grid_cols = width + rim
    assert count == span and width == span and kernels % 2 == 0

    assert kernels % BATCH == 0 and BATCH % 2 == 0

    strips = lax.axis_size("row")
    down = [(i, i + 1) for i in range(strips - 1)]
    up = [(i + 1, i) for i in range(strips - 1)]
    above = lax.ppermute(mask_field, "row", down)
    below = lax.ppermute(mask_field, "row", up)

    scale = 1.0 / (grid_rows * grid_cols)
    tables = [
        analysis(grid_rows, span, 0),
        analysis(grid_cols, span, 0),
        synthesis(grid_cols, width, 0),
        synthesis(grid_rows, count, 0, scale),
        analysis(grid_rows, grid_rows, 2 * rim),
        analysis(grid_cols, width, rim),
        synthesis(grid_cols, width, rim),
        synthesis(grid_rows, grid_rows, 2 * rim, scale),
    ]
    tables = [jnp.asarray(halves(t)) for t in tables]

    smem = pl.BlockSpec(memory_space=pltpu.SMEM)
    vmem = pl.BlockSpec(memory_space=pltpu.VMEM)
    spectra = pl.pallas_call(
        spectra_body,
        grid=(kernels // BATCH,),
        out_shape=jax.ShapeDtypeStruct((kernels, 2 * grid_cols, grid_rows), f32),
        in_specs=[smem, pl.BlockSpec((BATCH, 2, span, span), lambda i: (i, 0, 0, 0)), vmem, vmem],
        out_specs=pl.BlockSpec((BATCH, 2 * grid_cols, grid_rows), lambda i: (i, 0, 0)),
        compiler_params=pltpu.CompilerParams(vmem_limit_bytes=24 * 1024 * 1024),
        cost_estimate=pl.CostEstimate(flops=18 * 10**9, bytes_accessed=14 * 10**6, transcendentals=0),
        name="spectra",
    )(kernel_radii, kernel_taps, tables[0], tables[1])

    resist, own, up_rim, down_rim = pl.pallas_call(
        main_body,
        out_shape=[
            jax.ShapeDtypeStruct((GROUPS, count, width), f32),
            jax.ShapeDtypeStruct((2, count, width), f32),
            jax.ShapeDtypeStruct((2, rim, width), f32),
            jax.ShapeDtypeStruct((2, rim, width), f32),
        ],
        in_specs=[smem] * 2 + [vmem] * 4 + [pl.BlockSpec(memory_space=pl.ANY)] + [vmem] * 8,
        out_specs=[vmem] * 4,
        scratch_shapes=[
            pltpu.VMEM((kernels, 2 * grid_cols, grid_rows), f32),
            pltpu.VMEM((kernels // 2, 2 * count, 2 * width), f32),
            pltpu.VMEM((2 * grid_cols, grid_rows), f32),
            pltpu.VMEM((GROUPS, count, width), f32),
            pltpu.VMEM((2 * grid_cols, grid_rows), f32),
            pltpu.SemaphoreType.DMA((kernels // BATCH,)),
        ],
        compiler_params=pltpu.CompilerParams(vmem_limit_bytes=56 * 1024 * 1024),
        name="fields",
    )(kernel_group, kernel_weight, mask_field, above, below, target, spectra, *tables)

    from_below = lax.ppermute(up_rim, "row", up)
    from_above = lax.ppermute(down_rim, "row", down)
    gradient = (
        own
        + jnp.pad(from_above, ((0, 0), (0, count - rim), (0, 0)))
        + jnp.pad(from_below, ((0, 0), (count - rim, 0), (0, 0)))
    )
    return resist, gradient


def solution(mesh):
    in_specs = (P(None, ("win", "row"), None), P(("win", "row"), None), P(), P(), P(), P())
    out_specs = (P(None, ("win", "row"), None), P(None, ("win", "row"), None))
    return jax.shard_map(
        on_device, mesh=mesh, in_specs=in_specs, out_specs=out_specs, check_vma=False
    )
```

time: 71.4 us -> 65.2 us (0.913)
  Pallas kernels: 47.8 us -> 36.2 us
  local copies, waits for them, and re-layouts: 1.52 us -> 9.5 us
  starting transfers between devices: 13.5 us -> 12.1 us
  waiting for transfers between devices: 6.05 us -> 4.76 us
    pallas_call x1 -> x2, Pallas kernels: 47.8 us -> 36.2 us  [the longest x1 26.4 us: on_device(): pl.pallas_call(main_body, out_shape=[jax.ShapeDtypeStruct((GROUPS, count,...]
    unnamed x4 -> x14, local copies, waits for them, and re-layouts: 0.64 us -> 9.5 us
    ppermute x2, waiting for transfers between devices: 1.3 us -> 0.01 us  [the longest x1 0.01 us: on_device(): above = lax.ppermute(mask_field, 'row', down)]
    slice x1 -> x0, local copies, waits for them, and re-layouts: 0.89 us -> none  [on_device(): below = lax.ppermute(mask_field[:, :rim], 'row', up)]
    ppermute x2, starting transfers between devices: 6.46 us -> 5.63 us  [the longest x1 3.71 us: on_device(): above = lax.ppermute(mask_field, 'row', down)]
  transfers between devices with their start and end apart: 4 -> 4, of which waited for: 2 -> 1; matrix products, arithmetic and copies ran while one was open for 0% -> 0% of each run, Pallas kernels for 0% -> 15%
where the time goes in v1:
time: 65.2 us; the launch traced here: 64.9 us
  Pallas kernels  36.2 us (56%)
  starting transfers between devices  12.1 us (19%)
  local copies, waits for them, and re-layouts  9.5 us (15%)
  waiting for transfers between devices  4.76 us (7%)
  other arithmetic  1.58 us (2%)
  between operations  0.71 us (1%)
    pallas_call x1, Pallas kernels, on_device(): pl.pallas_call(main_body, out_shape=[jax.ShapeDtypeStruct((GROUPS, count,...  26.4 us
    pallas_call x1, Pallas kernels, on_device(): pl.pallas_call(spectra_body, grid=(kernels // BATCH,), out_shape=jax.Shap...  9.8 us
    unnamed x14, local copies, waits for them, and re-layouts  9.5 us
    ppermute x1, waiting for transfers between devices, on_device(): from_below = lax.ppermute(up_rim, 'row', up)  4.76 us
    ppermute x1, starting transfers between devices, on_device(): from_above = lax.ppermute(down_rim, 'row', down)  4.54 us
    ppermute x1, starting transfers between devices, on_device(): above = lax.ppermute(mask_field, 'row', down)  3.71 us
    ppermute x1, starting transfers between devices, on_device(): below = lax.ppermute(mask_field, 'row', up)  1.92 us
    ppermute x1, starting transfers between devices, on_device(): from_below = lax.ppermute(up_rim, 'row', up)  1.92 us
  transfers between devices with their start and end apart: 4, of which 1 were waited for; matrix products, arithmetic and copies ran while one was open for 0% of the time, Pallas kernels for 15%

profile of v1, /device:TPU:21, one launch (start us, length us, event | category | flops | bytes accessed | tf_op | source)
XLA Modules:
  0.0 64.9 jit_solution(7772703628589708102)
XLA Ops:
  0.6 3.7 %collective-permute-start = (f32[2,128,128]{2,1,0:T(8,128)}, f32[2,128,128]{2,1,0:T(8,128)S(1)}, u32[]{:S(2)}, u32[]{:S(2)}) collective-permute-start(f32[2,128,128]{2,1,0:T(8,128)} %own.1), channel_id=1, source_target_pairs={{0,1},{1,2},{2,3},{3,4},{4,5},{5,6},{6,7},{7,8},{8,9},{9,10},{10,1... | collective-permute-start | bytes 393224 | tf_op jit(solution)/shard_map/ppermute | solution.py:201
  4.3 1.9 %collective-permute-start.1 = (f32[2,128,128]{2,1,0:T(8,128)}, f32[2,128,128]{2,1,0:T(8,128)S(1)}, u32[]{:S(2)}, u32[]{:S(2)}) collective-permute-start(f32[2,128,128]{2,1,0:T(8,128)} %own.1), channel_id=1, source_target_pairs={{1,0},{2,1},{3,2},{4,3},{5,4},{6,5},{7,6},{8,7},{9,8},{10,9},{11,1... | collective-permute-start | bytes 393224 | tf_op jit(solution)/shard_map/ppermute | solution.py:202
  6.3 0.0 copy-start.1
  6.3 1.0 %copy-done.1 = bf16[512,512]{1,0:T(8,128)(2,1)S(1)} copy-done((bf16[512,512]{1,0:T(8,128)(2,1)S(1)}, bf16[512,512]{1,0:T(8,128)(2,1)}, u32[]{:S(2)}) %copy-start.1) | copy-done | bytes 524312
  7.3 0.0 copy-start.2
  7.3 1.0 %copy-done.2 = bf16[384,512]{1,0:T(8,128)(2,1)S(1)} copy-done((bf16[384,512]{1,0:T(8,128)(2,1)S(1)}, bf16[384,512]{1,0:T(8,128)(2,1)}, u32[]{:S(2)}) %copy-start.2) | copy-done | bytes 393240
  8.3 0.0 copy-start.3
  8.3 1.9 %copy-done.3 = f32[24,2,128,128]{3,2,1,0:T(8,128)S(1)} copy-done((f32[24,2,128,128]{3,2,1,0:T(8,128)S(1)}, f32[24,2,128,128]{3,2,1,0:T(8,128)}, u32[]{:S(2)}) %copy-start.3) | copy-done | bytes 3145752
  10.2 0.0 copy-start.4
  10.2 0.7 %copy-done.4 = s32[24]{0:T(128)S(1)} copy-done((s32[24]{0:T(128)S(1)}, s32[24]{0:T(128)}, u32[]{:S(2)}) %copy-start.4) | copy-done | bytes 120
  10.9 9.8 %spectra.1.spec_far = f32[24,384,256]{2,1,0:T(8,128)S(1)} custom-call(s32[24]{0:T(128)S(1)} %copy-done.4, f32[24,2,128,128]{3,2,1,0:T(8,128)S(1)} %copy-done.3, bf16[512,512]{1,0:T(8,128)(2,1)S(1)} %copy-done.1, bf16[384,512]{1,0:T(8,128)(2,1)S(1)} %copy-done.2), custom_call_target="tpu_custom_call" | custom-call | flops 17999998976 | bytes 14000000 | tf_op jit(solution)/shard_map/spectra/pallas_call | solution.py:219
  20.7 0.0 copy-start
  20.7 3.6 %copy-done = f32[24,384,256]{2,1,0:T(8,128)} copy-done((f32[24,384,256]{2,1,0:T(8,128)}, f32[24,384,256]{2,1,0:T(8,128)S(1)}, u32[]{:S(2)}) %copy-start) | copy-done | bytes 9437208
  24.3 0.0 collective-permute-done.above
  24.3 0.0 copy-start.5
  24.3 0.0 collective-permute-done.1.below
  24.3 0.6 copy-done.5
  25.0 0.6 copy-done.6
  25.6 26.4 %fields.1 = (f32[3,128,128]{2,1,0:T(8,128)}, f32[2,128,128]{2,1,0:T(8,128)}, f32[2,64,128]{2,1,0:T(8,128)}, f32[2,64,128]{2,1,0:T(8,128)}) custom-call(s32[24]{0:T(128)} %group.1, f32[24]{0:T(128)} %weight.1, f32[2,128,128]{2,1,0:T(8,128)} %own.1, f32[2,128,128]{2,1,0:T(8,128)} %copy-done.5, f32[2,128,128]{2,1,0:T(8,128)} %copy-done.6, s32[128,128]{1,0:T(8,128)} %target.1, ...), custom_call_target="tpu_custom_call" | custom-call | tf_op jit(solution)/shard_map/fields/pallas_call | solution.py:230
  52.0 4.5 %collective-permute-start.2 = (f32[2,64,128]{2,1,0:T(8,128)}, f32[2,64,128]{2,1,0:T(8,128)S(1)}, u32[]{:S(2)}, u32[]{:S(2)}) collective-permute-start(f32[2,64,128]{2,1,0:T(8,128)} %get-tuple-element.8), channel_id=1, source_target_pairs={{0,1},{1,2},{2,3},{3,4},{4,5},{5,6},{6,7},{7,8},{8,9},{9,10},{10,1... | collective-permute-start | bytes 196616 | tf_op jit(solution)/shard_map/ppermute | solution.py:253
  56.6 1.9 %collective-permute-start.3 = (f32[2,64,128]{2,1,0:T(8,128)}, f32[2,64,128]{2,1,0:T(8,128)S(1)}, u32[]{:S(2)}, u32[]{:S(2)}) collective-permute-start(f32[2,64,128]{2,1,0:T(8,128)} %get-tuple-element.9), channel_id=1, source_target_pairs={{1,0},{2,1},{3,2},{4,3},{5,4},{6,5},{7,6},{8,7},{9,8},{10,9},{11,1... | collective-permute-start | bytes 196616 | tf_op jit(solution)/shard_map/ppermute | solution.py:252
  58.5 0.0 collective-permute-done.2
  58.5 4.8 %collective-permute-done.3 = f32[2,64,128]{2,1,0:T(8,128)S(1)} collective-permute-done((f32[2,64,128]{2,1,0:T(8,128)}, f32[2,64,128]{2,1,0:T(8,128)S(1)}, u32[]{:S(2)}, u32[]{:S(2)}) %collective-permute-start.3) | collective-permute-done | bytes 65568 | tf_op jit(solution)/shard_map/ppermute | solution.py:252
  63.3 1.6 %pad_add_fusion = f32[2,128,128]{2,1,0:T(8,128)} fusion(f32[2,64,128]{2,1,0:T(8,128)S(1)} %collective-permute-done.3, f32[2,128,128]{2,1,0:T(8,128)} %get-tuple-element.7, f32[2,64,128]{2,1,0:T(8,128)S(1)} %collective-permute-done.2), kind=kLoop, calls=%fused_computation | loop fusion | flops 65536 | bytes 393216 | tf_op jit(solution)/shard_map/add | solution.py:255
  (1 shorter events, 0.0 us)
Async XLA Ops:
  0.6 23.7 %collective-permute-start = (f32[2,128,128]{2,1,0:T(8,128)}, f32[2,128,128]{2,1,0:T(8,128)S(1)}, u32[]{:S(2)}, u32[]{:S(2)}) collective-permute-start(f32[2,128,128]{2,1,0:T(8,128)} %own.1), channel_id=1, source_target_pairs={{0,1},{1,2},{2,3},{3,4},{4,5},{5,6},{6,7},{7,8},{8,9},{9,10},{10,1... | collective-permute-start | bytes 393224 | tf_op jit(solution)/shard_map/ppermute | solution.py:201
  4.3 20.0 %collective-permute-start.1 = (f32[2,128,128]{2,1,0:T(8,128)}, f32[2,128,128]{2,1,0:T(8,128)S(1)}, u32[]{:S(2)}, u32[]{:S(2)}) collective-permute-start(f32[2,128,128]{2,1,0:T(8,128)} %own.1), channel_id=1, source_target_pairs={{1,0},{2,1},{3,2},{4,3},{5,4},{6,5},{7,6},{8,7},{9,8},{10,9},{11,1... | collective-permute-start | bytes 393224 | tf_op jit(solution)/shard_map/ppermute | solution.py:202
  6.3 1.0 %copy-start.1 = (bf16[512,512]{1,0:T(8,128)(2,1)S(1)}, bf16[512,512]{1,0:T(8,128)(2,1)}, u32[]{:S(2)}) copy-start(bf16[512,512]{1,0:T(8,128)(2,1)} %constant.19.clone.row_tab) | copy-start | bytes 1572868
  7.3 1.0 %copy-start.2 = (bf16[384,512]{1,0:T(8,128)(2,1)S(1)}, bf16[384,512]{1,0:T(8,128)(2,1)}, u32[]{:S(2)}) copy-start(bf16[384,512]{1,0:T(8,128)(2,1)} %constant.20.clone.col_tab) | copy-start | bytes 1179652
  8.3 1.9 %copy-start.3 = (f32[24,2,128,128]{3,2,1,0:T(8,128)S(1)}, f32[24,2,128,128]{3,2,1,0:T(8,128)}, u32[]{:S(2)}) copy-start(f32[24,2,128,128]{3,2,1,0:T(8,128)} %taps.1) | copy-start | bytes 9437188
  10.2 0.7 %copy-start.4 = (s32[24]{0:T(128)S(1)}, s32[24]{0:T(128)}, u32[]{:S(2)}) copy-start(s32[24]{0:T(128)} %radii.1) | copy-start | bytes 292
  20.7 3.6 %copy-start = (f32[24,384,256]{2,1,0:T(8,128)}, f32[24,384,256]{2,1,0:T(8,128)S(1)}, u32[]{:S(2)}) copy-start(f32[24,384,256]{2,1,0:T(8,128)S(1)} %spectra.1.spec_far) | copy-start | bytes 28311556
  24.3 0.7 %copy-start.5 = (f32[2,128,128]{2,1,0:T(8,128)}, f32[2,128,128]{2,1,0:T(8,128)S(1)}, u32[]{:S(2)}) copy-start(f32[2,128,128]{2,1,0:T(8,128)S(1)} %collective-permute-done.above) | copy-start | bytes 393220
  25.0 0.6 copy-start.6
  52.0 6.5 %collective-permute-start.2 = (f32[2,64,128]{2,1,0:T(8,128)}, f32[2,64,128]{2,1,0:T(8,128)S(1)}, u32[]{:S(2)}, u32[]{:S(2)}) collective-permute-start(f32[2,64,128]{2,1,0:T(8,128)} %get-tuple-element.8), channel_id=1, source_target_pairs={{0,1},{1,2},{2,3},{3,4},{4,5},{5,6},{6,7},{7,8},{8,9},{9,10},{10,1... | collective-permute-start | bytes 196616 | tf_op jit(solution)/shard_map/ppermute | solution.py:253
  56.6 6.7 %collective-permute-start.3 = (f32[2,64,128]{2,1,0:T(8,128)}, f32[2,64,128]{2,1,0:T(8,128)S(1)}, u32[]{:S(2)}, u32[]{:S(2)}) collective-permute-start(f32[2,64,128]{2,1,0:T(8,128)} %get-tuple-element.9), channel_id=1, source_target_pairs={{1,0},{2,1},{3,2},{4,3},{5,4},{6,5},{7,6},{8,7},{9,8},{10,9},{11,1... | collective-permute-start | bytes 196616 | tf_op jit(solution)/shard_map/ppermute | solution.py:252

commit v2 on v1

v2 whole, which is shorter than its diff:
```python
import math

import jax
import jax.numpy as jnp
import ml_dtypes
import numpy as np
from jax import lax
from jax.experimental import pallas as pl
from jax.experimental.pallas import tpu as pltpu
from jax.sharding import PartitionSpec as P

RMAX = 64
GROUPS = 3
STEEPNESS = 1.0
THRESHOLD = 2.0
BATCH = 4

f32 = jnp.float32
bf16 = jnp.bfloat16
MIB = 1024 * 1024


def halves(table, axis):
    high = table.astype(ml_dtypes.bfloat16)
    low = (table - high.astype(np.float64)).astype(ml_dtypes.bfloat16)
    return np.concatenate([high, low], axis=axis)


def analysis(freqs, points, shift):
    f = np.arange(freqs)[:, None]
    n = np.arange(points)[None, :] - shift
    angle = 2.0 * math.pi * ((f * n) % freqs) / freqs
    cos, sin = np.cos(angle), np.sin(angle)
    return np.block([[cos, sin], [-sin, cos]])


def synthesis(freqs, points, shift, scale=1.0):
    return analysis(freqs, points, shift).T * scale


def grouped(freqs, lanes):
    head, tail = np.arange(lanes), np.arange(lanes, freqs)
    return np.concatenate([head, freqs + head, tail, freqs + tail])


def split(x):
    high = x.astype(bf16)
    low = (x - high.astype(f32)).astype(bf16)
    return high, low


def dot(left, right):
    return jnp.dot(left, right, preferred_element_type=f32)


def over_rows(table, x):
    high, low = split(x)
    left = table[...]
    left = jnp.concatenate([left, left[:, :x.shape[0]]], axis=1)
    return dot(left, jnp.concatenate([high, high, low], axis=0))


def over_lanes(x, table):
    high, low = split(x)
    right = table[...]
    right = jnp.concatenate([right, right[:x.shape[1]]], axis=0)
    return dot(jnp.concatenate([high, high, low], axis=1), right)


def to_freqs(x, head, tail):
    high, low = split(x)
    depth = x.shape[1]
    right = head[...]
    right = jnp.concatenate([right, right[:depth]], axis=0)
    first = dot(jnp.concatenate([high, high, low], axis=1), right)
    right = tail[...]
    rest = dot(jnp.concatenate([high, low], axis=1), jnp.concatenate([right, right], axis=0))
    lanes = rest.shape[1] // 2
    return first, rest[:, :lanes] + rest[:, lanes:]


def side(x):
    rows = x.shape[0] // 2
    return jnp.concatenate([x[:rows], x[rows:]], axis=1)


def dft(pairs, row_tab, head, tail):
    tiles = []
    for pair in pairs:
        width = pair.shape[1] // 2
        half = over_rows(row_tab, pair)
        tiles += [side(half[:, :width]), side(half[:, width:])]
    rows = tiles[0].shape[0]
    first, rest = to_freqs(jnp.concatenate(tiles, axis=0), head, tail)
    return [(first[j * rows:(j + 1) * rows], rest[j * rows:(j + 1) * rows]) for j in range(len(tiles))]


def swap(x):
    return pltpu.roll(x, x.shape[1] // 2, 1)


def spectra_body(radii, taps, row_tab, head, tail, spec):
    batch, _, span, _ = taps.shape
    first = pl.program_id(0) * batch
    row_at = lax.broadcasted_iota(jnp.int32, (span, span), 0) - span // 2
    col_at = lax.broadcasted_iota(jnp.int32, (span, span), 1) - span // 2
    reach = jnp.maximum(jnp.maximum(row_at, -1 - row_at), jnp.maximum(col_at, -1 - col_at))
    pairs = []
    for i in range(batch // 2):
        planes = []
        for j in range(2):
            inside = reach < radii[first + 2 * i + j]
            parts = [jnp.where(inside, taps[2 * i + j, c], 0.0) for c in range(2)]
            planes.append(jnp.concatenate(parts, axis=0))
        pairs.append(jnp.concatenate(planes, axis=1))
    for k, (a, b) in enumerate(dft(pairs, row_tab, head, tail)):
        spec[k, :, :a.shape[1]] = a
        spec[k, :, a.shape[1]:] = b


def main_body(
    group, weight,
    own, above, below, target, mask_row, mask_head, mask_tail, spec_far, *rest,
):
    tables_far, rest = rest[:7], rest[7:]
    resist, grad_own, grad_up, grad_down = rest[:4]
    spec, field, mask_spec, slopes, grad_spec, spec_sems, table_sems = rest[4:11]
    tables = rest[11:]
    kernels, grid_rows, _ = spec.shape
    count, width = target.shape
    rim = (grid_rows - count) // 2
    steps = spec_sems.shape[0]
    batch = kernels // steps

    def fetch(i):
        here = pl.ds(i * batch, batch)
        return pltpu.make_async_copy(spec_far.at[here], spec.at[here], spec_sems.at[i])

    def fetch_table(i):
        return pltpu.make_async_copy(tables_far[i], tables[i], table_sems.at[i])

    col_inv, row_inv, row_tab, head, tail, grad_col, grad_row = tables
    for i in range(2):
        fetch_table(i).start()
    for i in range(steps):
        fetch(i).start()
    for i in range(2, 7):
        fetch_table(i).start()

    mask = jnp.concatenate(
        [part for c in range(2) for part in (above[c, count - rim:], own[c], below[c, :rim])], axis=0
    )
    m_first, m_rest = to_freqs(side(over_rows(mask_row, mask)), mask_head, mask_tail)
    lane = lax.broadcasted_iota(jnp.int32, m_rest.shape, 1)
    real_half = lane < m_rest.shape[1] // 2
    turned = swap(m_rest)
    mask_spec[:, :2 * width] = m_first
    mask_spec[:, 2 * width:3 * width] = jnp.where(real_half, m_rest, turned)
    mask_spec[:, 3 * width:] = jnp.where(real_half, -turned, m_rest)

    slopes[...] = jnp.zeros(slopes.shape, f32)
    grad_spec[...] = jnp.zeros(grad_spec.shape, f32)
    for i in range(2):
        fetch_table(i).wait()

    def forward(i, carry):
        fetch(i).wait()
        m_re, m_im = mask_spec[:, :width], mask_spec[:, width:2 * width]
        m_same, m_cross = mask_spec[:, 2 * width:3 * width], mask_spec[:, 3 * width:]
        products = []
        for j in range(batch):
            k = i * batch + j
            s_re, s_im, s_rest = spec[k, :, :width], spec[k, :, width:2 * width], spec[k, :, 2 * width:]
            products.append(jnp.concatenate([
                s_re * m_re - s_im * m_im,
                s_re * m_im + s_im * m_re,
                s_rest * m_same + swap(s_rest) * m_cross,
            ], axis=1))
        back = over_lanes(jnp.concatenate(products, axis=0), col_inv)
        for p in range(batch // 2):
            mine = []
            for c in range(2):
                planes = [back[(2 * p + j) * grid_rows:(2 * p + j + 1) * grid_rows, c * width:(c + 1) * width] for j in range(2)]
                mine.append(jnp.concatenate(planes, axis=1))
            pair = over_rows(row_inv, jnp.concatenate(mine, axis=0))
            field[i * (batch // 2) + p] = pair
            power = pair[:count] * pair[:count] + pair[count:] * pair[count:]
            for j in range(2):
                k = i * batch + 2 * p + j
                g = group[k]
                slopes[g] = slopes[g] + weight[k] * power[:, j * width:(j + 1) * width]
        return carry

    lax.fori_loop(0, steps, forward, 0)

    wanted = target[...].astype(f32)
    for g in range(GROUPS):
        seen = jax.nn.sigmoid(STEEPNESS * (slopes[g] - THRESHOLD))
        resist[g] = seen
        slopes[g] = 2.0 * (seen - wanted) * seen * (1.0 - seen) * STEEPNESS
    for i in range(2, 7):
        fetch_table(i).wait()

    def backward(i, carry):
        pairs = []
        for p in range(batch // 2):
            factors = []
            for j in range(2):
                k = i * batch + 2 * p + j
                factors.append((2.0 * weight[k]) * slopes[group[k]])
            factor = jnp.concatenate(factors, axis=1)
            pairs.append(field[i * (batch // 2) + p] * jnp.concatenate([factor, factor], axis=0))
        found = dft(pairs, row_tab, head, tail)
        total = [grad_spec[:, c * width:(c + 1) * width] for c in range(4)]
        for j in range(batch):
            k = i * batch + j
            s_re, s_im, s_rest = spec[k, :, :width], spec[k, :, width:2 * width], spec[k, :, 2 * width:]
            first, rest = found[j]
            c_re, c_im = first[:, :width], first[:, width:]
            total[0] = total[0] + (s_re * c_re + s_im * c_im)
            total[1] = total[1] + (s_re * c_im - s_im * c_re)
            total[2] = total[2] + s_rest * rest
            total[3] = total[3] + s_rest * swap(rest)
        for c in range(4):
            grad_spec[:, c * width:(c + 1) * width] = total[c]
        return carry

    lax.fori_loop(0, steps, backward, 0)

    same, cross = grad_spec[:, 2 * width:3 * width], grad_spec[:, 3 * width:]
    tail_sum = jnp.where(real_half, same + swap(same), swap(cross) - cross)
    total = jnp.concatenate([grad_spec[:, :2 * width], tail_sum], axis=1)
    back = over_lanes(total, grad_col)
    full = over_rows(grad_row, jnp.concatenate([back[:, :width], back[:, width:]], axis=0))
    for c in range(2):
        base = c * grid_rows
        grad_up[c] = full[base:base + rim]
        grad_own[c] = full[base + rim:base + rim + count]
        grad_down[c] = full[base + rim + count:base + grid_rows]


def on_device(mask_field, target, kernel_taps, kernel_radii, kernel_group, kernel_weight):
    _, count, width = mask_field.shape
    kernels, _, span, _ = kernel_taps.shape
    rim = span // 2
    grid_rows = count + 2 * rim
    grid_cols = width + rim
    assert count == span and width == span and kernels % BATCH == 0 and BATCH % 2 == 0

    strips = lax.axis_size("row")
    down = [(i, i + 1) for i in range(strips - 1)]
    up = [(i + 1, i) for i in range(strips - 1)]
    above = lax.ppermute(mask_field, "row", down)
    below = lax.ppermute(mask_field, "row", up)

    scale = 1.0 / (grid_rows * grid_cols)
    order = grouped(grid_cols, width)

    def head_and_tail(shift):
        table = analysis(grid_cols, width, shift).T[:, order]
        return halves(table[:, :2 * width], 0), halves(table[:, 2 * width:], 1)

    row_tab = halves(analysis(grid_rows, span, 0), 1)
    head, tail = head_and_tail(0)
    mask_row = halves(analysis(grid_rows, grid_rows, 2 * rim), 1)
    mask_head, mask_tail = head_and_tail(rim)
    col_inv = halves(synthesis(grid_cols, width, 0).T[order], 0)
    row_inv = halves(synthesis(grid_rows, count, 0, scale), 1)
    grad_col = halves(synthesis(grid_cols, width, rim).T[order], 0)
    grad_row = halves(synthesis(grid_rows, grid_rows, 2 * rim, scale), 1)

    smem = pl.BlockSpec(memory_space=pltpu.SMEM)
    vmem = pl.BlockSpec(memory_space=pltpu.VMEM)
    anywhere = pl.BlockSpec(memory_space=pl.ANY)
    spectra = pl.pallas_call(
        spectra_body,
        grid=(kernels // BATCH,),
        out_shape=jax.ShapeDtypeStruct((kernels, grid_rows, 2 * grid_cols), f32),
        in_specs=[smem, pl.BlockSpec((BATCH, 2, span, span), lambda i: (i, 0, 0, 0)), vmem, vmem, vmem],
        out_specs=pl.BlockSpec((BATCH, grid_rows, 2 * grid_cols), lambda i: (i, 0, 0)),
        compiler_params=pltpu.CompilerParams(vmem_limit_bytes=56 * MIB),
        cost_estimate=pl.CostEstimate(flops=18 * 10**9, bytes_accessed=14 * 10**6, transcendentals=0),
        name="spectra",
    )(kernel_radii, kernel_taps, *map(jnp.asarray, (row_tab, head, tail)))

    far = [jnp.asarray(t) for t in (col_inv, row_inv, row_tab, head, tail, grad_col, grad_row)]
    resist, own, up_rim, down_rim = pl.pallas_call(
        main_body,
        out_shape=[
            jax.ShapeDtypeStruct((GROUPS, count, width), f32),
            jax.ShapeDtypeStruct((2, count, width), f32),
            jax.ShapeDtypeStruct((2, rim, width), f32),
            jax.ShapeDtypeStruct((2, rim, width), f32),
        ],
        in_specs=[smem] * 2 + [vmem] * 7 + [anywhere] * 8,
        out_specs=[vmem] * 4,
        scratch_shapes=[
            pltpu.VMEM((kernels, grid_rows, 2 * grid_cols), f32),
            pltpu.VMEM((kernels // 2, 2 * count, 2 * width), f32),
            pltpu.VMEM((grid_rows, 4 * width), f32),
            pltpu.VMEM((GROUPS, count, width), f32),
            pltpu.VMEM((grid_rows, 4 * width), f32),
            pltpu.SemaphoreType.DMA((kernels // BATCH,)),
            pltpu.SemaphoreType.DMA((len(far),)),
        ] + [pltpu.VMEM(t.shape, bf16) for t in far],
        compiler_params=pltpu.CompilerParams(vmem_limit_bytes=56 * MIB),
        name="fields",
    )(
        kernel_group, kernel_weight, mask_field, above, below, target,
        *map(jnp.asarray, (mask_row, mask_head, mask_tail)), spectra, *far,
    )

    from_below = lax.ppermute(up_rim, "row", up)
    from_above = lax.ppermute(down_rim, "row", down)
    gradient = (
        own
        + jnp.pad(from_above, ((0, 0), (0, count - rim), (0, 0)))
        + jnp.pad(from_below, ((0, 0), (count - rim, 0), (0, 0)))
    )
    return resist, gradient


def solution(mesh):
    in_specs = (P(None, ("win", "row"), None), P(("win", "row"), None), P(), P(), P(), P())
    out_specs = (P(None, ("win", "row"), None), P(None, ("win", "row"), None))
    return jax.shard_map(
        on_device, mesh=mesh, in_specs=in_specs, out_specs=out_specs, check_vma=False
    )
```

time: 65.2 us -> 58.9 us (0.903)
  local copies, waits for them, and re-layouts: 9.5 us -> 1.3 us
  Pallas kernels: 36.2 us -> 38.2 us
    unnamed x14 -> x4, local copies, waits for them, and re-layouts: 9.5 us -> 1.3 us
    pallas_call x1, Pallas kernels: 9.8 us -> 11.6 us  [on_device(): pl.pallas_call(spectra_body, grid=(kernels // BATCH,), out_shape=jax.Shap...]
  transfers between devices with their start and end apart: 4 -> 4, of which waited for: 1 -> 1; matrix products, arithmetic and copies ran while one was open for 0% -> 0% of each run, Pallas kernels for 15% -> 20%
where the time goes in v2:
time: 58.9 us; the launch traced here: 58.6 us
  Pallas kernels  38.2 us (65%)
  starting transfers between devices  12.1 us (21%)
  waiting for transfers between devices  4.76 us (8%)
  other arithmetic  1.58 us (3%)
  local copies, waits for them, and re-layouts  1.3 us (2%)
  between operations  0.69 us (1%)
    pallas_call x1, Pallas kernels, on_device(): pl.pallas_call(main_body, out_shape=[jax.ShapeDtypeStruct((GROUPS, count,...  26.6 us
    pallas_call x1, Pallas kernels, on_device(): pl.pallas_call(spectra_body, grid=(kernels // BATCH,), out_shape=jax.Shap...  11.6 us
    ppermute x1, waiting for transfers between devices, on_device(): from_below = lax.ppermute(up_rim, 'row', up)  4.76 us
    ppermute x1, starting transfers between devices, on_device(): from_above = lax.ppermute(down_rim, 'row', down)  4.53 us
    ppermute x1, starting transfers between devices, on_device(): above = lax.ppermute(mask_field, 'row', down)  3.71 us
    ppermute x1, starting transfers between devices, on_device(): below = lax.ppermute(mask_field, 'row', up)  1.92 us
    ppermute x1, starting transfers between devices, on_device(): from_below = lax.ppermute(up_rim, 'row', up)  1.92 us
    add x1, other arithmetic, on_device(): own + jnp.pad(from_above, ((0, 0), (0, count - rim), (0, 0)))  1.58 us
  transfers between devices with their start and end apart: 4, of which 1 were waited for; matrix products, arithmetic and copies ran while one was open for 0% of the time, Pallas kernels for 20%

profile of v2, /device:TPU:21, one launch (start us, length us, event | category | flops | bytes accessed | tf_op | source)
XLA Modules:
  0.0 58.6 jit_solution(3317263165646611294)
XLA Ops:
  0.6 3.7 %collective-permute-start = (f32[2,128,128]{2,1,0:T(8,128)}, f32[2,128,128]{2,1,0:T(8,128)S(1)}, u32[]{:S(2)}, u32[]{:S(2)}) collective-permute-start(f32[2,128,128]{2,1,0:T(8,128)} %own.1), channel_id=1, source_target_pairs={{0,1},{1,2},{2,3},{3,4},{4,5},{5,6},{6,7},{7,8},{8,9},{9,10},{10,1... | collective-permute-start | bytes 393224 | tf_op jit(solution)/shard_map/ppermute | solution.py:253
  4.3 1.9 %collective-permute-start.1 = (f32[2,128,128]{2,1,0:T(8,128)}, f32[2,128,128]{2,1,0:T(8,128)S(1)}, u32[]{:S(2)}, u32[]{:S(2)}) collective-permute-start(f32[2,128,128]{2,1,0:T(8,128)} %own.1), channel_id=1, source_target_pairs={{1,0},{2,1},{3,2},{4,3},{5,4},{6,5},{7,6},{8,7},{9,8},{10,9},{11,1... | collective-permute-start | bytes 393224 | tf_op jit(solution)/shard_map/ppermute | solution.py:254
  6.3 11.6 %spectra.1.spec_far = f32[24,256,384]{2,1,0:T(8,128)} custom-call(s32[24]{0:T(128)} %radii.1, f32[24,2,128,128]{3,2,1,0:T(8,128)} %taps.1, bf16[512,512]{1,0:T(8,128)(2,1)} %constant.23.clone.row_tab.rest_2_, bf16[512,256]{1,0:T(8,128)(2,1)} %constant.24.clone.head.rest_3_, bf16[256,256]{1,0:T(8,128)(2,1)} %constant.25.clone.tail.rest_4_), custom_call_target="tpu_custom_call" | custom-call | flops 17999998976 | bytes 14000000 | tf_op jit(solution)/shard_map/spectra/pallas_call | solution.py:275
  17.9 0.0 collective-permute-done.above
  17.9 0.0 copy-start
  17.9 0.0 collective-permute-done.1.below
  17.9 0.6 %copy-done = f32[2,128,128]{2,1,0:T(8,128)} copy-done((f32[2,128,128]{2,1,0:T(8,128)}, f32[2,128,128]{2,1,0:T(8,128)S(1)}, u32[]{:S(2)}) %copy-start) | copy-done | bytes 131096
  18.6 0.0 copy-start.1
  18.6 0.7 %copy-done.1 = f32[2,128,128]{2,1,0:T(8,128)} copy-done((f32[2,128,128]{2,1,0:T(8,128)}, f32[2,128,128]{2,1,0:T(8,128)S(1)}, u32[]{:S(2)}) %copy-start.1) | copy-done | bytes 131096
  19.2 26.6 %fields.1 = (f32[3,128,128]{2,1,0:T(8,128)}, f32[2,128,128]{2,1,0:T(8,128)}, f32[2,64,128]{2,1,0:T(8,128)}, f32[2,64,128]{2,1,0:T(8,128)}) custom-call(s32[24]{0:T(128)} %group.1, f32[24]{0:T(128)} %weight.1, f32[2,128,128]{2,1,0:T(8,128)} %own.1, f32[2,128,128]{2,1,0:T(8,128)} %copy-done, f32[2,128,128]{2,1,0:T(8,128)} %copy-done.1, s32[128,128]{1,0:T(8,128)} %target.1, ...), custom_call_target="tpu_custom_call" | custom-call | tf_op jit(solution)/shard_map/fields/pallas_call | solution.py:287
  45.8 4.5 %collective-permute-start.2 = (f32[2,64,128]{2,1,0:T(8,128)}, f32[2,64,128]{2,1,0:T(8,128)S(1)}, u32[]{:S(2)}, u32[]{:S(2)}) collective-permute-start(f32[2,64,128]{2,1,0:T(8,128)} %get-tuple-element.8), channel_id=1, source_target_pairs={{0,1},{1,2},{2,3},{3,4},{4,5},{5,6},{6,7},{7,8},{8,9},{9,10},{10,1... | collective-permute-start | bytes 196616 | tf_op jit(solution)/shard_map/ppermute | solution.py:314
  50.3 1.9 %collective-permute-start.3 = (f32[2,64,128]{2,1,0:T(8,128)}, f32[2,64,128]{2,1,0:T(8,128)S(1)}, u32[]{:S(2)}, u32[]{:S(2)}) collective-permute-start(f32[2,64,128]{2,1,0:T(8,128)} %get-tuple-element.9), channel_id=1, source_target_pairs={{1,0},{2,1},{3,2},{4,3},{5,4},{6,5},{7,6},{8,7},{9,8},{10,9},{11,1... | collective-permute-start | bytes 196616 | tf_op jit(solution)/shard_map/ppermute | solution.py:313
  52.3 0.0 collective-permute-done.2
  52.3 4.8 %collective-permute-done.3 = f32[2,64,128]{2,1,0:T(8,128)S(1)} collective-permute-done((f32[2,64,128]{2,1,0:T(8,128)}, f32[2,64,128]{2,1,0:T(8,128)S(1)}, u32[]{:S(2)}, u32[]{:S(2)}) %collective-permute-start.3) | collective-permute-done | bytes 65568 | tf_op jit(solution)/shard_map/ppermute | solution.py:313
  57.0 1.6 %pad_add_fusion = f32[2,128,128]{2,1,0:T(8,128)} fusion(f32[2,64,128]{2,1,0:T(8,128)S(1)} %collective-permute-done.3, f32[2,128,128]{2,1,0:T(8,128)} %get-tuple-element.7, f32[2,64,128]{2,1,0:T(8,128)S(1)} %collective-permute-done.2), kind=kLoop, calls=%fused_computation | loop fusion | flops 65536 | bytes 393216 | tf_op jit(solution)/shard_map/add | solution.py:316
Async XLA Ops:
  0.6 17.3 %collective-permute-start = (f32[2,128,128]{2,1,0:T(8,128)}, f32[2,128,128]{2,1,0:T(8,128)S(1)}, u32[]{:S(2)}, u32[]{:S(2)}) collective-permute-start(f32[2,128,128]{2,1,0:T(8,128)} %own.1), channel_id=1, source_target_pairs={{0,1},{1,2},{2,3},{3,4},{4,5},{5,6},{6,7},{7,8},{8,9},{9,10},{10,1... | collective-permute-start | bytes 393224 | tf_op jit(solution)/shard_map/ppermute | solution.py:253
  4.3 13.6 %collective-permute-start.1 = (f32[2,128,128]{2,1,0:T(8,128)}, f32[2,128,128]{2,1,0:T(8,128)S(1)}, u32[]{:S(2)}, u32[]{:S(2)}) collective-permute-start(f32[2,128,128]{2,1,0:T(8,128)} %own.1), channel_id=1, source_target_pairs={{1,0},{2,1},{3,2},{4,3},{5,4},{6,5},{7,6},{8,7},{9,8},{10,9},{11,1... | collective-permute-start | bytes 393224 | tf_op jit(solution)/shard_map/ppermute | solution.py:254
  17.9 0.7 %copy-start = (f32[2,128,128]{2,1,0:T(8,128)}, f32[2,128,128]{2,1,0:T(8,128)S(1)}, u32[]{:S(2)}) copy-start(f32[2,128,128]{2,1,0:T(8,128)S(1)} %collective-permute-done.above) | copy-start | bytes 393220
  18.6 0.7 %copy-start.1 = (f32[2,128,128]{2,1,0:T(8,128)}, f32[2,128,128]{2,1,0:T(8,128)S(1)}, u32[]{:S(2)}) copy-start(f32[2,128,128]{2,1,0:T(8,128)S(1)} %collective-permute-done.1.below) | copy-start | bytes 393220
  45.8 6.5 %collective-permute-start.2 = (f32[2,64,128]{2,1,0:T(8,128)}, f32[2,64,128]{2,1,0:T(8,128)S(1)}, u32[]{:S(2)}, u32[]{:S(2)}) collective-permute-start(f32[2,64,128]{2,1,0:T(8,128)} %get-tuple-element.8), channel_id=1, source_target_pairs={{0,1},{1,2},{2,3},{3,4},{4,5},{5,6},{6,7},{7,8},{8,9},{9,10},{10,1... | collective-permute-start | bytes 196616 | tf_op jit(solution)/shard_map/ppermute | solution.py:314
  50.3 6.7 %collective-permute-start.3 = (f32[2,64,128]{2,1,0:T(8,128)}, f32[2,64,128]{2,1,0:T(8,128)S(1)}, u32[]{:S(2)}, u32[]{:S(2)}) collective-permute-start(f32[2,64,128]{2,1,0:T(8,128)} %get-tuple-element.9), channel_id=1, source_target_pairs={{1,0},{2,1},{3,2},{4,3},{5,4},{6,5},{7,6},{8,7},{9,8},{10,9},{11,1... | collective-permute-start | bytes 196616 | tf_op jit(solution)/shard_map/ppermute | solution.py:313

commit v3 on v2

--- a/solution.py
+++ b/solution.py
@@ -84,12 +84,10 @@
     return jnp.concatenate([x[:rows], x[rows:]], axis=1)
 
 
-def dft(pairs, row_tab, head, tail):
-    tiles = []
-    for pair in pairs:
-        width = pair.shape[1] // 2
-        half = over_rows(row_tab, pair)
-        tiles += [side(half[:, :width]), side(half[:, width:])]
+def dft(planes, row_tab, head, tail):
+    width = planes.shape[0] // 2
+    half = over_rows(row_tab, planes)
+    tiles = [side(half[:, at:at + width]) for at in range(0, planes.shape[1], width)]
     rows = tiles[0].shape[0]
     first, rest = to_freqs(jnp.concatenate(tiles, axis=0), head, tail)
     return [(first[j * rows:(j + 1) * rows], rest[j * rows:(j + 1) * rows]) for j in range(len(tiles))]
@@ -105,15 +103,12 @@
     row_at = lax.broadcasted_iota(jnp.int32, (span, span), 0) - span // 2
     col_at = lax.broadcasted_iota(jnp.int32, (span, span), 1) - span // 2
     reach = jnp.maximum(jnp.maximum(row_at, -1 - row_at), jnp.maximum(col_at, -1 - col_at))
-    pairs = []
-    for i in range(batch // 2):
-        planes = []
-        for j in range(2):
-            inside = reach < radii[first + 2 * i + j]
-            parts = [jnp.where(inside, taps[2 * i + j, c], 0.0) for c in range(2)]
-            planes.append(jnp.concatenate(parts, axis=0))
-        pairs.append(jnp.concatenate(planes, axis=1))
-    for k, (a, b) in enumerate(dft(pairs, row_tab, head, tail)):
+    planes = []
+    for k in range(batch):
+        inside = reach < radii[first + k]
+        parts = [jnp.where(inside, taps[k, c], 0.0) for c in range(2)]
+        planes.append(jnp.concatenate(parts, axis=0))
+    for k, (a, b) in enumerate(dft(jnp.concatenate(planes, axis=1), row_tab, head, tail)):
         spec[k, :, :a.shape[1]] = a
         spec[k, :, a.shape[1]:] = b
 
@@ -177,18 +172,17 @@
                 s_rest * m_same + swap(s_rest) * m_cross,
             ], axis=1))
         back = over_lanes(jnp.concatenate(products, axis=0), col_inv)
-        for p in range(batch // 2):
-            mine = []
-            for c in range(2):
-                planes = [back[(2 * p + j) * grid_rows:(2 * p + j + 1) * grid_rows, c * width:(c + 1) * width] for j in range(2)]
-                mine.append(jnp.concatenate(planes, axis=1))
-            pair = over_rows(row_inv, jnp.concatenate(mine, axis=0))
-            field[i * (batch // 2) + p] = pair
-            power = pair[:count] * pair[:count] + pair[count:] * pair[count:]
-            for j in range(2):
-                k = i * batch + 2 * p + j
-                g = group[k]
-                slopes[g] = slopes[g] + weight[k] * power[:, j * width:(j + 1) * width]
+        mine = []
+        for c in range(2):
+            planes = [back[j * grid_rows:(j + 1) * grid_rows, c * width:(c + 1) * width] for j in range(batch)]
+            mine.append(jnp.concatenate(planes, axis=1))
+        found = over_rows(row_inv, jnp.concatenate(mine, axis=0))
+        field[i] = found
+        power = found[:count] * found[:count] + found[count:] * found[count:]
+        for j in range(batch):
+            k = i * batch + j
+            g = group[k]
+            slopes[g] = slopes[g] + weight[k] * power[:, j * width:(j + 1) * width]
         return carry
 
     lax.fori_loop(0, steps, forward, 0)
@@ -202,15 +196,13 @@
         fetch_table(i).wait()
 
     def backward(i, carry):
-        pairs = []
-        for p in range(batch // 2):
-            factors = []
-            for j in range(2):
-                k = i * batch + 2 * p + j
-                factors.append((2.0 * weight[k]) * slopes[group[k]])
-            factor = jnp.concatenate(factors, axis=1)
-            pairs.append(field[i * (batch // 2) + p] * jnp.concatenate([factor, factor], axis=0))
-        found = dft(pairs, row_tab, head, tail)
+        factors = []
+        for j in range(batch):
+            k = i * batch + j
+            factors.append((2.0 * weight[k]) * slopes[group[k]])
+        factor = jnp.concatenate(factors, axis=1)
+        cot = field[i] * jnp.concatenate([factor, factor], axis=0)
+        found = dft(cot, row_tab, head, tail)
         total = [grad_spec[:, c * width:(c + 1) * width] for c in range(4)]
         for j in range(batch):
             k = i * batch + j
@@ -245,7 +237,7 @@
     rim = span // 2
     grid_rows = count + 2 * rim
     grid_cols = width + rim
-    assert count == span and width == span and kernels % BATCH == 0 and BATCH % 2 == 0
+    assert count == span and width == span and kernels % BATCH == 0
 
     strips = lax.axis_size("row")
     down = [(i, i + 1) for i in range(strips - 1)]
@@ -296,7 +288,7 @@
         out_specs=[vmem] * 4,
         scratch_shapes=[
             pltpu.VMEM((kernels, grid_rows, 2 * grid_cols), f32),
-            pltpu.VMEM((kernels // 2, 2 * count, 2 * width), f32),
+            pltpu.VMEM((kernels // BATCH, 2 * count, BATCH * width), f32),
             pltpu.VMEM((grid_rows, 4 * width), f32),
             pltpu.VMEM((GROUPS, count, width), f32),
             pltpu.VMEM((grid_rows, 4 * width), f32),

time: 58.9 us -> 59 us (level)
  no operation moved by 1% of the time
where the time goes in v3:
time: 59 us; the launch traced here: 58.6 us
  Pallas kernels  38.2 us (65%)
  starting transfers between devices  12.1 us (21%)
  waiting for transfers between devices  4.76 us (8%)
  other arithmetic  1.58 us (3%)
  local copies, waits for them, and re-layouts  1.3 us (2%)
  between operations  0.69 us (1%)
    pallas_call x1, Pallas kernels, on_device(): pl.pallas_call(main_body, out_shape=[jax.ShapeDtypeStruct((GROUPS, count,...  26.6 us
    pallas_call x1, Pallas kernels, on_device(): pl.pallas_call(spectra_body, grid=(kernels // BATCH,), out_shape=jax.Shap...  11.6 us
    ppermute x1, waiting for transfers between devices, on_device(): from_below = lax.ppermute(up_rim, 'row', up)  4.76 us
    ppermute x1, starting transfers between devices, on_device(): from_above = lax.ppermute(down_rim, 'row', down)  4.54 us
    ppermute x1, starting transfers between devices, on_device(): above = lax.ppermute(mask_field, 'row', down)  3.71 us
    ppermute x1, starting transfers between devices, on_device(): below = lax.ppermute(mask_field, 'row', up)  1.92 us
    ppermute x1, starting transfers between devices, on_device(): from_below = lax.ppermute(up_rim, 'row', up)  1.92 us
    add x1, other arithmetic, on_device(): own + jnp.pad(from_above, ((0, 0), (0, count - rim), (0, 0)))  1.58 us
  transfers between devices with their start and end apart: 4, of which 1 were waited for; matrix products, arithmetic and copies ran while one was open for 0% of the time, Pallas kernels for 20%

profile of v3, /device:TPU:21, one launch (start us, length us, event | category | flops | bytes accessed | tf_op | source)
XLA Modules:
  0.0 58.6 jit_solution(9272077955972385497)
XLA Ops:
  0.6 3.7 %collective-permute-start = (f32[2,128,128]{2,1,0:T(8,128)}, f32[2,128,128]{2,1,0:T(8,128)S(1)}, u32[]{:S(2)}, u32[]{:S(2)}) collective-permute-start(f32[2,128,128]{2,1,0:T(8,128)} %own.1), channel_id=1, source_target_pairs={{0,1},{1,2},{2,3},{3,4},{4,5},{5,6},{6,7},{7,8},{8,9},{9,10},{10,1... | collective-permute-start | bytes 393224 | tf_op jit(solution)/shard_map/ppermute | solution.py:245
  4.3 1.9 %collective-permute-start.1 = (f32[2,128,128]{2,1,0:T(8,128)}, f32[2,128,128]{2,1,0:T(8,128)S(1)}, u32[]{:S(2)}, u32[]{:S(2)}) collective-permute-start(f32[2,128,128]{2,1,0:T(8,128)} %own.1), channel_id=1, source_target_pairs={{1,0},{2,1},{3,2},{4,3},{5,4},{6,5},{7,6},{8,7},{9,8},{10,9},{11,1... | collective-permute-start | bytes 393224 | tf_op jit(solution)/shard_map/ppermute | solution.py:246
  6.3 11.6 %spectra.1.spec_far = f32[24,256,384]{2,1,0:T(8,128)} custom-call(s32[24]{0:T(128)} %radii.1, f32[24,2,128,128]{3,2,1,0:T(8,128)} %taps.1, bf16[512,512]{1,0:T(8,128)(2,1)} %constant.23.clone.row_tab.rest_2_, bf16[512,256]{1,0:T(8,128)(2,1)} %constant.24.clone.head.rest_3_, bf16[256,256]{1,0:T(8,128)(2,1)} %constant.25.clone.tail.rest_4_), custom_call_target="tpu_custom_call" | custom-call | flops 17999998976 | bytes 14000000 | tf_op jit(solution)/shard_map/spectra/pallas_call | solution.py:267
  17.9 0.0 collective-permute-done.above
  17.9 0.0 copy-start
  17.9 0.0 collective-permute-done.1.below
  17.9 0.6 %copy-done = f32[2,128,128]{2,1,0:T(8,128)} copy-done((f32[2,128,128]{2,1,0:T(8,128)}, f32[2,128,128]{2,1,0:T(8,128)S(1)}, u32[]{:S(2)}) %copy-start) | copy-done | bytes 131096
  18.6 0.0 copy-start.1
  18.6 0.7 %copy-done.1 = f32[2,128,128]{2,1,0:T(8,128)} copy-done((f32[2,128,128]{2,1,0:T(8,128)}, f32[2,128,128]{2,1,0:T(8,128)S(1)}, u32[]{:S(2)}) %copy-start.1) | copy-done | bytes 131096
  19.2 26.6 %fields.1 = (f32[3,128,128]{2,1,0:T(8,128)}, f32[2,128,128]{2,1,0:T(8,128)}, f32[2,64,128]{2,1,0:T(8,128)}, f32[2,64,128]{2,1,0:T(8,128)}) custom-call(s32[24]{0:T(128)} %group.1, f32[24]{0:T(128)} %weight.1, f32[2,128,128]{2,1,0:T(8,128)} %own.1, f32[2,128,128]{2,1,0:T(8,128)} %copy-done, f32[2,128,128]{2,1,0:T(8,128)} %copy-done.1, s32[128,128]{1,0:T(8,128)} %target.1, ...), custom_call_target="tpu_custom_call" | custom-call | tf_op jit(solution)/shard_map/fields/pallas_call | solution.py:279
  45.8 4.5 %collective-permute-start.2 = (f32[2,64,128]{2,1,0:T(8,128)}, f32[2,64,128]{2,1,0:T(8,128)S(1)}, u32[]{:S(2)}, u32[]{:S(2)}) collective-permute-start(f32[2,64,128]{2,1,0:T(8,128)} %get-tuple-element.8), channel_id=1, source_target_pairs={{0,1},{1,2},{2,3},{3,4},{4,5},{5,6},{6,7},{7,8},{8,9},{9,10},{10,1... | collective-permute-start | bytes 196616 | tf_op jit(solution)/shard_map/ppermute | solution.py:306
  50.4 1.9 %collective-permute-start.3 = (f32[2,64,128]{2,1,0:T(8,128)}, f32[2,64,128]{2,1,0:T(8,128)S(1)}, u32[]{:S(2)}, u32[]{:S(2)}) collective-permute-start(f32[2,64,128]{2,1,0:T(8,128)} %get-tuple-element.9), channel_id=1, source_target_pairs={{1,0},{2,1},{3,2},{4,3},{5,4},{6,5},{7,6},{8,7},{9,8},{10,9},{11,1... | collective-permute-start | bytes 196616 | tf_op jit(solution)/shard_map/ppermute | solution.py:305
  52.3 0.0 collective-permute-done.2
  52.3 4.8 %collective-permute-done.3 = f32[2,64,128]{2,1,0:T(8,128)S(1)} collective-permute-done((f32[2,64,128]{2,1,0:T(8,128)}, f32[2,64,128]{2,1,0:T(8,128)S(1)}, u32[]{:S(2)}, u32[]{:S(2)}) %collective-permute-start.3) | collective-permute-done | bytes 65568 | tf_op jit(solution)/shard_map/ppermute | solution.py:305
  57.0 1.6 %pad_add_fusion = f32[2,128,128]{2,1,0:T(8,128)} fusion(f32[2,64,128]{2,1,0:T(8,128)S(1)} %collective-permute-done.3, f32[2,128,128]{2,1,0:T(8,128)} %get-tuple-element.7, f32[2,64,128]{2,1,0:T(8,128)S(1)} %collective-permute-done.2), kind=kLoop, calls=%fused_computation | loop fusion | flops 65536 | bytes 393216 | tf_op jit(solution)/shard_map/add | solution.py:308
Async XLA Ops:
  0.6 17.3 %collective-permute-start = (f32[2,128,128]{2,1,0:T(8,128)}, f32[2,128,128]{2,1,0:T(8,128)S(1)}, u32[]{:S(2)}, u32[]{:S(2)}) collective-permute-start(f32[2,128,128]{2,1,0:T(8,128)} %own.1), channel_id=1, source_target_pairs={{0,1},{1,2},{2,3},{3,4},{4,5},{5,6},{6,7},{7,8},{8,9},{9,10},{10,1... | collective-permute-start | bytes 393224 | tf_op jit(solution)/shard_map/ppermute | solution.py:245
  4.3 13.6 %collective-permute-start.1 = (f32[2,128,128]{2,1,0:T(8,128)}, f32[2,128,128]{2,1,0:T(8,128)S(1)}, u32[]{:S(2)}, u32[]{:S(2)}) collective-permute-start(f32[2,128,128]{2,1,0:T(8,128)} %own.1), channel_id=1, source_target_pairs={{1,0},{2,1},{3,2},{4,3},{5,4},{6,5},{7,6},{8,7},{9,8},{10,9},{11,1... | collective-permute-start | bytes 393224 | tf_op jit(solution)/shard_map/ppermute | solution.py:246
  17.9 0.7 %copy-start = (f32[2,128,128]{2,1,0:T(8,128)}, f32[2,128,128]{2,1,0:T(8,128)S(1)}, u32[]{:S(2)}) copy-start(f32[2,128,128]{2,1,0:T(8,128)S(1)} %collective-permute-done.above) | copy-start | bytes 393220
  18.6 0.7 %copy-start.1 = (f32[2,128,128]{2,1,0:T(8,128)}, f32[2,128,128]{2,1,0:T(8,128)S(1)}, u32[]{:S(2)}) copy-start(f32[2,128,128]{2,1,0:T(8,128)S(1)} %collective-permute-done.1.below) | copy-start | bytes 393220
  45.8 6.5 %collective-permute-start.2 = (f32[2,64,128]{2,1,0:T(8,128)}, f32[2,64,128]{2,1,0:T(8,128)S(1)}, u32[]{:S(2)}, u32[]{:S(2)}) collective-permute-start(f32[2,64,128]{2,1,0:T(8,128)} %get-tuple-element.8), channel_id=1, source_target_pairs={{0,1},{1,2},{2,3},{3,4},{4,5},{5,6},{6,7},{7,8},{8,9},{9,10},{10,1... | collective-permute-start | bytes 196616 | tf_op jit(solution)/shard_map/ppermute | solution.py:306
  50.4 6.7 %collective-permute-start.3 = (f32[2,64,128]{2,1,0:T(8,128)}, f32[2,64,128]{2,1,0:T(8,128)S(1)}, u32[]{:S(2)}, u32[]{:S(2)}) collective-permute-start(f32[2,64,128]{2,1,0:T(8,128)} %get-tuple-element.9), channel_id=1, source_target_pairs={{1,0},{2,1},{3,2},{4,3},{5,4},{6,5},{7,6},{8,7},{9,8},{10,9},{11,1... | collective-permute-start | bytes 196616 | tf_op jit(solution)/shard_map/ppermute | solution.py:305

commit v4 on v3

--- a/solution.py
+++ b/solution.py
@@ -49,32 +49,36 @@
     return high, low
 
 
-def dot(left, right):
-    return jnp.dot(left, right, preferred_element_type=f32)
-
-
-def over_rows(table, x):
+def dot(left, right, piece):
+    parts = [
+        jnp.dot(left[at:at + piece], right, preferred_element_type=f32)
+        for at in range(0, left.shape[0], piece)
+    ]
+    return jnp.concatenate(parts, axis=0)
+
+
+def over_rows(table, x, piece):
     high, low = split(x)
     left = table[...]
     left = jnp.concatenate([left, left[:, :x.shape[0]]], axis=1)
-    return dot(left, jnp.concatenate([high, high, low], axis=0))
-
-
-def over_lanes(x, table):
+    return dot(left, jnp.concatenate([high, high, low], axis=0), piece)
+
+
+def over_lanes(x, table, piece):
     high, low = split(x)
     right = table[...]
     right = jnp.concatenate([right, right[:x.shape[1]]], axis=0)
-    return dot(jnp.concatenate([high, high, low], axis=1), right)
-
-
-def to_freqs(x, head, tail):
+    return dot(jnp.concatenate([high, high, low], axis=1), right, piece)
+
+
+def to_freqs(x, head, tail, piece):
     high, low = split(x)
     depth = x.shape[1]
     right = head[...]
     right = jnp.concatenate([right, right[:depth]], axis=0)
-    first = dot(jnp.concatenate([high, high, low], axis=1), right)
+    first = dot(jnp.concatenate([high, high, low], axis=1), right, piece)
     right = tail[...]
-    rest = dot(jnp.concatenate([high, low], axis=1), jnp.concatenate([right, right], axis=0))
+    rest = dot(jnp.concatenate([high, low], axis=1), jnp.concatenate([right, right], axis=0), piece)
     lanes = rest.shape[1] // 2
     return first, rest[:, :lanes] + rest[:, lanes:]
 
@@ -84,12 +88,12 @@
     return jnp.concatenate([x[:rows], x[rows:]], axis=1)
 
 
-def dft(planes, row_tab, head, tail):
+def dft(planes, row_tab, head, tail, piece):
     width = planes.shape[0] // 2
-    half = over_rows(row_tab, planes)
+    half = over_rows(row_tab, planes, piece)
     tiles = [side(half[:, at:at + width]) for at in range(0, planes.shape[1], width)]
     rows = tiles[0].shape[0]
-    first, rest = to_freqs(jnp.concatenate(tiles, axis=0), head, tail)
+    first, rest = to_freqs(jnp.concatenate(tiles, axis=0), head, tail, piece)
     return [(first[j * rows:(j + 1) * rows], rest[j * rows:(j + 1) * rows]) for j in range(len(tiles))]
 
 
@@ -108,7 +112,7 @@
         inside = reach < radii[first + k]
         parts = [jnp.where(inside, taps[k, c], 0.0) for c in range(2)]
         planes.append(jnp.concatenate(parts, axis=0))
-    for k, (a, b) in enumerate(dft(jnp.concatenate(planes, axis=1), row_tab, head, tail)):
+    for k, (a, b) in enumerate(dft(jnp.concatenate(planes, axis=1), row_tab, head, tail, 128)):
         spec[k, :, :a.shape[1]] = a
         spec[k, :, a.shape[1]:] = b
 
@@ -145,7 +149,7 @@
     mask = jnp.concatenate(
         [part for c in range(2) for part in (above[c, count - rim:], own[c], below[c, :rim])], axis=0
     )
-    m_first, m_rest = to_freqs(side(over_rows(mask_row, mask)), mask_head, mask_tail)
+    m_first, m_rest = to_freqs(side(over_rows(mask_row, mask, 256)), mask_head, mask_tail, 256)
     lane = lax.broadcasted_iota(jnp.int32, m_rest.shape, 1)
     real_half = lane < m_rest.shape[1] // 2
     turned = swap(m_rest)
@@ -171,12 +175,12 @@
                 s_re * m_im + s_im * m_re,
                 s_rest * m_same + swap(s_rest) * m_cross,
             ], axis=1))
-        back = over_lanes(jnp.concatenate(products, axis=0), col_inv)
+        back = over_lanes(jnp.concatenate(products, axis=0), col_inv, 256)
         mine = []
         for c in range(2):
             planes = [back[j * grid_rows:(j + 1) * grid_rows, c * width:(c + 1) * width] for j in range(batch)]
             mine.append(jnp.concatenate(planes, axis=1))
-        found = over_rows(row_inv, jnp.concatenate(mine, axis=0))
+        found = over_rows(row_inv, jnp.concatenate(mine, axis=0), 256)
         field[i] = found
         power = found[:count] * found[:count] + found[count:] * found[count:]
         for j in range(batch):
@@ -202,7 +206,7 @@
             factors.append((2.0 * weight[k]) * slopes[group[k]])
         factor = jnp.concatenate(factors, axis=1)
         cot = field[i] * jnp.concatenate([factor, factor], axis=0)
-        found = dft(cot, row_tab, head, tail)
+        found = dft(cot, row_tab, head, tail, 256)
         total = [grad_spec[:, c * width:(c + 1) * width] for c in range(4)]
         for j in range(batch):
             k = i * batch + j
@@ -222,8 +226,8 @@
     same, cross = grad_spec[:, 2 * width:3 * width], grad_spec[:, 3 * width:]
     tail_sum = jnp.where(real_half, same + swap(same), swap(cross) - cross)
     total = jnp.concatenate([grad_spec[:, :2 * width], tail_sum], axis=1)
-    back = over_lanes(total, grad_col)
-    full = over_rows(grad_row, jnp.concatenate([back[:, :width], back[:, width:]], axis=0))
+    back = over_lanes(total, grad_col, 256)
+    full = over_rows(grad_row, jnp.concatenate([back[:, :width], back[:, width:]], axis=0), 256)
     for c in range(2):
         base = c * grid_rows
         grad_up[c] = full[base:base + rim]

time: 59 us -> 54.5 us (0.924)
  Pallas kernels: 38.2 us -> 33.6 us
    pallas_call x1, Pallas kernels: 26.6 us -> 22.5 us  [on_device(): pl.pallas_call(main_body, out_shape=[jax.ShapeDtypeStruct((GROUPS, count,...]
  transfers between devices with their start and end apart: 4 -> 4, of which waited for: 1 -> 1; matrix products, arithmetic and copies ran while one was open for 0% -> 0% of each run, Pallas kernels for 20% -> 21%
where the time goes in v4:
time: 54.5 us; the launch traced here: 54.1 us
  Pallas kernels  33.6 us (62%)
  starting transfers between devices  12.1 us (22%)
  waiting for transfers between devices  4.76 us (9%)
  other arithmetic  1.58 us (3%)
  local copies, waits for them, and re-layouts  1.3 us (2%)
  between operations  0.69 us (1%)
    pallas_call x1, Pallas kernels, on_device(): pl.pallas_call(main_body, out_shape=[jax.ShapeDtypeStruct((GROUPS, count,...  22.5 us
    pallas_call x1, Pallas kernels, on_device(): pl.pallas_call(spectra_body, grid=(kernels // BATCH,), out_shape=jax.Shap...  11.1 us
    ppermute x1, waiting for transfers between devices, on_device(): from_below = lax.ppermute(up_rim, 'row', up)  4.76 us
    ppermute x1, starting transfers between devices, on_device(): from_above = lax.ppermute(down_rim, 'row', down)  4.54 us
    ppermute x1, starting transfers between devices, on_device(): above = lax.ppermute(mask_field, 'row', down)  3.71 us
    ppermute x1, starting transfers between devices, on_device(): below = lax.ppermute(mask_field, 'row', up)  1.92 us
    ppermute x1, starting transfers between devices, on_device(): from_below = lax.ppermute(up_rim, 'row', up)  1.92 us
    add x1, other arithmetic, on_device(): own + jnp.pad(from_above, ((0, 0), (0, count - rim), (0, 0)))  1.58 us
  transfers between devices with their start and end apart: 4, of which 1 were waited for; matrix products, arithmetic and copies ran while one was open for 0% of the time, Pallas kernels for 21%

profile of v4, /device:TPU:21, one launch (start us, length us, event | category | flops | bytes accessed | tf_op | source)
XLA Modules:
  0.0 54.1 jit_solution(16133120046336991310)
XLA Ops:
  0.6 3.7 %collective-permute-start = (f32[2,128,128]{2,1,0:T(8,128)}, f32[2,128,128]{2,1,0:T(8,128)S(1)}, u32[]{:S(2)}, u32[]{:S(2)}) collective-permute-start(f32[2,128,128]{2,1,0:T(8,128)} %own.1), channel_id=1, source_target_pairs={{0,1},{1,2},{2,3},{3,4},{4,5},{5,6},{6,7},{7,8},{8,9},{9,10},{10,1... | collective-permute-start | bytes 393224 | tf_op jit(solution)/shard_map/ppermute | solution.py:249
  4.3 1.9 %collective-permute-start.1 = (f32[2,128,128]{2,1,0:T(8,128)}, f32[2,128,128]{2,1,0:T(8,128)S(1)}, u32[]{:S(2)}, u32[]{:S(2)}) collective-permute-start(f32[2,128,128]{2,1,0:T(8,128)} %own.1), channel_id=1, source_target_pairs={{1,0},{2,1},{3,2},{4,3},{5,4},{6,5},{7,6},{8,7},{9,8},{10,9},{11,1... | collective-permute-start | bytes 393224 | tf_op jit(solution)/shard_map/ppermute | solution.py:250
  6.3 11.1 %spectra.1.spec_far = f32[24,256,384]{2,1,0:T(8,128)} custom-call(s32[24]{0:T(128)} %radii.1, f32[24,2,128,128]{3,2,1,0:T(8,128)} %taps.1, bf16[512,512]{1,0:T(8,128)(2,1)} %constant.23.clone.row_tab.rest_2_, bf16[512,256]{1,0:T(8,128)(2,1)} %constant.24.clone.head.rest_3_, bf16[256,256]{1,0:T(8,128)(2,1)} %constant.25.clone.tail.rest_4_), custom_call_target="tpu_custom_call" | custom-call | flops 17999998976 | bytes 14000000 | tf_op jit(solution)/shard_map/spectra/pallas_call | solution.py:271
  17.4 0.0 collective-permute-done.above
  17.4 0.0 copy-start
  17.4 0.0 collective-permute-done.1.below
  17.4 0.6 %copy-done = f32[2,128,128]{2,1,0:T(8,128)} copy-done((f32[2,128,128]{2,1,0:T(8,128)}, f32[2,128,128]{2,1,0:T(8,128)S(1)}, u32[]{:S(2)}) %copy-start) | copy-done | bytes 131096
  18.1 0.0 copy-start.1
  18.1 0.7 %copy-done.1 = f32[2,128,128]{2,1,0:T(8,128)} copy-done((f32[2,128,128]{2,1,0:T(8,128)}, f32[2,128,128]{2,1,0:T(8,128)S(1)}, u32[]{:S(2)}) %copy-start.1) | copy-done | bytes 131096
  18.7 22.5 %fields.1 = (f32[3,128,128]{2,1,0:T(8,128)}, f32[2,128,128]{2,1,0:T(8,128)}, f32[2,64,128]{2,1,0:T(8,128)}, f32[2,64,128]{2,1,0:T(8,128)}) custom-call(s32[24]{0:T(128)} %group.1, f32[24]{0:T(128)} %weight.1, f32[2,128,128]{2,1,0:T(8,128)} %own.1, f32[2,128,128]{2,1,0:T(8,128)} %copy-done, f32[2,128,128]{2,1,0:T(8,128)} %copy-done.1, s32[128,128]{1,0:T(8,128)} %target.1, ...), custom_call_target="tpu_custom_call" | custom-call | tf_op jit(solution)/shard_map/fields/pallas_call | solution.py:283
  41.2 4.5 %collective-permute-start.2 = (f32[2,64,128]{2,1,0:T(8,128)}, f32[2,64,128]{2,1,0:T(8,128)S(1)}, u32[]{:S(2)}, u32[]{:S(2)}) collective-permute-start(f32[2,64,128]{2,1,0:T(8,128)} %get-tuple-element.8), channel_id=1, source_target_pairs={{0,1},{1,2},{2,3},{3,4},{4,5},{5,6},{6,7},{7,8},{8,9},{9,10},{10,1... | collective-permute-start | bytes 196616 | tf_op jit(solution)/shard_map/ppermute | solution.py:310
  45.8 1.9 %collective-permute-start.3 = (f32[2,64,128]{2,1,0:T(8,128)}, f32[2,64,128]{2,1,0:T(8,128)S(1)}, u32[]{:S(2)}, u32[]{:S(2)}) collective-permute-start(f32[2,64,128]{2,1,0:T(8,128)} %get-tuple-element.9), channel_id=1, source_target_pairs={{1,0},{2,1},{3,2},{4,3},{5,4},{6,5},{7,6},{8,7},{9,8},{10,9},{11,1... | collective-permute-start | bytes 196616 | tf_op jit(solution)/shard_map/ppermute | solution.py:309
  47.7 0.0 collective-permute-done.2
  47.7 4.8 %collective-permute-done.3 = f32[2,64,128]{2,1,0:T(8,128)S(1)} collective-permute-done((f32[2,64,128]{2,1,0:T(8,128)}, f32[2,64,128]{2,1,0:T(8,128)S(1)}, u32[]{:S(2)}, u32[]{:S(2)}) %collective-permute-start.3) | collective-permute-done | bytes 65568 | tf_op jit(solution)/shard_map/ppermute | solution.py:309
  52.5 1.6 %pad_add_fusion = f32[2,128,128]{2,1,0:T(8,128)} fusion(f32[2,64,128]{2,1,0:T(8,128)S(1)} %collective-permute-done.3, f32[2,128,128]{2,1,0:T(8,128)} %get-tuple-element.7, f32[2,64,128]{2,1,0:T(8,128)S(1)} %collective-permute-done.2), kind=kLoop, calls=%fused_computation | loop fusion | flops 65536 | bytes 393216 | tf_op jit(solution)/shard_map/add | solution.py:312
Async XLA Ops:
  0.6 16.8 %collective-permute-start = (f32[2,128,128]{2,1,0:T(8,128)}, f32[2,128,128]{2,1,0:T(8,128)S(1)}, u32[]{:S(2)}, u32[]{:S(2)}) collective-permute-start(f32[2,128,128]{2,1,0:T(8,128)} %own.1), channel_id=1, source_target_pairs={{0,1},{1,2},{2,3},{3,4},{4,5},{5,6},{6,7},{7,8},{8,9},{9,10},{10,1... | collective-permute-start | bytes 393224 | tf_op jit(solution)/shard_map/ppermute | solution.py:249
  4.3 13.1 %collective-permute-start.1 = (f32[2,128,128]{2,1,0:T(8,128)}, f32[2,128,128]{2,1,0:T(8,128)S(1)}, u32[]{:S(2)}, u32[]{:S(2)}) collective-permute-start(f32[2,128,128]{2,1,0:T(8,128)} %own.1), channel_id=1, source_target_pairs={{1,0},{2,1},{3,2},{4,3},{5,4},{6,5},{7,6},{8,7},{9,8},{10,9},{11,1... | collective-permute-start | bytes 393224 | tf_op jit(solution)/shard_map/ppermute | solution.py:250
  17.4 0.7 %copy-start = (f32[2,128,128]{2,1,0:T(8,128)}, f32[2,128,128]{2,1,0:T(8,128)S(1)}, u32[]{:S(2)}) copy-start(f32[2,128,128]{2,1,0:T(8,128)S(1)} %collective-permute-done.above) | copy-start | bytes 393220
  18.1 0.7 %copy-start.1 = (f32[2,128,128]{2,1,0:T(8,128)}, f32[2,128,128]{2,1,0:T(8,128)S(1)}, u32[]{:S(2)}) copy-start(f32[2,128,128]{2,1,0:T(8,128)S(1)} %collective-permute-done.1.below) | copy-start | bytes 393220
  41.2 6.5 %collective-permute-start.2 = (f32[2,64,128]{2,1,0:T(8,128)}, f32[2,64,128]{2,1,0:T(8,128)S(1)}, u32[]{:S(2)}, u32[]{:S(2)}) collective-permute-start(f32[2,64,128]{2,1,0:T(8,128)} %get-tuple-element.8), channel_id=1, source_target_pairs={{0,1},{1,2},{2,3},{3,4},{4,5},{5,6},{6,7},{7,8},{8,9},{9,10},{10,1... | collective-permute-start | bytes 196616 | tf_op jit(solution)/shard_map/ppermute | solution.py:310
  45.8 6.7 %collective-permute-start.3 = (f32[2,64,128]{2,1,0:T(8,128)}, f32[2,64,128]{2,1,0:T(8,128)S(1)}, u32[]{:S(2)}, u32[]{:S(2)}) collective-permute-start(f32[2,64,128]{2,1,0:T(8,128)} %get-tuple-element.9), channel_id=1, source_target_pairs={{1,0},{2,1},{3,2},{4,3},{5,4},{6,5},{7,6},{8,7},{9,8},{10,9},{11,1... | collective-permute-start | bytes 196616 | tf_op jit(solution)/shard_map/ppermute | solution.py:309

commit v5 on v4

--- a/solution.py
+++ b/solution.py
@@ -112,17 +112,17 @@
         inside = reach < radii[first + k]
         parts = [jnp.where(inside, taps[k, c], 0.0) for c in range(2)]
         planes.append(jnp.concatenate(parts, axis=0))
-    for k, (a, b) in enumerate(dft(jnp.concatenate(planes, axis=1), row_tab, head, tail, 128)):
+    for k, (a, b) in enumerate(dft(jnp.concatenate(planes, axis=1), row_tab, head, tail, 256)):
         spec[k, :, :a.shape[1]] = a
         spec[k, :, a.shape[1]:] = b
 
 
 def main_body(
-    group, weight,
-    own, above, below, target, mask_row, mask_head, mask_tail, spec_far, *rest,
+    group, weight, place,
+    own, near, far, target, mask_row, mask_head, mask_tail, spec_far, *rest,
 ):
     tables_far, rest = rest[:7], rest[7:]
-    resist, grad_own, grad_up, grad_down = rest[:4]
+    resist, grad_own, near_rim, far_rim = rest[:4]
     spec, field, mask_spec, slopes, grad_spec, spec_sems, table_sems = rest[4:11]
     tables = rest[11:]
     kernels, grid_rows, _ = spec.shape
@@ -146,9 +146,15 @@
     for i in range(2, 7):
         fetch_table(i).start()
 
-    mask = jnp.concatenate(
-        [part for c in range(2) for part in (above[c, count - rim:], own[c], below[c, :rim])], axis=0
-    )
+    odd = place[0] % 2
+    has_above = place[0] > 0
+    has_below = place[0] < place[1] - 1
+    parts = []
+    for c in range(2):
+        above = jnp.where(odd == 1, near[0, c, count - rim:], far[0, c, count - rim:])
+        below = jnp.where(odd == 1, far[1, c, :rim], near[1, c, :rim])
+        parts += [jnp.where(has_above, above, 0.0), own[c], jnp.where(has_below, below, 0.0)]
+    mask = jnp.concatenate(parts, axis=0)
     m_first, m_rest = to_freqs(side(over_rows(mask_row, mask, 256)), mask_head, mask_tail, 256)
     lane = lax.broadcasted_iota(jnp.int32, m_rest.shape, 1)
     real_half = lane < m_rest.shape[1] // 2
@@ -230,9 +236,10 @@
     full = over_rows(grad_row, jnp.concatenate([back[:, :width], back[:, width:]], axis=0), 256)
     for c in range(2):
         base = c * grid_rows
-        grad_up[c] = full[base:base + rim]
+        rise, fall = full[base:base + rim], full[base + rim + count:base + grid_rows]
+        near_rim[c] = jnp.where(odd == 1, rise, fall)
+        far_rim[c] = jnp.where(odd == 1, fall, rise)
         grad_own[c] = full[base + rim:base + rim + count]
-        grad_down[c] = full[base + rim + count:base + grid_rows]
 
 
 def on_device(mask_field, target, kernel_taps, kernel_radii, kernel_group, kernel_weight):
@@ -244,10 +251,14 @@
     assert count == span and width == span and kernels % BATCH == 0
 
     strips = lax.axis_size("row")
-    down = [(i, i + 1) for i in range(strips - 1)]
-    up = [(i + 1, i) for i in range(strips - 1)]
-    above = lax.ppermute(mask_field, "row", down)
-    below = lax.ppermute(mask_field, "row", up)
+    assert strips % 2 == 0
+    at = lax.axis_index("row")
+    odd = at % 2
+    near_pairs = [[i, i + 1] for i in range(0, strips, 2)]
+    far_pairs = [[i, (i + 1) % strips] for i in range(1, strips, 2)]
+    near = lax.all_gather(mask_field, "row", axis_index_groups=near_pairs)
+    far = lax.all_gather(mask_field, "row", axis_index_groups=far_pairs)
+    place = jnp.stack([at, jnp.int32(strips)]).astype(jnp.int32)
 
     scale = 1.0 / (grid_rows * grid_cols)
     order = grouped(grid_cols, width)
@@ -279,8 +290,8 @@
         name="spectra",
     )(kernel_radii, kernel_taps, *map(jnp.asarray, (row_tab, head, tail)))
 
-    far = [jnp.asarray(t) for t in (col_inv, row_inv, row_tab, head, tail, grad_col, grad_row)]
-    resist, own, up_rim, down_rim = pl.pallas_call(
+    late = [jnp.asarray(t) for t in (col_inv, row_inv, row_tab, head, tail, grad_col, grad_row)]
+    resist, own, near_rim, far_rim = pl.pallas_call(
         main_body,
         out_shape=[
             jax.ShapeDtypeStruct((GROUPS, count, width), f32),
@@ -288,7 +299,7 @@
             jax.ShapeDtypeStruct((2, rim, width), f32),
             jax.ShapeDtypeStruct((2, rim, width), f32),
         ],
-        in_specs=[smem] * 2 + [vmem] * 7 + [anywhere] * 8,
+        in_specs=[smem] * 3 + [vmem] * 7 + [anywhere] * 8,
         out_specs=[vmem] * 4,
         scratch_shapes=[
             pltpu.VMEM((kernels, grid_rows, 2 * grid_cols), f32),
@@ -297,17 +308,21 @@
             pltpu.VMEM((GROUPS, count, width), f32),
             pltpu.VMEM((grid_rows, 4 * width), f32),
             pltpu.SemaphoreType.DMA((kernels // BATCH,)),
-            pltpu.SemaphoreType.DMA((len(far),)),
-        ] + [pltpu.VMEM(t.shape, bf16) for t in far],
+            pltpu.SemaphoreType.DMA((len(late),)),
+        ] + [pltpu.VMEM(t.shape, bf16) for t in late],
         compiler_params=pltpu.CompilerParams(vmem_limit_bytes=56 * MIB),
         name="fields",
     )(
-        kernel_group, kernel_weight, mask_field, above, below, target,
-        *map(jnp.asarray, (mask_row, mask_head, mask_tail)), spectra, *far,
+        kernel_group, kernel_weight, place, mask_field, near, far, target,
+        *map(jnp.asarray, (mask_row, mask_head, mask_tail)), spectra, *late,
     )
 
-    from_below = lax.ppermute(up_rim, "row", up)
-    from_above = lax.ppermute(down_rim, "row", down)
+    near_rims = lax.all_gather(near_rim, "row", axis_index_groups=near_pairs)
+    far_rims = lax.all_gather(far_rim, "row", axis_index_groups=far_pairs)
+    from_above = jnp.where(odd == 1, near_rims[0], far_rims[0])
+    from_above = jnp.where(at > 0, from_above, 0.0)
+    from_below = jnp.where(odd == 1, far_rims[1], near_rims[1])
+    from_below = jnp.where(at < strips - 1, from_below, 0.0)
     gradient = (
         own
         + jnp.pad(from_above, ((0, 0), (0, count - rim), (0, 0)))

time: 54.5 us -> 60.8 us (1.12)
  the two profiles are of different devices: /device:TPU:21 before, /device:TPU:0 now
where the time goes in v5:
time: 60.8 us; the launch traced here: 60.3 us
  Pallas kernels  33.6 us (55%)
  blocking collectives  23.9 us (39%)
  other arithmetic  2.22 us (4%)
  between operations  0.65 us (1%)
    pallas_call x1, Pallas kernels, on_device(): pl.pallas_call(main_body, out_shape=[jax.ShapeDtypeStruct((GROUPS, count,...  22.5 us
    pallas_call x1, Pallas kernels, on_device(): pl.pallas_call(spectra_body, grid=(kernels // BATCH,), out_shape=jax.Shap...  11.1 us
    all_gather x1, blocking collectives, on_device(): far = lax.all_gather(mask_field, 'row', axis_index_groups=far_pairs)  10.8 us
    all_gather x1, blocking collectives, on_device(): far_rims = lax.all_gather(far_rim, 'row', axis_index_groups=far_pairs)  7.28 us
    all_gather x1, blocking collectives, on_device(): near = lax.all_gather(mask_field, 'row', axis_index_groups=near_pairs)  3.77 us
    all_gather x1, blocking collectives, on_device(): near_rims = lax.all_gather(near_rim, 'row', axis_index_groups=near_pairs)  2.1 us
    add x1, other arithmetic, on_device(): own + jnp.pad(from_above, ((0, 0), (0, count - rim), (0, 0)))  1.58 us

profile of v5, /device:TPU:0, one launch (start us, length us, event | category | flops | bytes accessed | tf_op | source)
XLA Modules:
  0.0 60.3 jit_solution(2082413713677142208)
XLA Ops:
  0.6 0.6 %pad_add_fusion.1.place = s32[2]{0:T(128)} fusion(s32[1]{0:T(128)} %constant.40.clone.1, s32[1]{0:T(128)} %bitcast), kind=kLoop, calls=%fused_computation.5 | loop fusion | flops 2 | bytes 16 | tf_op jit(solution)/shard_map/stack | solution.py:261
  1.2 3.8 %all-gather = f32[4,128,128]{2,1,0:T(8,128)} all-gather(f32[2,128,128]{2,1,0:T(8,128)} %own.1), channel_id=2, replica_groups={{0,1},{2,3},{4,5},{6,7},{8,9},{10,11},{12,13},{14,15},{16,17},{18,19},{..., dimensions={0}, use_global_device_ids=true | all-gather | bytes 393216 | tf_op jit(solution)/shard_map/all_gather | solution.py:259
  5.0 10.8 %all-gather.1 = f32[4,128,128]{2,1,0:T(8,128)} all-gather(f32[2,128,128]{2,1,0:T(8,128)} %own.1), channel_id=3, replica_groups={{1,2},{3,4},{5,6},{7,8},{9,10},{11,12},{13,14},{15,0},{17,18},{19,20},{..., dimensions={0}, use_global_device_ids=true | all-gather | bytes 393216 | tf_op jit(solution)/shard_map/all_gather | solution.py:260
  15.8 11.1 %spectra.1.spec_far = f32[24,256,384]{2,1,0:T(8,128)} custom-call(s32[24]{0:T(128)} %radii.1, f32[24,2,128,128]{3,2,1,0:T(8,128)} %taps.1, bf16[512,512]{1,0:T(8,128)(2,1)} %constant.46.clone.row_tab.rest_2_, bf16[512,256]{1,0:T(8,128)(2,1)} %constant.47.clone.head.rest_3_, bf16[256,256]{1,0:T(8,128)(2,1)} %constant.48.clone.tail.rest_4_), custom_call_target="tpu_custom_call" | custom-call | flops 17999998976 | bytes 14000000 | tf_op jit(solution)/shard_map/spectra/pallas_call | solution.py:282
  26.8 22.5 %fields.1 = (f32[3,128,128]{2,1,0:T(8,128)}, f32[2,128,128]{2,1,0:T(8,128)}, f32[2,64,128]{2,1,0:T(8,128)}, f32[2,64,128]{2,1,0:T(8,128)}) custom-call(s32[24]{0:T(128)} %group.1, f32[24]{0:T(128)} %weight.1, s32[2]{0:T(128)} %pad_add_fusion.1.place, f32[2,128,128]{2,1,0:T(8,128)} %own.1, f32[2,2,128,128]{3,2,1,0:T(8,128)} %bitcast.3, ...), custom_call_target="tpu_custom_call" | custom-call | tf_op jit(solution)/shard_map/fields/pallas_call | solution.py:294
  49.4 7.3 %all-gather.3 = f32[4,64,128]{2,1,0:T(8,128)S(1)} all-gather(f32[2,64,128]{2,1,0:T(8,128)} %get-tuple-element.9), channel_id=5, replica_groups={{1,2},{3,4},{5,6},{7,8},{9,10},{11,12},{13,14},{15,0},{17,18},{19,20},{..., dimensions={0}, use_global_device_ids=true | all-gather | bytes 196608 | tf_op jit(solution)/shard_map/all_gather | solution.py:321
  56.6 2.1 %all-gather.2 = f32[4,64,128]{2,1,0:T(8,128)S(1)} all-gather(f32[2,64,128]{2,1,0:T(8,128)} %get-tuple-element.8), channel_id=4, replica_groups={{0,1},{2,3},{4,5},{6,7},{8,9},{10,11},{12,13},{14,15},{16,17},{18,19},{..., dimensions={0}, use_global_device_ids=true | all-gather | bytes 196608 | tf_op jit(solution)/shard_map/all_gather | solution.py:320
  58.8 1.6 %pad_add_fusion = f32[2,128,128]{2,1,0:T(8,128)} fusion(f32[2,64,128]{2,1,0:T(8,128)S(1)} %get-tuple-element.11, f32[2,128,128]{2,1,0:T(8,128)} %get-tuple-element.7, f32[2,64,128]{2,1,0:T(8,128)S(1)} %get-tuple-element.10), kind=kLoop, calls=%fused_computation | loop fusion | flops 65536 | bytes 393216 | tf_op jit(solution)/shard_map/add | solution.py:327
  (1 shorter events, 0.0 us)

commit v6 on v5

--- a/solution.py
+++ b/solution.py
@@ -18,6 +18,7 @@
 f32 = jnp.float32
 bf16 = jnp.bfloat16
 MIB = 1024 * 1024
+LIMIT = 40
 
 
 def halves(table, axis):
@@ -146,14 +147,12 @@
     for i in range(2, 7):
         fetch_table(i).start()
 
-    odd = place[0] % 2
-    has_above = place[0] > 0
-    has_below = place[0] < place[1] - 1
+    odd = place[0] % 2 == 1
     parts = []
     for c in range(2):
-        above = jnp.where(odd == 1, near[0, c, count - rim:], far[0, c, count - rim:])
-        below = jnp.where(odd == 1, far[1, c, :rim], near[1, c, :rim])
-        parts += [jnp.where(has_above, above, 0.0), own[c], jnp.where(has_below, below, 0.0)]
+        above = jnp.where(odd, near[c, count - rim:], far[c, count - rim:])
+        below = jnp.where(odd, far[c, :rim], near[c, :rim])
+        parts += [above, own[c], below]
     mask = jnp.concatenate(parts, axis=0)
     m_first, m_rest = to_freqs(side(over_rows(mask_row, mask, 256)), mask_head, mask_tail, 256)
     lane = lax.broadcasted_iota(jnp.int32, m_rest.shape, 1)
@@ -237,8 +236,8 @@
     for c in range(2):
         base = c * grid_rows
         rise, fall = full[base:base + rim], full[base + rim + count:base + grid_rows]
-        near_rim[c] = jnp.where(odd == 1, rise, fall)
-        far_rim[c] = jnp.where(odd == 1, fall, rise)
+        near_rim[c] = jnp.where(odd, rise, fall)
+        far_rim[c] = jnp.where(odd, fall, rise)
         grad_own[c] = full[base + rim:base + rim + count]
 
 
@@ -253,12 +252,12 @@
     strips = lax.axis_size("row")
     assert strips % 2 == 0
     at = lax.axis_index("row")
-    odd = at % 2
-    near_pairs = [[i, i + 1] for i in range(0, strips, 2)]
-    far_pairs = [[i, (i + 1) % strips] for i in range(1, strips, 2)]
-    near = lax.all_gather(mask_field, "row", axis_index_groups=near_pairs)
-    far = lax.all_gather(mask_field, "row", axis_index_groups=far_pairs)
-    place = jnp.stack([at, jnp.int32(strips)]).astype(jnp.int32)
+    odd = at % 2 == 1
+    near_pairs = [(i, i ^ 1) for i in range(strips)]
+    far_pairs = [(i, ((i + 1) ^ 1) - 1) for i in range(1, strips - 1)]
+    near = lax.ppermute(mask_field, "row", near_pairs)
+    far = lax.ppermute(mask_field, "row", far_pairs)
+    place = at.astype(jnp.int32).reshape(1)
 
     scale = 1.0 / (grid_rows * grid_cols)
     order = grouped(grid_cols, width)
@@ -310,19 +309,17 @@
             pltpu.SemaphoreType.DMA((kernels // BATCH,)),
             pltpu.SemaphoreType.DMA((len(late),)),
         ] + [pltpu.VMEM(t.shape, bf16) for t in late],
-        compiler_params=pltpu.CompilerParams(vmem_limit_bytes=56 * MIB),
+        compiler_params=pltpu.CompilerParams(vmem_limit_bytes=LIMIT * MIB),
         name="fields",
     )(
         kernel_group, kernel_weight, place, mask_field, near, far, target,
         *map(jnp.asarray, (mask_row, mask_head, mask_tail)), spectra, *late,
     )
 
-    near_rims = lax.all_gather(near_rim, "row", axis_index_groups=near_pairs)
-    far_rims = lax.all_gather(far_rim, "row", axis_index_groups=far_pairs)
-    from_above = jnp.where(odd == 1, near_rims[0], far_rims[0])
-    from_above = jnp.where(at > 0, from_above, 0.0)
-    from_below = jnp.where(odd == 1, far_rims[1], near_rims[1])
-    from_below = jnp.where(at < strips - 1, from_below, 0.0)
+    near_in = lax.ppermute(near_rim, "row", near_pairs)
+    far_in = lax.ppermute(far_rim, "row", far_pairs)
+    from_above = jnp.where(odd, near_in, far_in)
+    from_below = jnp.where(odd, far_in, near_in)
     gradient = (
         own
         + jnp.pad(from_above, ((0, 0), (0, count - rim), (0, 0)))

time: 60.8 us -> 53.9 us (0.89)
  the two profiles are of different devices: /device:TPU:0 before, /device:TPU:21 now
where the time goes in v6:
time: 53.9 us; the launch traced here: 53.2 us
  Pallas kernels  32.9 us (61%)
  starting transfers between devices  7.59 us (14%)
  local copies, waits for them, and re-layouts  7.13 us (13%)
  waiting for transfers between devices  3.13 us (6%)
  other arithmetic  1.6 us (3%)
  between operations  0.82 us (2%)
    pallas_call x1, Pallas kernels, on_device(): pl.pallas_call(main_body, out_shape=[jax.ShapeDtypeStruct((GROUPS, count,...  21.8 us
    pallas_call x1, Pallas kernels, on_device(): pl.pallas_call(spectra_body, grid=(kernels // BATCH,), out_shape=jax.Shap...  11.1 us
    unnamed x30, local copies, waits for them, and re-layouts  7.13 us
    ppermute x1, starting transfers between devices, on_device(): far_in = lax.ppermute(far_rim, 'row', far_pairs)  3.53 us
    ppermute x1, starting transfers between devices, on_device(): far = lax.ppermute(mask_field, 'row', far_pairs)  3.32 us
    ppermute x1, waiting for transfers between devices, on_device(): far_in = lax.ppermute(far_rim, 'row', far_pairs)  3.12 us
    add x1, other arithmetic, on_device(): own + jnp.pad(from_above, ((0, 0), (0, count - rim), (0, 0)))  1.58 us
  transfers between devices with their start and end apart: 4, of which 1 were waited for; matrix products, arithmetic and copies ran while one was open for 0% of the time, Pallas kernels for 21%

profile of v6, /device:TPU:21, one launch (start us, length us, event | category | flops | bytes accessed | tf_op | source)
XLA Modules:
  0.0 53.2 jit_solution(2784244441276256595)
XLA Ops:
  0.6 0.0 copy-start
  0.6 0.0 copy-start.1
  0.7 0.0 copy-start.2
  0.7 0.0 copy-start.3
  0.7 0.0 copy-start.4
  0.7 0.7 %collective-permute-start = (f32[2,128,128]{2,1,0:T(8,128)}, f32[2,128,128]{2,1,0:T(8,128)}, u32[]{:S(2)}, u32[]{:S(2)}) collective-permute-start(f32[2,128,128]{2,1,0:T(8,128)} %own.1), channel_id=1, source_target_pairs={{0,1},{1,0},{2,3},{3,2},{4,5},{5,4},{6,7},{7,6},{8,9},{9,8},{10,11... | collective-permute-start | bytes 393224 | tf_op jit(solution)/shard_map/ppermute | solution.py:258
  1.5 3.3 %collective-permute-start.1 = (f32[2,128,128]{2,1,0:T(8,128)}, f32[2,128,128]{2,1,0:T(8,128)}, u32[]{:S(2)}, u32[]{:S(2)}) collective-permute-start(f32[2,128,128]{2,1,0:T(8,128)} %own.1), channel_id=1, source_target_pairs={{1,2},{2,1},{3,4},{4,3},{5,6},{6,5},{7,8},{8,7},{9,10},{10,9},{11,... | collective-permute-start | bytes 393224 | tf_op jit(solution)/shard_map/ppermute | solution.py:259
  4.8 11.1 %spectra.1.spec_far = f32[24,256,384]{2,1,0:T(8,128)} custom-call(s32[24]{0:T(128)} %radii.1, f32[24,2,128,128]{3,2,1,0:T(8,128)} %taps.1, bf16[512,512]{1,0:T(8,128)(2,1)} %constant.41.clone.row_tab.rest_2_, bf16[512,256]{1,0:T(8,128)(2,1)} %constant.42.clone.head.rest_3_, bf16[256,256]{1,0:T(8,128)(2,1)} %constant.43.clone.tail.rest_4_), custom_call_target="tpu_custom_call" | custom-call | flops 17999998976 | bytes 14000000 | tf_op jit(solution)/shard_map/spectra/pallas_call | solution.py:281
  15.9 0.0 collective-permute-done.near
  15.9 0.0 collective-permute-done.1.far
  16.0 0.0 copy-start.5
  16.0 1.0 %copy-done.5 = bf16[768,256]{1,0:T(8,128)(2,1)S(1)} copy-done((bf16[768,256]{1,0:T(8,128)(2,1)S(1)}, bf16[768,256]{1,0:T(8,128)(2,1)}, u32[]{:S(2)}) %copy-start.5) | copy-done | bytes 393240
  17.0 0.9 %copy-done.6 = bf16[512,256]{1,0:T(8,128)(2,1)S(1)} copy-done((bf16[512,256]{1,0:T(8,128)(2,1)S(1)}, bf16[512,256]{1,0:T(8,128)(2,1)}, u32[]{:S(2)}) %copy-start.6) | copy-done | bytes 262168
  17.9 0.9 %copy-done.7 = bf16[512,256]{1,0:T(8,128)(2,1)S(1)} copy-done((bf16[512,256]{1,0:T(8,128)(2,1)S(1)}, bf16[512,256]{1,0:T(8,128)(2,1)}, u32[]{:S(2)}) %copy-start.7) | copy-done | bytes 262168
  18.9 0.9 %copy-done.8 = f32[2,128,128]{2,1,0:T(8,128)S(1)} copy-done((f32[2,128,128]{2,1,0:T(8,128)S(1)}, f32[2,128,128]{2,1,0:T(8,128)}, u32[]{:S(2)}) %copy-start.8) | copy-done | bytes 131096
  19.8 0.9 %copy-done.9 = bf16[256,256]{1,0:T(8,128)(2,1)S(1)} copy-done((bf16[256,256]{1,0:T(8,128)(2,1)S(1)}, bf16[256,256]{1,0:T(8,128)(2,1)}, u32[]{:S(2)}) %copy-start.9) | copy-done | bytes 131096
  20.7 0.9 %copy-done.10 = bf16[256,256]{1,0:T(8,128)(2,1)S(1)} copy-done((bf16[256,256]{1,0:T(8,128)(2,1)S(1)}, bf16[256,256]{1,0:T(8,128)(2,1)}, u32[]{:S(2)}) %copy-start.10) | copy-done | bytes 131096
  21.6 0.8 %copy-done.12 = s32[128,128]{1,0:T(8,128)S(1)} copy-done((s32[128,128]{1,0:T(8,128)S(1)}, s32[128,128]{1,0:T(8,128)}, u32[]{:S(2)}) %copy-start.12) | copy-done | bytes 65560
  22.4 21.8 %fields.1 = (f32[3,128,128]{2,1,0:T(8,128)}, f32[2,128,128]{2,1,0:T(8,128)S(1)}, f32[2,64,128]{2,1,0:T(8,128)}, f32[2,64,128]{2,1,0:T(8,128)}) custom-call(s32[24]{0:T(128)S(1)} %copy-done.13, f32[24]{0:T(128)S(1)} %copy-done.14, s32[1]{0:T(128)} %bitcast.place, f32[2,128,128]{2,1,0:T(8,128)S(1)} %copy-done.8, f32[2,128,128]{2,1,0:T(8,128)} %collective-permute-done.near, ...), custom_call_target="tpu_custom_call" | custom-call | tf_op jit(solution)/shard_map/fields/pallas_call | solution.py:293
  44.2 0.0 copy-start.11
  44.3 0.6 %copy-done.11 = f32[2,128,128]{2,1,0:T(8,128)} copy-done((f32[2,128,128]{2,1,0:T(8,128)}, f32[2,128,128]{2,1,0:T(8,128)S(1)}, u32[]{:S(2)}) %copy-start.11) | copy-done | bytes 131096
  44.9 3.5 %collective-permute-start.3 = (f32[2,64,128]{2,1,0:T(8,128)}, f32[2,64,128]{2,1,0:T(8,128)S(1)}, u32[]{:S(2)}, u32[]{:S(2)}) collective-permute-start(f32[2,64,128]{2,1,0:T(8,128)} %get-tuple-element.9), channel_id=1, source_target_pairs={{1,2},{2,1},{3,4},{4,3},{5,6},{6,5},{7,8},{8,7},{9,10},{10,9},{11,... | collective-permute-start | bytes 196616 | tf_op jit(solution)/shard_map/ppermute | solution.py:320
  48.5 3.1 %collective-permute-done.3 = f32[2,64,128]{2,1,0:T(8,128)S(1)} collective-permute-done((f32[2,64,128]{2,1,0:T(8,128)}, f32[2,64,128]{2,1,0:T(8,128)S(1)}, u32[]{:S(2)}, u32[]{:S(2)}) %collective-permute-start.3) | collective-permute-done | bytes 65568 | tf_op jit(solution)/shard_map/ppermute | solution.py:320
  51.6 1.6 %pad_add_fusion = f32[2,128,128]{2,1,0:T(8,128)} fusion(f32[2,64,128]{2,1,0:T(8,128)S(1)} %get-tuple-element.11, f32[2,128,128]{2,1,0:T(8,128)} %copy-done.11, f32[2,64,128]{2,1,0:T(8,128)S(1)} %get-tuple-element.10), kind=kLoop, calls=%fused_computation | loop fusion | flops 65536 | bytes 393216 | tf_op jit(solution)/shard_map/add | solution.py:324
  (18 shorter events, 0.0 us)
Async XLA Ops:
  0.6 15.3 %copy-start = (bf16[512,1024]{1,0:T(8,128)(2,1)S(1)}, bf16[512,1024]{1,0:T(8,128)(2,1)}, u32[]{:S(2)}) copy-start(bf16[512,1024]{1,0:T(8,128)(2,1)} %constant.48.clone.mask_row) | copy-start | bytes 3145732
  0.6 15.3 %copy-start.1 = (bf16[512,1024]{1,0:T(8,128)(2,1)S(1)}, bf16[512,1024]{1,0:T(8,128)(2,1)}, u32[]{:S(2)}) copy-start(bf16[512,1024]{1,0:T(8,128)(2,1)} %constant.47.clone.rest_6_) | copy-start | bytes 3145732
  0.7 15.3 %copy-start.2 = (bf16[512,512]{1,0:T(8,128)(2,1)S(1)}, bf16[512,512]{1,0:T(8,128)(2,1)}, u32[]{:S(2)}) copy-start(bf16[512,512]{1,0:T(8,128)(2,1)} %constant.41.clone.row_tab.rest_2_) | copy-start | bytes 1572868
  0.7 15.2 %copy-start.3 = (bf16[256,1024]{1,0:T(8,128)(2,1)S(1)}, bf16[256,1024]{1,0:T(8,128)(2,1)}, u32[]{:S(2)}) copy-start(bf16[256,1024]{1,0:T(8,128)(2,1)} %constant.45.clone.rest_1_) | copy-start | bytes 1572868
  0.7 15.2 %copy-start.4 = (bf16[768,256]{1,0:T(8,128)(2,1)S(1)}, bf16[768,256]{1,0:T(8,128)(2,1)}, u32[]{:S(2)}) copy-start(bf16[768,256]{1,0:T(8,128)(2,1)} %constant.44.clone.rest_0_) | copy-start | bytes 1179652
  0.7 15.2 %copy-start.13 = (s32[24]{0:T(128)S(1)}, s32[24]{0:T(128)}, u32[]{:S(2)}) copy-start(s32[24]{0:T(128)} %group.1) | copy-start | bytes 292
  0.7 15.2 %copy-start.14 = (f32[24]{0:T(128)S(1)}, f32[24]{0:T(128)}, u32[]{:S(2)}) copy-start(f32[24]{0:T(128)} %weight.1) | copy-start | bytes 292
  0.7 15.2 %collective-permute-start = (f32[2,128,128]{2,1,0:T(8,128)}, f32[2,128,128]{2,1,0:T(8,128)}, u32[]{:S(2)}, u32[]{:S(2)}) collective-permute-start(f32[2,128,128]{2,1,0:T(8,128)} %own.1), channel_id=1, source_target_pairs={{0,1},{1,0},{2,3},{3,2},{4,5},{5,4},{6,7},{7,6},{8,9},{9,8},{10,11... | collective-permute-start | bytes 393224 | tf_op jit(solution)/shard_map/ppermute | solution.py:258
  1.5 14.4 %collective-permute-start.1 = (f32[2,128,128]{2,1,0:T(8,128)}, f32[2,128,128]{2,1,0:T(8,128)}, u32[]{:S(2)}, u32[]{:S(2)}) collective-permute-start(f32[2,128,128]{2,1,0:T(8,128)} %own.1), channel_id=1, source_target_pairs={{1,2},{2,1},{3,4},{4,3},{5,6},{6,5},{7,8},{8,7},{9,10},{10,9},{11,... | collective-permute-start | bytes 393224 | tf_op jit(solution)/shard_map/ppermute | solution.py:259
  16.0 1.0 %copy-start.5 = (bf16[768,256]{1,0:T(8,128)(2,1)S(1)}, bf16[768,256]{1,0:T(8,128)(2,1)}, u32[]{:S(2)}) copy-start(bf16[768,256]{1,0:T(8,128)(2,1)} %constant.46.clone.rest_5_) | copy-start | bytes 1179652
  17.0 0.9 %copy-start.6 = (bf16[512,256]{1,0:T(8,128)(2,1)S(1)}, bf16[512,256]{1,0:T(8,128)(2,1)}, u32[]{:S(2)}) copy-start(bf16[512,256]{1,0:T(8,128)(2,1)} %constant.42.clone.head.rest_3_) | copy-start | bytes 786436
  17.9 0.9 %copy-start.7 = (bf16[512,256]{1,0:T(8,128)(2,1)S(1)}, bf16[512,256]{1,0:T(8,128)(2,1)}, u32[]{:S(2)}) copy-start(bf16[512,256]{1,0:T(8,128)(2,1)} %constant.49.clone.mask_head) | copy-start | bytes 786436
  18.9 0.9 %copy-start.8 = (f32[2,128,128]{2,1,0:T(8,128)S(1)}, f32[2,128,128]{2,1,0:T(8,128)}, u32[]{:S(2)}) copy-start(f32[2,128,128]{2,1,0:T(8,128)} %own.1) | copy-start | bytes 393220
  19.8 0.9 %copy-start.9 = (bf16[256,256]{1,0:T(8,128)(2,1)S(1)}, bf16[256,256]{1,0:T(8,128)(2,1)}, u32[]{:S(2)}) copy-start(bf16[256,256]{1,0:T(8,128)(2,1)} %constant.43.clone.tail.rest_4_) | copy-start | bytes 393220
  20.7 0.9 %copy-start.10 = (bf16[256,256]{1,0:T(8,128)(2,1)S(1)}, bf16[256,256]{1,0:T(8,128)(2,1)}, u32[]{:S(2)}) copy-start(bf16[256,256]{1,0:T(8,128)(2,1)} %constant.50.clone.mask_tail) | copy-start | bytes 393220
  21.6 0.8 %copy-start.12 = (s32[128,128]{1,0:T(8,128)S(1)}, s32[128,128]{1,0:T(8,128)}, u32[]{:S(2)}) copy-start(s32[128,128]{1,0:T(8,128)} %target.1) | copy-start | bytes 196612
  44.2 0.7 %copy-start.11 = (f32[2,128,128]{2,1,0:T(8,128)}, f32[2,128,128]{2,1,0:T(8,128)S(1)}, u32[]{:S(2)}) copy-start(f32[2,128,128]{2,1,0:T(8,128)S(1)} %get-tuple-element.7) | copy-start | bytes 393220
  44.9 3.6 %collective-permute-start.2 = (f32[2,64,128]{2,1,0:T(8,128)}, f32[2,64,128]{2,1,0:T(8,128)S(1)}, u32[]{:S(2)}, u32[]{:S(2)}) collective-permute-start(f32[2,64,128]{2,1,0:T(8,128)} %get-tuple-element.8), channel_id=1, source_target_pairs={{0,1},{1,0},{2,3},{3,2},{4,5},{5,4},{6,7},{7,6},{8,9},{9,8},{10,11... | collective-permute-start | bytes 196616 | tf_op jit(solution)/shard_map/ppermute | solution.py:319
  44.9 6.7 %collective-permute-start.3 = (f32[2,64,128]{2,1,0:T(8,128)}, f32[2,64,128]{2,1,0:T(8,128)S(1)}, u32[]{:S(2)}, u32[]{:S(2)}) collective-permute-start(f32[2,64,128]{2,1,0:T(8,128)} %get-tuple-element.9), channel_id=1, source_target_pairs={{1,2},{2,1},{3,4},{4,3},{5,6},{6,5},{7,8},{8,7},{9,10},{10,9},{11,... | collective-permute-start | bytes 196616 | tf_op jit(solution)/shard_map/ppermute | solution.py:320

commit v7 on v6

v7 whole, which is shorter than its diff:
```python
import math

import jax
import jax.numpy as jnp
import ml_dtypes
import numpy as np
from jax import lax
from jax.experimental import pallas as pl
from jax.experimental.pallas import tpu as pltpu
from jax.sharding import PartitionSpec as P

RMAX = 64
GROUPS = 3
STEEPNESS = 1.0
THRESHOLD = 2.0
BATCH = 8
PIECE = 256

f32 = jnp.float32
bf16 = jnp.bfloat16
MIB = 1024 * 1024
LIMIT = 40


def halves(table, axis):
    high = table.astype(ml_dtypes.bfloat16)
    low = (table - high.astype(np.float64)).astype(ml_dtypes.bfloat16)
    return np.concatenate([high, low], axis=axis)


def analysis(freqs, points, shift):
    f = np.arange(freqs)[:, None]
    n = np.arange(points)[None, :] - shift
    angle = 2.0 * math.pi * ((f * n) % freqs) / freqs
    cos, sin = np.cos(angle), np.sin(angle)
    return np.block([[cos, sin], [-sin, cos]])


def synthesis(freqs, points, shift, scale=1.0):
    return analysis(freqs, points, shift).T * scale


def grouped(freqs, lanes):
    head, tail = np.arange(lanes), np.arange(lanes, freqs)
    return np.concatenate([head, freqs + head, tail, freqs + tail])


def split(x):
    high = x.astype(bf16)
    low = (x - high.astype(f32)).astype(bf16)
    return high, low


def dot(left, right):
    parts = [
        jnp.dot(left[at:at + PIECE], right, preferred_element_type=f32)
        for at in range(0, left.shape[0], PIECE)
    ]
    return jnp.concatenate(parts, axis=0)


def over_rows(table, x):
    high, low = split(x)
    left = table[...]
    left = jnp.concatenate([left, left[:, :x.shape[0]]], axis=1)
    return dot(left, jnp.concatenate([high, high, low], axis=0))


def over_lanes(x, table):
    high, low = split(x)
    right = table[...]
    right = jnp.concatenate([right, right[:x.shape[1]]], axis=0)
    return dot(jnp.concatenate([high, high, low], axis=1), right)


def to_freqs(x, head, tail):
    high, low = split(x)
    right = head[...]
    right = jnp.concatenate([right, right[:x.shape[1]]], axis=0)
    first = dot(jnp.concatenate([high, high, low], axis=1), right)
    right = tail[...]
    rest = dot(jnp.concatenate([high, low], axis=1), jnp.concatenate([right, right], axis=0))
    lanes = rest.shape[1] // 2
    return first, rest[:, :lanes] + rest[:, lanes:]


def side(x):
    rows = x.shape[0] // 2
    return jnp.concatenate([x[:rows], x[rows:]], axis=1)


def row_stage(pair, row_tab):
    width = pair.shape[1] // 2
    half = over_rows(row_tab, pair)
    return [side(half[:, :width]), side(half[:, width:])]


def staggered(count, first, second):
    held = None
    for i in range(count):
        new = first(i)
        if i:
            second(i - 1, held)
        held = new
    second(count - 1, held)


def swap(x):
    return pltpu.roll(x, x.shape[1] // 2, 1)


def spectra_body(radii, taps, row_tab, head, tail, spec):
    batch, _, span, _ = taps.shape
    first = pl.program_id(0) * batch
    row_at = lax.broadcasted_iota(jnp.int32, (span, span), 0) - span // 2
    col_at = lax.broadcasted_iota(jnp.int32, (span, span), 1) - span // 2
    reach = jnp.maximum(jnp.maximum(row_at, -1 - row_at), jnp.maximum(col_at, -1 - col_at))

    def rows_of(p):
        planes = []
        for k in (2 * p, 2 * p + 1):
            inside = reach < radii[first + k]
            parts = [jnp.where(inside, taps[k, c], 0.0) for c in range(2)]
            planes.append(jnp.concatenate(parts, axis=0))
        return row_stage(jnp.concatenate(planes, axis=1), row_tab)

    def cols_of(p, tiles):
        for j in range(2):
            a, b = to_freqs(tiles[j], head, tail)
            spec[2 * p + j, :, :a.shape[1]] = a
            spec[2 * p + j, :, a.shape[1]:] = b

    staggered(batch // 2, rows_of, cols_of)


def main_body(
    group, weight, place,
    own, near, far, target, mask_row, mask_head, mask_tail, spec_far, *rest,
):
    tables_far, rest = rest[:7], rest[7:]
    resist_far, grad_own, near_rim, far_rim = rest[:4]
    spec, field, mask_spec, resist, slopes, grad_spec, spec_sems, table_sems, out_sem = rest[4:13]
    tables = rest[13:]
    kernels, grid_rows, _ = spec.shape
    count, width = target.shape
    rim = (grid_rows - count) // 2
    steps = spec_sems.shape[0]
    batch = kernels // steps

    def fetch(i):
        here = pl.ds(i * batch, batch)
        return pltpu.make_async_copy(spec_far.at[here], spec.at[here], spec_sems.at[i])

    def fetch_table(i):
        return pltpu.make_async_copy(tables_far[i], tables[i], table_sems.at[i])

    col_inv, row_inv, row_tab, head, tail, grad_col, grad_row = tables
    for i in range(2):
        fetch_table(i).start()
    for i in range(steps):
        fetch(i).start()
    for i in range(2, 7):
        fetch_table(i).start()

    odd = place[0] % 2 == 1
    parts = []
    for c in range(2):
        above = jnp.where(odd, near[c, count - rim:], far[c, count - rim:])
        below = jnp.where(odd, far[c, :rim], near[c, :rim])
        parts += [above, own[c], below]
    mask = jnp.concatenate(parts, axis=0)
    m_first, m_rest = to_freqs(side(over_rows(mask_row, mask)), mask_head, mask_tail)
    lane = lax.broadcasted_iota(jnp.int32, m_rest.shape, 1)
    real_half = lane < m_rest.shape[1] // 2
    turned = swap(m_rest)
    mask_spec[:, :2 * width] = m_first
    mask_spec[:, 2 * width:3 * width] = jnp.where(real_half, m_rest, turned)
    mask_spec[:, 3 * width:] = jnp.where(real_half, -turned, m_rest)

    slopes[...] = jnp.zeros(slopes.shape, f32)
    grad_spec[...] = jnp.zeros(grad_spec.shape, f32)
    for i in range(2):
        fetch_table(i).wait()

    def forward(i, carry):
        fetch(i).wait()
        m_re, m_im = mask_spec[:, :width], mask_spec[:, width:2 * width]
        m_same, m_cross = mask_spec[:, 2 * width:3 * width], mask_spec[:, 3 * width:]

        def cols_of(p):
            planes = []
            for j in range(2):
                k = i * batch + 2 * p + j
                s_re, s_im, s_rest = spec[k, :, :width], spec[k, :, width:2 * width], spec[k, :, 2 * width:]
                product = jnp.concatenate([
                    s_re * m_re - s_im * m_im,
                    s_re * m_im + s_im * m_re,
                    s_rest * m_same + swap(s_rest) * m_cross,
                ], axis=1)
                back = over_lanes(product, col_inv)
                planes.append(jnp.concatenate([back[:, :width], back[:, width:]], axis=0))
            return jnp.concatenate(planes, axis=1)

        def rows_of(p, pair):
            found = over_rows(row_inv, pair)
            field[i * (batch // 2) + p] = found
            power = found[:count] * found[:count] + found[count:] * found[count:]
            for j in range(2):
                k = i * batch + 2 * p + j
                g = group[k]
                slopes[g] = slopes[g] + weight[k] * power[:, j * width:(j + 1) * width]

        staggered(batch // 2, cols_of, rows_of)
        return carry

    lax.fori_loop(0, steps, forward, 0)

    wanted = target[...].astype(f32)
    for g in range(GROUPS):
        seen = jax.nn.sigmoid(STEEPNESS * (slopes[g] - THRESHOLD))
        resist[g] = seen
        slopes[g] = 2.0 * (seen - wanted) * seen * (1.0 - seen) * STEEPNESS
    out = pltpu.make_async_copy(resist, resist_far, out_sem)
    out.start()
    for i in range(2, 7):
        fetch_table(i).wait()

    def backward(i, carry):
        def rows_of(p):
            factors = []
            for j in range(2):
                k = i * batch + 2 * p + j
                factors.append((2.0 * weight[k]) * slopes[group[k]])
            factor = jnp.concatenate(factors, axis=1)
            cot = field[i * (batch // 2) + p] * jnp.concatenate([factor, factor], axis=0)
            return row_stage(cot, row_tab)

        def cols_of(p, tiles):
            total = [grad_spec[:, c * width:(c + 1) * width] for c in range(4)]
            for j in range(2):
                k = i * batch + 2 * p + j
                s_re, s_im, s_rest = spec[k, :, :width], spec[k, :, width:2 * width], spec[k, :, 2 * width:]
                first, rest = to_freqs(tiles[j], head, tail)
                c_re, c_im = first[:, :width], first[:, width:]
                total[0] = total[0] + (s_re * c_re + s_im * c_im)
                total[1] = total[1] + (s_re * c_im - s_im * c_re)
                total[2] = total[2] + s_rest * rest
                total[3] = total[3] + s_rest * swap(rest)
            for c in range(4):
                grad_spec[:, c * width:(c + 1) * width] = total[c]

        staggered(batch // 2, rows_of, cols_of)
        return carry

    lax.fori_loop(0, steps, backward, 0)

    same, cross = grad_spec[:, 2 * width:3 * width], grad_spec[:, 3 * width:]
    tail_sum = jnp.where(real_half, same + swap(same), swap(cross) - cross)
    total = jnp.concatenate([grad_spec[:, :2 * width], tail_sum], axis=1)
    back = over_lanes(total, grad_col)
    full = over_rows(grad_row, jnp.concatenate([back[:, :width], back[:, width:]], axis=0))
    for c in range(2):
        base = c * grid_rows
        rise, fall = full[base:base + rim], full[base + rim + count:base + grid_rows]
        near_rim[c] = jnp.where(odd, rise, fall)
        far_rim[c] = jnp.where(odd, fall, rise)
        grad_own[c] = full[base + rim:base + rim + count]
    out.wait()


def join_body(place, own, near, far, out):
    odd = place[0] % 2 == 1
    rim = near.shape[1]
    count = own.shape[1]
    for c in range(2):
        out[c, :rim] = own[c, :rim] + jnp.where(odd, near[c], far[c])
        if count > 2 * rim:
            out[c, rim:count - rim] = own[c, rim:count - rim]
        out[c, count - rim:] = own[c, count - rim:] + jnp.where(odd, far[c], near[c])


def on_device(mask_field, target, kernel_taps, kernel_radii, kernel_group, kernel_weight):
    _, count, width = mask_field.shape
    kernels, _, span, _ = kernel_taps.shape
    rim = span // 2
    grid_rows = count + 2 * rim
    grid_cols = width + rim
    assert count == span and width == span and kernels % BATCH == 0 and BATCH % 2 == 0 and count >= 2 * rim

    strips = lax.axis_size("row")
    assert strips % 2 == 0
    at = lax.axis_index("row")
    near_pairs = [(i, i ^ 1) for i in range(strips)]
    far_pairs = [(i, ((i + 1) ^ 1) - 1) for i in range(1, strips - 1)]
    near = lax.ppermute(mask_field, "row", near_pairs)
    far = lax.ppermute(mask_field, "row", far_pairs)
    place = at.astype(jnp.int32).reshape(1)

    scale = 1.0 / (grid_rows * grid_cols)
    order = grouped(grid_cols, width)

    def head_and_tail(shift):
        table = analysis(grid_cols, width, shift).T[:, order]
        return halves(table[:, :2 * width], 0), halves(table[:, 2 * width:], 1)

    row_tab = halves(analysis(grid_rows, span, 0), 1)
    head, tail = head_and_tail(0)
    mask_row = halves(analysis(grid_rows, grid_rows, 2 * rim), 1)
    mask_head, mask_tail = head_and_tail(rim)
    col_inv = halves(synthesis(grid_cols, width, 0).T[order], 0)
    row_inv = halves(synthesis(grid_rows, count, 0, scale), 1)
    grad_col = halves(synthesis(grid_cols, width, rim).T[order], 0)
    grad_row = halves(synthesis(grid_rows, grid_rows, 2 * rim, scale), 1)

    smem = pl.BlockSpec(memory_space=pltpu.SMEM)
    vmem = pl.BlockSpec(memory_space=pltpu.VMEM)
    hbm = pl.BlockSpec(memory_space=pltpu.HBM)
    spectra = pl.pallas_call(
        spectra_body,
        grid=(kernels // BATCH,),
        out_shape=jax.ShapeDtypeStruct((kernels, grid_rows, 2 * grid_cols), f32),
        in_specs=[smem, pl.BlockSpec((BATCH, 2, span, span), lambda i: (i, 0, 0, 0)), vmem, vmem, vmem],
        out_specs=pl.BlockSpec((BATCH, grid_rows, 2 * grid_cols), lambda i: (i, 0, 0)),
        compiler_params=pltpu.CompilerParams(vmem_limit_bytes=56 * MIB),
        cost_estimate=pl.CostEstimate(flops=18 * 10**9, bytes_accessed=14 * 10**6, transcendentals=0),
        name="spectra",
    )(kernel_radii, kernel_taps, *map(jnp.asarray, (row_tab, head, tail)))

    late = [jnp.asarray(t) for t in (col_inv, row_inv, row_tab, head, tail, grad_col, grad_row)]
    resist, own, near_rim, far_rim = pl.pallas_call(
        main_body,
        out_shape=[
            jax.ShapeDtypeStruct((GROUPS, count, width), f32),
            jax.ShapeDtypeStruct((2, count, width), f32),
            jax.ShapeDtypeStruct((2, rim, width), f32),
            jax.ShapeDtypeStruct((2, rim, width), f32),
        ],
        in_specs=[smem] * 3 + [vmem] * 7 + [hbm] * 8,
        out_specs=[hbm] + [vmem] * 3,
        scratch_shapes=[
            pltpu.VMEM((kernels, grid_rows, 2 * grid_cols), f32),
            pltpu.VMEM((kernels // 2, 2 * count, 2 * width), f32),
            pltpu.VMEM((grid_rows, 4 * width), f32),
            pltpu.VMEM((GROUPS, count, width), f32),
            pltpu.VMEM((GROUPS, count, width), f32),
            pltpu.VMEM((grid_rows, 4 * width), f32),
            pltpu.SemaphoreType.DMA((kernels // BATCH,)),
            pltpu.SemaphoreType.DMA((len(late),)),
            pltpu.SemaphoreType.DMA,
        ] + [pltpu.VMEM(t.shape, bf16) for t in late],
        compiler_params=pltpu.CompilerParams(vmem_limit_bytes=LIMIT * MIB),
        name="fields",
    )(
        kernel_group, kernel_weight, place, mask_field, near, far, target,
        *map(jnp.asarray, (mask_row, mask_head, mask_tail)), spectra, *late,
    )

    near_in = lax.ppermute(near_rim, "row", near_pairs)
    far_in = lax.ppermute(far_rim, "row", far_pairs)
    gradient = pl.pallas_call(
        join_body,
        out_shape=jax.ShapeDtypeStruct((2, count, width), f32),
        in_specs=[smem] + [vmem] * 3,
        out_specs=vmem,
        name="join",
    )(place, own, near_in, far_in)
    return resist, gradient


def solution(mesh):
    in_specs = (P(None, ("win", "row"), None), P(("win", "row"), None), P(), P(), P(), P())
    out_specs = (P(None, ("win", "row"), None), P(None, ("win", "row"), None))
    return jax.shard_map(
        on_device, mesh=mesh, in_specs=in_specs, out_specs=out_specs, check_vma=False
    )
```

time: 53.9 us -> 51.4 us (0.954)
  other arithmetic: 1.6 us -> 0 us
  Pallas kernels: 32.9 us -> 31.8 us
  local copies, waits for them, and re-layouts: 7.13 us -> 7.74 us
    pallas_call x1, Pallas kernels: 21.8 us -> 19.8 us  [on_device(): pl.pallas_call(main_body, out_shape=[jax.ShapeDtypeStruct((GROUPS, count,...]
    pallas_call x0 -> x1, Pallas kernels: none -> 1.62 us  [on_device(): pl.pallas_call(join_body, out_shape=jax.ShapeDtypeStruct((2, count, width...]
    add x1 -> x0, other arithmetic: 1.58 us -> none  [on_device(): own + jnp.pad(from_above, ((0, 0), (0, count - rim), (0, 0)))]
    pallas_call x1, Pallas kernels: 11.1 us -> 10.4 us  [on_device(): pl.pallas_call(spectra_body, grid=(kernels // BATCH,), out_shape=jax.Shap...]
    unnamed x30 -> x34, local copies, waits for them, and re-layouts: 7.13 us -> 7.74 us
  transfers between devices with their start and end apart: 4 -> 4, of which waited for: 1 -> 1; matrix products, arithmetic and copies ran while one was open for 0% -> 0% of each run, Pallas kernels for 21% -> 20%
where the time goes in v7:
time: 51.4 us; the launch traced here: 50.9 us
  Pallas kernels  31.8 us (62%)
  local copies, waits for them, and re-layouts  7.74 us (15%)
  starting transfers between devices  7.61 us (15%)
  waiting for transfers between devices  2.9 us (6%)
  between operations  0.81 us (2%)
    pallas_call x1, Pallas kernels, on_device(): pl.pallas_call(main_body, out_shape=[jax.ShapeDtypeStruct((GROUPS, count,...  19.8 us
    pallas_call x1, Pallas kernels, on_device(): pl.pallas_call(spectra_body, grid=(kernels // BATCH,), out_shape=jax.Shap...  10.4 us
    unnamed x34, local copies, waits for them, and re-layouts  7.74 us
    ppermute x1, starting transfers between devices, on_device(): far_in = lax.ppermute(far_rim, 'row', far_pairs)  3.55 us
    ppermute x1, starting transfers between devices, on_device(): far = lax.ppermute(mask_field, 'row', far_pairs)  3.32 us
    ppermute x1, waiting for transfers between devices, on_device(): far_in = lax.ppermute(far_rim, 'row', far_pairs)  2.89 us
    pallas_call x1, Pallas kernels, on_device(): pl.pallas_call(join_body, out_shape=jax.ShapeDtypeStruct((2, count, width...  1.62 us
  transfers between devices with their start and end apart: 4, of which 1 were waited for; matrix products, arithmetic and copies ran while one was open for 0% of the time, Pallas kernels for 20%

profile of v7, /device:TPU:21, one launch (start us, length us, event | category | flops | bytes accessed | tf_op | source)
XLA Modules:
  0.0 50.9 jit_solution(3431257944405205811)
XLA Ops:
  0.6 0.0 copy-start
  0.6 0.0 copy-start.1
  0.7 0.0 copy-start.2
  0.7 0.0 copy-start.3
  0.7 0.0 copy-start.4
  0.7 0.7 %collective-permute-start = (f32[2,128,128]{2,1,0:T(8,128)}, f32[2,128,128]{2,1,0:T(8,128)}, u32[]{:S(2)}, u32[]{:S(2)}) collective-permute-start(f32[2,128,128]{2,1,0:T(8,128)} %own.1), channel_id=1, source_target_pairs={{0,1},{1,0},{2,3},{3,2},{4,5},{5,4},{6,7},{7,6},{8,9},{9,8},{10,11... | collective-permute-start | bytes 393224 | tf_op jit(solution)/shard_map/ppermute | solution.py:295
  1.5 3.3 %collective-permute-start.1 = (f32[2,128,128]{2,1,0:T(8,128)}, f32[2,128,128]{2,1,0:T(8,128)}, u32[]{:S(2)}, u32[]{:S(2)}) collective-permute-start(f32[2,128,128]{2,1,0:T(8,128)} %own.1), channel_id=1, source_target_pairs={{1,2},{2,1},{3,4},{4,3},{5,6},{6,5},{7,8},{8,7},{9,10},{10,9},{11,... | collective-permute-start | bytes 393224 | tf_op jit(solution)/shard_map/ppermute | solution.py:296
  4.8 10.4 %spectra.1.spec_far = f32[24,256,384]{2,1,0:T(8,128)} custom-call(s32[24]{0:T(128)} %radii.1, f32[24,2,128,128]{3,2,1,0:T(8,128)} %taps.1, bf16[512,512]{1,0:T(8,128)(2,1)} %constant.24.clone.row_tab.rest_2_, bf16[512,256]{1,0:T(8,128)(2,1)} %constant.25.clone.head.rest_3_, bf16[256,256]{1,0:T(8,128)(2,1)} %constant.26.clone.tail.rest_4_), custom_call_target="tpu_custom_call" | custom-call | flops 17999998976 | bytes 14000000 | tf_op jit(solution)/shard_map/spectra/pallas_call | solution.py:318
  15.2 0.0 collective-permute-done.near
  15.2 0.0 collective-permute-done.1.far
  15.3 0.0 copy-start.5
  15.3 1.0 %copy-done.5 = bf16[768,256]{1,0:T(8,128)(2,1)S(1)} copy-done((bf16[768,256]{1,0:T(8,128)(2,1)S(1)}, bf16[768,256]{1,0:T(8,128)(2,1)}, u32[]{:S(2)}) %copy-start.5) | copy-done | bytes 393240
  16.3 0.9 %copy-done.6 = bf16[512,256]{1,0:T(8,128)(2,1)S(1)} copy-done((bf16[512,256]{1,0:T(8,128)(2,1)S(1)}, bf16[512,256]{1,0:T(8,128)(2,1)}, u32[]{:S(2)}) %copy-start.6) | copy-done | bytes 262168
  17.2 0.9 %copy-done.7 = bf16[512,256]{1,0:T(8,128)(2,1)S(1)} copy-done((bf16[512,256]{1,0:T(8,128)(2,1)S(1)}, bf16[512,256]{1,0:T(8,128)(2,1)}, u32[]{:S(2)}) %copy-start.7) | copy-done | bytes 262168
  18.2 0.9 %copy-done.8 = f32[2,128,128]{2,1,0:T(8,128)S(1)} copy-done((f32[2,128,128]{2,1,0:T(8,128)S(1)}, f32[2,128,128]{2,1,0:T(8,128)}, u32[]{:S(2)}) %copy-start.8) | copy-done | bytes 131096
  19.1 0.9 %copy-done.9 = bf16[256,256]{1,0:T(8,128)(2,1)S(1)} copy-done((bf16[256,256]{1,0:T(8,128)(2,1)S(1)}, bf16[256,256]{1,0:T(8,128)(2,1)}, u32[]{:S(2)}) %copy-start.9) | copy-done | bytes 131096
  20.0 0.9 %copy-done.10 = bf16[256,256]{1,0:T(8,128)(2,1)S(1)} copy-done((bf16[256,256]{1,0:T(8,128)(2,1)S(1)}, bf16[256,256]{1,0:T(8,128)(2,1)}, u32[]{:S(2)}) %copy-start.10) | copy-done | bytes 131096
  20.9 0.8 %copy-done.12 = s32[128,128]{1,0:T(8,128)S(1)} copy-done((s32[128,128]{1,0:T(8,128)S(1)}, s32[128,128]{1,0:T(8,128)}, u32[]{:S(2)}) %copy-start.12) | copy-done | bytes 65560
  21.7 19.8 %fields.1 = (f32[3,128,128]{2,1,0:T(8,128)}, f32[2,128,128]{2,1,0:T(8,128)S(1)}, f32[2,64,128]{2,1,0:T(8,128)S(1)}, f32[2,64,128]{2,1,0:T(8,128)S(1)}) custom-call(s32[24]{0:T(128)S(1)} %copy-done.13, f32[24]{0:T(128)S(1)} %copy-done.14, s32[1]{0:T(128)} %bitcast.place, f32[2,128,128]{2,1,0:T(8,128)S(1)} %copy-done.8, ...), custom_call_target="tpu_custom_call" | custom-call | tf_op jit(solution)/shard_map/fields/pallas_call | solution.py:330
  41.5 0.6 %copy-done.11 = f32[2,128,128]{2,1,0:T(8,128)} copy-done((f32[2,128,128]{2,1,0:T(8,128)}, f32[2,128,128]{2,1,0:T(8,128)S(1)}, u32[]{:S(2)}) %copy-start.11) | copy-done | bytes 131096
  42.2 3.5 %collective-permute-start.3 = (f32[2,64,128]{2,1,0:T(8,128)S(1)}, f32[2,64,128]{2,1,0:T(8,128)S(1)}, u32[]{:S(2)}, u32[]{:S(2)}) collective-permute-start(f32[2,64,128]{2,1,0:T(8,128)S(1)} %get-tuple-element.9), channel_id=1, source_target_pairs={{1,2},{2,1},{3,4},{4,3},{5,6},{6,5},{7,8},{8,7},{9,10},{10,9},{11,... | collective-permute-start | bytes 196616 | tf_op jit(solution)/shard_map/ppermute | solution.py:359
  45.8 2.9 %collective-permute-done.3.far = f32[2,64,128]{2,1,0:T(8,128)S(1)} collective-permute-done((f32[2,64,128]{2,1,0:T(8,128)S(1)}, f32[2,64,128]{2,1,0:T(8,128)S(1)}, u32[]{:S(2)}, u32[]{:S(2)}) %collective-permute-start.3) | collective-permute-done | bytes 65568 | tf_op jit(solution)/shard_map/ppermute | solution.py:359
  48.7 0.6 %copy-done.16 = f32[2,64,128]{2,1,0:T(8,128)} copy-done((f32[2,64,128]{2,1,0:T(8,128)}, f32[2,64,128]{2,1,0:T(8,128)S(1)}, u32[]{:S(2)}) %copy-start.16) | copy-done | bytes 65560
  49.3 1.6 %join.1 = f32[2,128,128]{2,1,0:T(8,128)} custom-call(s32[1]{0:T(128)} %bitcast.place, f32[2,128,128]{2,1,0:T(8,128)} %copy-done.11, f32[2,64,128]{2,1,0:T(8,128)} %copy-done.15, f32[2,64,128]{2,1,0:T(8,128)} %copy-done.16), custom_call_target="tpu_custom_call" | custom-call | tf_op jit(solution)/shard_map/join/pallas_call | solution.py:360
  (21 shorter events, 0.0 us)
Async XLA Ops:
  0.6 14.6 %copy-start = (bf16[512,1024]{1,0:T(8,128)(2,1)S(1)}, bf16[512,1024]{1,0:T(8,128)(2,1)}, u32[]{:S(2)}) copy-start(bf16[512,1024]{1,0:T(8,128)(2,1)} %constant.31.clone.mask_row) | copy-start | bytes 3145732
  0.6 14.6 %copy-start.1 = (bf16[512,1024]{1,0:T(8,128)(2,1)S(1)}, bf16[512,1024]{1,0:T(8,128)(2,1)}, u32[]{:S(2)}) copy-start(bf16[512,1024]{1,0:T(8,128)(2,1)} %constant.30.clone.rest_6_) | copy-start | bytes 3145732
  0.7 14.6 %copy-start.2 = (bf16[512,512]{1,0:T(8,128)(2,1)S(1)}, bf16[512,512]{1,0:T(8,128)(2,1)}, u32[]{:S(2)}) copy-start(bf16[512,512]{1,0:T(8,128)(2,1)} %constant.24.clone.row_tab.rest_2_) | copy-start | bytes 1572868
  0.7 14.6 %copy-start.3 = (bf16[256,1024]{1,0:T(8,128)(2,1)S(1)}, bf16[256,1024]{1,0:T(8,128)(2,1)}, u32[]{:S(2)}) copy-start(bf16[256,1024]{1,0:T(8,128)(2,1)} %constant.28.clone.rest_1_) | copy-start | bytes 1572868
  0.7 14.6 %copy-start.4 = (bf16[768,256]{1,0:T(8,128)(2,1)S(1)}, bf16[768,256]{1,0:T(8,128)(2,1)}, u32[]{:S(2)}) copy-start(bf16[768,256]{1,0:T(8,128)(2,1)} %constant.29.clone.rest_5_) | copy-start | bytes 1179652
  0.7 14.6 %copy-start.14 = (f32[24]{0:T(128)S(1)}, f32[24]{0:T(128)}, u32[]{:S(2)}) copy-start(f32[24]{0:T(128)} %weight.1) | copy-start | bytes 292
  0.7 14.6 %copy-start.13 = (s32[24]{0:T(128)S(1)}, s32[24]{0:T(128)}, u32[]{:S(2)}) copy-start(s32[24]{0:T(128)} %group.1) | copy-start | bytes 292
  0.7 14.5 %collective-permute-start = (f32[2,128,128]{2,1,0:T(8,128)}, f32[2,128,128]{2,1,0:T(8,128)}, u32[]{:S(2)}, u32[]{:S(2)}) collective-permute-start(f32[2,128,128]{2,1,0:T(8,128)} %own.1), channel_id=1, source_target_pairs={{0,1},{1,0},{2,3},{3,2},{4,5},{5,4},{6,7},{7,6},{8,9},{9,8},{10,11... | collective-permute-start | bytes 393224 | tf_op jit(solution)/shard_map/ppermute | solution.py:295
  1.5 13.7 %collective-permute-start.1 = (f32[2,128,128]{2,1,0:T(8,128)}, f32[2,128,128]{2,1,0:T(8,128)}, u32[]{:S(2)}, u32[]{:S(2)}) collective-permute-start(f32[2,128,128]{2,1,0:T(8,128)} %own.1), channel_id=1, source_target_pairs={{1,2},{2,1},{3,4},{4,3},{5,6},{6,5},{7,8},{8,7},{9,10},{10,9},{11,... | collective-permute-start | bytes 393224 | tf_op jit(solution)/shard_map/ppermute | solution.py:296
  15.3 1.0 %copy-start.5 = (bf16[768,256]{1,0:T(8,128)(2,1)S(1)}, bf16[768,256]{1,0:T(8,128)(2,1)}, u32[]{:S(2)}) copy-start(bf16[768,256]{1,0:T(8,128)(2,1)} %constant.27.clone.rest_0_) | copy-start | bytes 1179652
  16.3 0.9 %copy-start.6 = (bf16[512,256]{1,0:T(8,128)(2,1)S(1)}, bf16[512,256]{1,0:T(8,128)(2,1)}, u32[]{:S(2)}) copy-start(bf16[512,256]{1,0:T(8,128)(2,1)} %constant.25.clone.head.rest_3_) | copy-start | bytes 786436
  17.2 0.9 %copy-start.7 = (bf16[512,256]{1,0:T(8,128)(2,1)S(1)}, bf16[512,256]{1,0:T(8,128)(2,1)}, u32[]{:S(2)}) copy-start(bf16[512,256]{1,0:T(8,128)(2,1)} %constant.32.clone.mask_head) | copy-start | bytes 786436
  18.2 0.9 %copy-start.8 = (f32[2,128,128]{2,1,0:T(8,128)S(1)}, f32[2,128,128]{2,1,0:T(8,128)}, u32[]{:S(2)}) copy-start(f32[2,128,128]{2,1,0:T(8,128)} %own.1) | copy-start | bytes 393220
  19.1 0.9 %copy-start.9 = (bf16[256,256]{1,0:T(8,128)(2,1)S(1)}, bf16[256,256]{1,0:T(8,128)(2,1)}, u32[]{:S(2)}) copy-start(bf16[256,256]{1,0:T(8,128)(2,1)} %constant.26.clone.tail.rest_4_) | copy-start | bytes 393220
  20.0 0.9 %copy-start.10 = (bf16[256,256]{1,0:T(8,128)(2,1)S(1)}, bf16[256,256]{1,0:T(8,128)(2,1)}, u32[]{:S(2)}) copy-start(bf16[256,256]{1,0:T(8,128)(2,1)} %constant.33.clone.mask_tail) | copy-start | bytes 393220
  20.9 0.8 %copy-start.12 = (s32[128,128]{1,0:T(8,128)S(1)}, s32[128,128]{1,0:T(8,128)}, u32[]{:S(2)}) copy-start(s32[128,128]{1,0:T(8,128)} %target.1) | copy-start | bytes 196612
  41.5 0.6 %copy-start.11 = (f32[2,128,128]{2,1,0:T(8,128)}, f32[2,128,128]{2,1,0:T(8,128)S(1)}, u32[]{:S(2)}) copy-start(f32[2,128,128]{2,1,0:T(8,128)S(1)} %get-tuple-element.7.own) | copy-start | bytes 393220
  42.2 3.6 %collective-permute-start.2 = (f32[2,64,128]{2,1,0:T(8,128)S(1)}, f32[2,64,128]{2,1,0:T(8,128)S(1)}, u32[]{:S(2)}, u32[]{:S(2)}) collective-permute-start(f32[2,64,128]{2,1,0:T(8,128)S(1)} %get-tuple-element.8), channel_id=1, source_target_pairs={{0,1},{1,0},{2,3},{3,2},{4,5},{5,4},{6,7},{7,6},{8,9},{9,8},{10,11... | collective-permute-start | bytes 196616 | tf_op jit(solution)/shard_map/ppermute | solution.py:358
  42.2 6.5 %collective-permute-start.3 = (f32[2,64,128]{2,1,0:T(8,128)S(1)}, f32[2,64,128]{2,1,0:T(8,128)S(1)}, u32[]{:S(2)}, u32[]{:S(2)}) collective-permute-start(f32[2,64,128]{2,1,0:T(8,128)S(1)} %get-tuple-element.9), channel_id=1, source_target_pairs={{1,2},{2,1},{3,4},{4,3},{5,6},{6,5},{7,8},{8,7},{9,10},{10,9},{11,... | collective-permute-start | bytes 196616 | tf_op jit(solution)/shard_map/ppermute | solution.py:359
  45.7 2.9 %copy-start.15 = (f32[2,64,128]{2,1,0:T(8,128)}, f32[2,64,128]{2,1,0:T(8,128)S(1)}, u32[]{:S(2)}) copy-start(f32[2,64,128]{2,1,0:T(8,128)S(1)} %collective-permute-done.2.near) | copy-start | bytes 196612
  48.6 0.6 %copy-start.16 = (f32[2,64,128]{2,1,0:T(8,128)}, f32[2,64,128]{2,1,0:T(8,128)S(1)}, u32[]{:S(2)}) copy-start(f32[2,64,128]{2,1,0:T(8,128)S(1)} %collective-permute-done.3.far) | copy-start | bytes 196612

commit v8 on v7

--- a/solution.py
+++ b/solution.py
@@ -1,3 +1,4 @@
+import functools
 import math
 
 import jax
@@ -61,25 +62,21 @@
 
 def over_rows(table, x):
     high, low = split(x)
-    left = table[...]
-    left = jnp.concatenate([left, left[:, :x.shape[0]]], axis=1)
+    left = jnp.concatenate([table, table[:, :x.shape[0]]], axis=1)
     return dot(left, jnp.concatenate([high, high, low], axis=0))
 
 
 def over_lanes(x, table):
     high, low = split(x)
-    right = table[...]
-    right = jnp.concatenate([right, right[:x.shape[1]]], axis=0)
+    right = jnp.concatenate([table, table[:x.shape[1]]], axis=0)
     return dot(jnp.concatenate([high, high, low], axis=1), right)
 
 
 def to_freqs(x, head, tail):
     high, low = split(x)
-    right = head[...]
-    right = jnp.concatenate([right, right[:x.shape[1]]], axis=0)
+    right = jnp.concatenate([head, head[:x.shape[1]]], axis=0)
     first = dot(jnp.concatenate([high, high, low], axis=1), right)
-    right = tail[...]
-    rest = dot(jnp.concatenate([high, low], axis=1), jnp.concatenate([right, right], axis=0))
+    rest = dot(jnp.concatenate([high, low], axis=1), jnp.concatenate([tail, tail], axis=0))
     lanes = rest.shape[1] // 2
     return first, rest[:, :lanes] + rest[:, lanes:]
 
@@ -109,8 +106,9 @@
     return pltpu.roll(x, x.shape[1] // 2, 1)
 
 
-def spectra_body(radii, taps, row_tab, head, tail, spec):
+def spectra_body(radii, taps, row_ref, head_ref, tail_ref, spec):
     batch, _, span, _ = taps.shape
+    row_tab, head, tail = row_ref[...], head_ref[...], tail_ref[...]
     first = pl.program_id(0) * batch
     row_at = lax.broadcasted_iota(jnp.int32, (span, span), 0) - span // 2
     col_at = lax.broadcasted_iota(jnp.int32, (span, span), 1) - span // 2
@@ -135,12 +133,11 @@
 
 def main_body(
     group, weight, place,
-    own, near, far, target, mask_row, mask_head, mask_tail, spec_far, *rest,
+    own, near, far, target, spec_far, tables_far,
+    resist_far, grad_own, near_rim, far_rim,
+    spec, field, mask_spec, resist, slopes, grad_spec, tables, spec_sems, table_sems, out_sem,
+    *, layout, sections,
 ):
-    tables_far, rest = rest[:7], rest[7:]
-    resist_far, grad_own, near_rim, far_rim = rest[:4]
-    spec, field, mask_spec, resist, slopes, grad_spec, spec_sems, table_sems, out_sem = rest[4:13]
-    tables = rest[13:]
     kernels, grid_rows, _ = spec.shape
     count, width = target.shape
     rim = (grid_rows - count) // 2
@@ -152,15 +149,20 @@
         return pltpu.make_async_copy(spec_far.at[here], spec.at[here], spec_sems.at[i])
 
     def fetch_table(i):
-        return pltpu.make_async_copy(tables_far[i], tables[i], table_sems.at[i])
-
-    col_inv, row_inv, row_tab, head, tail, grad_col, grad_row = tables
-    for i in range(2):
-        fetch_table(i).start()
+        here = pl.ds(sections[i][0], sections[i][1])
+        return pltpu.make_async_copy(tables_far.at[here], tables.at[here], table_sems.at[i])
+
+    def table(name):
+        start, rows, blocks = layout[name]
+        parts = [tables[start + b * rows:start + (b + 1) * rows] for b in range(blocks)]
+        return jnp.concatenate(parts, axis=1)
+
+    fetch_table(0).start()
+    fetch_table(1).start()
     for i in range(steps):
         fetch(i).start()
-    for i in range(2, 7):
-        fetch_table(i).start()
+    fetch_table(2).start()
+    fetch_table(0).wait()
 
     odd = place[0] % 2 == 1
     parts = []
@@ -169,7 +171,7 @@
         below = jnp.where(odd, far[c, :rim], near[c, :rim])
         parts += [above, own[c], below]
     mask = jnp.concatenate(parts, axis=0)
-    m_first, m_rest = to_freqs(side(over_rows(mask_row, mask)), mask_head, mask_tail)
+    m_first, m_rest = to_freqs(side(over_rows(table("mask_row"), mask)), table("mask_head"), table("mask_tail"))
     lane = lax.broadcasted_iota(jnp.int32, m_rest.shape, 1)
     real_half = lane < m_rest.shape[1] // 2
     turned = swap(m_rest)
@@ -179,8 +181,8 @@
 
     slopes[...] = jnp.zeros(slopes.shape, f32)
     grad_spec[...] = jnp.zeros(grad_spec.shape, f32)
-    for i in range(2):
-        fetch_table(i).wait()
+    fetch_table(1).wait()
+    col_inv, row_inv = table("col_inv"), table("row_inv")
 
     def forward(i, carry):
         fetch(i).wait()
@@ -222,8 +224,8 @@
         slopes[g] = 2.0 * (seen - wanted) * seen * (1.0 - seen) * STEEPNESS
     out = pltpu.make_async_copy(resist, resist_far, out_sem)
     out.start()
-    for i in range(2, 7):
-        fetch_table(i).wait()
+    fetch_table(2).wait()
+    row_tab, head, tail = table("row_tab"), table("head"), table("tail")
 
     def backward(i, carry):
         def rows_of(p):
@@ -257,8 +259,8 @@
     same, cross = grad_spec[:, 2 * width:3 * width], grad_spec[:, 3 * width:]
     tail_sum = jnp.where(real_half, same + swap(same), swap(cross) - cross)
     total = jnp.concatenate([grad_spec[:, :2 * width], tail_sum], axis=1)
-    back = over_lanes(total, grad_col)
-    full = over_rows(grad_row, jnp.concatenate([back[:, :width], back[:, width:]], axis=0))
+    back = over_lanes(total, table("grad_col"))
+    full = over_rows(table("grad_row"), jnp.concatenate([back[:, :width], back[:, width:]], axis=0))
     for c in range(2):
         base = c * grid_rows
         rise, fall = full[base:base + rim], full[base + rim + count:base + grid_rows]
@@ -277,6 +279,20 @@
         if count > 2 * rim:
             out[c, rim:count - rim] = own[c, rim:count - rim]
         out[c, count - rim:] = own[c, count - rim:] + jnp.where(odd, far[c], near[c])
+
+
+def stacked(groups):
+    blocks, layout, sections, at = [], {}, [], 0
+    for group in groups:
+        start = at
+        for name, table in group.items():
+            rows, lanes = table.shape
+            layout[name] = (at, rows, lanes // 256)
+            for b in range(lanes // 256):
+                blocks.append(table[:, b * 256:(b + 1) * 256])
+            at += rows * (lanes // 256)
+        sections.append((start, at - start))
+    return np.concatenate(blocks, axis=0), layout, sections
 
 
 def on_device(mask_field, target, kernel_taps, kernel_radii, kernel_group, kernel_weight):
@@ -326,16 +342,20 @@
         name="spectra",
     )(kernel_radii, kernel_taps, *map(jnp.asarray, (row_tab, head, tail)))
 
-    late = [jnp.asarray(t) for t in (col_inv, row_inv, row_tab, head, tail, grad_col, grad_row)]
+    tables, layout, sections = stacked([
+        {"mask_row": mask_row, "mask_head": mask_head, "mask_tail": mask_tail},
+        {"col_inv": col_inv, "row_inv": row_inv},
+        {"row_tab": row_tab, "head": head, "tail": tail, "grad_col": grad_col, "grad_row": grad_row},
+    ])
     resist, own, near_rim, far_rim = pl.pallas_call(
-        main_body,
+        functools.partial(main_body, layout=layout, sections=sections),
         out_shape=[
             jax.ShapeDtypeStruct((GROUPS, count, width), f32),
             jax.ShapeDtypeStruct((2, count, width), f32),
             jax.ShapeDtypeStruct((2, rim, width), f32),
             jax.ShapeDtypeStruct((2, rim, width), f32),
         ],
-        in_specs=[smem] * 3 + [vmem] * 7 + [hbm] * 8,
+        in_specs=[smem] * 3 + [vmem] * 4 + [hbm] * 2,
         out_specs=[hbm] + [vmem] * 3,
         scratch_shapes=[
             pltpu.VMEM((kernels, grid_rows, 2 * grid_cols), f32),
@@ -344,16 +364,14 @@
             pltpu.VMEM((GROUPS, count, width), f32),
             pltpu.VMEM((GROUPS, count, width), f32),
             pltpu.VMEM((grid_rows, 4 * width), f32),
+            pltpu.VMEM(tables.shape, bf16),
             pltpu.SemaphoreType.DMA((kernels // BATCH,)),
-            pltpu.SemaphoreType.DMA((len(late),)),
+            pltpu.SemaphoreType.DMA((len(sections),)),
             pltpu.SemaphoreType.DMA,
-        ] + [pltpu.VMEM(t.shape, bf16) for t in late],
+        ],
         compiler_params=pltpu.CompilerParams(vmem_limit_bytes=LIMIT * MIB),
         name="fields",
-    )(
-        kernel_group, kernel_weight, place, mask_field, near, far, target,
-        *map(jnp.asarray, (mask_row, mask_head, mask_tail)), spectra, *late,
-    )
+    )(kernel_group, kernel_weight, place, mask_field, near, far, target, spectra, jnp.asarray(tables))
 
     near_in = lax.ppermute(near_rim, "row", near_pairs)
     far_in = lax.ppermute(far_rim, "row", far_pairs)
@@ -362,6 +380,7 @@
         out_shape=jax.ShapeDtypeStruct((2, count, width), f32),
         in_specs=[smem] + [vmem] * 3,
         out_specs=vmem,
+        compiler_params=pltpu.CompilerParams(vmem_limit_bytes=4 * MIB),
         name="join",
     )(place, own, near_in, far_in)
     return resist, gradient

time: 51.4 us -> 44.4 us (0.86)
  local copies, waits for them, and re-layouts: 7.74 us -> 2.35 us
  Pallas kernels: 31.8 us -> 30.7 us
    unnamed x34 -> x10, local copies, waits for them, and re-layouts: 7.74 us -> 2.35 us
    pallas_call x1, Pallas kernels: 1.62 us -> 0.68 us  [on_device(): pl.pallas_call(join_body, out_shape=jax.ShapeDtypeStruct((2, count, width...]
  transfers between devices with their start and end apart: 4 -> 4, of which waited for: 1 -> 1; matrix products, arithmetic and copies ran while one was open for 0% -> 0% of each run, Pallas kernels for 20% -> 24%
where the time goes in v8:
time: 44.4 us; the launch traced here: 44.1 us
  Pallas kernels  30.7 us (69%)
  starting transfers between devices  7.39 us (17%)
  waiting for transfers between devices  2.94 us (7%)
  local copies, waits for them, and re-layouts  2.35 us (5%)
  between operations  0.75 us (2%)
    pallas_call x1, Pallas kernels, on_device(): pl.pallas_call(functools.partial(main_body, layout=layout, sections=secti...  19.5 us
    pallas_call x1, Pallas kernels, on_device(): pl.pallas_call(spectra_body, grid=(kernels // BATCH,), out_shape=jax.Shap...  10.4 us
    ppermute x1, starting transfers between devices, on_device(): far_in = lax.ppermute(far_rim, 'row', far_pairs)  3.53 us
    ppermute x1, starting transfers between devices, on_device(): far = lax.ppermute(mask_field, 'row', far_pairs)  3.05 us
    ppermute x1, waiting for transfers between devices, on_device(): far_in = lax.ppermute(far_rim, 'row', far_pairs)  2.94 us
    unnamed x10, local copies, waits for them, and re-layouts  2.35 us
  transfers between devices with their start and end apart: 4, of which 1 were waited for; matrix products, arithmetic and copies ran while one was open for 0% of the time, Pallas kernels for 24%

profile of v8, /device:TPU:21, one launch (start us, length us, event | category | flops | bytes accessed | tf_op | source)
XLA Modules:
  0.0 44.1 jit_solution(4388918902060857145)
XLA Ops:
  0.6 0.0 copy-start.1
  0.6 0.0 copy-start.4
  0.7 0.0 copy-start.3
  0.7 0.0 copy-start.2
  0.7 0.7 %collective-permute-start = (f32[2,128,128]{2,1,0:T(8,128)}, f32[2,128,128]{2,1,0:T(8,128)S(1)}, u32[]{:S(2)}, u32[]{:S(2)}) collective-permute-start(f32[2,128,128]{2,1,0:T(8,128)} %own.1), channel_id=1, source_target_pairs={{0,1},{1,0},{2,3},{3,2},{4,5},{5,4},{6,7},{7,6},{8,9},{9,8},{10,11... | collective-permute-start | bytes 393224 | tf_op jit(solution)/shard_map/ppermute | solution.py:311
  1.4 3.0 %collective-permute-start.1 = (f32[2,128,128]{2,1,0:T(8,128)}, f32[2,128,128]{2,1,0:T(8,128)S(1)}, u32[]{:S(2)}, u32[]{:S(2)}) collective-permute-start(f32[2,128,128]{2,1,0:T(8,128)} %own.1), channel_id=1, source_target_pairs={{1,2},{2,1},{3,4},{4,3},{5,6},{6,5},{7,8},{8,7},{9,10},{10,9},{11,... | collective-permute-start | bytes 393224 | tf_op jit(solution)/shard_map/ppermute | solution.py:312
  4.5 10.4 %spectra.1.spec_far = f32[24,256,384]{2,1,0:T(8,128)} custom-call(s32[24]{0:T(128)} %radii.1, f32[24,2,128,128]{3,2,1,0:T(8,128)} %taps.1, bf16[512,512]{1,0:T(8,128)(2,1)} %constant.12.clone.row_ref, bf16[512,256]{1,0:T(8,128)(2,1)} %constant.13.clone.head_ref, bf16[256,256]{1,0:T(8,128)(2,1)} %constant.14.clone.tail_ref), custom_call_target="tpu_custom_call" | custom-call | flops 17999998976 | bytes 14000000 | tf_op jit(solution)/shard_map/spectra/pallas_call | solution.py:334
  14.9 0.0 collective-permute-done.near
  14.9 0.0 collective-permute-done.1.far
  14.9 0.0 copy-done.1
  14.9 0.0 copy-done.4
  14.9 0.0 copy-done.3
  14.9 0.0 copy-done.2
  14.9 0.0 copy-start
  15.0 2.3 %copy-done = bf16[9216,256]{1,0:T(8,128)(2,1)S(1)} copy-done((bf16[9216,256]{1,0:T(8,128)(2,1)S(1)}, bf16[9216,256]{1,0:T(8,128)(2,1)}, u32[]{:S(2)}) %copy-start) | copy-done | bytes 4718616
  17.3 19.5 %fields.1 = (f32[3,128,128]{2,1,0:T(8,128)}, f32[2,128,128]{2,1,0:T(8,128)S(1)}, f32[2,64,128]{2,1,0:T(8,128)S(1)}, f32[2,64,128]{2,1,0:T(8,128)S(1)}) custom-call(s32[24]{0:T(128)S(1)} %copy-done.3, f32[24]{0:T(128)S(1)} %copy-done.4, s32[1]{0:T(128)} %bitcast.place, f32[2,128,128]{2,1,0:T(8,128)S(1)} %copy-done.1, ...), custom_call_target="tpu_custom_call" | custom-call | tf_op jit(solution)/shard_map/fields/pallas_call | solution.py:350
  36.8 0.1 collective-permute-start.2
  36.9 3.5 %collective-permute-start.3 = (f32[2,64,128]{2,1,0:T(8,128)S(1)}, f32[2,64,128]{2,1,0:T(8,128)S(1)}, u32[]{:S(2)}, u32[]{:S(2)}) collective-permute-start(f32[2,64,128]{2,1,0:T(8,128)S(1)} %get-tuple-element.9), channel_id=1, source_target_pairs={{1,2},{2,1},{3,4},{4,3},{5,6},{6,5},{7,8},{8,7},{9,10},{10,9},{11,... | collective-permute-start | bytes 196616 | tf_op jit(solution)/shard_map/ppermute | solution.py:377
  40.5 0.0 collective-permute-done.2.near
  40.5 2.9 %collective-permute-done.3.far = f32[2,64,128]{2,1,0:T(8,128)S(1)} collective-permute-done((f32[2,64,128]{2,1,0:T(8,128)S(1)}, f32[2,64,128]{2,1,0:T(8,128)S(1)}, u32[]{:S(2)}, u32[]{:S(2)}) %collective-permute-start.3) | collective-permute-done | bytes 65568 | tf_op jit(solution)/shard_map/ppermute | solution.py:377
  43.4 0.7 %join.1 = f32[2,128,128]{2,1,0:T(8,128)} custom-call(s32[1]{0:T(128)} %bitcast.place, f32[2,128,128]{2,1,0:T(8,128)S(1)} %get-tuple-element.7.own, f32[2,64,128]{2,1,0:T(8,128)S(1)} %collective-permute-done.2.near, f32[2,64,128]{2,1,0:T(8,128)S(1)} %collective-permute-done.3.far), custom_call_target="tpu_custom_call" | custom-call | tf_op jit(solution)/shard_map/join/pallas_call | solution.py:378
Async XLA Ops:
  0.6 14.3 %copy-start.1 = (f32[2,128,128]{2,1,0:T(8,128)S(1)}, f32[2,128,128]{2,1,0:T(8,128)}, u32[]{:S(2)}) copy-start(f32[2,128,128]{2,1,0:T(8,128)} %own.1) | copy-start | bytes 393220
  0.6 14.3 %copy-start.4 = (f32[24]{0:T(128)S(1)}, f32[24]{0:T(128)}, u32[]{:S(2)}) copy-start(f32[24]{0:T(128)} %weight.1) | copy-start | bytes 292
  0.7 14.3 %copy-start.3 = (s32[24]{0:T(128)S(1)}, s32[24]{0:T(128)}, u32[]{:S(2)}) copy-start(s32[24]{0:T(128)} %group.1) | copy-start | bytes 292
  0.7 14.3 %copy-start.2 = (s32[128,128]{1,0:T(8,128)S(1)}, s32[128,128]{1,0:T(8,128)}, u32[]{:S(2)}) copy-start(s32[128,128]{1,0:T(8,128)} %target.1) | copy-start | bytes 196612
  0.7 14.2 %collective-permute-start = (f32[2,128,128]{2,1,0:T(8,128)}, f32[2,128,128]{2,1,0:T(8,128)S(1)}, u32[]{:S(2)}, u32[]{:S(2)}) collective-permute-start(f32[2,128,128]{2,1,0:T(8,128)} %own.1), channel_id=1, source_target_pairs={{0,1},{1,0},{2,3},{3,2},{4,5},{5,4},{6,7},{7,6},{8,9},{9,8},{10,11... | collective-permute-start | bytes 393224 | tf_op jit(solution)/shard_map/ppermute | solution.py:311
  1.4 13.5 %collective-permute-start.1 = (f32[2,128,128]{2,1,0:T(8,128)}, f32[2,128,128]{2,1,0:T(8,128)S(1)}, u32[]{:S(2)}, u32[]{:S(2)}) collective-permute-start(f32[2,128,128]{2,1,0:T(8,128)} %own.1), channel_id=1, source_target_pairs={{1,2},{2,1},{3,4},{4,3},{5,6},{6,5},{7,8},{8,7},{9,10},{10,9},{11,... | collective-permute-start | bytes 393224 | tf_op jit(solution)/shard_map/ppermute | solution.py:312
  14.9 2.3 %copy-start = (bf16[9216,256]{1,0:T(8,128)(2,1)S(1)}, bf16[9216,256]{1,0:T(8,128)(2,1)}, u32[]{:S(2)}) copy-start(bf16[9216,256]{1,0:T(8,128)(2,1)} %constant.15.clone.tables_far) | copy-start | bytes 14155780
  36.8 3.6 %collective-permute-start.2 = (f32[2,64,128]{2,1,0:T(8,128)S(1)}, f32[2,64,128]{2,1,0:T(8,128)S(1)}, u32[]{:S(2)}, u32[]{:S(2)}) collective-permute-start(f32[2,64,128]{2,1,0:T(8,128)S(1)} %get-tuple-element.8), channel_id=1, source_target_pairs={{0,1},{1,0},{2,3},{3,2},{4,5},{5,4},{6,7},{7,6},{8,9},{9,8},{10,11... | collective-permute-start | bytes 196616 | tf_op jit(solution)/shard_map/ppermute | solution.py:376
  36.9 6.5 %collective-permute-start.3 = (f32[2,64,128]{2,1,0:T(8,128)S(1)}, f32[2,64,128]{2,1,0:T(8,128)S(1)}, u32[]{:S(2)}, u32[]{:S(2)}) collective-permute-start(f32[2,64,128]{2,1,0:T(8,128)S(1)} %get-tuple-element.9), channel_id=1, source_target_pairs={{1,2},{2,1},{3,4},{4,3},{5,6},{6,5},{7,8},{8,7},{9,10},{10,9},{11,... | collective-permute-start | bytes 196616 | tf_op jit(solution)/shard_map/ppermute | solution.py:377

commit v9 on v8

--- a/solution.py
+++ b/solution.py
@@ -15,12 +15,10 @@
 STEEPNESS = 1.0
 THRESHOLD = 2.0
 BATCH = 8
-PIECE = 256
 
 f32 = jnp.float32
 bf16 = jnp.bfloat16
 MIB = 1024 * 1024
-LIMIT = 40
 
 
 def halves(table, axis):
@@ -52,31 +50,31 @@
     return high, low
 
 
-def dot(left, right):
+def dot(left, right, piece):
     parts = [
-        jnp.dot(left[at:at + PIECE], right, preferred_element_type=f32)
-        for at in range(0, left.shape[0], PIECE)
+        jnp.dot(left[at:at + piece], right, preferred_element_type=f32)
+        for at in range(0, left.shape[0], piece)
     ]
     return jnp.concatenate(parts, axis=0)
 
 
-def over_rows(table, x):
+def over_rows(table, x, piece=128):
     high, low = split(x)
     left = jnp.concatenate([table, table[:, :x.shape[0]]], axis=1)
-    return dot(left, jnp.concatenate([high, high, low], axis=0))
-
-
-def over_lanes(x, table):
+    return dot(left, jnp.concatenate([high, high, low], axis=0), piece)
+
+
+def over_lanes(x, table, piece=128):
     high, low = split(x)
     right = jnp.concatenate([table, table[:x.shape[1]]], axis=0)
-    return dot(jnp.concatenate([high, high, low], axis=1), right)
-
-
-def to_freqs(x, head, tail):
+    return dot(jnp.concatenate([high, high, low], axis=1), right, piece)
+
+
+def to_freqs(x, head, tail, piece=128):
     high, low = split(x)
     right = jnp.concatenate([head, head[:x.shape[1]]], axis=0)
-    first = dot(jnp.concatenate([high, high, low], axis=1), right)
-    rest = dot(jnp.concatenate([high, low], axis=1), jnp.concatenate([tail, tail], axis=0))
+    first = dot(jnp.concatenate([high, high, low], axis=1), right, piece)
+    rest = dot(jnp.concatenate([high, low], axis=1), jnp.concatenate([tail, tail], axis=0), piece)
     lanes = rest.shape[1] // 2
     return first, rest[:, :lanes] + rest[:, lanes:]
 
@@ -86,9 +84,9 @@
     return jnp.concatenate([x[:rows], x[rows:]], axis=1)
 
 
-def row_stage(pair, row_tab):
+def row_stage(pair, row_tab, piece=128):
     width = pair.shape[1] // 2
-    half = over_rows(row_tab, pair)
+    half = over_rows(row_tab, pair, piece)
     return [side(half[:, :width]), side(half[:, width:])]
 
 
@@ -120,11 +118,11 @@
             inside = reach < radii[first + k]
             parts = [jnp.where(inside, taps[k, c], 0.0) for c in range(2)]
             planes.append(jnp.concatenate(parts, axis=0))
-        return row_stage(jnp.concatenate(planes, axis=1), row_tab)
+        return row_stage(jnp.concatenate(planes, axis=1), row_tab, 64)
 
     def cols_of(p, tiles):
         for j in range(2):
-            a, b = to_freqs(tiles[j], head, tail)
+            a, b = to_freqs(tiles[j], head, tail, 64)
             spec[2 * p + j, :, :a.shape[1]] = a
             spec[2 * p + j, :, a.shape[1]:] = b
 
@@ -369,7 +367,7 @@
             pltpu.SemaphoreType.DMA((len(sections),)),
             pltpu.SemaphoreType.DMA,
         ],
-        compiler_params=pltpu.CompilerParams(vmem_limit_bytes=LIMIT * MIB),
+        compiler_params=pltpu.CompilerParams(vmem_limit_bytes=56 * MIB),
         name="fields",
     )(kernel_group, kernel_weight, place, mask_field, near, far, target, spectra, jnp.asarray(tables))
 

time: 44.4 us -> 55.6 us (1.25)
  Pallas kernels: 30.7 us -> 42.4 us
  local copies, waits for them, and re-layouts: 2.35 us -> 1.57 us
    pallas_call x1, Pallas kernels: 10.4 us -> 21.2 us  [on_device(): pl.pallas_call(spectra_body, grid=(kernels // BATCH,), out_shape=jax.Shap...]
    pallas_call x1, Pallas kernels: 19.5 us -> 20.5 us  [on_device(): pl.pallas_call(functools.partial(main_body, layout=layout, sections=secti...]
    unnamed x10 -> x6, local copies, waits for them, and re-layouts: 2.35 us -> 1.57 us
  transfers between devices with their start and end apart: 4 -> 4, of which waited for: 1 -> 1; matrix products, arithmetic and copies ran while one was open for 0% -> 0% of each run, Pallas kernels for 24% -> 38%
where the time goes in v9:
time: 55.6 us; the launch traced here: 55.2 us
  Pallas kernels  42.4 us (76%)
  starting transfers between devices  7.38 us (13%)
  waiting for transfers between devices  3.16 us (6%)
  local copies, waits for them, and re-layouts  1.57 us (3%)
  between operations  0.69 us (1%)
    pallas_call x1, Pallas kernels, on_device(): pl.pallas_call(spectra_body, grid=(kernels // BATCH,), out_shape=jax.Shap...  21.2 us
    pallas_call x1, Pallas kernels, on_device(): pl.pallas_call(functools.partial(main_body, layout=layout, sections=secti...  20.5 us
    ppermute x1, starting transfers between devices, on_device(): far_in = lax.ppermute(far_rim, 'row', far_pairs)  3.52 us
    ppermute x1, waiting for transfers between devices, on_device(): far_in = lax.ppermute(far_rim, 'row', far_pairs)  3.16 us
    ppermute x1, starting transfers between devices, on_device(): far = lax.ppermute(mask_field, 'row', far_pairs)  3.05 us
    unnamed x6, local copies, waits for them, and re-layouts  1.57 us
  transfers between devices with their start and end apart: 4, of which 1 were waited for; matrix products, arithmetic and copies ran while one was open for 0% of the time, Pallas kernels for 38%

profile of v9, /device:TPU:21, one launch (start us, length us, event | category | flops | bytes accessed | tf_op | source)
XLA Modules:
  0.0 55.2 jit_solution(5786043379594469007)
XLA Ops:
  0.6 0.7 %collective-permute-start = (f32[2,128,128]{2,1,0:T(8,128)}, f32[2,128,128]{2,1,0:T(8,128)S(1)}, u32[]{:S(2)}, u32[]{:S(2)}) collective-permute-start(f32[2,128,128]{2,1,0:T(8,128)} %own.1), channel_id=1, source_target_pairs={{0,1},{1,0},{2,3},{3,2},{4,5},{5,4},{6,7},{7,6},{8,9},{9,8},{10,11... | collective-permute-start | bytes 393224 | tf_op jit(solution)/shard_map/ppermute | solution.py:309
  1.4 3.1 %collective-permute-start.1 = (f32[2,128,128]{2,1,0:T(8,128)}, f32[2,128,128]{2,1,0:T(8,128)S(1)}, u32[]{:S(2)}, u32[]{:S(2)}) collective-permute-start(f32[2,128,128]{2,1,0:T(8,128)} %own.1), channel_id=1, source_target_pairs={{1,2},{2,1},{3,4},{4,3},{5,6},{6,5},{7,8},{8,7},{9,10},{10,9},{11,... | collective-permute-start | bytes 393224 | tf_op jit(solution)/shard_map/ppermute | solution.py:310
  4.4 21.2 %spectra.1.spec_far = f32[24,256,384]{2,1,0:T(8,128)} custom-call(s32[24]{0:T(128)} %radii.1, f32[24,2,128,128]{3,2,1,0:T(8,128)} %taps.1, bf16[512,512]{1,0:T(8,128)(2,1)} %constant.12.clone.row_ref, bf16[512,256]{1,0:T(8,128)(2,1)} %constant.13.clone.head_ref, bf16[256,256]{1,0:T(8,128)(2,1)} %constant.14.clone.tail_ref), custom_call_target="tpu_custom_call" | custom-call | flops 17999998976 | bytes 14000000 | tf_op jit(solution)/shard_map/spectra/pallas_call | solution.py:332
  25.6 0.0 collective-permute-done.near
  25.6 0.0 copy-start.1
  25.6 0.0 collective-permute-done.1.far
  25.7 0.0 copy-start.2
  25.7 0.6 %copy-done.1 = f32[2,128,128]{2,1,0:T(8,128)} copy-done((f32[2,128,128]{2,1,0:T(8,128)}, f32[2,128,128]{2,1,0:T(8,128)S(1)}, u32[]{:S(2)}) %copy-start.1) | copy-done | bytes 131096
  26.3 0.0 copy-done.2
  26.3 20.5 %fields.1 = (f32[3,128,128]{2,1,0:T(8,128)}, f32[2,128,128]{2,1,0:T(8,128)}, f32[2,64,128]{2,1,0:T(8,128)}, f32[2,64,128]{2,1,0:T(8,128)}) custom-call(s32[24]{0:T(128)} %group.1, f32[24]{0:T(128)} %weight.1, s32[1]{0:T(128)} %bitcast.place, f32[2,128,128]{2,1,0:T(8,128)} %own.1, f32[2,128,128]{2,1,0:T(8,128)} %copy-done.1, f32[2,128,128]{2,1,0:T(8,128)} %copy-done.2, ...), custom_call_target="tpu_custom_call" | custom-call | tf_op jit(solution)/shard_map/fields/pallas_call | solution.py:348
  46.9 0.1 collective-permute-start.2
  46.9 3.5 %collective-permute-start.3 = (f32[2,64,128]{2,1,0:T(8,128)}, f32[2,64,128]{2,1,0:T(8,128)S(1)}, u32[]{:S(2)}, u32[]{:S(2)}) collective-permute-start(f32[2,64,128]{2,1,0:T(8,128)} %get-tuple-element.9), channel_id=1, source_target_pairs={{1,2},{2,1},{3,4},{4,3},{5,6},{6,5},{7,8},{8,7},{9,10},{10,9},{11,... | collective-permute-start | bytes 196616 | tf_op jit(solution)/shard_map/ppermute | solution.py:375
  50.5 0.0 collective-permute-done.2.near
  50.5 3.2 %collective-permute-done.3.far = f32[2,64,128]{2,1,0:T(8,128)S(1)} collective-permute-done((f32[2,64,128]{2,1,0:T(8,128)}, f32[2,64,128]{2,1,0:T(8,128)S(1)}, u32[]{:S(2)}, u32[]{:S(2)}) %collective-permute-start.3) | collective-permute-done | bytes 65568 | tf_op jit(solution)/shard_map/ppermute | solution.py:375
  53.6 0.0 copy-start
  53.6 0.9 %copy-done = f32[2,128,128]{2,1,0:T(8,128)S(1)} copy-done((f32[2,128,128]{2,1,0:T(8,128)S(1)}, f32[2,128,128]{2,1,0:T(8,128)}, u32[]{:S(2)}) %copy-start) | copy-done | bytes 131096
  54.5 0.7 %join.1 = f32[2,128,128]{2,1,0:T(8,128)} custom-call(s32[1]{0:T(128)} %bitcast.place, f32[2,128,128]{2,1,0:T(8,128)S(1)} %copy-done, f32[2,64,128]{2,1,0:T(8,128)S(1)} %collective-permute-done.2.near, f32[2,64,128]{2,1,0:T(8,128)S(1)} %collective-permute-done.3.far), custom_call_target="tpu_custom_call" | custom-call | tf_op jit(solution)/shard_map/join/pallas_call | solution.py:376
Async XLA Ops:
  0.6 25.0 %collective-permute-start = (f32[2,128,128]{2,1,0:T(8,128)}, f32[2,128,128]{2,1,0:T(8,128)S(1)}, u32[]{:S(2)}, u32[]{:S(2)}) collective-permute-start(f32[2,128,128]{2,1,0:T(8,128)} %own.1), channel_id=1, source_target_pairs={{0,1},{1,0},{2,3},{3,2},{4,5},{5,4},{6,7},{7,6},{8,9},{9,8},{10,11... | collective-permute-start | bytes 393224 | tf_op jit(solution)/shard_map/ppermute | solution.py:309
  1.4 24.3 %collective-permute-start.1 = (f32[2,128,128]{2,1,0:T(8,128)}, f32[2,128,128]{2,1,0:T(8,128)S(1)}, u32[]{:S(2)}, u32[]{:S(2)}) collective-permute-start(f32[2,128,128]{2,1,0:T(8,128)} %own.1), channel_id=1, source_target_pairs={{1,2},{2,1},{3,4},{4,3},{5,6},{6,5},{7,8},{8,7},{9,10},{10,9},{11,... | collective-permute-start | bytes 393224 | tf_op jit(solution)/shard_map/ppermute | solution.py:310
  25.6 0.7 %copy-start.1 = (f32[2,128,128]{2,1,0:T(8,128)}, f32[2,128,128]{2,1,0:T(8,128)S(1)}, u32[]{:S(2)}) copy-start(f32[2,128,128]{2,1,0:T(8,128)S(1)} %collective-permute-done.near) | copy-start | bytes 393220
  25.7 0.7 %copy-start.2 = (f32[2,128,128]{2,1,0:T(8,128)}, f32[2,128,128]{2,1,0:T(8,128)S(1)}, u32[]{:S(2)}) copy-start(f32[2,128,128]{2,1,0:T(8,128)S(1)} %collective-permute-done.1.far) | copy-start | bytes 393220
  46.9 3.6 %collective-permute-start.2 = (f32[2,64,128]{2,1,0:T(8,128)}, f32[2,64,128]{2,1,0:T(8,128)S(1)}, u32[]{:S(2)}, u32[]{:S(2)}) collective-permute-start(f32[2,64,128]{2,1,0:T(8,128)} %get-tuple-element.8), channel_id=1, source_target_pairs={{0,1},{1,0},{2,3},{3,2},{4,5},{5,4},{6,7},{7,6},{8,9},{9,8},{10,11... | collective-permute-start | bytes 196616 | tf_op jit(solution)/shard_map/ppermute | solution.py:374
  46.9 6.7 %collective-permute-start.3 = (f32[2,64,128]{2,1,0:T(8,128)}, f32[2,64,128]{2,1,0:T(8,128)S(1)}, u32[]{:S(2)}, u32[]{:S(2)}) collective-permute-start(f32[2,64,128]{2,1,0:T(8,128)} %get-tuple-element.9), channel_id=1, source_target_pairs={{1,2},{2,1},{3,4},{4,3},{5,6},{6,5},{7,8},{8,7},{9,10},{10,9},{11,... | collective-permute-start | bytes 196616 | tf_op jit(solution)/shard_map/ppermute | solution.py:375
  53.6 0.9 %copy-start = (f32[2,128,128]{2,1,0:T(8,128)S(1)}, f32[2,128,128]{2,1,0:T(8,128)}, u32[]{:S(2)}) copy-start(f32[2,128,128]{2,1,0:T(8,128)} %get-tuple-element.7.own) | copy-start | bytes 393220

commit v10 on v8

--- a/solution.py
+++ b/solution.py
@@ -14,7 +14,8 @@
 GROUPS = 3
 STEEPNESS = 1.0
 THRESHOLD = 2.0
-BATCH = 8
+SPECTRA_BATCH = 12
+BATCH = 24
 PIECE = 256
 
 f32 = jnp.float32
@@ -90,6 +91,13 @@
     width = pair.shape[1] // 2
     half = over_rows(row_tab, pair)
     return [side(half[:, :width]), side(half[:, width:])]
+
+
+def loop(steps, body):
+    if steps == 1:
+        body(0, 0)
+    else:
+        lax.fori_loop(0, steps, body, 0)
 
 
 def staggered(count, first, second):
@@ -141,11 +149,11 @@
     kernels, grid_rows, _ = spec.shape
     count, width = target.shape
     rim = (grid_rows - count) // 2
-    steps = spec_sems.shape[0]
-    batch = kernels // steps
+    batch = BATCH
+    steps = kernels // batch
 
     def fetch(i):
-        here = pl.ds(i * batch, batch)
+        here = pl.ds(2 * i, 2)
         return pltpu.make_async_copy(spec_far.at[here], spec.at[here], spec_sems.at[i])
 
     def fetch_table(i):
@@ -159,7 +167,7 @@
 
     fetch_table(0).start()
     fetch_table(1).start()
-    for i in range(steps):
+    for i in range(kernels // 2):
         fetch(i).start()
     fetch_table(2).start()
     fetch_table(0).wait()
@@ -185,11 +193,11 @@
     col_inv, row_inv = table("col_inv"), table("row_inv")
 
     def forward(i, carry):
-        fetch(i).wait()
         m_re, m_im = mask_spec[:, :width], mask_spec[:, width:2 * width]
         m_same, m_cross = mask_spec[:, 2 * width:3 * width], mask_spec[:, 3 * width:]
 
         def cols_of(p):
+            fetch(i * (batch // 2) + p).wait()
             planes = []
             for j in range(2):
                 k = i * batch + 2 * p + j
@@ -215,7 +223,7 @@
         staggered(batch // 2, cols_of, rows_of)
         return carry
 
-    lax.fori_loop(0, steps, forward, 0)
+    loop(steps, forward)
 
     wanted = target[...].astype(f32)
     for g in range(GROUPS):
@@ -254,7 +262,7 @@
         staggered(batch // 2, rows_of, cols_of)
         return carry
 
-    lax.fori_loop(0, steps, backward, 0)
+    loop(steps, backward)
 
     same, cross = grad_spec[:, 2 * width:3 * width], grad_spec[:, 3 * width:]
     tail_sum = jnp.where(real_half, same + swap(same), swap(cross) - cross)
@@ -301,7 +309,7 @@
     rim = span // 2
     grid_rows = count + 2 * rim
     grid_cols = width + rim
-    assert count == span and width == span and kernels % BATCH == 0 and BATCH % 2 == 0 and count >= 2 * rim
+    assert count == span and width == span and kernels % BATCH == 0 and kernels % SPECTRA_BATCH == 0 and count >= 2 * rim
 
     strips = lax.axis_size("row")
     assert strips % 2 == 0
@@ -333,10 +341,10 @@
     hbm = pl.BlockSpec(memory_space=pltpu.HBM)
     spectra = pl.pallas_call(
         spectra_body,
-        grid=(kernels // BATCH,),
+        grid=(kernels // SPECTRA_BATCH,),
         out_shape=jax.ShapeDtypeStruct((kernels, grid_rows, 2 * grid_cols), f32),
-        in_specs=[smem, pl.BlockSpec((BATCH, 2, span, span), lambda i: (i, 0, 0, 0)), vmem, vmem, vmem],
-        out_specs=pl.BlockSpec((BATCH, grid_rows, 2 * grid_cols), lambda i: (i, 0, 0)),
+        in_specs=[smem, pl.BlockSpec((SPECTRA_BATCH, 2, span, span), lambda i: (i, 0, 0, 0)), vmem, vmem, vmem],
+        out_specs=pl.BlockSpec((SPECTRA_BATCH, grid_rows, 2 * grid_cols), lambda i: (i, 0, 0)),
         compiler_params=pltpu.CompilerParams(vmem_limit_bytes=56 * MIB),
         cost_estimate=pl.CostEstimate(flops=18 * 10**9, bytes_accessed=14 * 10**6, transcendentals=0),
         name="spectra",
@@ -365,7 +373,7 @@
             pltpu.VMEM((GROUPS, count, width), f32),
             pltpu.VMEM((grid_rows, 4 * width), f32),
             pltpu.VMEM(tables.shape, bf16),
-            pltpu.SemaphoreType.DMA((kernels // BATCH,)),
+            pltpu.SemaphoreType.DMA((kernels // 2,)),
             pltpu.SemaphoreType.DMA((len(sections),)),
             pltpu.SemaphoreType.DMA,
         ],

time: 44.4 us -> 46.6 us (1.050)
  Pallas kernels: 30.7 us -> 32.8 us
    pallas_call x1, Pallas kernels: 19.5 us -> 21.4 us  [on_device(): pl.pallas_call(functools.partial(main_body, layout=layout, sections=secti...]
  transfers between devices with their start and end apart: 4 -> 4, of which waited for: 1 -> 1; matrix products, arithmetic and copies ran while one was open for 0% -> 0% of each run, Pallas kernels for 24% -> 23%
where the time goes in v10:
time: 46.6 us; the launch traced here: 46.3 us
  Pallas kernels  32.8 us (70%)
  starting transfers between devices  7.38 us (16%)
  waiting for transfers between devices  2.95 us (6%)
  local copies, waits for them, and re-layouts  2.35 us (5%)
  between operations  0.75 us (2%)
    pallas_call x1, Pallas kernels, on_device(): pl.pallas_call(functools.partial(main_body, layout=layout, sections=secti...  21.4 us
    pallas_call x1, Pallas kernels, on_device(): pl.pallas_call(spectra_body, grid=(kernels // SPECTRA_BATCH,), out_shape=...  10.8 us
    ppermute x1, starting transfers between devices, on_device(): far_in = lax.ppermute(far_rim, 'row', far_pairs)  3.52 us
    ppermute x1, starting transfers between devices, on_device(): far = lax.ppermute(mask_field, 'row', far_pairs)  3.05 us
    ppermute x1, waiting for transfers between devices, on_device(): far_in = lax.ppermute(far_rim, 'row', far_pairs)  2.95 us
    unnamed x10, local copies, waits for them, and re-layouts  2.35 us
  transfers between devices with their start and end apart: 4, of which 1 were waited for; matrix products, arithmetic and copies ran while one was open for 0% of the time, Pallas kernels for 23%

profile of v10, /device:TPU:21, one launch (start us, length us, event | category | flops | bytes accessed | tf_op | source)
XLA Modules:
  0.0 46.3 jit_solution(4917580523135142884)
XLA Ops:
  0.6 0.0 copy-start.1
  0.6 0.0 copy-start.4
  0.7 0.0 copy-start.3
  0.7 0.0 copy-start.2
  0.7 0.7 %collective-permute-start = (f32[2,128,128]{2,1,0:T(8,128)}, f32[2,128,128]{2,1,0:T(8,128)S(1)}, u32[]{:S(2)}, u32[]{:S(2)}) collective-permute-start(f32[2,128,128]{2,1,0:T(8,128)} %own.1), channel_id=1, source_target_pairs={{0,1},{1,0},{2,3},{3,2},{4,5},{5,4},{6,7},{7,6},{8,9},{9,8},{10,11... | collective-permute-start | bytes 393224 | tf_op jit(solution)/shard_map/ppermute | solution.py:319
  1.4 3.0 %collective-permute-start.1 = (f32[2,128,128]{2,1,0:T(8,128)}, f32[2,128,128]{2,1,0:T(8,128)S(1)}, u32[]{:S(2)}, u32[]{:S(2)}) collective-permute-start(f32[2,128,128]{2,1,0:T(8,128)} %own.1), channel_id=1, source_target_pairs={{1,2},{2,1},{3,4},{4,3},{5,6},{6,5},{7,8},{8,7},{9,10},{10,9},{11,... | collective-permute-start | bytes 393224 | tf_op jit(solution)/shard_map/ppermute | solution.py:320
  4.5 10.8 %spectra.1.spec_far = f32[24,256,384]{2,1,0:T(8,128)} custom-call(s32[24]{0:T(128)} %radii.1, f32[24,2,128,128]{3,2,1,0:T(8,128)} %taps.1, bf16[512,512]{1,0:T(8,128)(2,1)} %constant.12.clone.row_ref, bf16[512,256]{1,0:T(8,128)(2,1)} %constant.13.clone.head_ref, bf16[256,256]{1,0:T(8,128)(2,1)} %constant.14.clone.tail_ref), custom_call_target="tpu_custom_call" | custom-call | flops 17999998976 | bytes 14000000 | tf_op jit(solution)/shard_map/spectra/pallas_call | solution.py:342
  15.3 0.0 collective-permute-done.near
  15.3 0.0 collective-permute-done.1.far
  15.3 0.0 copy-done.1
  15.3 0.0 copy-done.4
  15.3 0.0 copy-done.3
  15.3 0.0 copy-done.2
  15.3 0.0 copy-start
  15.3 2.3 %copy-done = bf16[9216,256]{1,0:T(8,128)(2,1)S(1)} copy-done((bf16[9216,256]{1,0:T(8,128)(2,1)S(1)}, bf16[9216,256]{1,0:T(8,128)(2,1)}, u32[]{:S(2)}) %copy-start) | copy-done | bytes 4718616
  17.7 21.4 %fields.1 = (f32[3,128,128]{2,1,0:T(8,128)}, f32[2,128,128]{2,1,0:T(8,128)S(1)}, f32[2,64,128]{2,1,0:T(8,128)S(1)}, f32[2,64,128]{2,1,0:T(8,128)S(1)}) custom-call(s32[24]{0:T(128)S(1)} %copy-done.3, f32[24]{0:T(128)S(1)} %copy-done.4, s32[1]{0:T(128)} %bitcast.place, f32[2,128,128]{2,1,0:T(8,128)S(1)} %copy-done.1, ...), custom_call_target="tpu_custom_call" | custom-call | tf_op jit(solution)/shard_map/fields/pallas_call | solution.py:358
  39.0 0.1 collective-permute-start.2
  39.1 3.5 %collective-permute-start.3 = (f32[2,64,128]{2,1,0:T(8,128)S(1)}, f32[2,64,128]{2,1,0:T(8,128)S(1)}, u32[]{:S(2)}, u32[]{:S(2)}) collective-permute-start(f32[2,64,128]{2,1,0:T(8,128)S(1)} %get-tuple-element.9), channel_id=1, source_target_pairs={{1,2},{2,1},{3,4},{4,3},{5,6},{6,5},{7,8},{8,7},{9,10},{10,9},{11,... | collective-permute-start | bytes 196616 | tf_op jit(solution)/shard_map/ppermute | solution.py:385
  42.6 0.0 collective-permute-done.2.near
  42.6 2.9 %collective-permute-done.3.far = f32[2,64,128]{2,1,0:T(8,128)S(1)} collective-permute-done((f32[2,64,128]{2,1,0:T(8,128)S(1)}, f32[2,64,128]{2,1,0:T(8,128)S(1)}, u32[]{:S(2)}, u32[]{:S(2)}) %collective-permute-start.3) | collective-permute-done | bytes 65568 | tf_op jit(solution)/shard_map/ppermute | solution.py:385
  45.6 0.7 %join.1 = f32[2,128,128]{2,1,0:T(8,128)} custom-call(s32[1]{0:T(128)} %bitcast.place, f32[2,128,128]{2,1,0:T(8,128)S(1)} %get-tuple-element.7.own, f32[2,64,128]{2,1,0:T(8,128)S(1)} %collective-permute-done.2.near, f32[2,64,128]{2,1,0:T(8,128)S(1)} %collective-permute-done.3.far), custom_call_target="tpu_custom_call" | custom-call | tf_op jit(solution)/shard_map/join/pallas_call | solution.py:386
Async XLA Ops:
  0.6 14.6 %copy-start.1 = (f32[2,128,128]{2,1,0:T(8,128)S(1)}, f32[2,128,128]{2,1,0:T(8,128)}, u32[]{:S(2)}) copy-start(f32[2,128,128]{2,1,0:T(8,128)} %own.1) | copy-start | bytes 393220
  0.6 14.6 %copy-start.4 = (f32[24]{0:T(128)S(1)}, f32[24]{0:T(128)}, u32[]{:S(2)}) copy-start(f32[24]{0:T(128)} %weight.1) | copy-start | bytes 292
  0.7 14.6 %copy-start.3 = (s32[24]{0:T(128)S(1)}, s32[24]{0:T(128)}, u32[]{:S(2)}) copy-start(s32[24]{0:T(128)} %group.1) | copy-start | bytes 292
  0.7 14.6 %copy-start.2 = (s32[128,128]{1,0:T(8,128)S(1)}, s32[128,128]{1,0:T(8,128)}, u32[]{:S(2)}) copy-start(s32[128,128]{1,0:T(8,128)} %target.1) | copy-start | bytes 196612
  0.7 14.6 %collective-permute-start = (f32[2,128,128]{2,1,0:T(8,128)}, f32[2,128,128]{2,1,0:T(8,128)S(1)}, u32[]{:S(2)}, u32[]{:S(2)}) collective-permute-start(f32[2,128,128]{2,1,0:T(8,128)} %own.1), channel_id=1, source_target_pairs={{0,1},{1,0},{2,3},{3,2},{4,5},{5,4},{6,7},{7,6},{8,9},{9,8},{10,11... | collective-permute-start | bytes 393224 | tf_op jit(solution)/shard_map/ppermute | solution.py:319
  1.4 13.9 %collective-permute-start.1 = (f32[2,128,128]{2,1,0:T(8,128)}, f32[2,128,128]{2,1,0:T(8,128)S(1)}, u32[]{:S(2)}, u32[]{:S(2)}) collective-permute-start(f32[2,128,128]{2,1,0:T(8,128)} %own.1), channel_id=1, source_target_pairs={{1,2},{2,1},{3,4},{4,3},{5,6},{6,5},{7,8},{8,7},{9,10},{10,9},{11,... | collective-permute-start | bytes 393224 | tf_op jit(solution)/shard_map/ppermute | solution.py:320
  15.3 2.3 %copy-start = (bf16[9216,256]{1,0:T(8,128)(2,1)S(1)}, bf16[9216,256]{1,0:T(8,128)(2,1)}, u32[]{:S(2)}) copy-start(bf16[9216,256]{1,0:T(8,128)(2,1)} %constant.15.clone.tables_far) | copy-start | bytes 14155780
  39.0 3.6 %collective-permute-start.2 = (f32[2,64,128]{2,1,0:T(8,128)S(1)}, f32[2,64,128]{2,1,0:T(8,128)S(1)}, u32[]{:S(2)}, u32[]{:S(2)}) collective-permute-start(f32[2,64,128]{2,1,0:T(8,128)S(1)} %get-tuple-element.8), channel_id=1, source_target_pairs={{0,1},{1,0},{2,3},{3,2},{4,5},{5,4},{6,7},{7,6},{8,9},{9,8},{10,11... | collective-permute-start | bytes 196616 | tf_op jit(solution)/shard_map/ppermute | solution.py:384
  39.1 6.5 %collective-permute-start.3 = (f32[2,64,128]{2,1,0:T(8,128)S(1)}, f32[2,64,128]{2,1,0:T(8,128)S(1)}, u32[]{:S(2)}, u32[]{:S(2)}) collective-permute-start(f32[2,64,128]{2,1,0:T(8,128)S(1)} %get-tuple-element.9), channel_id=1, source_target_pairs={{1,2},{2,1},{3,4},{4,3},{5,6},{6,5},{7,8},{8,7},{9,10},{10,9},{11,... | collective-permute-start | bytes 196616 | tf_op jit(solution)/shard_map/ppermute | solution.py:385

commit v11 on v8

--- a/solution.py
+++ b/solution.py
@@ -60,10 +60,16 @@
     return jnp.concatenate(parts, axis=0)
 
 
-def over_rows(table, x):
+def over_rows(table, x, piece=PIECE):
     high, low = split(x)
-    left = jnp.concatenate([table, table[:, :x.shape[0]]], axis=1)
-    return dot(left, jnp.concatenate([high, high, low], axis=0))
+    depth = x.shape[0]
+    parts = []
+    for at in range(0, table.shape[0], piece):
+        t_high, t_low = table[at:at + piece, :depth], table[at:at + piece, depth:]
+        both = jnp.dot(jnp.concatenate([t_high, t_low], axis=0), high, preferred_element_type=f32)
+        third = jnp.dot(t_high, low, preferred_element_type=f32)
+        parts.append(both[:piece] + (both[piece:] + third))
+    return jnp.concatenate(parts, axis=0)
 
 
 def over_lanes(x, table):
@@ -72,13 +78,19 @@
     return dot(jnp.concatenate([high, high, low], axis=1), right)
 
 
-def to_freqs(x, head, tail):
+def to_freqs(x, head, tail, piece=PIECE):
     high, low = split(x)
-    right = jnp.concatenate([head, head[:x.shape[1]]], axis=0)
-    first = dot(jnp.concatenate([high, high, low], axis=1), right)
-    rest = dot(jnp.concatenate([high, low], axis=1), jnp.concatenate([tail, tail], axis=0))
-    lanes = rest.shape[1] // 2
-    return first, rest[:, :lanes] + rest[:, lanes:]
+    depth = x.shape[1]
+    lanes = tail.shape[1] // 2
+    first, rest = [], []
+    for at in range(0, x.shape[0], piece):
+        stack = jnp.concatenate([high[at:at + piece], low[at:at + piece]], axis=0)
+        both = jnp.dot(stack, head[:depth], preferred_element_type=f32)
+        third = jnp.dot(high[at:at + piece], head[depth:], preferred_element_type=f32)
+        first.append(both[:piece] + (both[piece:] + third))
+        both = jnp.dot(stack, tail, preferred_element_type=f32)
+        rest.append(both[:piece, :lanes] + (both[:piece, lanes:] + both[piece:, :lanes]))
+    return jnp.concatenate(first, axis=0), jnp.concatenate(rest, axis=0)
 
 
 def side(x):
@@ -86,9 +98,9 @@
     return jnp.concatenate([x[:rows], x[rows:]], axis=1)
 
 
-def row_stage(pair, row_tab):
+def row_stage(pair, row_tab, piece=PIECE):
     width = pair.shape[1] // 2
-    half = over_rows(row_tab, pair)
+    half = over_rows(row_tab, pair, piece)
     return [side(half[:, :width]), side(half[:, width:])]
 
 
@@ -120,11 +132,11 @@
             inside = reach < radii[first + k]
             parts = [jnp.where(inside, taps[k, c], 0.0) for c in range(2)]
             planes.append(jnp.concatenate(parts, axis=0))
-        return row_stage(jnp.concatenate(planes, axis=1), row_tab)
+        return row_stage(jnp.concatenate(planes, axis=1), row_tab, 128)
 
     def cols_of(p, tiles):
         for j in range(2):
-            a, b = to_freqs(tiles[j], head, tail)
+            a, b = to_freqs(tiles[j], head, tail, 128)
             spec[2 * p + j, :, :a.shape[1]] = a
             spec[2 * p + j, :, a.shape[1]:] = b
 

time: 44.4 us -> 44.3 us (level)
  no operation moved by 1% of the time
where the time goes in v11:
time: 44.3 us; the launch traced here: 43.9 us
  Pallas kernels  30.5 us (69%)
  starting transfers between devices  7.38 us (17%)
  waiting for transfers between devices  2.95 us (7%)
  local copies, waits for them, and re-layouts  2.35 us (5%)
  between operations  0.75 us (2%)
    pallas_call x1, Pallas kernels, on_device(): pl.pallas_call(functools.partial(main_body, layout=layout, sections=secti...  19.4 us
    pallas_call x1, Pallas kernels, on_device(): pl.pallas_call(spectra_body, grid=(kernels // BATCH,), out_shape=jax.Shap...  10.4 us
    ppermute x1, starting transfers between devices, on_device(): far_in = lax.ppermute(far_rim, 'row', far_pairs)  3.52 us
    ppermute x1, starting transfers between devices, on_device(): far = lax.ppermute(mask_field, 'row', far_pairs)  3.05 us
    ppermute x1, waiting for transfers between devices, on_device(): far_in = lax.ppermute(far_rim, 'row', far_pairs)  2.95 us
    unnamed x10, local copies, waits for them, and re-layouts  2.35 us
  transfers between devices with their start and end apart: 4, of which 1 were waited for; matrix products, arithmetic and copies ran while one was open for 0% of the time, Pallas kernels for 24%

profile of v11, /device:TPU:21, one launch (start us, length us, event | category | flops | bytes accessed | tf_op | source)
XLA Modules:
  0.0 43.9 jit_solution(5126484121939620925)
XLA Ops:
  0.6 0.0 copy-start.1
  0.6 0.0 copy-start.4
  0.7 0.0 copy-start.3
  0.7 0.0 copy-start.2
  0.7 0.7 %collective-permute-start = (f32[2,128,128]{2,1,0:T(8,128)}, f32[2,128,128]{2,1,0:T(8,128)S(1)}, u32[]{:S(2)}, u32[]{:S(2)}) collective-permute-start(f32[2,128,128]{2,1,0:T(8,128)} %own.1), channel_id=1, source_target_pairs={{0,1},{1,0},{2,3},{3,2},{4,5},{5,4},{6,7},{7,6},{8,9},{9,8},{10,11... | collective-permute-start | bytes 393224 | tf_op jit(solution)/shard_map/ppermute | solution.py:323
  1.4 3.0 %collective-permute-start.1 = (f32[2,128,128]{2,1,0:T(8,128)}, f32[2,128,128]{2,1,0:T(8,128)S(1)}, u32[]{:S(2)}, u32[]{:S(2)}) collective-permute-start(f32[2,128,128]{2,1,0:T(8,128)} %own.1), channel_id=1, source_target_pairs={{1,2},{2,1},{3,4},{4,3},{5,6},{6,5},{7,8},{8,7},{9,10},{10,9},{11,... | collective-permute-start | bytes 393224 | tf_op jit(solution)/shard_map/ppermute | solution.py:324
  4.5 10.4 %spectra.1.spec_far = f32[24,256,384]{2,1,0:T(8,128)} custom-call(s32[24]{0:T(128)} %radii.1, f32[24,2,128,128]{3,2,1,0:T(8,128)} %taps.1, bf16[512,512]{1,0:T(8,128)(2,1)} %constant.12.clone.row_ref, bf16[512,256]{1,0:T(8,128)(2,1)} %constant.13.clone.head_ref, bf16[256,256]{1,0:T(8,128)(2,1)} %constant.14.clone.tail_ref), custom_call_target="tpu_custom_call" | custom-call | flops 17999998976 | bytes 14000000 | tf_op jit(solution)/shard_map/spectra/pallas_call | solution.py:346
  14.9 0.0 collective-permute-done.near
  14.9 0.0 collective-permute-done.1.far
  14.9 0.0 copy-done.1
  14.9 0.0 copy-done.4
  14.9 0.0 copy-done.3
  14.9 0.0 copy-done.2
  15.0 0.0 copy-start
  15.0 2.3 %copy-done = bf16[9216,256]{1,0:T(8,128)(2,1)S(1)} copy-done((bf16[9216,256]{1,0:T(8,128)(2,1)S(1)}, bf16[9216,256]{1,0:T(8,128)(2,1)}, u32[]{:S(2)}) %copy-start) | copy-done | bytes 4718616
  17.3 19.4 %fields.1 = (f32[3,128,128]{2,1,0:T(8,128)}, f32[2,128,128]{2,1,0:T(8,128)S(1)}, f32[2,64,128]{2,1,0:T(8,128)S(1)}, f32[2,64,128]{2,1,0:T(8,128)S(1)}) custom-call(s32[24]{0:T(128)S(1)} %copy-done.3, f32[24]{0:T(128)S(1)} %copy-done.4, s32[1]{0:T(128)} %bitcast.place, f32[2,128,128]{2,1,0:T(8,128)S(1)} %copy-done.1, ...), custom_call_target="tpu_custom_call" | custom-call | tf_op jit(solution)/shard_map/fields/pallas_call | solution.py:362
  36.7 0.1 collective-permute-start.2
  36.7 3.5 %collective-permute-start.3 = (f32[2,64,128]{2,1,0:T(8,128)S(1)}, f32[2,64,128]{2,1,0:T(8,128)S(1)}, u32[]{:S(2)}, u32[]{:S(2)}) collective-permute-start(f32[2,64,128]{2,1,0:T(8,128)S(1)} %get-tuple-element.9), channel_id=1, source_target_pairs={{1,2},{2,1},{3,4},{4,3},{5,6},{6,5},{7,8},{8,7},{9,10},{10,9},{11,... | collective-permute-start | bytes 196616 | tf_op jit(solution)/shard_map/ppermute | solution.py:389
  40.3 0.0 collective-permute-done.2.near
  40.3 2.9 %collective-permute-done.3.far = f32[2,64,128]{2,1,0:T(8,128)S(1)} collective-permute-done((f32[2,64,128]{2,1,0:T(8,128)S(1)}, f32[2,64,128]{2,1,0:T(8,128)S(1)}, u32[]{:S(2)}, u32[]{:S(2)}) %collective-permute-start.3) | collective-permute-done | bytes 65568 | tf_op jit(solution)/shard_map/ppermute | solution.py:389
  43.2 0.7 %join.1 = f32[2,128,128]{2,1,0:T(8,128)} custom-call(s32[1]{0:T(128)} %bitcast.place, f32[2,128,128]{2,1,0:T(8,128)S(1)} %get-tuple-element.7.own, f32[2,64,128]{2,1,0:T(8,128)S(1)} %collective-permute-done.2.near, f32[2,64,128]{2,1,0:T(8,128)S(1)} %collective-permute-done.3.far), custom_call_target="tpu_custom_call" | custom-call | tf_op jit(solution)/shard_map/join/pallas_call | solution.py:390
Async XLA Ops:
  0.6 14.3 %copy-start.1 = (f32[2,128,128]{2,1,0:T(8,128)S(1)}, f32[2,128,128]{2,1,0:T(8,128)}, u32[]{:S(2)}) copy-start(f32[2,128,128]{2,1,0:T(8,128)} %own.1) | copy-start | bytes 393220
  0.6 14.3 %copy-start.4 = (f32[24]{0:T(128)S(1)}, f32[24]{0:T(128)}, u32[]{:S(2)}) copy-start(f32[24]{0:T(128)} %weight.1) | copy-start | bytes 292
  0.7 14.3 %copy-start.3 = (s32[24]{0:T(128)S(1)}, s32[24]{0:T(128)}, u32[]{:S(2)}) copy-start(s32[24]{0:T(128)} %group.1) | copy-start | bytes 292
  0.7 14.3 %copy-start.2 = (s32[128,128]{1,0:T(8,128)S(1)}, s32[128,128]{1,0:T(8,128)}, u32[]{:S(2)}) copy-start(s32[128,128]{1,0:T(8,128)} %target.1) | copy-start | bytes 196612
  0.7 14.2 %collective-permute-start = (f32[2,128,128]{2,1,0:T(8,128)}, f32[2,128,128]{2,1,0:T(8,128)S(1)}, u32[]{:S(2)}, u32[]{:S(2)}) collective-permute-start(f32[2,128,128]{2,1,0:T(8,128)} %own.1), channel_id=1, source_target_pairs={{0,1},{1,0},{2,3},{3,2},{4,5},{5,4},{6,7},{7,6},{8,9},{9,8},{10,11... | collective-permute-start | bytes 393224 | tf_op jit(solution)/shard_map/ppermute | solution.py:323
  1.4 13.5 %collective-permute-start.1 = (f32[2,128,128]{2,1,0:T(8,128)}, f32[2,128,128]{2,1,0:T(8,128)S(1)}, u32[]{:S(2)}, u32[]{:S(2)}) collective-permute-start(f32[2,128,128]{2,1,0:T(8,128)} %own.1), channel_id=1, source_target_pairs={{1,2},{2,1},{3,4},{4,3},{5,6},{6,5},{7,8},{8,7},{9,10},{10,9},{11,... | collective-permute-start | bytes 393224 | tf_op jit(solution)/shard_map/ppermute | solution.py:324
  15.0 2.3 %copy-start = (bf16[9216,256]{1,0:T(8,128)(2,1)S(1)}, bf16[9216,256]{1,0:T(8,128)(2,1)}, u32[]{:S(2)}) copy-start(bf16[9216,256]{1,0:T(8,128)(2,1)} %constant.15.clone.tables_far) | copy-start | bytes 14155780
  36.7 3.6 %collective-permute-start.2 = (f32[2,64,128]{2,1,0:T(8,128)S(1)}, f32[2,64,128]{2,1,0:T(8,128)S(1)}, u32[]{:S(2)}, u32[]{:S(2)}) collective-permute-start(f32[2,64,128]{2,1,0:T(8,128)S(1)} %get-tuple-element.8), channel_id=1, source_target_pairs={{0,1},{1,0},{2,3},{3,2},{4,5},{5,4},{6,7},{7,6},{8,9},{9,8},{10,11... | collective-permute-start | bytes 196616 | tf_op jit(solution)/shard_map/ppermute | solution.py:388
  36.7 6.5 %collective-permute-start.3 = (f32[2,64,128]{2,1,0:T(8,128)S(1)}, f32[2,64,128]{2,1,0:T(8,128)S(1)}, u32[]{:S(2)}, u32[]{:S(2)}) collective-permute-start(f32[2,64,128]{2,1,0:T(8,128)S(1)} %get-tuple-element.9), channel_id=1, source_target_pairs={{1,2},{2,1},{3,4},{4,3},{5,6},{6,5},{7,8},{8,7},{9,10},{10,9},{11,... | collective-permute-start | bytes 196616 | tf_op jit(solution)/shard_map/ppermute | solution.py:389

commit v12 on v8

--- a/solution.py
+++ b/solution.py
@@ -20,7 +20,7 @@
 f32 = jnp.float32
 bf16 = jnp.bfloat16
 MIB = 1024 * 1024
-LIMIT = 40
+LIMIT = 53
 
 
 def halves(table, axis):
@@ -60,36 +60,49 @@
     return jnp.concatenate(parts, axis=0)
 
 
-def over_rows(table, x):
-    high, low = split(x)
-    left = jnp.concatenate([table, table[:, :x.shape[0]]], axis=1)
-    return dot(left, jnp.concatenate([high, high, low], axis=0))
-
-
-def over_lanes(x, table):
-    high, low = split(x)
-    right = jnp.concatenate([table, table[:x.shape[1]]], axis=0)
+def over_rows(table, parts, piece=PIECE):
+    high, low = parts
+    depth = high.shape[0]
+    pieces = []
+    for at in range(0, table.shape[0], piece):
+        t_high, t_low = table[at:at + piece, :depth], table[at:at + piece, depth:]
+        both = jnp.dot(jnp.concatenate([t_high, t_low], axis=0), high, preferred_element_type=f32)
+        third = jnp.dot(t_high, low, preferred_element_type=f32)
+        pieces.append(both[:piece] + (both[piece:] + third))
+    return pieces
+
+
+def over_lanes(parts, table):
+    high, low = parts
+    right = jnp.concatenate([table, table[:high.shape[1]]], axis=0)
     return dot(jnp.concatenate([high, high, low], axis=1), right)
 
 
-def to_freqs(x, head, tail):
-    high, low = split(x)
-    right = jnp.concatenate([head, head[:x.shape[1]]], axis=0)
-    first = dot(jnp.concatenate([high, high, low], axis=1), right)
-    rest = dot(jnp.concatenate([high, low], axis=1), jnp.concatenate([tail, tail], axis=0))
-    lanes = rest.shape[1] // 2
-    return first, rest[:, :lanes] + rest[:, lanes:]
-
-
-def side(x):
-    rows = x.shape[0] // 2
-    return jnp.concatenate([x[:rows], x[rows:]], axis=1)
+def to_freqs(parts, head, tail):
+    high, low = parts
+    rows, depth = high.shape
+    lanes = tail.shape[1] // 2
+    stack = jnp.concatenate([high, low], axis=0)
+    both = jnp.dot(stack, head[:depth], preferred_element_type=f32)
+    third = jnp.dot(high, head[depth:], preferred_element_type=f32)
+    first = both[:rows] + (both[rows:] + third)
+    both = jnp.dot(stack, tail, preferred_element_type=f32)
+    return first, both[:rows, :lanes] + (both[:rows, lanes:] + both[rows:, :lanes])
+
+
+def beside(pieces):
+    parts = [split(piece) for piece in pieces]
+    return [jnp.concatenate(part, axis=1) for part in zip(*parts)]
 
 
 def row_stage(pair, row_tab):
     width = pair.shape[1] // 2
-    half = over_rows(row_tab, pair)
-    return [side(half[:, :width]), side(half[:, width:])]
+    pieces = over_rows(row_tab, split(pair), row_tab.shape[0] // 2)
+    parts = [split(piece) for piece in pieces]
+    return [
+        [jnp.concatenate([part[:, at:at + width] for part in both], axis=1) for both in zip(*parts)]
+        for at in (0, width)
+    ]
 
 
 def staggered(count, first, second):
@@ -106,29 +119,52 @@
     return pltpu.roll(x, x.shape[1] // 2, 1)
 
 
-def spectra_body(radii, taps, row_ref, head_ref, tail_ref, spec):
-    batch, _, span, _ = taps.shape
+def spectra_body(radii, taps_far, row_ref, head_ref, tail_ref, spec_far, taps, spec, in_sems, out_sems):
+    kernels, _, span, _ = taps.shape
     row_tab, head, tail = row_ref[...], head_ref[...], tail_ref[...]
-    first = pl.program_id(0) * batch
+    steps = in_sems.shape[0]
+    batch = kernels // steps
+
+    def fetch(i):
+        here = pl.ds(i * batch, batch)
+        return pltpu.make_async_copy(taps_far.at[here], taps.at[here], in_sems.at[i])
+
+    def put(i):
+        here = pl.ds(2 * i, 2)
+        return pltpu.make_async_copy(spec.at[here], spec_far.at[here], out_sems.at[i])
+
+    for i in range(steps):
+        fetch(i).start()
     row_at = lax.broadcasted_iota(jnp.int32, (span, span), 0) - span // 2
     col_at = lax.broadcasted_iota(jnp.int32, (span, span), 1) - span // 2
     reach = jnp.maximum(jnp.maximum(row_at, -1 - row_at), jnp.maximum(col_at, -1 - col_at))
 
-    def rows_of(p):
-        planes = []
-        for k in (2 * p, 2 * p + 1):
-            inside = reach < radii[first + k]
-            parts = [jnp.where(inside, taps[k, c], 0.0) for c in range(2)]
-            planes.append(jnp.concatenate(parts, axis=0))
-        return row_stage(jnp.concatenate(planes, axis=1), row_tab)
-
-    def cols_of(p, tiles):
-        for j in range(2):
-            a, b = to_freqs(tiles[j], head, tail)
-            spec[2 * p + j, :, :a.shape[1]] = a
-            spec[2 * p + j, :, a.shape[1]:] = b
-
-    staggered(batch // 2, rows_of, cols_of)
+    def step(i, carry):
+        fetch(i).wait()
+
+        def rows_of(p):
+            planes = []
+            for j in range(2):
+                k = i * batch + 2 * p + j
+                inside = reach < radii[k]
+                parts = [jnp.where(inside, taps[k, c], 0.0) for c in range(2)]
+                planes.append(jnp.concatenate(parts, axis=0))
+            return row_stage(jnp.concatenate(planes, axis=1), row_tab)
+
+        def cols_of(p, tiles):
+            for j in range(2):
+                k = i * batch + 2 * p + j
+                a, b = to_freqs(tiles[j], head, tail)
+                spec[k, :, :a.shape[1]] = a
+                spec[k, :, a.shape[1]:] = b
+            put(i * (batch // 2) + p).start()
+
+        staggered(batch // 2, rows_of, cols_of)
+        return carry
+
+    lax.fori_loop(0, steps, step, 0)
+    for i in range(kernels // 2):
+        put(i).wait()
 
 
 def main_body(
@@ -171,7 +207,8 @@
         below = jnp.where(odd, far[c, :rim], near[c, :rim])
         parts += [above, own[c], below]
     mask = jnp.concatenate(parts, axis=0)
-    m_first, m_rest = to_freqs(side(over_rows(table("mask_row"), mask)), table("mask_head"), table("mask_tail"))
+    half = over_rows(table("mask_row"), split(mask), grid_rows)
+    m_first, m_rest = to_freqs(beside(half), table("mask_head"), table("mask_tail"))
     lane = lax.broadcasted_iota(jnp.int32, m_rest.shape, 1)
     real_half = lane < m_rest.shape[1] // 2
     turned = swap(m_rest)
@@ -199,12 +236,12 @@
                     s_re * m_im + s_im * m_re,
                     s_rest * m_same + swap(s_rest) * m_cross,
                 ], axis=1)
-                back = over_lanes(product, col_inv)
-                planes.append(jnp.concatenate([back[:, :width], back[:, width:]], axis=0))
-            return jnp.concatenate(planes, axis=1)
+                back = over_lanes(split(product), col_inv)
+                planes.append(split(jnp.concatenate([back[:, :width], back[:, width:]], axis=0)))
+            return [jnp.concatenate(part, axis=1) for part in zip(*planes)]
 
         def rows_of(p, pair):
-            found = over_rows(row_inv, pair)
+            found, = over_rows(row_inv, pair, 2 * count)
             field[i * (batch // 2) + p] = found
             power = found[:count] * found[:count] + found[count:] * found[count:]
             for j in range(2):
@@ -259,14 +296,14 @@
     same, cross = grad_spec[:, 2 * width:3 * width], grad_spec[:, 3 * width:]
     tail_sum = jnp.where(real_half, same + swap(same), swap(cross) - cross)
     total = jnp.concatenate([grad_spec[:, :2 * width], tail_sum], axis=1)
-    back = over_lanes(total, table("grad_col"))
-    full = over_rows(table("grad_row"), jnp.concatenate([back[:, :width], back[:, width:]], axis=0))
+    back = over_lanes(split(total), table("grad_col"))
+    back = split(jnp.concatenate([back[:, :width], back[:, width:]], axis=0))
+    full = over_rows(table("grad_row"), back, grid_rows)
     for c in range(2):
-        base = c * grid_rows
-        rise, fall = full[base:base + rim], full[base + rim + count:base + grid_rows]
+        rise, fall = full[c][:rim], full[c][rim + count:]
         near_rim[c] = jnp.where(odd, rise, fall)
         far_rim[c] = jnp.where(odd, fall, rise)
-        grad_own[c] = full[base + rim:base + rim + count]
+        grad_own[c] = full[c][rim:rim + count]
     out.wait()
 
 
@@ -333,10 +370,15 @@
     hbm = pl.BlockSpec(memory_space=pltpu.HBM)
     spectra = pl.pallas_call(
         spectra_body,
-        grid=(kernels // BATCH,),
         out_shape=jax.ShapeDtypeStruct((kernels, grid_rows, 2 * grid_cols), f32),
-        in_specs=[smem, pl.BlockSpec((BATCH, 2, span, span), lambda i: (i, 0, 0, 0)), vmem, vmem, vmem],
-        out_specs=pl.BlockSpec((BATCH, grid_rows, 2 * grid_cols), lambda i: (i, 0, 0)),
+        in_specs=[smem, hbm, vmem, vmem, vmem],
+        out_specs=hbm,
+        scratch_shapes=[
+            pltpu.VMEM(kernel_taps.shape, f32),
+            pltpu.VMEM((kernels, grid_rows, 2 * grid_cols), f32),
+            pltpu.SemaphoreType.DMA((kernels // BATCH,)),
+            pltpu.SemaphoreType.DMA((kernels // 2,)),
+        ],
         compiler_params=pltpu.CompilerParams(vmem_limit_bytes=56 * MIB),
         cost_estimate=pl.CostEstimate(flops=18 * 10**9, bytes_accessed=14 * 10**6, transcendentals=0),
         name="spectra",

time: 44.4 us -> 42.3 us (0.953)
  local copies, waits for them, and re-layouts: 2.35 us -> 0.02 us
    unnamed x10 -> x8, local copies, waits for them, and re-layouts: 2.35 us -> 0.02 us
  transfers between devices with their start and end apart: 4 -> 4, of which waited for: 1 -> 1; matrix products, arithmetic and copies ran while one was open for 0% -> 0% of each run, Pallas kernels for 24% -> 25%
where the time goes in v12:
time: 42.3 us; the launch traced here: 42 us
  Pallas kernels  30.9 us (73%)
  starting transfers between devices  7.38 us (17%)
  waiting for transfers between devices  2.95 us (7%)
  between operations  0.76 us (2%)
    pallas_call x1, Pallas kernels, on_device(): pl.pallas_call(functools.partial(main_body, layout=layout, sections=secti...  19.6 us
    pallas_call x1, Pallas kernels, on_device(): pl.pallas_call(spectra_body, out_shape=jax.ShapeDtypeStruct((kernels, gri...  10.6 us
    ppermute x1, starting transfers between devices, on_device(): far_in = lax.ppermute(far_rim, 'row', far_pairs)  3.52 us
    ppermute x1, starting transfers between devices, on_device(): far = lax.ppermute(mask_field, 'row', far_pairs)  3.05 us
    ppermute x1, waiting for transfers between devices, on_device(): far_in = lax.ppermute(far_rim, 'row', far_pairs)  2.95 us
  transfers between devices with their start and end apart: 4, of which 1 were waited for; matrix products, arithmetic and copies ran while one was open for 0% of the time, Pallas kernels for 25%

profile of v12, /device:TPU:21, one launch (start us, length us, event | category | flops | bytes accessed | tf_op | source)
XLA Modules:
  0.0 42.0 jit_solution(1624725450320740703)
XLA Ops:
  0.6 0.0 copy-start
  0.6 0.0 copy-start.3
  0.7 0.0 copy-start.2
  0.7 0.0 copy-start.1
  0.7 0.7 %collective-permute-start = (f32[2,128,128]{2,1,0:T(8,128)}, f32[2,128,128]{2,1,0:T(8,128)S(1)}, u32[]{:S(2)}, u32[]{:S(2)}) collective-permute-start(f32[2,128,128]{2,1,0:T(8,128)} %own.1), channel_id=1, source_target_pairs={{0,1},{1,0},{2,3},{3,2},{4,5},{5,4},{6,7},{7,6},{8,9},{9,8},{10,11... | collective-permute-start | bytes 393224 | tf_op jit(solution)/shard_map/ppermute | solution.py:348
  1.4 3.0 %collective-permute-start.1 = (f32[2,128,128]{2,1,0:T(8,128)}, f32[2,128,128]{2,1,0:T(8,128)S(1)}, u32[]{:S(2)}, u32[]{:S(2)}) collective-permute-start(f32[2,128,128]{2,1,0:T(8,128)} %own.1), channel_id=1, source_target_pairs={{1,2},{2,1},{3,4},{4,3},{5,6},{6,5},{7,8},{8,7},{9,10},{10,9},{11,... | collective-permute-start | bytes 393224 | tf_op jit(solution)/shard_map/ppermute | solution.py:349
  4.5 10.6 %spectra.1.spec_far = f32[24,256,384]{2,1,0:T(8,128)} custom-call(s32[24]{0:T(128)} %radii.1, f32[24,2,128,128]{3,2,1,0:T(8,128)} %taps_far.1, bf16[512,512]{1,0:T(8,128)(2,1)} %constant.12.clone.row_ref, bf16[512,256]{1,0:T(8,128)(2,1)} %constant.13.clone.head_ref, bf16[256,256]{1,0:T(8,128)(2,1)} %constant.14.clone.tail_ref), custom_call_target="tpu_custom_call" | custom-call | flops 17999998976 | bytes 14000000 | tf_op jit(solution)/shard_map/spectra/pallas_call | solution.py:371
  15.1 0.0 collective-permute-done.near
  15.1 0.0 collective-permute-done.1.far
  15.1 0.0 copy-done
  15.1 0.0 copy-done.3
  15.1 0.0 copy-done.2
  15.1 0.0 copy-done.1
  15.1 19.6 %fields.1 = (f32[3,128,128]{2,1,0:T(8,128)}, f32[2,128,128]{2,1,0:T(8,128)S(1)}, f32[2,64,128]{2,1,0:T(8,128)S(1)}, f32[2,64,128]{2,1,0:T(8,128)S(1)}) custom-call(s32[24]{0:T(128)S(1)} %copy-done.2, f32[24]{0:T(128)S(1)} %copy-done.3, s32[1]{0:T(128)} %bitcast.place, f32[2,128,128]{2,1,0:T(8,128)S(1)} %copy-done, ...), custom_call_target="tpu_custom_call" | custom-call | tf_op jit(solution)/shard_map/fields/pallas_call | solution.py:392
  34.7 0.1 collective-permute-start.2
  34.8 3.5 %collective-permute-start.3 = (f32[2,64,128]{2,1,0:T(8,128)S(1)}, f32[2,64,128]{2,1,0:T(8,128)S(1)}, u32[]{:S(2)}, u32[]{:S(2)}) collective-permute-start(f32[2,64,128]{2,1,0:T(8,128)S(1)} %get-tuple-element.9), channel_id=1, source_target_pairs={{1,2},{2,1},{3,4},{4,3},{5,6},{6,5},{7,8},{8,7},{9,10},{10,9},{11,... | collective-permute-start | bytes 196616 | tf_op jit(solution)/shard_map/ppermute | solution.py:419
  38.3 0.0 collective-permute-done.2.near
  38.3 2.9 %collective-permute-done.3.far = f32[2,64,128]{2,1,0:T(8,128)S(1)} collective-permute-done((f32[2,64,128]{2,1,0:T(8,128)S(1)}, f32[2,64,128]{2,1,0:T(8,128)S(1)}, u32[]{:S(2)}, u32[]{:S(2)}) %collective-permute-start.3) | collective-permute-done | bytes 65568 | tf_op jit(solution)/shard_map/ppermute | solution.py:419
  41.3 0.7 %join.1 = f32[2,128,128]{2,1,0:T(8,128)} custom-call(s32[1]{0:T(128)} %bitcast.place, f32[2,128,128]{2,1,0:T(8,128)S(1)} %get-tuple-element.7.own, f32[2,64,128]{2,1,0:T(8,128)S(1)} %collective-permute-done.2.near, f32[2,64,128]{2,1,0:T(8,128)S(1)} %collective-permute-done.3.far), custom_call_target="tpu_custom_call" | custom-call | tf_op jit(solution)/shard_map/join/pallas_call | solution.py:420
Async XLA Ops:
  0.6 14.4 %copy-start = (f32[2,128,128]{2,1,0:T(8,128)S(1)}, f32[2,128,128]{2,1,0:T(8,128)}, u32[]{:S(2)}) copy-start(f32[2,128,128]{2,1,0:T(8,128)} %own.1) | copy-start | bytes 393220
  0.6 14.4 %copy-start.3 = (f32[24]{0:T(128)S(1)}, f32[24]{0:T(128)}, u32[]{:S(2)}) copy-start(f32[24]{0:T(128)} %weight.1) | copy-start | bytes 292
  0.7 14.4 %copy-start.2 = (s32[24]{0:T(128)S(1)}, s32[24]{0:T(128)}, u32[]{:S(2)}) copy-start(s32[24]{0:T(128)} %group.1) | copy-start | bytes 292
  0.7 14.4 %copy-start.1 = (s32[128,128]{1,0:T(8,128)S(1)}, s32[128,128]{1,0:T(8,128)}, u32[]{:S(2)}) copy-start(s32[128,128]{1,0:T(8,128)} %target.1) | copy-start | bytes 196612
  0.7 14.4 %collective-permute-start = (f32[2,128,128]{2,1,0:T(8,128)}, f32[2,128,128]{2,1,0:T(8,128)S(1)}, u32[]{:S(2)}, u32[]{:S(2)}) collective-permute-start(f32[2,128,128]{2,1,0:T(8,128)} %own.1), channel_id=1, source_target_pairs={{0,1},{1,0},{2,3},{3,2},{4,5},{5,4},{6,7},{7,6},{8,9},{9,8},{10,11... | collective-permute-start | bytes 393224 | tf_op jit(solution)/shard_map/ppermute | solution.py:348
  1.4 13.7 %collective-permute-start.1 = (f32[2,128,128]{2,1,0:T(8,128)}, f32[2,128,128]{2,1,0:T(8,128)S(1)}, u32[]{:S(2)}, u32[]{:S(2)}) collective-permute-start(f32[2,128,128]{2,1,0:T(8,128)} %own.1), channel_id=1, source_target_pairs={{1,2},{2,1},{3,4},{4,3},{5,6},{6,5},{7,8},{8,7},{9,10},{10,9},{11,... | collective-permute-start | bytes 393224 | tf_op jit(solution)/shard_map/ppermute | solution.py:349
  34.7 3.6 %collective-permute-start.2 = (f32[2,64,128]{2,1,0:T(8,128)S(1)}, f32[2,64,128]{2,1,0:T(8,128)S(1)}, u32[]{:S(2)}, u32[]{:S(2)}) collective-permute-start(f32[2,64,128]{2,1,0:T(8,128)S(1)} %get-tuple-element.8), channel_id=1, source_target_pairs={{0,1},{1,0},{2,3},{3,2},{4,5},{5,4},{6,7},{7,6},{8,9},{9,8},{10,11... | collective-permute-start | bytes 196616 | tf_op jit(solution)/shard_map/ppermute | solution.py:418
  34.8 6.5 %collective-permute-start.3 = (f32[2,64,128]{2,1,0:T(8,128)S(1)}, f32[2,64,128]{2,1,0:T(8,128)S(1)}, u32[]{:S(2)}, u32[]{:S(2)}) collective-permute-start(f32[2,64,128]{2,1,0:T(8,128)S(1)} %get-tuple-element.9), channel_id=1, source_target_pairs={{1,2},{2,1},{3,4},{4,3},{5,6},{6,5},{7,8},{8,7},{9,10},{10,9},{11,... | collective-permute-start | bytes 196616 | tf_op jit(solution)/shard_map/ppermute | solution.py:419

commit v13 on v12

--- a/solution.py
+++ b/solution.py
@@ -41,6 +41,14 @@
     return analysis(freqs, points, shift).T * scale
 
 
+def class_table(freqs, points, c):
+    f = np.arange(c, freqs, 4)[:, None]
+    n = np.arange(points)[None, :]
+    angle = 2.0 * math.pi * ((f * n) % freqs) / freqs
+    cos, sin = np.cos(angle), np.sin(angle)
+    return np.block([[cos, sin], [-sin, cos]])
+
+
 def grouped(freqs, lanes):
     head, tail = np.arange(lanes), np.arange(lanes, freqs)
     return np.concatenate([head, freqs + head, tail, freqs + tail])
@@ -60,16 +68,56 @@
     return jnp.concatenate(parts, axis=0)
 
 
-def over_rows(table, parts, piece=PIECE):
-    high, low = parts
-    depth = high.shape[0]
-    pieces = []
-    for at in range(0, table.shape[0], piece):
-        t_high, t_low = table[at:at + piece, :depth], table[at:at + piece, depth:]
-        both = jnp.dot(jnp.concatenate([t_high, t_low], axis=0), high, preferred_element_type=f32)
-        third = jnp.dot(t_high, low, preferred_element_type=f32)
-        pieces.append(both[:piece] + (both[piece:] + third))
-    return pieces
+def class_product(table, c, parts):
+    depth = parts[0].shape[0]
+    left = table[:, c * depth:(c + 1) * depth]
+    found = dot(jnp.concatenate([left, left], axis=1), jnp.concatenate(parts, axis=0))
+    half = found.shape[0] // 2
+    return found[:half] + found[half:]
+
+
+def turned(x, sign):
+    re, im = x
+    return (-im, re) if sign > 0 else (im, -re)
+
+
+def plus(x, y):
+    return x[0] + y[0], x[1] + y[1]
+
+
+def minus(x, y):
+    return x[0] - y[0], x[1] - y[1]
+
+
+def to_row_freqs(x, table):
+    if len(x) == 2:
+        even, odd, even_less, odd_less = x[0], x[1], x[0], x[1]
+    else:
+        even, odd = plus(x[0], x[2]), plus(x[1], x[3])
+        even_less, odd_less = minus(x[0], x[2]), minus(x[1], x[3])
+    folded = [
+        plus(even, odd),
+        plus(even_less, turned(odd_less, -1)),
+        minus(even, odd),
+        plus(even_less, turned(odd_less, 1)),
+    ]
+    return [class_product(table, c, split(jnp.concatenate(y, axis=0))) for c, y in enumerate(folded)]
+
+
+def from_row_freqs(classes, table, quarters):
+    v = []
+    for c, parts in enumerate(classes):
+        found = class_product(table, c, parts)
+        half = found.shape[0] // 2
+        v.append((found[:half], found[half:]))
+    out = []
+    for q in quarters:
+        if q % 2 == 0:
+            even, odd = plus(v[0], v[2]), plus(v[1], v[3])
+        else:
+            even, odd = minus(v[0], v[2]), turned(minus(v[1], v[3]), 1)
+        out.append(plus(even, odd) if q < 2 else minus(even, odd))
+    return out
 
 
 def over_lanes(parts, table):
@@ -90,19 +138,21 @@
     return first, both[:rows, :lanes] + (both[:rows, lanes:] + both[rows:, :lanes])
 
 
-def beside(pieces):
-    parts = [split(piece) for piece in pieces]
-    return [jnp.concatenate(part, axis=1) for part in zip(*parts)]
-
-
-def row_stage(pair, row_tab):
-    width = pair.shape[1] // 2
-    pieces = over_rows(row_tab, split(pair), row_tab.shape[0] // 2)
-    parts = [split(piece) for piece in pieces]
-    return [
-        [jnp.concatenate([part[:, at:at + width] for part in both], axis=1) for both in zip(*parts)]
-        for at in (0, width)
-    ]
+def beside(classes, at, width):
+    tiles = []
+    for found in classes:
+        half = found.shape[0] // 2
+        tiles.append(jnp.concatenate([found[:half, at:at + width], found[half:, at:at + width]], axis=1))
+    return split(jnp.concatenate(tiles, axis=0))
+
+
+def row_stage(quarters, row_fwd, width):
+    classes = to_row_freqs(quarters, row_fwd)
+    return [beside(classes, at, width) for at in range(0, quarters[0][0].shape[1], width)]
+
+
+def quarters_of(re, im, quarter):
+    return [(re[at:at + quarter], im[at:at + quarter]) for at in range(0, re.shape[0], quarter)]
 
 
 def staggered(count, first, second):
@@ -115,13 +165,25 @@
     second(count - 1, held)
 
 
+def side_by_side(planes, c, width):
+    quarter = planes[0][0].shape[0] // 4
+    rows = slice(c * quarter, (c + 1) * quarter)
+    return [
+        jnp.concatenate([
+            jnp.concatenate([plane[part][rows, at:at + width] for plane in planes], axis=1)
+            for at in (0, width)
+        ], axis=0)
+        for part in range(2)
+    ]
+
+
 def swap(x):
     return pltpu.roll(x, x.shape[1] // 2, 1)
 
 
 def spectra_body(radii, taps_far, row_ref, head_ref, tail_ref, spec_far, taps, spec, in_sems, out_sems):
     kernels, _, span, _ = taps.shape
-    row_tab, head, tail = row_ref[...], head_ref[...], tail_ref[...]
+    row_fwd, head, tail = row_ref[...], head_ref[...], tail_ref[...]
     steps = in_sems.shape[0]
     batch = kernels // steps
 
@@ -143,13 +205,14 @@
         fetch(i).wait()
 
         def rows_of(p):
-            planes = []
+            planes = [[], []]
             for j in range(2):
                 k = i * batch + 2 * p + j
                 inside = reach < radii[k]
-                parts = [jnp.where(inside, taps[k, c], 0.0) for c in range(2)]
-                planes.append(jnp.concatenate(parts, axis=0))
-            return row_stage(jnp.concatenate(planes, axis=1), row_tab)
+                for c in range(2):
+                    planes[c].append(jnp.where(inside, taps[k, c], 0.0))
+            re, im = [jnp.concatenate(plane, axis=1) for plane in planes]
+            return row_stage(quarters_of(re, im, span // 2), row_fwd, span)
 
         def cols_of(p, tiles):
             for j in range(2):
@@ -201,14 +264,14 @@
     fetch_table(0).wait()
 
     odd = place[0] % 2 == 1
-    parts = []
+    row_fwd = table("row_fwd")
+    above, below = [], []
     for c in range(2):
-        above = jnp.where(odd, near[c, count - rim:], far[c, count - rim:])
-        below = jnp.where(odd, far[c, :rim], near[c, :rim])
-        parts += [above, own[c], below]
-    mask = jnp.concatenate(parts, axis=0)
-    half = over_rows(table("mask_row"), split(mask), grid_rows)
-    m_first, m_rest = to_freqs(beside(half), table("mask_head"), table("mask_tail"))
+        above.append(jnp.where(odd, near[c, count - rim:], far[c, count - rim:]))
+        below.append(jnp.where(odd, far[c, :rim], near[c, :rim]))
+    upper, lower = quarters_of(own[0], own[1], rim)
+    mask, = row_stage([lower, tuple(below), tuple(above), upper], row_fwd, width)
+    m_first, m_rest = to_freqs(mask, table("mask_head"), table("mask_tail"))
     lane = lax.broadcasted_iota(jnp.int32, m_rest.shape, 1)
     real_half = lane < m_rest.shape[1] // 2
     turned = swap(m_rest)
@@ -237,13 +300,16 @@
                     s_rest * m_same + swap(s_rest) * m_cross,
                 ], axis=1)
                 back = over_lanes(split(product), col_inv)
-                planes.append(split(jnp.concatenate([back[:, :width], back[:, width:]], axis=0)))
-            return [jnp.concatenate(part, axis=1) for part in zip(*planes)]
+                planes.append(split(back))
+            return [side_by_side(planes, c, width) for c in range(4)]
 
         def rows_of(p, pair):
-            found, = over_rows(row_inv, pair, 2 * count)
-            field[i * (batch // 2) + p] = found
-            power = found[:count] * found[:count] + found[count:] * found[count:]
+            upper, lower = from_row_freqs(pair, row_inv, (0, 1))
+            re = jnp.concatenate([upper[0], lower[0]], axis=0)
+            im = jnp.concatenate([upper[1], lower[1]], axis=0)
+            field[i * (batch // 2) + p, :count] = re
+            field[i * (batch // 2) + p, count:] = im
+            power = re * re + im * im
             for j in range(2):
                 k = i * batch + 2 * p + j
                 g = group[k]
@@ -262,7 +328,7 @@
     out = pltpu.make_async_copy(resist, resist_far, out_sem)
     out.start()
     fetch_table(2).wait()
-    row_tab, head, tail = table("row_tab"), table("head"), table("tail")
+    head, tail = table("head"), table("tail")
 
     def backward(i, carry):
         def rows_of(p):
@@ -271,8 +337,9 @@
                 k = i * batch + 2 * p + j
                 factors.append((2.0 * weight[k]) * slopes[group[k]])
             factor = jnp.concatenate(factors, axis=1)
-            cot = field[i * (batch // 2) + p] * jnp.concatenate([factor, factor], axis=0)
-            return row_stage(cot, row_tab)
+            re = field[i * (batch // 2) + p, :count] * factor
+            im = field[i * (batch // 2) + p, count:] * factor
+            return row_stage(quarters_of(re, im, rim), row_fwd, width)
 
         def cols_of(p, tiles):
             total = [grad_spec[:, c * width:(c + 1) * width] for c in range(4)]
@@ -296,14 +363,14 @@
     same, cross = grad_spec[:, 2 * width:3 * width], grad_spec[:, 3 * width:]
     tail_sum = jnp.where(real_half, same + swap(same), swap(cross) - cross)
     total = jnp.concatenate([grad_spec[:, :2 * width], tail_sum], axis=1)
-    back = over_lanes(split(total), table("grad_col"))
-    back = split(jnp.concatenate([back[:, :width], back[:, width:]], axis=0))
-    full = over_rows(table("grad_row"), back, grid_rows)
+    back = split(over_lanes(split(total), table("grad_col")))
+    classes = [side_by_side([back], c, width) for c in range(4)]
+    rise, upper, lower, fall = from_row_freqs(classes, row_inv, (2, 3, 0, 1))
     for c in range(2):
-        rise, fall = full[c][:rim], full[c][rim + count:]
-        near_rim[c] = jnp.where(odd, rise, fall)
-        far_rim[c] = jnp.where(odd, fall, rise)
-        grad_own[c] = full[c][rim:rim + count]
+        near_rim[c] = jnp.where(odd, rise[c], fall[c])
+        far_rim[c] = jnp.where(odd, fall[c], rise[c])
+        grad_own[c, :rim] = upper[c]
+        grad_own[c, rim:] = lower[c]
     out.wait()
 
 
@@ -338,7 +405,7 @@
     rim = span // 2
     grid_rows = count + 2 * rim
     grid_cols = width + rim
-    assert count == span and width == span and kernels % BATCH == 0 and BATCH % 2 == 0 and count >= 2 * rim
+    assert count == span and width == span and kernels % BATCH == 0 and BATCH % 2 == 0 and count == 2 * rim
 
     strips = lax.axis_size("row")
     assert strips % 2 == 0
@@ -356,14 +423,14 @@
         table = analysis(grid_cols, width, shift).T[:, order]
         return halves(table[:, :2 * width], 0), halves(table[:, 2 * width:], 1)
 
-    row_tab = halves(analysis(grid_rows, span, 0), 1)
+    quarter = grid_rows // 4
+    by_class = [class_table(grid_rows, quarter, c) for c in range(4)]
+    row_fwd = np.concatenate([halves(t, 0) for t in by_class], axis=1)
+    row_inv = np.concatenate([halves(t.T * scale, 0) for t in by_class], axis=1)
     head, tail = head_and_tail(0)
-    mask_row = halves(analysis(grid_rows, grid_rows, 2 * rim), 1)
     mask_head, mask_tail = head_and_tail(rim)
     col_inv = halves(synthesis(grid_cols, width, 0).T[order], 0)
-    row_inv = halves(synthesis(grid_rows, count, 0, scale), 1)
     grad_col = halves(synthesis(grid_cols, width, rim).T[order], 0)
-    grad_row = halves(synthesis(grid_rows, grid_rows, 2 * rim, scale), 1)
 
     smem = pl.BlockSpec(memory_space=pltpu.SMEM)
     vmem = pl.BlockSpec(memory_space=pltpu.VMEM)
@@ -382,12 +449,12 @@
         compiler_params=pltpu.CompilerParams(vmem_limit_bytes=56 * MIB),
         cost_estimate=pl.CostEstimate(flops=18 * 10**9, bytes_accessed=14 * 10**6, transcendentals=0),
         name="spectra",
-    )(kernel_radii, kernel_taps, *map(jnp.asarray, (row_tab, head, tail)))
+    )(kernel_radii, kernel_taps, *map(jnp.asarray, (row_fwd, head, tail)))
 
     tables, layout, sections = stacked([
-        {"mask_row": mask_row, "mask_head": mask_head, "mask_tail": mask_tail},
+        {"row_fwd": row_fwd, "mask_head": mask_head, "mask_tail": mask_tail},
         {"col_inv": col_inv, "row_inv": row_inv},
-        {"row_tab": row_tab, "head": head, "tail": tail, "grad_col": grad_col, "grad_row": grad_row},
+        {"head": head, "tail": tail, "grad_col": grad_col},
     ])
     resist, own, near_rim, far_rim = pl.pallas_call(
         functools.partial(main_body, layout=layout, sections=sections),

time: 42.3 us -> 39.4 us (0.931)
  Pallas kernels: 30.9 us -> 28 us
    pallas_call x1, Pallas kernels: 19.6 us -> 17.5 us  [on_device(): pl.pallas_call(functools.partial(main_body, layout=layout, sections=secti...]
    pallas_call x1, Pallas kernels: 10.6 us -> 9.81 us  [on_device(): pl.pallas_call(spectra_body, out_shape=jax.ShapeDtypeStruct((kernels, gri...]
where the time goes in v13:
time: 39.4 us; the launch traced here: 39.1 us
  Pallas kernels  28 us (71%)
  starting transfers between devices  7.38 us (19%)
  waiting for transfers between devices  2.95 us (7%)
  between operations  0.76 us (2%)
    pallas_call x1, Pallas kernels, on_device(): pl.pallas_call(functools.partial(main_body, layout=layout, sections=secti...  17.5 us
    pallas_call x1, Pallas kernels, on_device(): pl.pallas_call(spectra_body, out_shape=jax.ShapeDtypeStruct((kernels, gri...  9.81 us
    ppermute x1, starting transfers between devices, on_device(): far_in = lax.ppermute(far_rim, 'row', far_pairs)  3.52 us
    ppermute x1, starting transfers between devices, on_device(): far = lax.ppermute(mask_field, 'row', far_pairs)  3.05 us
    ppermute x1, waiting for transfers between devices, on_device(): far_in = lax.ppermute(far_rim, 'row', far_pairs)  2.95 us
  transfers between devices with their start and end apart: 4, of which 1 were waited for; matrix products, arithmetic and copies ran while one was open for 0% of the time, Pallas kernels for 25%

profile of v13, /device:TPU:21, one launch (start us, length us, event | category | flops | bytes accessed | tf_op | source)
XLA Modules:
  0.0 39.1 jit_solution(13701179313100331686)
XLA Ops:
  0.6 0.0 copy-start
  0.6 0.0 copy-start.3
  0.7 0.0 copy-start.2
  0.7 0.0 copy-start.1
  0.7 0.7 %collective-permute-start = (f32[2,128,128]{2,1,0:T(8,128)}, f32[2,128,128]{2,1,0:T(8,128)S(1)}, u32[]{:S(2)}, u32[]{:S(2)}) collective-permute-start(f32[2,128,128]{2,1,0:T(8,128)} %own.1), channel_id=1, source_target_pairs={{0,1},{1,0},{2,3},{3,2},{4,5},{5,4},{6,7},{7,6},{8,9},{9,8},{10,11... | collective-permute-start | bytes 393224 | tf_op jit(solution)/shard_map/ppermute | solution.py:415
  1.4 3.0 %collective-permute-start.1 = (f32[2,128,128]{2,1,0:T(8,128)}, f32[2,128,128]{2,1,0:T(8,128)S(1)}, u32[]{:S(2)}, u32[]{:S(2)}) collective-permute-start(f32[2,128,128]{2,1,0:T(8,128)} %own.1), channel_id=1, source_target_pairs={{1,2},{2,1},{3,4},{4,3},{5,6},{6,5},{7,8},{8,7},{9,10},{10,9},{11,... | collective-permute-start | bytes 393224 | tf_op jit(solution)/shard_map/ppermute | solution.py:416
  4.5 9.8 %spectra.1.spec_far = f32[24,256,384]{2,1,0:T(8,128)} custom-call(s32[24]{0:T(128)} %radii.1, f32[24,2,128,128]{3,2,1,0:T(8,128)} %taps_far.1, bf16[256,512]{1,0:T(8,128)(2,1)} %constant.12.clone.row_ref, bf16[512,256]{1,0:T(8,128)(2,1)} %constant.13.clone.head_ref, bf16[256,256]{1,0:T(8,128)(2,1)} %constant.14.clone.tail_ref), custom_call_target="tpu_custom_call" | custom-call | flops 17999998976 | bytes 14000000 | tf_op jit(solution)/shard_map/spectra/pallas_call | solution.py:438
  14.3 0.0 collective-permute-done.near
  14.3 0.0 collective-permute-done.1.far
  14.3 0.0 copy-done
  14.3 0.0 copy-done.3
  14.3 0.0 copy-done.2
  14.3 0.0 copy-done.1
  14.4 17.5 %fields.1 = (f32[3,128,128]{2,1,0:T(8,128)}, f32[2,128,128]{2,1,0:T(8,128)S(1)}, f32[2,64,128]{2,1,0:T(8,128)S(1)}, f32[2,64,128]{2,1,0:T(8,128)S(1)}) custom-call(s32[24]{0:T(128)S(1)} %copy-done.2, f32[24]{0:T(128)S(1)} %copy-done.3, s32[1]{0:T(128)} %bitcast.place, f32[2,128,128]{2,1,0:T(8,128)S(1)} %copy-done, ...), custom_call_target="tpu_custom_call" | custom-call | tf_op jit(solution)/shard_map/fields/pallas_call | solution.py:459
  31.8 0.1 collective-permute-start.2
  31.9 3.5 %collective-permute-start.3 = (f32[2,64,128]{2,1,0:T(8,128)S(1)}, f32[2,64,128]{2,1,0:T(8,128)S(1)}, u32[]{:S(2)}, u32[]{:S(2)}) collective-permute-start(f32[2,64,128]{2,1,0:T(8,128)S(1)} %get-tuple-element.9), channel_id=1, source_target_pairs={{1,2},{2,1},{3,4},{4,3},{5,6},{6,5},{7,8},{8,7},{9,10},{10,9},{11,... | collective-permute-start | bytes 196616 | tf_op jit(solution)/shard_map/ppermute | solution.py:486
  35.4 0.0 collective-permute-done.2.near
  35.4 2.9 %collective-permute-done.3.far = f32[2,64,128]{2,1,0:T(8,128)S(1)} collective-permute-done((f32[2,64,128]{2,1,0:T(8,128)S(1)}, f32[2,64,128]{2,1,0:T(8,128)S(1)}, u32[]{:S(2)}, u32[]{:S(2)}) %collective-permute-start.3) | collective-permute-done | bytes 65568 | tf_op jit(solution)/shard_map/ppermute | solution.py:486
  38.4 0.7 %join.1 = f32[2,128,128]{2,1,0:T(8,128)} custom-call(s32[1]{0:T(128)} %bitcast.place, f32[2,128,128]{2,1,0:T(8,128)S(1)} %get-tuple-element.7.own, f32[2,64,128]{2,1,0:T(8,128)S(1)} %collective-permute-done.2.near, f32[2,64,128]{2,1,0:T(8,128)S(1)} %collective-permute-done.3.far), custom_call_target="tpu_custom_call" | custom-call | tf_op jit(solution)/shard_map/join/pallas_call | solution.py:487
Async XLA Ops:
  0.6 13.7 %copy-start = (f32[2,128,128]{2,1,0:T(8,128)S(1)}, f32[2,128,128]{2,1,0:T(8,128)}, u32[]{:S(2)}) copy-start(f32[2,128,128]{2,1,0:T(8,128)} %own.1) | copy-start | bytes 393220
  0.6 13.7 %copy-start.3 = (f32[24]{0:T(128)S(1)}, f32[24]{0:T(128)}, u32[]{:S(2)}) copy-start(f32[24]{0:T(128)} %weight.1) | copy-start | bytes 292
  0.7 13.7 %copy-start.2 = (s32[24]{0:T(128)S(1)}, s32[24]{0:T(128)}, u32[]{:S(2)}) copy-start(s32[24]{0:T(128)} %group.1) | copy-start | bytes 292
  0.7 13.7 %copy-start.1 = (s32[128,128]{1,0:T(8,128)S(1)}, s32[128,128]{1,0:T(8,128)}, u32[]{:S(2)}) copy-start(s32[128,128]{1,0:T(8,128)} %target.1) | copy-start | bytes 196612
  0.7 13.6 %collective-permute-start = (f32[2,128,128]{2,1,0:T(8,128)}, f32[2,128,128]{2,1,0:T(8,128)S(1)}, u32[]{:S(2)}, u32[]{:S(2)}) collective-permute-start(f32[2,128,128]{2,1,0:T(8,128)} %own.1), channel_id=1, source_target_pairs={{0,1},{1,0},{2,3},{3,2},{4,5},{5,4},{6,7},{7,6},{8,9},{9,8},{10,11... | collective-permute-start | bytes 393224 | tf_op jit(solution)/shard_map/ppermute | solution.py:415
  1.4 12.9 %collective-permute-start.1 = (f32[2,128,128]{2,1,0:T(8,128)}, f32[2,128,128]{2,1,0:T(8,128)S(1)}, u32[]{:S(2)}, u32[]{:S(2)}) collective-permute-start(f32[2,128,128]{2,1,0:T(8,128)} %own.1), channel_id=1, source_target_pairs={{1,2},{2,1},{3,4},{4,3},{5,6},{6,5},{7,8},{8,7},{9,10},{10,9},{11,... | collective-permute-start | bytes 393224 | tf_op jit(solution)/shard_map/ppermute | solution.py:416
  31.8 3.6 %collective-permute-start.2 = (f32[2,64,128]{2,1,0:T(8,128)S(1)}, f32[2,64,128]{2,1,0:T(8,128)S(1)}, u32[]{:S(2)}, u32[]{:S(2)}) collective-permute-start(f32[2,64,128]{2,1,0:T(8,128)S(1)} %get-tuple-element.8), channel_id=1, source_target_pairs={{0,1},{1,0},{2,3},{3,2},{4,5},{5,4},{6,7},{7,6},{8,9},{9,8},{10,11... | collective-permute-start | bytes 196616 | tf_op jit(solution)/shard_map/ppermute | solution.py:485
  31.9 6.5 %collective-permute-start.3 = (f32[2,64,128]{2,1,0:T(8,128)S(1)}, f32[2,64,128]{2,1,0:T(8,128)S(1)}, u32[]{:S(2)}, u32[]{:S(2)}) collective-permute-start(f32[2,64,128]{2,1,0:T(8,128)S(1)} %get-tuple-element.9), channel_id=1, source_target_pairs={{1,2},{2,1},{3,4},{4,3},{5,6},{6,5},{7,8},{8,7},{9,10},{10,9},{11,... | collective-permute-start | bytes 196616 | tf_op jit(solution)/shard_map/ppermute | solution.py:486

commit v14 on v8

v14 whole, which is shorter than its diff:
```python
import functools
import math

import jax
import jax.numpy as jnp
import ml_dtypes
import numpy as np
from jax import lax
from jax.experimental import pallas as pl
from jax.experimental.pallas import tpu as pltpu
from jax.sharding import PartitionSpec as P

RMAX = 64
GROUPS = 3
STEEPNESS = 1.0
THRESHOLD = 2.0
UNIT = 4
UNITS = 2
PIECE = 256
TURN = math.sqrt(0.75)

f32 = jnp.float32
bf16 = jnp.bfloat16
MIB = 1024 * 1024
LIMIT = 53


def halves(table, axis):
    high = table.astype(ml_dtypes.bfloat16)
    low = (table - high.astype(np.float64)).astype(ml_dtypes.bfloat16)
    return np.concatenate([high, low], axis=axis)


def class_table(freqs, points, c, classes):
    f = np.arange(c, freqs, classes)[:, None]
    n = np.arange(points)[None, :]
    angle = 2.0 * math.pi * ((f * n) % freqs) / freqs
    cos, sin = np.cos(angle), np.sin(angle)
    return np.block([[cos, sin], [-sin, cos]])


def split(x):
    high = x.astype(bf16)
    low = (x - high.astype(f32)).astype(bf16)
    return high, low


def dot(left, right):
    parts = [
        jnp.dot(left[at:at + PIECE], right, preferred_element_type=f32)
        for at in range(0, left.shape[0], PIECE)
    ]
    return jnp.concatenate(parts, axis=0)


def swap(x):
    return pltpu.roll(x, x.shape[1] // 2, 1)


def first_half(x):
    return lax.broadcasted_iota(jnp.int32, x.shape, 1) < x.shape[1] // 2


def exchange(x, y):
    first = first_half(x)
    return jnp.where(first, x, swap(y)), jnp.where(first, swap(x), y)


def turned(x, sign):
    re, im = x
    return (-im, re) if sign > 0 else (im, -re)


def plus(x, y):
    return x[0] + y[0], x[1] + y[1]


def minus(x, y):
    return x[0] - y[0], x[1] - y[1]


def row_product(table, c, x):
    parts = split(x)
    depth = x.shape[0]
    left = table[:, c * depth:(c + 1) * depth]
    found = dot(jnp.concatenate([left, left], axis=1), jnp.concatenate(parts, axis=0))
    half = found.shape[0] // 2
    found = found[:half] + found[half:]
    return found[:half // 2], found[half // 2:]


def to_row_freqs(x, table):
    if len(x) == 2:
        even, odd, even_less, odd_less = x[0], x[1], x[0], x[1]
    else:
        even, odd = plus(x[0], x[2]), plus(x[1], x[3])
        even_less, odd_less = minus(x[0], x[2]), minus(x[1], x[3])
    folded = [
        plus(even, odd),
        plus(even_less, turned(odd_less, -1)),
        minus(even, odd),
        plus(even_less, turned(odd_less, 1)),
    ]
    return [row_product(table, c, jnp.concatenate(y, axis=0)) for c, y in enumerate(folded)]


def from_row_freqs(classes, table, quarters):
    v = [row_product(table, c, jnp.concatenate(y, axis=0)) for c, y in enumerate(classes)]
    out = []
    for q in quarters:
        if q % 2 == 0:
            even, odd = plus(v[0], v[2]), plus(v[1], v[3])
        else:
            even, odd = minus(v[0], v[2]), turned(minus(v[1], v[3]), 1)
        out.append(plus(even, odd) if q < 2 else minus(even, odd))
    return out


def quarters_of(re, im, quarter):
    return [(re[at:at + quarter], im[at:at + quarter]) for at in range(0, re.shape[0], quarter)]


def lane_turned(x):
    return swap(x) * jnp.where(first_half(x), TURN, -TURN)


def col_products(planes, table):
    rows = planes[0][0].shape[0]
    depth = table.shape[0] // 3
    out = [[] for _ in planes]
    for c in range(3):
        high, low = split(jnp.concatenate([plane[c] for plane in planes], axis=0))
        right = table[c * depth:(c + 1) * depth]
        found = dot(jnp.concatenate([high, low], axis=1), jnp.concatenate([right, right], axis=0))
        found = found[:, :depth] + found[:, depth:]
        for k in range(len(planes)):
            out[k].append(found[k * rows:(k + 1) * rows])
    return out


def to_col_freqs(planes, table, shifted=False):
    folded = []
    for left, right in planes:
        if shifted:
            left, right = right, left
        near, far = left - 0.5 * right, lane_turned(right)
        one, two = near + far, near - far
        folded.append([left + right, two, one] if shifted else [left + right, one, two])
    return col_products(folded, table)


def from_col_freqs(planes, table, shifted=False):
    out = []
    for v in col_products(planes, table):
        total, far = v[1] + v[2], lane_turned(v[1] - v[2])
        whole, part = v[0] + total, v[0] - 0.5 * total
        out.append((part + far, whole) if shifted else (whole, part - far))
    return out


def pairs_apart(planes):
    re, im = [], []
    for k in range(0, len(planes), 2):
        for x, y in zip(planes[k], planes[k + 1]):
            r, i = exchange(x, y)
            re.append(r)
            im.append(i)
    return jnp.concatenate(re, axis=1), jnp.concatenate(im, axis=1)


def pairs_together(re, im, width):
    planes = []
    for at in range(0, re.shape[1], 3 * width):
        both = [
            exchange(re[:, at + c * width:at + (c + 1) * width], im[:, at + c * width:at + (c + 1) * width])
            for c in range(3)
        ]
        planes += [[x for x, _ in both], [y for _, y in both]]
    return planes


def staggered(count, first, second):
    held = None
    for i in range(count):
        new = first(i)
        if i:
            second(i - 1, held)
        held = new
    second(count - 1, held)


def spectra_body(radii, taps_far, row_ref, col_ref, spec_far, taps, spec, in_sems, out_sems):
    kernels, _, span, _ = taps.shape
    row_fwd, col_fwd = row_ref[...], col_ref[...]
    quarter = span // 2
    steps = kernels // (UNIT * UNITS)

    def fetch(u):
        here = pl.ds(u * UNIT, UNIT)
        return pltpu.make_async_copy(taps_far.at[here], taps.at[here], in_sems.at[u])

    def put(u):
        return pltpu.make_async_copy(spec.at[u], spec_far.at[u], out_sems.at[u])

    for u in range(kernels // UNIT):
        fetch(u).start()
    row_at = lax.broadcasted_iota(jnp.int32, (span, span), 0) - span // 2
    col_at = lax.broadcasted_iota(jnp.int32, (span, span), 1) - span // 2
    reach = jnp.maximum(jnp.maximum(row_at, -1 - row_at), jnp.maximum(col_at, -1 - col_at))

    def step(i, carry):
        def cols_of(p):
            u = i * UNITS + p
            fetch(u).wait()
            planes = []
            for j in range(UNIT):
                k = u * UNIT + j
                inside = reach < radii[k]
                planes.append(exchange(*[jnp.where(inside, taps[k, c], 0.0) for c in range(2)]))
            return pairs_apart(to_col_freqs(planes, col_fwd))

        def rows_of(p, both):
            u = i * UNITS + p
            for c, found in enumerate(to_row_freqs(quarters_of(*both, quarter), row_fwd)):
                for part in range(2):
                    spec[u, part, c * quarter:(c + 1) * quarter] = found[part]
            put(u).start()

        staggered(UNITS, cols_of, rows_of)
        return carry

    lax.fori_loop(0, steps, step, 0)
    for u in range(kernels // UNIT):
        put(u).wait()


def main_body(
    group, weight, place,
    own, near, far, target, spec_far, tables_far,
    resist_far, grad_own, near_rim, far_rim,
    spec, field, mask_spec, resist, slopes, grad_spec, tables, spec_sems, table_sem, out_sem,
    *, layout,
):
    count, width = target.shape
    rim = count // 2
    units = spec.shape[0]
    steps = units // UNITS

    def fetch(u):
        return pltpu.make_async_copy(spec_far.at[u], spec.at[u], spec_sems.at[u])

    def table(name):
        start, rows, blocks = layout[name]
        parts = [tables[start + b * rows:start + (b + 1) * rows] for b in range(blocks)]
        return jnp.concatenate(parts, axis=1)

    fetch_tables = pltpu.make_async_copy(tables_far, tables, table_sem)
    fetch_tables.start()
    for u in range(units):
        fetch(u).start()
    slopes[...] = jnp.zeros(slopes.shape, f32)
    grad_spec[...] = jnp.zeros(grad_spec.shape, f32)
    fetch_tables.wait()
    row_fwd, row_inv, col_fwd, col_inv = [table(name) for name in ("row_fwd", "row_inv", "col_fwd", "col_inv")]

    odd = place[0] % 2 == 1
    mask = []
    for c in range(2):
        above = jnp.where(odd, near[c, count - rim:], far[c, count - rim:])
        below = jnp.where(odd, far[c, :rim], near[c, :rim])
        mask.append(jnp.concatenate([own[c, rim:], below, above, own[c, :rim]], axis=0))
    plane, = to_col_freqs([exchange(*mask)], col_fwd, shifted=True)
    both = pairs_apart([plane, plane])
    for c, found in enumerate(to_row_freqs(quarters_of(*both, rim), row_fwd)):
        for part in range(2):
            mask_spec[part, c * rim:(c + 1) * rim] = found[part]

    def forward(i, carry):
        def rows_of(p):
            u = i * UNITS + p
            fetch(u).wait()
            classes = []
            for c in range(4):
                here = slice(c * rim, (c + 1) * rim)
                m_re, m_im = [jnp.concatenate([mask_spec[part, here]] * (UNIT // 2), axis=1) for part in range(2)]
                s_re, s_im = spec[u, 0, here], spec[u, 1, here]
                classes.append((s_re * m_re - s_im * m_im, s_re * m_im + s_im * m_re))
            upper, lower = from_row_freqs(classes, row_inv, (0, 1))
            return [jnp.concatenate([upper[part], lower[part]], axis=0) for part in range(2)]

        def cols_of(p, both):
            u = i * UNITS + p
            found = from_col_freqs(pairs_together(*both, width), col_inv)
            for j in range(UNIT):
                k = u * UNIT + j
                for side in range(2):
                    x = found[j][side]
                    field[k, side] = x
                    slopes[group[k], side] = slopes[group[k], side] + weight[k] * (x * x)

        staggered(UNITS, rows_of, cols_of)
        return carry

    lax.fori_loop(0, steps, forward, 0)

    wanted = target[...].astype(f32)
    for g in range(GROUPS):
        left, right = [slopes[g, side] + swap(slopes[g, side]) for side in range(2)]
        seen = jax.nn.sigmoid(STEEPNESS * (jnp.where(first_half(left), left, right) - THRESHOLD))
        resist[g] = seen
        slope = 2.0 * (seen - wanted) * seen * (1.0 - seen) * STEEPNESS
        slopes[g, 0], slopes[g, 1] = exchange(slope, slope)
    out = pltpu.make_async_copy(resist, resist_far, out_sem)
    out.start()

    def backward(i, carry):
        def cols_of(p):
            u = i * UNITS + p
            planes = []
            for j in range(UNIT):
                k = u * UNIT + j
                planes.append([field[k, side] * ((2.0 * weight[k]) * slopes[group[k], side]) for side in range(2)])
            return pairs_apart(to_col_freqs(planes, col_fwd))

        def rows_of(p, both):
            u = i * UNITS + p
            for c, (c_re, c_im) in enumerate(to_row_freqs(quarters_of(*both, rim), row_fwd)):
                here = slice(c * rim, (c + 1) * rim)
                s_re, s_im = spec[u, 0, here], spec[u, 1, here]
                terms = s_re * c_re + s_im * c_im, s_re * c_im - s_im * c_re
                for part in range(2):
                    total = grad_spec[part, here]
                    lanes = total.shape[1]
                    for at in range(0, terms[part].shape[1], lanes):
                        total = total + terms[part][:, at:at + lanes]
                    grad_spec[part, here] = total

        staggered(UNITS, cols_of, rows_of)
        return carry

    lax.fori_loop(0, steps, backward, 0)

    classes = [tuple(grad_spec[part, c * rim:(c + 1) * rim] for part in range(2)) for c in range(4)]
    quarters = from_row_freqs(classes, row_inv, (2, 3, 0, 1))
    re, im = [jnp.concatenate([x[part] for x in quarters], axis=0) for part in range(2)]
    first, second = pairs_together(re, im, width)
    plane = [x + y for x, y in zip(first, second)]
    halves_found, = from_col_freqs([plane], col_inv, shifted=True)
    for c, full in enumerate(exchange(*halves_found)):
        rise, fall = full[:rim], full[rim + count:]
        near_rim[c] = jnp.where(odd, rise, fall)
        far_rim[c] = jnp.where(odd, fall, rise)
        grad_own[c] = full[rim:rim + count]
    out.wait()


def join_body(place, own, near, far, out):
    odd = place[0] % 2 == 1
    rim = near.shape[1]
    for c in range(2):
        out[c, :rim] = own[c, :rim] + jnp.where(odd, near[c], far[c])
        out[c, rim:] = own[c, rim:] + jnp.where(odd, far[c], near[c])


def stacked(tables):
    blocks, layout, at = [], {}, 0
    for name, table in tables.items():
        rows, lanes = table.shape
        layout[name] = (at, rows, lanes // 256)
        for b in range(lanes // 256):
            blocks.append(table[:, b * 256:(b + 1) * 256])
        at += rows * (lanes // 256)
    return np.concatenate(blocks, axis=0), layout


def on_device(mask_field, target, kernel_taps, kernel_radii, kernel_group, kernel_weight):
    _, count, width = mask_field.shape
    kernels, _, span, _ = kernel_taps.shape
    rim = span // 2
    grid_rows = count + 2 * rim
    grid_cols = width + rim
    units = kernels // UNIT
    assert count == span and width == span and kernels % (UNIT * UNITS) == 0 and span == 128

    strips = lax.axis_size("row")
    assert strips % 2 == 0
    at = lax.axis_index("row")
    near_pairs = [(i, i ^ 1) for i in range(strips)]
    far_pairs = [(i, ((i + 1) ^ 1) - 1) for i in range(1, strips - 1)]
    near = lax.ppermute(mask_field, "row", near_pairs)
    far = lax.ppermute(mask_field, "row", far_pairs)
    place = at.astype(jnp.int32).reshape(1)

    scale = 1.0 / (grid_rows * grid_cols)
    row_classes = [class_table(grid_rows, rim, c, 4) for c in range(4)]
    col_classes = [class_table(grid_cols, rim, c, 3) for c in range(3)]
    row_fwd = np.concatenate([halves(t, 0) for t in row_classes], axis=1)
    row_inv = np.concatenate([halves(t.T * scale, 0) for t in row_classes], axis=1)
    col_fwd = np.concatenate([halves(t.T, 1) for t in col_classes], axis=0)
    col_inv = np.concatenate([halves(t, 1) for t in col_classes], axis=0)
    tables, layout = stacked({"row_fwd": row_fwd, "row_inv": row_inv, "col_fwd": col_fwd, "col_inv": col_inv})

    smem = pl.BlockSpec(memory_space=pltpu.SMEM)
    vmem = pl.BlockSpec(memory_space=pltpu.VMEM)
    hbm = pl.BlockSpec(memory_space=pltpu.HBM)
    spec_shape = (units, 2, grid_rows, UNIT * grid_cols)
    spectra = pl.pallas_call(
        spectra_body,
        out_shape=jax.ShapeDtypeStruct(spec_shape, f32),
        in_specs=[smem, hbm, vmem, vmem],
        out_specs=hbm,
        scratch_shapes=[
            pltpu.VMEM(kernel_taps.shape, f32),
            pltpu.VMEM(spec_shape, f32),
            pltpu.SemaphoreType.DMA((units,)),
            pltpu.SemaphoreType.DMA((units,)),
        ],
        compiler_params=pltpu.CompilerParams(vmem_limit_bytes=56 * MIB),
        cost_estimate=pl.CostEstimate(flops=18 * 10**9, bytes_accessed=14 * 10**6, transcendentals=0),
        name="spectra",
    )(kernel_radii, kernel_taps, *map(jnp.asarray, (row_fwd, col_fwd)))

    resist, own, near_rim, far_rim = pl.pallas_call(
        functools.partial(main_body, layout=layout),
        out_shape=[
            jax.ShapeDtypeStruct((GROUPS, count, width), f32),
            jax.ShapeDtypeStruct((2, count, width), f32),
            jax.ShapeDtypeStruct((2, rim, width), f32),
            jax.ShapeDtypeStruct((2, rim, width), f32),
        ],
        in_specs=[smem] * 3 + [vmem] * 4 + [hbm] * 2,
        out_specs=[hbm] + [vmem] * 3,
        scratch_shapes=[
            pltpu.VMEM(spec_shape, f32),
            pltpu.VMEM((kernels, 2, count, width), f32),
            pltpu.VMEM((2, grid_rows, 2 * grid_cols), f32),
            pltpu.VMEM((GROUPS, count, width), f32),
            pltpu.VMEM((GROUPS, 2, count, width), f32),
            pltpu.VMEM((2, grid_rows, 2 * grid_cols), f32),
            pltpu.VMEM(tables.shape, bf16),
            pltpu.SemaphoreType.DMA((units,)),
            pltpu.SemaphoreType.DMA,
            pltpu.SemaphoreType.DMA,
        ],
        compiler_params=pltpu.CompilerParams(vmem_limit_bytes=LIMIT * MIB),
        name="fields",
    )(kernel_group, kernel_weight, place, mask_field, near, far, target, spectra, jnp.asarray(tables))

    near_in = lax.ppermute(near_rim, "row", near_pairs)
    far_in = lax.ppermute(far_rim, "row", far_pairs)
    gradient = pl.pallas_call(
        join_body,
        out_shape=jax.ShapeDtypeStruct((2, count, width), f32),
        in_specs=[smem] + [vmem] * 3,
        out_specs=vmem,
        compiler_params=pltpu.CompilerParams(vmem_limit_bytes=4 * MIB),
        name="join",
    )(place, own, near_in, far_in)
    return resist, gradient


def solution(mesh):
    in_specs = (P(None, ("win", "row"), None), P(("win", "row"), None), P(), P(), P(), P())
    out_specs = (P(None, ("win", "row"), None), P(None, ("win", "row"), None))
    return jax.shard_map(
        on_device, mesh=mesh, in_specs=in_specs, out_specs=out_specs, check_vma=False
    )
```

time: 44.4 us -> 40 us (0.901)
  local copies, waits for them, and re-layouts: 2.35 us -> 0.02 us
  Pallas kernels: 30.7 us -> 28.6 us
    unnamed x10 -> x8, local copies, waits for them, and re-layouts: 2.35 us -> 0.02 us
    pallas_call x2, Pallas kernels: 30 us -> 27.9 us  [the longest x1 18.4 us: on_device(): pl.pallas_call(functools.partial(main_body, layout=layout), out_shape=[ja...]
where the time goes in v14:
time: 40 us; the launch traced here: 39.7 us
  Pallas kernels  28.6 us (72%)
  starting transfers between devices  7.38 us (18%)
  waiting for transfers between devices  2.95 us (7%)
  between operations  0.76 us (2%)
    pallas_call x1, Pallas kernels, on_device(): pl.pallas_call(functools.partial(main_body, layout=layout), out_shape=[ja...  18.4 us
    pallas_call x1, Pallas kernels, on_device(): pl.pallas_call(spectra_body, out_shape=jax.ShapeDtypeStruct(spec_shape, f...  9.53 us
    ppermute x1, starting transfers between devices, on_device(): far_in = lax.ppermute(far_rim, 'row', far_pairs)  3.52 us
    ppermute x1, starting transfers between devices, on_device(): far = lax.ppermute(mask_field, 'row', far_pairs)  3.05 us
    ppermute x1, waiting for transfers between devices, on_device(): far_in = lax.ppermute(far_rim, 'row', far_pairs)  2.95 us
  transfers between devices with their start and end apart: 4, of which 1 were waited for; matrix products, arithmetic and copies ran while one was open for 0% of the time, Pallas kernels for 24%

profile of v14, /device:TPU:21, one launch (start us, length us, event | category | flops | bytes accessed | tf_op | source)
XLA Modules:
  0.0 39.7 jit_solution(7886601308676416437)
XLA Ops:
  0.6 0.0 copy-start
  0.6 0.0 copy-start.3
  0.7 0.0 copy-start.2
  0.7 0.0 copy-start.1
  0.7 0.7 %collective-permute-start = (f32[2,128,128]{2,1,0:T(8,128)}, f32[2,128,128]{2,1,0:T(8,128)S(1)}, u32[]{:S(2)}, u32[]{:S(2)}) collective-permute-start(f32[2,128,128]{2,1,0:T(8,128)} %own.1), channel_id=1, source_target_pairs={{0,1},{1,0},{2,3},{3,2},{4,5},{5,4},{6,7},{7,6},{8,9},{9,8},{10,11... | collective-permute-start | bytes 393224 | tf_op jit(solution)/shard_map/ppermute | solution.py:390
  1.4 3.0 %collective-permute-start.1 = (f32[2,128,128]{2,1,0:T(8,128)}, f32[2,128,128]{2,1,0:T(8,128)S(1)}, u32[]{:S(2)}, u32[]{:S(2)}) collective-permute-start(f32[2,128,128]{2,1,0:T(8,128)} %own.1), channel_id=1, source_target_pairs={{1,2},{2,1},{3,4},{4,3},{5,6},{6,5},{7,8},{8,7},{9,10},{10,9},{11,... | collective-permute-start | bytes 393224 | tf_op jit(solution)/shard_map/ppermute | solution.py:391
  4.5 9.5 %spectra.1.spec_far = f32[6,2,256,768]{3,2,1,0:T(8,128)} custom-call(s32[24]{0:T(128)} %radii.1, f32[24,2,128,128]{3,2,1,0:T(8,128)} %taps_far.1, bf16[256,512]{1,0:T(8,128)(2,1)} %constant.10.clone.row_ref, bf16[384,256]{1,0:T(8,128)(2,1)} %constant.11.clone.col_ref), custom_call_target="tpu_custom_call" | custom-call | flops 17999998976 | bytes 14000000 | tf_op jit(solution)/shard_map/spectra/pallas_call | solution.py:407
  14.0 0.0 collective-permute-done.near
  14.0 0.0 collective-permute-done.1.far
  14.0 0.0 copy-done
  14.0 0.0 copy-done.3
  14.1 0.0 copy-done.2
  14.1 0.0 copy-done.1
  14.1 18.4 %fields.1 = (f32[3,128,128]{2,1,0:T(8,128)}, f32[2,128,128]{2,1,0:T(8,128)S(1)}, f32[2,64,128]{2,1,0:T(8,128)S(1)}, f32[2,64,128]{2,1,0:T(8,128)S(1)}) custom-call(s32[24]{0:T(128)S(1)} %copy-done.2, f32[24]{0:T(128)S(1)} %copy-done.3, s32[1]{0:T(128)} %bitcast.place, f32[2,128,128]{2,1,0:T(8,128)S(1)} %copy-done, ...), custom_call_target="tpu_custom_call" | custom-call | tf_op jit(solution)/shard_map/fields/pallas_call | solution.py:423
  32.4 0.1 collective-permute-start.2
  32.5 3.5 %collective-permute-start.3 = (f32[2,64,128]{2,1,0:T(8,128)S(1)}, f32[2,64,128]{2,1,0:T(8,128)S(1)}, u32[]{:S(2)}, u32[]{:S(2)}) collective-permute-start(f32[2,64,128]{2,1,0:T(8,128)S(1)} %get-tuple-element.9), channel_id=1, source_target_pairs={{1,2},{2,1},{3,4},{4,3},{5,6},{6,5},{7,8},{8,7},{9,10},{10,9},{11,... | collective-permute-start | bytes 196616 | tf_op jit(solution)/shard_map/ppermute | solution.py:450
  36.0 0.0 collective-permute-done.2.near
  36.1 2.9 %collective-permute-done.3.far = f32[2,64,128]{2,1,0:T(8,128)S(1)} collective-permute-done((f32[2,64,128]{2,1,0:T(8,128)S(1)}, f32[2,64,128]{2,1,0:T(8,128)S(1)}, u32[]{:S(2)}, u32[]{:S(2)}) %collective-permute-start.3) | collective-permute-done | bytes 65568 | tf_op jit(solution)/shard_map/ppermute | solution.py:450
  39.0 0.7 %join.1 = f32[2,128,128]{2,1,0:T(8,128)} custom-call(s32[1]{0:T(128)} %bitcast.place, f32[2,128,128]{2,1,0:T(8,128)S(1)} %get-tuple-element.7.own, f32[2,64,128]{2,1,0:T(8,128)S(1)} %collective-permute-done.2.near, f32[2,64,128]{2,1,0:T(8,128)S(1)} %collective-permute-done.3.far), custom_call_target="tpu_custom_call" | custom-call | tf_op jit(solution)/shard_map/join/pallas_call | solution.py:451
Async XLA Ops:
  0.6 13.4 %copy-start = (f32[2,128,128]{2,1,0:T(8,128)S(1)}, f32[2,128,128]{2,1,0:T(8,128)}, u32[]{:S(2)}) copy-start(f32[2,128,128]{2,1,0:T(8,128)} %own.1) | copy-start | bytes 393220
  0.6 13.4 %copy-start.3 = (f32[24]{0:T(128)S(1)}, f32[24]{0:T(128)}, u32[]{:S(2)}) copy-start(f32[24]{0:T(128)} %weight.1) | copy-start | bytes 292
  0.7 13.4 %copy-start.2 = (s32[24]{0:T(128)S(1)}, s32[24]{0:T(128)}, u32[]{:S(2)}) copy-start(s32[24]{0:T(128)} %group.1) | copy-start | bytes 292
  0.7 13.4 %copy-start.1 = (s32[128,128]{1,0:T(8,128)S(1)}, s32[128,128]{1,0:T(8,128)}, u32[]{:S(2)}) copy-start(s32[128,128]{1,0:T(8,128)} %target.1) | copy-start | bytes 196612
  0.7 13.3 %collective-permute-start = (f32[2,128,128]{2,1,0:T(8,128)}, f32[2,128,128]{2,1,0:T(8,128)S(1)}, u32[]{:S(2)}, u32[]{:S(2)}) collective-permute-start(f32[2,128,128]{2,1,0:T(8,128)} %own.1), channel_id=1, source_target_pairs={{0,1},{1,0},{2,3},{3,2},{4,5},{5,4},{6,7},{7,6},{8,9},{9,8},{10,11... | collective-permute-start | bytes 393224 | tf_op jit(solution)/shard_map/ppermute | solution.py:390
  1.4 12.6 %collective-permute-start.1 = (f32[2,128,128]{2,1,0:T(8,128)}, f32[2,128,128]{2,1,0:T(8,128)S(1)}, u32[]{:S(2)}, u32[]{:S(2)}) collective-permute-start(f32[2,128,128]{2,1,0:T(8,128)} %own.1), channel_id=1, source_target_pairs={{1,2},{2,1},{3,4},{4,3},{5,6},{6,5},{7,8},{8,7},{9,10},{10,9},{11,... | collective-permute-start | bytes 393224 | tf_op jit(solution)/shard_map/ppermute | solution.py:391
  32.4 3.6 %collective-permute-start.2 = (f32[2,64,128]{2,1,0:T(8,128)S(1)}, f32[2,64,128]{2,1,0:T(8,128)S(1)}, u32[]{:S(2)}, u32[]{:S(2)}) collective-permute-start(f32[2,64,128]{2,1,0:T(8,128)S(1)} %get-tuple-element.8), channel_id=1, source_target_pairs={{0,1},{1,0},{2,3},{3,2},{4,5},{5,4},{6,7},{7,6},{8,9},{9,8},{10,11... | collective-permute-start | bytes 196616 | tf_op jit(solution)/shard_map/ppermute | solution.py:449
  32.5 6.5 %collective-permute-start.3 = (f32[2,64,128]{2,1,0:T(8,128)S(1)}, f32[2,64,128]{2,1,0:T(8,128)S(1)}, u32[]{:S(2)}, u32[]{:S(2)}) collective-permute-start(f32[2,64,128]{2,1,0:T(8,128)S(1)} %get-tuple-element.9), channel_id=1, source_target_pairs={{1,2},{2,1},{3,4},{4,3},{5,6},{6,5},{7,8},{8,7},{9,10},{10,9},{11,... | collective-permute-start | bytes 196616 | tf_op jit(solution)/shard_map/ppermute | solution.py:450

commit v15 on v14

--- a/solution.py
+++ b/solution.py
@@ -15,7 +15,8 @@
 STEEPNESS = 1.0
 THRESHOLD = 2.0
 UNIT = 4
-UNITS = 2
+SPECTRA_UNITS = 6
+UNITS = 3
 PIECE = 256
 TURN = math.sqrt(0.75)
 
@@ -179,6 +180,13 @@
     return planes
 
 
+def loop(steps, body):
+    if steps == 1:
+        body(0, 0)
+    else:
+        lax.fori_loop(0, steps, body, 0)
+
+
 def staggered(count, first, second):
     held = None
     for i in range(count):
@@ -193,7 +201,7 @@
     kernels, _, span, _ = taps.shape
     row_fwd, col_fwd = row_ref[...], col_ref[...]
     quarter = span // 2
-    steps = kernels // (UNIT * UNITS)
+    steps = kernels // (UNIT * SPECTRA_UNITS)
 
     def fetch(u):
         here = pl.ds(u * UNIT, UNIT)
@@ -210,7 +218,7 @@
 
     def step(i, carry):
         def cols_of(p):
-            u = i * UNITS + p
+            u = i * SPECTRA_UNITS + p
             fetch(u).wait()
             planes = []
             for j in range(UNIT):
@@ -220,16 +228,16 @@
             return pairs_apart(to_col_freqs(planes, col_fwd))
 
         def rows_of(p, both):
-            u = i * UNITS + p
+            u = i * SPECTRA_UNITS + p
             for c, found in enumerate(to_row_freqs(quarters_of(*both, quarter), row_fwd)):
                 for part in range(2):
                     spec[u, part, c * quarter:(c + 1) * quarter] = found[part]
             put(u).start()
 
-        staggered(UNITS, cols_of, rows_of)
+        staggered(SPECTRA_UNITS, cols_of, rows_of)
         return carry
 
-    lax.fori_loop(0, steps, step, 0)
+    loop(steps, step)
     for u in range(kernels // UNIT):
         put(u).wait()
 
@@ -301,7 +309,7 @@
         staggered(UNITS, rows_of, cols_of)
         return carry
 
-    lax.fori_loop(0, steps, forward, 0)
+    loop(steps, forward)
 
     wanted = target[...].astype(f32)
     for g in range(GROUPS):
@@ -338,7 +346,7 @@
         staggered(UNITS, cols_of, rows_of)
         return carry
 
-    lax.fori_loop(0, steps, backward, 0)
+    loop(steps, backward)
 
     classes = [tuple(grad_spec[part, c * rim:(c + 1) * rim] for part in range(2)) for c in range(4)]
     quarters = from_row_freqs(classes, row_inv, (2, 3, 0, 1))
@@ -380,7 +388,7 @@
     grid_rows = count + 2 * rim
     grid_cols = width + rim
     units = kernels // UNIT
-    assert count == span and width == span and kernels % (UNIT * UNITS) == 0 and span == 128
+    assert count == span and width == span and units % UNITS == 0 and units % SPECTRA_UNITS == 0 and kernels % UNIT == 0 and span == 128
 
     strips = lax.axis_size("row")
     assert strips % 2 == 0

time: 40 us -> 39.9 us (level)
  transfers between devices with their start and end apart: 4 -> 4, of which waited for: 1 -> 1; matrix products, arithmetic and copies ran while one was open for 0% -> 0% of each run, Pallas kernels for 24% -> 23%
where the time goes in v15:
time: 39.9 us; the launch traced here: 39.6 us
  Pallas kernels  28.5 us (71%)
  starting transfers between devices  7.36 us (18%)
  waiting for transfers between devices  2.97 us (7%)
  between operations  0.76 us (2%)
    pallas_call x1, Pallas kernels, on_device(): pl.pallas_call(functools.partial(main_body, layout=layout), out_shape=[ja...  18.6 us
    pallas_call x1, Pallas kernels, on_device(): pl.pallas_call(spectra_body, out_shape=jax.ShapeDtypeStruct(spec_shape, f...  9.2 us
    ppermute x1, starting transfers between devices, on_device(): far_in = lax.ppermute(far_rim, 'row', far_pairs)  3.5 us
    ppermute x1, starting transfers between devices, on_device(): far = lax.ppermute(mask_field, 'row', far_pairs)  3.05 us
    ppermute x1, waiting for transfers between devices, on_device(): far_in = lax.ppermute(far_rim, 'row', far_pairs)  2.96 us
  transfers between devices with their start and end apart: 4, of which 1 were waited for; matrix products, arithmetic and copies ran while one was open for 0% of the time, Pallas kernels for 23%

profile of v15, /device:TPU:21, one launch (start us, length us, event | category | flops | bytes accessed | tf_op | source)
XLA Modules:
  0.0 39.6 jit_solution(4347509432880382225)
XLA Ops:
  0.6 0.0 copy-start
  0.6 0.0 copy-start.3
  0.7 0.0 copy-start.2
  0.7 0.0 copy-start.1
  0.7 0.7 %collective-permute-start = (f32[2,128,128]{2,1,0:T(8,128)}, f32[2,128,128]{2,1,0:T(8,128)S(1)}, u32[]{:S(2)}, u32[]{:S(2)}) collective-permute-start(f32[2,128,128]{2,1,0:T(8,128)} %own.1), channel_id=1, source_target_pairs={{0,1},{1,0},{2,3},{3,2},{4,5},{5,4},{6,7},{7,6},{8,9},{9,8},{10,11... | collective-permute-start | bytes 393224 | tf_op jit(solution)/shard_map/ppermute | solution.py:398
  1.4 3.0 %collective-permute-start.1 = (f32[2,128,128]{2,1,0:T(8,128)}, f32[2,128,128]{2,1,0:T(8,128)S(1)}, u32[]{:S(2)}, u32[]{:S(2)}) collective-permute-start(f32[2,128,128]{2,1,0:T(8,128)} %own.1), channel_id=1, source_target_pairs={{1,2},{2,1},{3,4},{4,3},{5,6},{6,5},{7,8},{8,7},{9,10},{10,9},{11,... | collective-permute-start | bytes 393224 | tf_op jit(solution)/shard_map/ppermute | solution.py:399
  4.5 9.2 %spectra.1.spec_far = f32[6,2,256,768]{3,2,1,0:T(8,128)} custom-call(s32[24]{0:T(128)} %radii.1, f32[24,2,128,128]{3,2,1,0:T(8,128)} %taps_far.1, bf16[256,512]{1,0:T(8,128)(2,1)} %constant.10.clone.row_ref, bf16[384,256]{1,0:T(8,128)(2,1)} %constant.11.clone.col_ref), custom_call_target="tpu_custom_call" | custom-call | flops 17999998976 | bytes 14000000 | tf_op jit(solution)/shard_map/spectra/pallas_call | solution.py:415
  13.7 0.0 collective-permute-done.near
  13.7 0.0 collective-permute-done.1.far
  13.7 0.0 copy-done
  13.7 0.0 copy-done.3
  13.7 0.0 copy-done.2
  13.7 0.0 copy-done.1
  13.7 18.6 %fields.1 = (f32[3,128,128]{2,1,0:T(8,128)}, f32[2,128,128]{2,1,0:T(8,128)S(1)}, f32[2,64,128]{2,1,0:T(8,128)S(1)}, f32[2,64,128]{2,1,0:T(8,128)S(1)}) custom-call(s32[24]{0:T(128)S(1)} %copy-done.2, f32[24]{0:T(128)S(1)} %copy-done.3, s32[1]{0:T(128)} %bitcast.place, f32[2,128,128]{2,1,0:T(8,128)S(1)} %copy-done, ...), custom_call_target="tpu_custom_call" | custom-call | tf_op jit(solution)/shard_map/fields/pallas_call | solution.py:431
  32.3 0.1 collective-permute-start.2
  32.4 3.5 %collective-permute-start.3 = (f32[2,64,128]{2,1,0:T(8,128)S(1)}, f32[2,64,128]{2,1,0:T(8,128)S(1)}, u32[]{:S(2)}, u32[]{:S(2)}) collective-permute-start(f32[2,64,128]{2,1,0:T(8,128)S(1)} %get-tuple-element.9), channel_id=1, source_target_pairs={{1,2},{2,1},{3,4},{4,3},{5,6},{6,5},{7,8},{8,7},{9,10},{10,9},{11,... | collective-permute-start | bytes 196616 | tf_op jit(solution)/shard_map/ppermute | solution.py:458
  35.9 0.0 collective-permute-done.2.near
  35.9 3.0 %collective-permute-done.3.far = f32[2,64,128]{2,1,0:T(8,128)S(1)} collective-permute-done((f32[2,64,128]{2,1,0:T(8,128)S(1)}, f32[2,64,128]{2,1,0:T(8,128)S(1)}, u32[]{:S(2)}, u32[]{:S(2)}) %collective-permute-start.3) | collective-permute-done | bytes 65568 | tf_op jit(solution)/shard_map/ppermute | solution.py:458
  38.9 0.7 %join.1 = f32[2,128,128]{2,1,0:T(8,128)} custom-call(s32[1]{0:T(128)} %bitcast.place, f32[2,128,128]{2,1,0:T(8,128)S(1)} %get-tuple-element.7.own, f32[2,64,128]{2,1,0:T(8,128)S(1)} %collective-permute-done.2.near, f32[2,64,128]{2,1,0:T(8,128)S(1)} %collective-permute-done.3.far), custom_call_target="tpu_custom_call" | custom-call | tf_op jit(solution)/shard_map/join/pallas_call | solution.py:459
Async XLA Ops:
  0.6 13.1 %copy-start = (f32[2,128,128]{2,1,0:T(8,128)S(1)}, f32[2,128,128]{2,1,0:T(8,128)}, u32[]{:S(2)}) copy-start(f32[2,128,128]{2,1,0:T(8,128)} %own.1) | copy-start | bytes 393220
  0.6 13.1 %copy-start.3 = (f32[24]{0:T(128)S(1)}, f32[24]{0:T(128)}, u32[]{:S(2)}) copy-start(f32[24]{0:T(128)} %weight.1) | copy-start | bytes 292
  0.7 13.1 %copy-start.2 = (s32[24]{0:T(128)S(1)}, s32[24]{0:T(128)}, u32[]{:S(2)}) copy-start(s32[24]{0:T(128)} %group.1) | copy-start | bytes 292
  0.7 13.1 %copy-start.1 = (s32[128,128]{1,0:T(8,128)S(1)}, s32[128,128]{1,0:T(8,128)}, u32[]{:S(2)}) copy-start(s32[128,128]{1,0:T(8,128)} %target.1) | copy-start | bytes 196612
  0.7 13.0 %collective-permute-start = (f32[2,128,128]{2,1,0:T(8,128)}, f32[2,128,128]{2,1,0:T(8,128)S(1)}, u32[]{:S(2)}, u32[]{:S(2)}) collective-permute-start(f32[2,128,128]{2,1,0:T(8,128)} %own.1), channel_id=1, source_target_pairs={{0,1},{1,0},{2,3},{3,2},{4,5},{5,4},{6,7},{7,6},{8,9},{9,8},{10,11... | collective-permute-start | bytes 393224 | tf_op jit(solution)/shard_map/ppermute | solution.py:398
  1.4 12.3 %collective-permute-start.1 = (f32[2,128,128]{2,1,0:T(8,128)}, f32[2,128,128]{2,1,0:T(8,128)S(1)}, u32[]{:S(2)}, u32[]{:S(2)}) collective-permute-start(f32[2,128,128]{2,1,0:T(8,128)} %own.1), channel_id=1, source_target_pairs={{1,2},{2,1},{3,4},{4,3},{5,6},{6,5},{7,8},{8,7},{9,10},{10,9},{11,... | collective-permute-start | bytes 393224 | tf_op jit(solution)/shard_map/ppermute | solution.py:399
  32.3 3.6 %collective-permute-start.2 = (f32[2,64,128]{2,1,0:T(8,128)S(1)}, f32[2,64,128]{2,1,0:T(8,128)S(1)}, u32[]{:S(2)}, u32[]{:S(2)}) collective-permute-start(f32[2,64,128]{2,1,0:T(8,128)S(1)} %get-tuple-element.8), channel_id=1, source_target_pairs={{0,1},{1,0},{2,3},{3,2},{4,5},{5,4},{6,7},{7,6},{8,9},{9,8},{10,11... | collective-permute-start | bytes 196616 | tf_op jit(solution)/shard_map/ppermute | solution.py:457
  32.4 6.5 %collective-permute-start.3 = (f32[2,64,128]{2,1,0:T(8,128)S(1)}, f32[2,64,128]{2,1,0:T(8,128)S(1)}, u32[]{:S(2)}, u32[]{:S(2)}) collective-permute-start(f32[2,64,128]{2,1,0:T(8,128)S(1)} %get-tuple-element.9), channel_id=1, source_target_pairs={{1,2},{2,1},{3,4},{4,3},{5,6},{6,5},{7,8},{8,7},{9,10},{10,9},{11,... | collective-permute-start | bytes 196616 | tf_op jit(solution)/shard_map/ppermute | solution.py:458

commit v16 on v15

--- a/solution.py
+++ b/solution.py
@@ -15,8 +15,8 @@
 STEEPNESS = 1.0
 THRESHOLD = 2.0
 UNIT = 4
-SPECTRA_UNITS = 6
-UNITS = 3
+SPECTRA_UNITS = 3
+UNITS = 2
 PIECE = 256
 TURN = math.sqrt(0.75)
 
@@ -40,7 +40,11 @@
     return np.block([[cos, sin], [-sin, cos]])
 
 
-def split(x):
+def split(x, dtype):
+    if dtype == f32:
+        wide = x * 65537.0
+        high = wide - (wide - x)
+        return high, x - high
     high = x.astype(bf16)
     low = (x - high.astype(f32)).astype(bf16)
     return high, low
@@ -81,7 +85,7 @@
 
 
 def row_product(table, c, x):
-    parts = split(x)
+    parts = split(x, table.dtype)
     depth = x.shape[0]
     left = table[:, c * depth:(c + 1) * depth]
     found = dot(jnp.concatenate([left, left], axis=1), jnp.concatenate(parts, axis=0))
@@ -130,7 +134,7 @@
     depth = table.shape[0] // 3
     out = [[] for _ in planes]
     for c in range(3):
-        high, low = split(jnp.concatenate([plane[c] for plane in planes], axis=0))
+        high, low = split(jnp.concatenate([plane[c] for plane in planes], axis=0), table.dtype)
         right = table[c * depth:(c + 1) * depth]
         found = dot(jnp.concatenate([high, low], axis=1), jnp.concatenate([right, right], axis=0))
         found = found[:, :depth] + found[:, depth:]
@@ -426,7 +430,7 @@
         compiler_params=pltpu.CompilerParams(vmem_limit_bytes=56 * MIB),
         cost_estimate=pl.CostEstimate(flops=18 * 10**9, bytes_accessed=14 * 10**6, transcendentals=0),
         name="spectra",
-    )(kernel_radii, kernel_taps, *map(jnp.asarray, (row_fwd, col_fwd)))
+    )(kernel_radii, kernel_taps, *[jnp.asarray(t.astype(np.float32)) for t in (row_fwd, col_fwd)])
 
     resist, own, near_rim, far_rim = pl.pallas_call(
         functools.partial(main_body, layout=layout),

time: 39.9 us -> 40.6 us (1.018)
  Pallas kernels: 28.5 us -> 29.1 us
    pallas_call x1, Pallas kernels: 9.2 us -> 10.1 us  [on_device(): pl.pallas_call(spectra_body, out_shape=jax.ShapeDtypeStruct(spec_shape, f...]
  transfers between devices with their start and end apart: 4 -> 4, of which waited for: 1 -> 1; matrix products, arithmetic and copies ran while one was open for 0% -> 0% of each run, Pallas kernels for 23% -> 25%
where the time goes in v16:
time: 40.6 us; the launch traced here: 40.2 us
  Pallas kernels  29.1 us (72%)
  starting transfers between devices  7.39 us (18%)
  waiting for transfers between devices  2.94 us (7%)
  between operations  0.76 us (2%)
    pallas_call x1, Pallas kernels, on_device(): pl.pallas_call(functools.partial(main_body, layout=layout), out_shape=[ja...  18.4 us
    pallas_call x1, Pallas kernels, on_device(): pl.pallas_call(spectra_body, out_shape=jax.ShapeDtypeStruct(spec_shape, f...  10.1 us
    ppermute x1, starting transfers between devices, on_device(): far_in = lax.ppermute(far_rim, 'row', far_pairs)  3.53 us
    ppermute x1, starting transfers between devices, on_device(): far = lax.ppermute(mask_field, 'row', far_pairs)  3.05 us
    ppermute x1, waiting for transfers between devices, on_device(): far_in = lax.ppermute(far_rim, 'row', far_pairs)  2.94 us
  transfers between devices with their start and end apart: 4, of which 1 were waited for; matrix products, arithmetic and copies ran while one was open for 0% of the time, Pallas kernels for 25%

profile of v16, /device:TPU:21, one launch (start us, length us, event | category | flops | bytes accessed | tf_op | source)
XLA Modules:
  0.0 40.2 jit_solution(14488002361580539632)
XLA Ops:
  0.6 0.0 copy-start
  0.6 0.0 copy-start.3
  0.7 0.0 copy-start.2
  0.7 0.0 copy-start.1
  0.7 0.7 %collective-permute-start = (f32[2,128,128]{2,1,0:T(8,128)}, f32[2,128,128]{2,1,0:T(8,128)S(1)}, u32[]{:S(2)}, u32[]{:S(2)}) collective-permute-start(f32[2,128,128]{2,1,0:T(8,128)} %own.1), channel_id=1, source_target_pairs={{0,1},{1,0},{2,3},{3,2},{4,5},{5,4},{6,7},{7,6},{8,9},{9,8},{10,11... | collective-permute-start | bytes 393224 | tf_op jit(solution)/shard_map/ppermute | solution.py:402
  1.4 3.0 %collective-permute-start.1 = (f32[2,128,128]{2,1,0:T(8,128)}, f32[2,128,128]{2,1,0:T(8,128)S(1)}, u32[]{:S(2)}, u32[]{:S(2)}) collective-permute-start(f32[2,128,128]{2,1,0:T(8,128)} %own.1), channel_id=1, source_target_pairs={{1,2},{2,1},{3,4},{4,3},{5,6},{6,5},{7,8},{8,7},{9,10},{10,9},{11,... | collective-permute-start | bytes 393224 | tf_op jit(solution)/shard_map/ppermute | solution.py:403
  4.5 10.1 %spectra.1.spec_far = f32[6,2,256,768]{3,2,1,0:T(8,128)} custom-call(s32[24]{0:T(128)} %radii.1, f32[24,2,128,128]{3,2,1,0:T(8,128)} %taps_far.1, f32[256,512]{1,0:T(8,128)} %constant.10.clone.row_ref, f32[384,256]{1,0:T(8,128)} %constant.11.clone.col_ref), custom_call_target="tpu_custom_call" | custom-call | flops 17999998976 | bytes 14000000 | tf_op jit(solution)/shard_map/spectra/pallas_call | solution.py:419
  14.6 0.0 collective-permute-done.near
  14.6 0.0 collective-permute-done.1.far
  14.6 0.0 copy-done
  14.6 0.0 copy-done.3
  14.6 0.0 copy-done.2
  14.6 0.0 copy-done.1
  14.6 18.4 %fields.1 = (f32[3,128,128]{2,1,0:T(8,128)}, f32[2,128,128]{2,1,0:T(8,128)S(1)}, f32[2,64,128]{2,1,0:T(8,128)S(1)}, f32[2,64,128]{2,1,0:T(8,128)S(1)}) custom-call(s32[24]{0:T(128)S(1)} %copy-done.2, f32[24]{0:T(128)S(1)} %copy-done.3, s32[1]{0:T(128)} %bitcast.place, f32[2,128,128]{2,1,0:T(8,128)S(1)} %copy-done, ...), custom_call_target="tpu_custom_call" | custom-call | tf_op jit(solution)/shard_map/fields/pallas_call | solution.py:435
  33.0 0.1 collective-permute-start.2
  33.1 3.5 %collective-permute-start.3 = (f32[2,64,128]{2,1,0:T(8,128)S(1)}, f32[2,64,128]{2,1,0:T(8,128)S(1)}, u32[]{:S(2)}, u32[]{:S(2)}) collective-permute-start(f32[2,64,128]{2,1,0:T(8,128)S(1)} %get-tuple-element.9), channel_id=1, source_target_pairs={{1,2},{2,1},{3,4},{4,3},{5,6},{6,5},{7,8},{8,7},{9,10},{10,9},{11,... | collective-permute-start | bytes 196616 | tf_op jit(solution)/shard_map/ppermute | solution.py:462
  36.6 0.0 collective-permute-done.2.near
  36.6 2.9 %collective-permute-done.3.far = f32[2,64,128]{2,1,0:T(8,128)S(1)} collective-permute-done((f32[2,64,128]{2,1,0:T(8,128)S(1)}, f32[2,64,128]{2,1,0:T(8,128)S(1)}, u32[]{:S(2)}, u32[]{:S(2)}) %collective-permute-start.3) | collective-permute-done | bytes 65568 | tf_op jit(solution)/shard_map/ppermute | solution.py:462
  39.6 0.7 %join.1 = f32[2,128,128]{2,1,0:T(8,128)} custom-call(s32[1]{0:T(128)} %bitcast.place, f32[2,128,128]{2,1,0:T(8,128)S(1)} %get-tuple-element.7.own, f32[2,64,128]{2,1,0:T(8,128)S(1)} %collective-permute-done.2.near, f32[2,64,128]{2,1,0:T(8,128)S(1)} %collective-permute-done.3.far), custom_call_target="tpu_custom_call" | custom-call | tf_op jit(solution)/shard_map/join/pallas_call | solution.py:463
Async XLA Ops:
  0.6 14.0 %copy-start = (f32[2,128,128]{2,1,0:T(8,128)S(1)}, f32[2,128,128]{2,1,0:T(8,128)}, u32[]{:S(2)}) copy-start(f32[2,128,128]{2,1,0:T(8,128)} %own.1) | copy-start | bytes 393220
  0.6 14.0 %copy-start.3 = (f32[24]{0:T(128)S(1)}, f32[24]{0:T(128)}, u32[]{:S(2)}) copy-start(f32[24]{0:T(128)} %weight.1) | copy-start | bytes 292
  0.7 14.0 %copy-start.2 = (s32[24]{0:T(128)S(1)}, s32[24]{0:T(128)}, u32[]{:S(2)}) copy-start(s32[24]{0:T(128)} %group.1) | copy-start | bytes 292
  0.7 14.0 %copy-start.1 = (s32[128,128]{1,0:T(8,128)S(1)}, s32[128,128]{1,0:T(8,128)}, u32[]{:S(2)}) copy-start(s32[128,128]{1,0:T(8,128)} %target.1) | copy-start | bytes 196612
  0.7 13.9 %collective-permute-start = (f32[2,128,128]{2,1,0:T(8,128)}, f32[2,128,128]{2,1,0:T(8,128)S(1)}, u32[]{:S(2)}, u32[]{:S(2)}) collective-permute-start(f32[2,128,128]{2,1,0:T(8,128)} %own.1), channel_id=1, source_target_pairs={{0,1},{1,0},{2,3},{3,2},{4,5},{5,4},{6,7},{7,6},{8,9},{9,8},{10,11... | collective-permute-start | bytes 393224 | tf_op jit(solution)/shard_map/ppermute | solution.py:402
  1.4 13.2 %collective-permute-start.1 = (f32[2,128,128]{2,1,0:T(8,128)}, f32[2,128,128]{2,1,0:T(8,128)S(1)}, u32[]{:S(2)}, u32[]{:S(2)}) collective-permute-start(f32[2,128,128]{2,1,0:T(8,128)} %own.1), channel_id=1, source_target_pairs={{1,2},{2,1},{3,4},{4,3},{5,6},{6,5},{7,8},{8,7},{9,10},{10,9},{11,... | collective-permute-start | bytes 393224 | tf_op jit(solution)/shard_map/ppermute | solution.py:403
  33.0 3.6 %collective-permute-start.2 = (f32[2,64,128]{2,1,0:T(8,128)S(1)}, f32[2,64,128]{2,1,0:T(8,128)S(1)}, u32[]{:S(2)}, u32[]{:S(2)}) collective-permute-start(f32[2,64,128]{2,1,0:T(8,128)S(1)} %get-tuple-element.8), channel_id=1, source_target_pairs={{0,1},{1,0},{2,3},{3,2},{4,5},{5,4},{6,7},{7,6},{8,9},{9,8},{10,11... | collective-permute-start | bytes 196616 | tf_op jit(solution)/shard_map/ppermute | solution.py:461
  33.1 6.5 %collective-permute-start.3 = (f32[2,64,128]{2,1,0:T(8,128)S(1)}, f32[2,64,128]{2,1,0:T(8,128)S(1)}, u32[]{:S(2)}, u32[]{:S(2)}) collective-permute-start(f32[2,64,128]{2,1,0:T(8,128)S(1)} %get-tuple-element.9), channel_id=1, source_target_pairs={{1,2},{2,1},{3,4},{4,3},{5,6},{6,5},{7,8},{8,7},{9,10},{10,9},{11,... | collective-permute-start | bytes 196616 | tf_op jit(solution)/shard_map/ppermute | solution.py:462

commit v17 on v15

--- a/solution.py
+++ b/solution.py
@@ -15,8 +15,9 @@
 STEEPNESS = 1.0
 THRESHOLD = 2.0
 UNIT = 4
-SPECTRA_UNITS = 6
+SPECTRA_UNITS = 3
 UNITS = 3
+CHUNK = 32
 PIECE = 256
 TURN = math.sqrt(0.75)
 
@@ -90,23 +91,21 @@
     return found[:half // 2], found[half // 2:]
 
 
-def to_row_freqs(x, table):
+def fold_rows(x):
     if len(x) == 2:
         even, odd, even_less, odd_less = x[0], x[1], x[0], x[1]
     else:
         even, odd = plus(x[0], x[2]), plus(x[1], x[3])
         even_less, odd_less = minus(x[0], x[2]), minus(x[1], x[3])
-    folded = [
+    return [
         plus(even, odd),
         plus(even_less, turned(odd_less, -1)),
         minus(even, odd),
         plus(even_less, turned(odd_less, 1)),
     ]
-    return [row_product(table, c, jnp.concatenate(y, axis=0)) for c, y in enumerate(folded)]
-
-
-def from_row_freqs(classes, table, quarters):
-    v = [row_product(table, c, jnp.concatenate(y, axis=0)) for c, y in enumerate(classes)]
+
+
+def unfold_rows(v, quarters):
     out = []
     for q in quarters:
         if q % 2 == 0:
@@ -115,6 +114,15 @@
             even, odd = minus(v[0], v[2]), turned(minus(v[1], v[3]), 1)
         out.append(plus(even, odd) if q < 2 else minus(even, odd))
     return out
+
+
+def to_row_freqs(x, table):
+    return [row_product(table, c, jnp.concatenate(y, axis=0)) for c, y in enumerate(fold_rows(x))]
+
+
+def from_row_freqs(classes, table, quarters):
+    v = [row_product(table, c, jnp.concatenate(y, axis=0)) for c, y in enumerate(classes)]
+    return unfold_rows(v, quarters)
 
 
 def quarters_of(re, im, quarter):
@@ -139,24 +147,26 @@
     return out
 
 
+def fold_cols(left, right, shifted=False):
+    if shifted:
+        left, right = right, left
+    near, far = left - 0.5 * right, lane_turned(right)
+    one, two = near + far, near - far
+    return [left + right, two, one] if shifted else [left + right, one, two]
+
+
+def unfold_cols(v, shifted=False):
+    total, far = v[1] + v[2], lane_turned(v[1] - v[2])
+    whole, part = v[0] + total, v[0] - 0.5 * total
+    return (part + far, whole) if shifted else (whole, part - far)
+
+
 def to_col_freqs(planes, table, shifted=False):
-    folded = []
-    for left, right in planes:
-        if shifted:
-            left, right = right, left
-        near, far = left - 0.5 * right, lane_turned(right)
-        one, two = near + far, near - far
-        folded.append([left + right, two, one] if shifted else [left + right, one, two])
-    return col_products(folded, table)
+    return col_products([fold_cols(*halves_of, shifted) for halves_of in planes], table)
 
 
 def from_col_freqs(planes, table, shifted=False):
-    out = []
-    for v in col_products(planes, table):
-        total, far = v[1] + v[2], lane_turned(v[1] - v[2])
-        whole, part = v[0] + total, v[0] - 0.5 * total
-        out.append((part + far, whole) if shifted else (whole, part - far))
-    return out
+    return [unfold_cols(v, shifted) for v in col_products(planes, table)]
 
 
 def pairs_apart(planes):
@@ -188,16 +198,74 @@
 
 
 def staggered(count, first, second):
-    held = None
-    for i in range(count):
-        new = first(i)
-        if i:
-            second(i - 1, held)
-        held = new
-    second(count - 1, held)
-
-
-def spectra_body(radii, taps_far, row_ref, col_ref, spec_far, taps, spec, in_sems, out_sems):
+    for i in range(count + 1):
+        ahead = list_of(first, i) if i < count else iter(())
+        behind = list_of(second, i - 1) if i else iter(())
+        more = True
+        while more:
+            more = False
+            for steps in (ahead, behind):
+                for _ in steps:
+                    more = True
+                    break
+
+
+def list_of(stage, i):
+    return iter(stage(i))
+
+
+def put_cols(buf, c, row, x):
+    high, low = split(x)
+    lanes = x.shape[1]
+    buf[c, row:row + x.shape[0], :lanes] = high
+    buf[c, row:row + x.shape[0], lanes:] = low
+
+
+def put_rows(buf, c, row_class, pair, row, parts):
+    lanes = parts[0].shape[1]
+    quarter = buf.shape[2] // 4
+    here = slice(pair * lanes, (pair + 1) * lanes)
+    for part, x in enumerate(parts):
+        high, low = split(x)
+        at = part * quarter + row
+        buf[c, row_class, at:at + x.shape[0], here] = high
+        buf[c, row_class, 2 * quarter + at:2 * quarter + at + x.shape[0], here] = low
+
+
+def col_dot(buf, c, pair, table):
+    depth = table.shape[0] // 3
+    rows = 2 * buf.shape[1] // UNIT
+    right = table[c * depth:(c + 1) * depth]
+    left = buf[c, pair * rows:(pair + 1) * rows]
+    found = jnp.dot(left, jnp.concatenate([right, right], axis=0), preferred_element_type=f32)
+    return found[:, :depth] + found[:, depth:]
+
+
+def row_dot(buf, c, row_class, table):
+    depth = table.shape[1] // 4
+    left = table[:, row_class * depth:(row_class + 1) * depth]
+    found = jnp.dot(jnp.concatenate([left, left], axis=1), buf[c, row_class], preferred_element_type=f32)
+    half = found.shape[0] // 2
+    return found[:half] + found[half:]
+
+
+def cols_to_rows(col_buf, row_buf, table):
+    rows = col_buf.shape[1] // UNIT
+    quarter = rows // 2
+    for c in range(3):
+        for pair in range(UNIT // 2):
+            z = col_dot(col_buf, c, pair, table)
+            for r in range(0, quarter, CHUNK):
+                parts = [
+                    exchange(z[at + r:at + r + CHUNK], z[rows + at + r:rows + at + r + CHUNK])
+                    for at in (0, quarter)
+                ]
+                for row_class, y in enumerate(fold_rows(parts)):
+                    put_rows(row_buf, c, row_class, pair, r, y)
+            yield
+
+
+def spectra_body(radii, taps_far, row_ref, col_ref, spec_far, taps, spec, col_buf, row_bufs, in_sems, out_sems):
     kernels, _, span, _ = taps.shape
     row_fwd, col_fwd = row_ref[...], col_ref[...]
     quarter = span // 2
@@ -212,26 +280,33 @@
 
     for u in range(kernels // UNIT):
         fetch(u).start()
-    row_at = lax.broadcasted_iota(jnp.int32, (span, span), 0) - span // 2
-    col_at = lax.broadcasted_iota(jnp.int32, (span, span), 1) - span // 2
-    reach = jnp.maximum(jnp.maximum(row_at, -1 - row_at), jnp.maximum(col_at, -1 - col_at))
+    col_at = lax.broadcasted_iota(jnp.int32, (CHUNK, span), 1) - span // 2
+    col_reach = jnp.maximum(col_at, -1 - col_at)
 
     def step(i, carry):
         def cols_of(p):
             u = i * SPECTRA_UNITS + p
             fetch(u).wait()
-            planes = []
             for j in range(UNIT):
                 k = u * UNIT + j
-                inside = reach < radii[k]
-                planes.append(exchange(*[jnp.where(inside, taps[k, c], 0.0) for c in range(2)]))
-            return pairs_apart(to_col_freqs(planes, col_fwd))
-
-        def rows_of(p, both):
+                for r in range(0, span, CHUNK):
+                    row_at = lax.broadcasted_iota(jnp.int32, (CHUNK, span), 0) + (r - span // 2)
+                    inside = jnp.maximum(jnp.maximum(row_at, -1 - row_at), col_reach) < radii[k]
+                    planes = [jnp.where(inside, taps[k, c, r:r + CHUNK], 0.0) for c in range(2)]
+                    for c, y in enumerate(fold_cols(*exchange(*planes))):
+                        put_cols(col_buf, c, j * span + r, y)
+                yield
+            yield from cols_to_rows(col_buf, row_bufs.at[p % 2], col_fwd)
+
+        def rows_of(p):
             u = i * SPECTRA_UNITS + p
-            for c, found in enumerate(to_row_freqs(quarters_of(*both, quarter), row_fwd)):
-                for part in range(2):
-                    spec[u, part, c * quarter:(c + 1) * quarter] = found[part]
+            for c in range(3):
+                lanes = slice(c * 2 * span, (c + 1) * 2 * span)
+                for row_class in range(4):
+                    found = row_dot(row_bufs.at[p % 2], c, row_class, row_fwd)
+                    for part in range(2):
+                        spec[u, part, row_class * quarter:(row_class + 1) * quarter, lanes] = found[part * quarter:(part + 1) * quarter]
+                    yield
             put(u).start()
 
         staggered(SPECTRA_UNITS, cols_of, rows_of)
@@ -246,7 +321,8 @@
     group, weight, place,
     own, near, far, target, spec_far, tables_far,
     resist_far, grad_own, near_rim, far_rim,
-    spec, field, mask_spec, resist, slopes, grad_spec, tables, spec_sems, table_sem, out_sem,
+    spec, field, mask_spec, resist, slopes, grad_spec, tables, col_buf, row_buf, row_sums, col_sums,
+    spec_sems, table_sem, out_sem,
     *, layout,
 ):
     count, width = target.shape
@@ -286,25 +362,50 @@
     def forward(i, carry):
         def rows_of(p):
             u = i * UNITS + p
+            buf, sums, cols = row_buf.at[p % 2], row_sums.at[p % 2], col_buf.at[p % 2]
             fetch(u).wait()
-            classes = []
-            for c in range(4):
-                here = slice(c * rim, (c + 1) * rim)
-                m_re, m_im = [jnp.concatenate([mask_spec[part, here]] * (UNIT // 2), axis=1) for part in range(2)]
-                s_re, s_im = spec[u, 0, here], spec[u, 1, here]
-                classes.append((s_re * m_re - s_im * m_im, s_re * m_im + s_im * m_re))
-            upper, lower = from_row_freqs(classes, row_inv, (0, 1))
-            return [jnp.concatenate([upper[part], lower[part]], axis=0) for part in range(2)]
-
-        def cols_of(p, both):
+            for c in range(3):
+                for row_class in range(4):
+                    for r in range(0, rim, CHUNK):
+                        here = slice(row_class * rim + r, row_class * rim + r + CHUNK)
+                        m_re, m_im = [mask_spec[part, here, c * width:(c + 1) * width] for part in range(2)]
+                        for pair in range(UNIT // 2):
+                            lanes = slice((2 * c + pair) * width, (2 * c + pair + 1) * width)
+                            s_re, s_im = spec[u, 0, here, lanes], spec[u, 1, here, lanes]
+                            product = s_re * m_re - s_im * m_im, s_re * m_im + s_im * m_re
+                            put_rows(buf, c, row_class, pair, r, product)
+                    yield
+                for row_class in range(4):
+                    sums[c, row_class] = row_dot(buf, c, row_class, row_inv)
+                    yield
+                for pair in range(UNIT // 2):
+                    lanes = slice(pair * width, (pair + 1) * width)
+                    for r in range(0, rim, CHUNK // 2):
+                        v = [
+                            [sums[c, row_class, part * rim + r:part * rim + r + CHUNK // 2, lanes] for part in range(2)]
+                            for row_class in range(4)
+                        ]
+                        for q, (re, im) in enumerate(unfold_rows(v, (0, 1))):
+                            for j, x in enumerate(exchange(re, im)):
+                                put_cols(cols, c, (2 * pair + j) * count + q * rim + r, x)
+                    yield
+
+        def cols_of(p):
             u = i * UNITS + p
-            found = from_col_freqs(pairs_together(*both, width), col_inv)
-            for j in range(UNIT):
-                k = u * UNIT + j
-                for side in range(2):
-                    x = found[j][side]
-                    field[k, side] = x
-                    slopes[group[k], side] = slopes[group[k], side] + weight[k] * (x * x)
+            cols = col_buf.at[p % 2]
+            for pair in range(UNIT // 2):
+                for c in range(3):
+                    col_sums[c] = col_dot(cols, c, pair, col_inv)
+                    yield
+                for j in range(2):
+                    k = u * UNIT + 2 * pair + j
+                    for r in range(0, count, CHUNK):
+                        here = slice(r, r + CHUNK)
+                        v = [col_sums[c, j * count + r:j * count + r + CHUNK] for c in range(3)]
+                        for side, x in enumerate(unfold_cols(v)):
+                            field[k, side, here] = x
+                            slopes[group[k], side, here] = slopes[group[k], side, here] + weight[k] * (x * x)
+                    yield
 
         staggered(UNITS, rows_of, cols_of)
         return carry
@@ -324,24 +425,36 @@
     def backward(i, carry):
         def cols_of(p):
             u = i * UNITS + p
-            planes = []
+            cols = col_buf.at[0]
             for j in range(UNIT):
                 k = u * UNIT + j
-                planes.append([field[k, side] * ((2.0 * weight[k]) * slopes[group[k], side]) for side in range(2)])
-            return pairs_apart(to_col_freqs(planes, col_fwd))
-
-        def rows_of(p, both):
+                for r in range(0, count, CHUNK):
+                    here = slice(r, r + CHUNK)
+                    halves_of = [field[k, side, here] * ((2.0 * weight[k]) * slopes[group[k], side, here]) for side in range(2)]
+                    for c, y in enumerate(fold_cols(*halves_of)):
+                        put_cols(cols, c, j * count + r, y)
+                yield
+            yield from cols_to_rows(cols, row_buf.at[p % 2], col_fwd)
+
+        def rows_of(p):
             u = i * UNITS + p
-            for c, (c_re, c_im) in enumerate(to_row_freqs(quarters_of(*both, rim), row_fwd)):
-                here = slice(c * rim, (c + 1) * rim)
-                s_re, s_im = spec[u, 0, here], spec[u, 1, here]
-                terms = s_re * c_re + s_im * c_im, s_re * c_im - s_im * c_re
-                for part in range(2):
-                    total = grad_spec[part, here]
-                    lanes = total.shape[1]
-                    for at in range(0, terms[part].shape[1], lanes):
-                        total = total + terms[part][:, at:at + lanes]
-                    grad_spec[part, here] = total
+            for c in range(3):
+                for row_class in range(4):
+                    found = row_dot(row_buf.at[p % 2], c, row_class, row_fwd)
+                    for r in range(0, rim, CHUNK):
+                        here = slice(row_class * rim + r, row_class * rim + r + CHUNK)
+                        totals = [grad_spec[part, here, c * width:(c + 1) * width] for part in range(2)]
+                        for pair in range(UNIT // 2):
+                            lanes = slice((2 * c + pair) * width, (2 * c + pair + 1) * width)
+                            s_re, s_im = spec[u, 0, here, lanes], spec[u, 1, here, lanes]
+                            c_re, c_im = [
+                                found[part * rim + r:part * rim + r + CHUNK, pair * width:(pair + 1) * width]
+                                for part in range(2)
+                            ]
+                            totals = [totals[0] + (s_re * c_re + s_im * c_im), totals[1] + (s_re * c_im - s_im * c_re)]
+                        for part in range(2):
+                            grad_spec[part, here, c * width:(c + 1) * width] = totals[part]
+                    yield
 
         staggered(UNITS, cols_of, rows_of)
         return carry
@@ -388,7 +501,7 @@
     grid_rows = count + 2 * rim
     grid_cols = width + rim
     units = kernels // UNIT
-    assert count == span and width == span and units % UNITS == 0 and units % SPECTRA_UNITS == 0 and kernels % UNIT == 0 and span == 128
+    assert count == span and width == span and units % UNITS == 0 and units % SPECTRA_UNITS == 0 and kernels % UNIT == 0 and span == 128 and UNIT == 4
 
     strips = lax.axis_size("row")
     assert strips % 2 == 0
@@ -420,6 +533,8 @@
         scratch_shapes=[
             pltpu.VMEM(kernel_taps.shape, f32),
             pltpu.VMEM(spec_shape, f32),
+            pltpu.VMEM((3, UNIT * count, 2 * width), bf16),
+            pltpu.VMEM((2, 3, 4, grid_rows, 2 * width), bf16),
             pltpu.SemaphoreType.DMA((units,)),
             pltpu.SemaphoreType.DMA((units,)),
         ],
@@ -446,6 +561,10 @@
             pltpu.VMEM((GROUPS, 2, count, width), f32),
             pltpu.VMEM((2, grid_rows, 2 * grid_cols), f32),
             pltpu.VMEM(tables.shape, bf16),
+            pltpu.VMEM((2, 3, UNIT * count, 2 * width), bf16),
+            pltpu.VMEM((2, 3, 4, grid_rows, 2 * width), bf16),
+            pltpu.VMEM((2, 3, 4, count, 2 * width), f32),
+            pltpu.VMEM((3, 2 * count, width), f32),
             pltpu.SemaphoreType.DMA((units,)),
             pltpu.SemaphoreType.DMA,
             pltpu.SemaphoreType.DMA,

time: 39.9 us -> 41.4 us (1.038)
  Pallas kernels: 28.5 us -> 30 us
    pallas_call x1, Pallas kernels: 18.6 us -> 19.9 us  [on_device(): pl.pallas_call(functools.partial(main_body, layout=layout), out_shape=[ja...]
where the time goes in v17:
time: 41.4 us; the launch traced here: 41.1 us
  Pallas kernels  30 us (72%)
  starting transfers between devices  7.37 us (18%)
  waiting for transfers between devices  2.96 us (7%)
  between operations  0.76 us (2%)
    pallas_call x1, Pallas kernels, on_device(): pl.pallas_call(functools.partial(main_body, layout=layout), out_shape=[ja...  19.9 us
    pallas_call x1, Pallas kernels, on_device(): pl.pallas_call(spectra_body, out_shape=jax.ShapeDtypeStruct(spec_shape, f...  9.36 us
    ppermute x1, starting transfers between devices, on_device(): far_in = lax.ppermute(far_rim, 'row', far_pairs)  3.51 us
    ppermute x1, starting transfers between devices, on_device(): far = lax.ppermute(mask_field, 'row', far_pairs)  3.05 us
    ppermute x1, waiting for transfers between devices, on_device(): far_in = lax.ppermute(far_rim, 'row', far_pairs)  2.95 us
  transfers between devices with their start and end apart: 4, of which 1 were waited for; matrix products, arithmetic and copies ran while one was open for 0% of the time, Pallas kernels for 23%

profile of v17, /device:TPU:21, one launch (start us, length us, event | category | flops | bytes accessed | tf_op | source)
XLA Modules:
  0.0 41.1 jit_solution(15721927548750294378)
XLA Ops:
  0.6 0.0 copy-start
  0.6 0.0 copy-start.3
  0.7 0.0 copy-start.2
  0.7 0.0 copy-start.1
  0.7 0.7 %collective-permute-start = (f32[2,128,128]{2,1,0:T(8,128)}, f32[2,128,128]{2,1,0:T(8,128)S(1)}, u32[]{:S(2)}, u32[]{:S(2)}) collective-permute-start(f32[2,128,128]{2,1,0:T(8,128)} %own.1), channel_id=1, source_target_pairs={{0,1},{1,0},{2,3},{3,2},{4,5},{5,4},{6,7},{7,6},{8,9},{9,8},{10,11... | collective-permute-start | bytes 393224 | tf_op jit(solution)/shard_map/ppermute | solution.py:511
  1.4 3.0 %collective-permute-start.1 = (f32[2,128,128]{2,1,0:T(8,128)}, f32[2,128,128]{2,1,0:T(8,128)S(1)}, u32[]{:S(2)}, u32[]{:S(2)}) collective-permute-start(f32[2,128,128]{2,1,0:T(8,128)} %own.1), channel_id=1, source_target_pairs={{1,2},{2,1},{3,4},{4,3},{5,6},{6,5},{7,8},{8,7},{9,10},{10,9},{11,... | collective-permute-start | bytes 393224 | tf_op jit(solution)/shard_map/ppermute | solution.py:512
  4.5 9.4 %spectra.1.spec_far = f32[6,2,256,768]{3,2,1,0:T(8,128)} custom-call(s32[24]{0:T(128)} %radii.1, f32[24,2,128,128]{3,2,1,0:T(8,128)} %taps_far.1, bf16[256,512]{1,0:T(8,128)(2,1)} %constant.10.clone.row_ref, bf16[384,256]{1,0:T(8,128)(2,1)} %constant.11.clone.col_ref), custom_call_target="tpu_custom_call" | custom-call | flops 17999998976 | bytes 14000000 | tf_op jit(solution)/shard_map/spectra/pallas_call | solution.py:528
  13.8 0.0 collective-permute-done.near
  13.8 0.0 collective-permute-done.1.far
  13.9 0.0 copy-done
  13.9 0.0 copy-done.3
  13.9 0.0 copy-done.2
  13.9 0.0 copy-done.1
  13.9 19.9 %fields.1 = (f32[3,128,128]{2,1,0:T(8,128)}, f32[2,128,128]{2,1,0:T(8,128)S(1)}, f32[2,64,128]{2,1,0:T(8,128)S(1)}, f32[2,64,128]{2,1,0:T(8,128)S(1)}) custom-call(s32[24]{0:T(128)S(1)} %copy-done.2, f32[24]{0:T(128)S(1)} %copy-done.3, s32[1]{0:T(128)} %bitcast.place, f32[2,128,128]{2,1,0:T(8,128)S(1)} %copy-done, ...), custom_call_target="tpu_custom_call" | custom-call | tf_op jit(solution)/shard_map/fields/pallas_call | solution.py:546
  33.8 0.1 collective-permute-start.2
  33.9 3.5 %collective-permute-start.3 = (f32[2,64,128]{2,1,0:T(8,128)S(1)}, f32[2,64,128]{2,1,0:T(8,128)S(1)}, u32[]{:S(2)}, u32[]{:S(2)}) collective-permute-start(f32[2,64,128]{2,1,0:T(8,128)S(1)} %get-tuple-element.9), channel_id=1, source_target_pairs={{1,2},{2,1},{3,4},{4,3},{5,6},{6,5},{7,8},{8,7},{9,10},{10,9},{11,... | collective-permute-start | bytes 196616 | tf_op jit(solution)/shard_map/ppermute | solution.py:577
  37.4 0.0 collective-permute-done.2.near
  37.4 3.0 %collective-permute-done.3.far = f32[2,64,128]{2,1,0:T(8,128)S(1)} collective-permute-done((f32[2,64,128]{2,1,0:T(8,128)S(1)}, f32[2,64,128]{2,1,0:T(8,128)S(1)}, u32[]{:S(2)}, u32[]{:S(2)}) %collective-permute-start.3) | collective-permute-done | bytes 65568 | tf_op jit(solution)/shard_map/ppermute | solution.py:577
  40.4 0.7 %join.1 = f32[2,128,128]{2,1,0:T(8,128)} custom-call(s32[1]{0:T(128)} %bitcast.place, f32[2,128,128]{2,1,0:T(8,128)S(1)} %get-tuple-element.7.own, f32[2,64,128]{2,1,0:T(8,128)S(1)} %collective-permute-done.2.near, f32[2,64,128]{2,1,0:T(8,128)S(1)} %collective-permute-done.3.far), custom_call_target="tpu_custom_call" | custom-call | tf_op jit(solution)/shard_map/join/pallas_call | solution.py:578
Async XLA Ops:
  0.6 13.2 %copy-start = (f32[2,128,128]{2,1,0:T(8,128)S(1)}, f32[2,128,128]{2,1,0:T(8,128)}, u32[]{:S(2)}) copy-start(f32[2,128,128]{2,1,0:T(8,128)} %own.1) | copy-start | bytes 393220
  0.6 13.2 %copy-start.3 = (f32[24]{0:T(128)S(1)}, f32[24]{0:T(128)}, u32[]{:S(2)}) copy-start(f32[24]{0:T(128)} %weight.1) | copy-start | bytes 292
  0.7 13.2 %copy-start.2 = (s32[24]{0:T(128)S(1)}, s32[24]{0:T(128)}, u32[]{:S(2)}) copy-start(s32[24]{0:T(128)} %group.1) | copy-start | bytes 292
  0.7 13.2 %copy-start.1 = (s32[128,128]{1,0:T(8,128)S(1)}, s32[128,128]{1,0:T(8,128)}, u32[]{:S(2)}) copy-start(s32[128,128]{1,0:T(8,128)} %target.1) | copy-start | bytes 196612
  0.7 13.2 %collective-permute-start = (f32[2,128,128]{2,1,0:T(8,128)}, f32[2,128,128]{2,1,0:T(8,128)S(1)}, u32[]{:S(2)}, u32[]{:S(2)}) collective-permute-start(f32[2,128,128]{2,1,0:T(8,128)} %own.1), channel_id=1, source_target_pairs={{0,1},{1,0},{2,3},{3,2},{4,5},{5,4},{6,7},{7,6},{8,9},{9,8},{10,11... | collective-permute-start | bytes 393224 | tf_op jit(solution)/shard_map/ppermute | solution.py:511
  1.4 12.4 %collective-permute-start.1 = (f32[2,128,128]{2,1,0:T(8,128)}, f32[2,128,128]{2,1,0:T(8,128)S(1)}, u32[]{:S(2)}, u32[]{:S(2)}) collective-permute-start(f32[2,128,128]{2,1,0:T(8,128)} %own.1), channel_id=1, source_target_pairs={{1,2},{2,1},{3,4},{4,3},{5,6},{6,5},{7,8},{8,7},{9,10},{10,9},{11,... | collective-permute-start | bytes 393224 | tf_op jit(solution)/shard_map/ppermute | solution.py:512
  33.8 3.6 %collective-permute-start.2 = (f32[2,64,128]{2,1,0:T(8,128)S(1)}, f32[2,64,128]{2,1,0:T(8,128)S(1)}, u32[]{:S(2)}, u32[]{:S(2)}) collective-permute-start(f32[2,64,128]{2,1,0:T(8,128)S(1)} %get-tuple-element.8), channel_id=1, source_target_pairs={{0,1},{1,0},{2,3},{3,2},{4,5},{5,4},{6,7},{7,6},{8,9},{9,8},{10,11... | collective-permute-start | bytes 196616 | tf_op jit(solution)/shard_map/ppermute | solution.py:576
  33.9 6.5 %collective-permute-start.3 = (f32[2,64,128]{2,1,0:T(8,128)S(1)}, f32[2,64,128]{2,1,0:T(8,128)S(1)}, u32[]{:S(2)}, u32[]{:S(2)}) collective-permute-start(f32[2,64,128]{2,1,0:T(8,128)S(1)} %get-tuple-element.9), channel_id=1, source_target_pairs={{1,2},{2,1},{3,4},{4,3},{5,6},{6,5},{7,8},{8,7},{9,10},{10,9},{11,... | collective-permute-start | bytes 196616 | tf_op jit(solution)/shard_map/ppermute | solution.py:577

commit v18 on v15

--- a/solution.py
+++ b/solution.py
@@ -15,8 +15,8 @@
 STEEPNESS = 1.0
 THRESHOLD = 2.0
 UNIT = 4
-SPECTRA_UNITS = 6
-UNITS = 3
+SPECTRA_UNITS = 3
+UNITS = 2
 PIECE = 256
 TURN = math.sqrt(0.75)
 
@@ -40,9 +40,14 @@
     return np.block([[cos, sin], [-sin, cos]])
 
 
+def rounded(x):
+    half = jnp.full(x.shape, 0x8000, jnp.uint32)
+    return pltpu.stochastic_round(x, half, target_dtype=bf16)
+
+
 def split(x):
-    high = x.astype(bf16)
-    low = (x - high.astype(f32)).astype(bf16)
+    high = rounded(x)
+    low = rounded(x - high.astype(f32))
     return high, low
 
 

time: 39.9 us -> 40.6 us (1.018)
  Pallas kernels: 28.5 us -> 29.2 us
    pallas_call x1, Pallas kernels: 9.2 us -> 9.7 us  [on_device(): pl.pallas_call(spectra_body, out_shape=jax.ShapeDtypeStruct(spec_shape, f...]
  transfers between devices with their start and end apart: 4 -> 4, of which waited for: 1 -> 1; matrix products, arithmetic and copies ran while one was open for 0% -> 0% of each run, Pallas kernels for 23% -> 24%
where the time goes in v18:
time: 40.6 us; the launch traced here: 40.3 us
  Pallas kernels  29.2 us (72%)
  starting transfers between devices  7.36 us (18%)
  waiting for transfers between devices  2.97 us (7%)
  between operations  0.76 us (2%)
    pallas_call x1, Pallas kernels, on_device(): pl.pallas_call(functools.partial(main_body, layout=layout), out_shape=[ja...  18.8 us
    pallas_call x1, Pallas kernels, on_device(): pl.pallas_call(spectra_body, out_shape=jax.ShapeDtypeStruct(spec_shape, f...  9.7 us
    ppermute x1, starting transfers between devices, on_device(): far_in = lax.ppermute(far_rim, 'row', far_pairs)  3.5 us
    ppermute x1, starting transfers between devices, on_device(): far = lax.ppermute(mask_field, 'row', far_pairs)  3.05 us
    ppermute x1, waiting for transfers between devices, on_device(): far_in = lax.ppermute(far_rim, 'row', far_pairs)  2.96 us
  transfers between devices with their start and end apart: 4, of which 1 were waited for; matrix products, arithmetic and copies ran while one was open for 0% of the time, Pallas kernels for 24%

profile of v18, /device:TPU:21, one launch (start us, length us, event | category | flops | bytes accessed | tf_op | source)
XLA Modules:
  0.0 40.3 jit_solution(1980135998615409850)
XLA Ops:
  0.6 0.0 copy-start
  0.6 0.0 copy-start.3
  0.7 0.0 copy-start.2
  0.7 0.0 copy-start.1
  0.7 0.7 %collective-permute-start = (f32[2,128,128]{2,1,0:T(8,128)}, f32[2,128,128]{2,1,0:T(8,128)S(1)}, u32[]{:S(2)}, u32[]{:S(2)}) collective-permute-start(f32[2,128,128]{2,1,0:T(8,128)} %own.1), channel_id=1, source_target_pairs={{0,1},{1,0},{2,3},{3,2},{4,5},{5,4},{6,7},{7,6},{8,9},{9,8},{10,11... | collective-permute-start | bytes 393224 | tf_op jit(solution)/shard_map/ppermute | solution.py:403
  1.4 3.0 %collective-permute-start.1 = (f32[2,128,128]{2,1,0:T(8,128)}, f32[2,128,128]{2,1,0:T(8,128)S(1)}, u32[]{:S(2)}, u32[]{:S(2)}) collective-permute-start(f32[2,128,128]{2,1,0:T(8,128)} %own.1), channel_id=1, source_target_pairs={{1,2},{2,1},{3,4},{4,3},{5,6},{6,5},{7,8},{8,7},{9,10},{10,9},{11,... | collective-permute-start | bytes 393224 | tf_op jit(solution)/shard_map/ppermute | solution.py:404
  4.5 9.7 %spectra.1.spec_far = f32[6,2,256,768]{3,2,1,0:T(8,128)} custom-call(s32[24]{0:T(128)} %radii.1, f32[24,2,128,128]{3,2,1,0:T(8,128)} %taps_far.1, bf16[256,512]{1,0:T(8,128)(2,1)} %constant.10.clone.row_ref, bf16[384,256]{1,0:T(8,128)(2,1)} %constant.11.clone.col_ref), custom_call_target="tpu_custom_call" | custom-call | flops 17999998976 | bytes 14000000 | tf_op jit(solution)/shard_map/spectra/pallas_call | solution.py:420
  14.2 0.0 collective-permute-done.near
  14.2 0.0 collective-permute-done.1.far
  14.2 0.0 copy-done
  14.2 0.0 copy-done.3
  14.2 0.0 copy-done.2
  14.2 0.0 copy-done.1
  14.2 18.8 %fields.1 = (f32[3,128,128]{2,1,0:T(8,128)}, f32[2,128,128]{2,1,0:T(8,128)S(1)}, f32[2,64,128]{2,1,0:T(8,128)S(1)}, f32[2,64,128]{2,1,0:T(8,128)S(1)}) custom-call(s32[24]{0:T(128)S(1)} %copy-done.2, f32[24]{0:T(128)S(1)} %copy-done.3, s32[1]{0:T(128)} %bitcast.place, f32[2,128,128]{2,1,0:T(8,128)S(1)} %copy-done, ...), custom_call_target="tpu_custom_call" | custom-call | tf_op jit(solution)/shard_map/fields/pallas_call | solution.py:436
  33.0 0.1 collective-permute-start.2
  33.1 3.5 %collective-permute-start.3 = (f32[2,64,128]{2,1,0:T(8,128)S(1)}, f32[2,64,128]{2,1,0:T(8,128)S(1)}, u32[]{:S(2)}, u32[]{:S(2)}) collective-permute-start(f32[2,64,128]{2,1,0:T(8,128)S(1)} %get-tuple-element.9), channel_id=1, source_target_pairs={{1,2},{2,1},{3,4},{4,3},{5,6},{6,5},{7,8},{8,7},{9,10},{10,9},{11,... | collective-permute-start | bytes 196616 | tf_op jit(solution)/shard_map/ppermute | solution.py:463
  36.6 0.0 collective-permute-done.2.near
  36.6 3.0 %collective-permute-done.3.far = f32[2,64,128]{2,1,0:T(8,128)S(1)} collective-permute-done((f32[2,64,128]{2,1,0:T(8,128)S(1)}, f32[2,64,128]{2,1,0:T(8,128)S(1)}, u32[]{:S(2)}, u32[]{:S(2)}) %collective-permute-start.3) | collective-permute-done | bytes 65568 | tf_op jit(solution)/shard_map/ppermute | solution.py:463
  39.6 0.7 %join.1 = f32[2,128,128]{2,1,0:T(8,128)} custom-call(s32[1]{0:T(128)} %bitcast.place, f32[2,128,128]{2,1,0:T(8,128)S(1)} %get-tuple-element.7.own, f32[2,64,128]{2,1,0:T(8,128)S(1)} %collective-permute-done.2.near, f32[2,64,128]{2,1,0:T(8,128)S(1)} %collective-permute-done.3.far), custom_call_target="tpu_custom_call" | custom-call | tf_op jit(solution)/shard_map/join/pallas_call | solution.py:464
Async XLA Ops:
  0.6 13.6 %copy-start = (f32[2,128,128]{2,1,0:T(8,128)S(1)}, f32[2,128,128]{2,1,0:T(8,128)}, u32[]{:S(2)}) copy-start(f32[2,128,128]{2,1,0:T(8,128)} %own.1) | copy-start | bytes 393220
  0.6 13.6 %copy-start.3 = (f32[24]{0:T(128)S(1)}, f32[24]{0:T(128)}, u32[]{:S(2)}) copy-start(f32[24]{0:T(128)} %weight.1) | copy-start | bytes 292
  0.7 13.6 %copy-start.2 = (s32[24]{0:T(128)S(1)}, s32[24]{0:T(128)}, u32[]{:S(2)}) copy-start(s32[24]{0:T(128)} %group.1) | copy-start | bytes 292
  0.7 13.6 %copy-start.1 = (s32[128,128]{1,0:T(8,128)S(1)}, s32[128,128]{1,0:T(8,128)}, u32[]{:S(2)}) copy-start(s32[128,128]{1,0:T(8,128)} %target.1) | copy-start | bytes 196612
  0.7 13.5 %collective-permute-start = (f32[2,128,128]{2,1,0:T(8,128)}, f32[2,128,128]{2,1,0:T(8,128)S(1)}, u32[]{:S(2)}, u32[]{:S(2)}) collective-permute-start(f32[2,128,128]{2,1,0:T(8,128)} %own.1), channel_id=1, source_target_pairs={{0,1},{1,0},{2,3},{3,2},{4,5},{5,4},{6,7},{7,6},{8,9},{9,8},{10,11... | collective-permute-start | bytes 393224 | tf_op jit(solution)/shard_map/ppermute | solution.py:403
  1.4 12.8 %collective-permute-start.1 = (f32[2,128,128]{2,1,0:T(8,128)}, f32[2,128,128]{2,1,0:T(8,128)S(1)}, u32[]{:S(2)}, u32[]{:S(2)}) collective-permute-start(f32[2,128,128]{2,1,0:T(8,128)} %own.1), channel_id=1, source_target_pairs={{1,2},{2,1},{3,4},{4,3},{5,6},{6,5},{7,8},{8,7},{9,10},{10,9},{11,... | collective-permute-start | bytes 393224 | tf_op jit(solution)/shard_map/ppermute | solution.py:404
  33.0 3.6 %collective-permute-start.2 = (f32[2,64,128]{2,1,0:T(8,128)S(1)}, f32[2,64,128]{2,1,0:T(8,128)S(1)}, u32[]{:S(2)}, u32[]{:S(2)}) collective-permute-start(f32[2,64,128]{2,1,0:T(8,128)S(1)} %get-tuple-element.8), channel_id=1, source_target_pairs={{0,1},{1,0},{2,3},{3,2},{4,5},{5,4},{6,7},{7,6},{8,9},{9,8},{10,11... | collective-permute-start | bytes 196616 | tf_op jit(solution)/shard_map/ppermute | solution.py:462
  33.1 6.5 %collective-permute-start.3 = (f32[2,64,128]{2,1,0:T(8,128)S(1)}, f32[2,64,128]{2,1,0:T(8,128)S(1)}, u32[]{:S(2)}, u32[]{:S(2)}) collective-permute-start(f32[2,64,128]{2,1,0:T(8,128)S(1)} %get-tuple-element.9), channel_id=1, source_target_pairs={{1,2},{2,1},{3,4},{4,3},{5,6},{6,5},{7,8},{8,7},{9,10},{10,9},{11,... | collective-permute-start | bytes 196616 | tf_op jit(solution)/shard_map/ppermute | solution.py:463

commit v19 on v15

--- a/solution.py
+++ b/solution.py
@@ -15,8 +15,8 @@
 STEEPNESS = 1.0
 THRESHOLD = 2.0
 UNIT = 4
-SPECTRA_UNITS = 6
-UNITS = 3
+SPECTRA_UNITS = 3
+UNITS = 2
 PIECE = 256
 TURN = math.sqrt(0.75)
 
@@ -38,6 +38,14 @@
     angle = 2.0 * math.pi * ((f * n) % freqs) / freqs
     cos, sin = np.cos(angle), np.sin(angle)
     return np.block([[cos, sin], [-sin, cos]])
+
+
+def for_two(table):
+    half = table.shape[0] // 2
+    both = np.eye(2)
+    return np.block([
+        [np.kron(both, table[i:i + half, j:j + half]) for j in (0, half)] for i in (0, half)
+    ])
 
 
 def split(x):
@@ -121,63 +129,56 @@
     return [(re[at:at + quarter], im[at:at + quarter]) for at in range(0, re.shape[0], quarter)]
 
 
-def lane_turned(x):
-    return swap(x) * jnp.where(first_half(x), TURN, -TURN)
-
-
-def col_products(planes, table):
-    rows = planes[0][0].shape[0]
-    depth = table.shape[0] // 3
-    out = [[] for _ in planes]
+def scaled(x, by):
+    return x[0] * by, x[1] * by
+
+
+def col_products(pairs, table):
+    rows, lanes = pairs[0][0][0].shape
+    depth = 2 * lanes
+    out = [[] for _ in pairs]
     for c in range(3):
-        high, low = split(jnp.concatenate([plane[c] for plane in planes], axis=0))
-        right = table[c * depth:(c + 1) * depth]
-        found = dot(jnp.concatenate([high, low], axis=1), jnp.concatenate([right, right], axis=0))
-        found = found[:, :depth] + found[:, depth:]
-        for k in range(len(planes)):
-            out[k].append(found[k * rows:(k + 1) * rows])
+        x = jnp.concatenate([jnp.concatenate(pair[c], axis=1) for pair in pairs], axis=0)
+        high, low = split(x)
+        t_high, t_low = table[2 * c * depth:(2 * c + 1) * depth], table[(2 * c + 1) * depth:(2 * c + 2) * depth]
+        both = dot(jnp.concatenate([high, low], axis=0), t_high)
+        found = both[:x.shape[0]] + (both[x.shape[0]:] + dot(high, t_low))
+        for k in range(len(pairs)):
+            mine = found[k * rows:(k + 1) * rows]
+            out[k].append((mine[:, :lanes], mine[:, lanes:]))
     return out
 
 
-def to_col_freqs(planes, table, shifted=False):
-    folded = []
-    for left, right in planes:
-        if shifted:
-            left, right = right, left
-        near, far = left - 0.5 * right, lane_turned(right)
-        one, two = near + far, near - far
-        folded.append([left + right, two, one] if shifted else [left + right, one, two])
-    return col_products(folded, table)
-
-
-def from_col_freqs(planes, table, shifted=False):
-    out = []
-    for v in col_products(planes, table):
-        total, far = v[1] + v[2], lane_turned(v[1] - v[2])
-        whole, part = v[0] + total, v[0] - 0.5 * total
-        out.append((part + far, whole) if shifted else (whole, part - far))
-    return out
-
-
-def pairs_apart(planes):
-    re, im = [], []
-    for k in range(0, len(planes), 2):
-        for x, y in zip(planes[k], planes[k + 1]):
-            r, i = exchange(x, y)
-            re.append(r)
-            im.append(i)
-    return jnp.concatenate(re, axis=1), jnp.concatenate(im, axis=1)
-
-
-def pairs_together(re, im, width):
-    planes = []
-    for at in range(0, re.shape[1], 3 * width):
-        both = [
-            exchange(re[:, at + c * width:at + (c + 1) * width], im[:, at + c * width:at + (c + 1) * width])
-            for c in range(3)
-        ]
-        planes += [[x for x, _ in both], [y for _, y in both]]
-    return planes
+def fold_cols(left, right, shifted=False):
+    if shifted:
+        left, right = right, left
+    near, far = minus(left, scaled(right, 0.5)), scaled(turned(right, -1), TURN)
+    one, two = plus(near, far), minus(near, far)
+    return [plus(left, right), two, one] if shifted else [plus(left, right), one, two]
+
+
+def unfold_cols(v, shifted=False):
+    total, far = plus(v[1], v[2]), scaled(turned(minus(v[1], v[2]), -1), TURN)
+    whole, part = plus(v[0], total), minus(v[0], scaled(total, 0.5))
+    return (plus(part, far), whole) if shifted else (whole, minus(part, far))
+
+
+def to_col_freqs(pairs, table, shifted=False):
+    found = col_products([fold_cols(*pair, shifted) for pair in pairs], table)
+    return [jnp.concatenate([x[part] for pair in found for x in pair], axis=1) for part in range(2)]
+
+
+def from_col_freqs(both, table, lanes, shifted=False):
+    pairs = [
+        [tuple(x[:, at + c * lanes:at + (c + 1) * lanes] for x in both) for c in range(3)]
+        for at in range(0, both[0].shape[1], 3 * lanes)
+    ]
+    return [unfold_cols(v, shifted) for v in col_products(pairs, table)]
+
+
+def shared(x, y):
+    re, im = [exchange(x[part], y[part]) for part in range(2)]
+    return (re[0], im[0]), (re[1], im[1])
 
 
 def loop(steps, body):
@@ -224,8 +225,8 @@
             for j in range(UNIT):
                 k = u * UNIT + j
                 inside = reach < radii[k]
-                planes.append(exchange(*[jnp.where(inside, taps[k, c], 0.0) for c in range(2)]))
-            return pairs_apart(to_col_freqs(planes, col_fwd))
+                planes.append([jnp.where(inside, taps[k, c], 0.0) for c in range(2)])
+            return to_col_freqs([shared(planes[j], planes[j + 1]) for j in range(0, UNIT, 2)], col_fwd)
 
         def rows_of(p, both):
             u = i * SPECTRA_UNITS + p
@@ -277,8 +278,7 @@
         above = jnp.where(odd, near[c, count - rim:], far[c, count - rim:])
         below = jnp.where(odd, far[c, :rim], near[c, :rim])
         mask.append(jnp.concatenate([own[c, rim:], below, above, own[c, :rim]], axis=0))
-    plane, = to_col_freqs([exchange(*mask)], col_fwd, shifted=True)
-    both = pairs_apart([plane, plane])
+    both = to_col_freqs([shared(mask, mask)], col_fwd, shifted=True)
     for c, found in enumerate(to_row_freqs(quarters_of(*both, rim), row_fwd)):
         for part in range(2):
             mask_spec[part, c * rim:(c + 1) * rim] = found[part]
@@ -298,13 +298,16 @@
 
         def cols_of(p, both):
             u = i * UNITS + p
-            found = from_col_freqs(pairs_together(*both, width), col_inv)
-            for j in range(UNIT):
-                k = u * UNIT + j
-                for side in range(2):
-                    x = found[j][side]
-                    field[k, side] = x
-                    slopes[group[k], side] = slopes[group[k], side] + weight[k] * (x * x)
+            for pair, sides in enumerate(from_col_freqs(both, col_inv, width)):
+                first = first_half(sides[0][0])
+                for side, (re, im) in enumerate(sides):
+                    at = u * (UNIT // 2) + pair
+                    field[at, side, 0], field[at, side, 1] = re, im
+                    power = re * re + im * im
+                    for j in range(2):
+                        k = u * UNIT + 2 * pair + j
+                        mine = jnp.where(first, power, 0.0) if j == 0 else jnp.where(first, 0.0, power)
+                        slopes[group[k], side] = slopes[group[k], side] + weight[k] * mine
 
         staggered(UNITS, rows_of, cols_of)
         return carry
@@ -324,11 +327,19 @@
     def backward(i, carry):
         def cols_of(p):
             u = i * UNITS + p
-            planes = []
-            for j in range(UNIT):
-                k = u * UNIT + j
-                planes.append([field[k, side] * ((2.0 * weight[k]) * slopes[group[k], side]) for side in range(2)])
-            return pairs_apart(to_col_freqs(planes, col_fwd))
+            pairs = []
+            for pair in range(UNIT // 2):
+                at = u * (UNIT // 2) + pair
+                sides = []
+                for side in range(2):
+                    one, two = [
+                        (2.0 * weight[u * UNIT + 2 * pair + j]) * slopes[group[u * UNIT + 2 * pair + j], side]
+                        for j in range(2)
+                    ]
+                    factor = jnp.where(first_half(one), one, two)
+                    sides.append((field[at, side, 0] * factor, field[at, side, 1] * factor))
+                pairs.append(sides)
+            return to_col_freqs(pairs, col_fwd)
 
         def rows_of(p, both):
             u = i * UNITS + p
@@ -351,10 +362,9 @@
     classes = [tuple(grad_spec[part, c * rim:(c + 1) * rim] for part in range(2)) for c in range(4)]
     quarters = from_row_freqs(classes, row_inv, (2, 3, 0, 1))
     re, im = [jnp.concatenate([x[part] for x in quarters], axis=0) for part in range(2)]
-    first, second = pairs_together(re, im, width)
-    plane = [x + y for x, y in zip(first, second)]
-    halves_found, = from_col_freqs([plane], col_inv, shifted=True)
-    for c, full in enumerate(exchange(*halves_found)):
+    (left, right), = from_col_freqs((re, im), col_inv, width, shifted=True)
+    for c in range(2):
+        full = jnp.where(first_half(left[c]), left[c] + swap(left[c]), right[c] + swap(right[c]))
         rise, fall = full[:rim], full[rim + count:]
         near_rim[c] = jnp.where(odd, rise, fall)
         far_rim[c] = jnp.where(odd, fall, rise)
@@ -404,8 +414,8 @@
     col_classes = [class_table(grid_cols, rim, c, 3) for c in range(3)]
     row_fwd = np.concatenate([halves(t, 0) for t in row_classes], axis=1)
     row_inv = np.concatenate([halves(t.T * scale, 0) for t in row_classes], axis=1)
-    col_fwd = np.concatenate([halves(t.T, 1) for t in col_classes], axis=0)
-    col_inv = np.concatenate([halves(t, 1) for t in col_classes], axis=0)
+    col_fwd = np.concatenate([halves(for_two(t.T), 0) for t in col_classes], axis=0)
+    col_inv = np.concatenate([halves(for_two(t), 0) for t in col_classes], axis=0)
     tables, layout = stacked({"row_fwd": row_fwd, "row_inv": row_inv, "col_fwd": col_fwd, "col_inv": col_inv})
 
     smem = pl.BlockSpec(memory_space=pltpu.SMEM)
@@ -440,7 +450,7 @@
         out_specs=[hbm] + [vmem] * 3,
         scratch_shapes=[
             pltpu.VMEM(spec_shape, f32),
-            pltpu.VMEM((kernels, 2, count, width), f32),
+            pltpu.VMEM((kernels // 2, 2, 2, count, width), f32),
             pltpu.VMEM((2, grid_rows, 2 * grid_cols), f32),
             pltpu.VMEM((GROUPS, count, width), f32),
             pltpu.VMEM((GROUPS, 2, count, width), f32),

time: 39.9 us -> 41.9 us (1.050)
  Pallas kernels: 28.5 us -> 30.5 us
    pallas_call x1, Pallas kernels: 9.2 us -> 10.3 us  [on_device(): pl.pallas_call(spectra_body, out_shape=jax.ShapeDtypeStruct(spec_shape, f...]
    pallas_call x1, Pallas kernels: 18.6 us -> 19.6 us  [on_device(): pl.pallas_call(functools.partial(main_body, layout=layout), out_shape=[ja...]
  transfers between devices with their start and end apart: 4 -> 4, of which waited for: 1 -> 1; matrix products, arithmetic and copies ran while one was open for 0% -> 0% of each run, Pallas kernels for 23% -> 25%
where the time goes in v19:
time: 41.9 us; the launch traced here: 41.6 us
  Pallas kernels  30.5 us (73%)
  starting transfers between devices  7.38 us (18%)
  waiting for transfers between devices  2.95 us (7%)
  between operations  0.76 us (2%)
    pallas_call x1, Pallas kernels, on_device(): pl.pallas_call(functools.partial(main_body, layout=layout), out_shape=[ja...  19.6 us
    pallas_call x1, Pallas kernels, on_device(): pl.pallas_call(spectra_body, out_shape=jax.ShapeDtypeStruct(spec_shape, f...  10.3 us
    ppermute x1, starting transfers between devices, on_device(): far_in = lax.ppermute(far_rim, 'row', far_pairs)  3.52 us
    ppermute x1, starting transfers between devices, on_device(): far = lax.ppermute(mask_field, 'row', far_pairs)  3.05 us
    ppermute x1, waiting for transfers between devices, on_device(): far_in = lax.ppermute(far_rim, 'row', far_pairs)  2.95 us
  transfers between devices with their start and end apart: 4, of which 1 were waited for; matrix products, arithmetic and copies ran while one was open for 0% of the time, Pallas kernels for 25%

profile of v19, /device:TPU:21, one launch (start us, length us, event | category | flops | bytes accessed | tf_op | source)
XLA Modules:
  0.0 41.6 jit_solution(13573857452726142056)
XLA Ops:
  0.6 0.0 copy-start
  0.6 0.0 copy-start.3
  0.7 0.0 copy-start.2
  0.7 0.0 copy-start.1
  0.7 0.7 %collective-permute-start = (f32[2,128,128]{2,1,0:T(8,128)}, f32[2,128,128]{2,1,0:T(8,128)S(1)}, u32[]{:S(2)}, u32[]{:S(2)}) collective-permute-start(f32[2,128,128]{2,1,0:T(8,128)} %own.1), channel_id=1, source_target_pairs={{0,1},{1,0},{2,3},{3,2},{4,5},{5,4},{6,7},{7,6},{8,9},{9,8},{10,11... | collective-permute-start | bytes 393224 | tf_op jit(solution)/shard_map/ppermute | solution.py:408
  1.4 3.0 %collective-permute-start.1 = (f32[2,128,128]{2,1,0:T(8,128)}, f32[2,128,128]{2,1,0:T(8,128)S(1)}, u32[]{:S(2)}, u32[]{:S(2)}) collective-permute-start(f32[2,128,128]{2,1,0:T(8,128)} %own.1), channel_id=1, source_target_pairs={{1,2},{2,1},{3,4},{4,3},{5,6},{6,5},{7,8},{8,7},{9,10},{10,9},{11,... | collective-permute-start | bytes 393224 | tf_op jit(solution)/shard_map/ppermute | solution.py:409
  4.5 10.3 %spectra.1.spec_far = f32[6,2,256,768]{3,2,1,0:T(8,128)} custom-call(s32[24]{0:T(128)} %radii.1, f32[24,2,128,128]{3,2,1,0:T(8,128)} %taps_far.1, bf16[256,512]{1,0:T(8,128)(2,1)} %constant.10.clone.row_ref, bf16[1536,256]{1,0:T(8,128)(2,1)} %constant.11.clone.col_ref), custom_call_target="tpu_custom_call" | custom-call | flops 17999998976 | bytes 14000000 | tf_op jit(solution)/shard_map/spectra/pallas_call | solution.py:425
  14.7 0.0 collective-permute-done.near
  14.7 0.0 collective-permute-done.1.far
  14.7 0.0 copy-done
  14.8 0.0 copy-done.3
  14.8 0.0 copy-done.2
  14.8 0.0 copy-done.1
  14.8 19.6 %fields.1 = (f32[3,128,128]{2,1,0:T(8,128)}, f32[2,128,128]{2,1,0:T(8,128)S(1)}, f32[2,64,128]{2,1,0:T(8,128)S(1)}, f32[2,64,128]{2,1,0:T(8,128)S(1)}) custom-call(s32[24]{0:T(128)S(1)} %copy-done.2, f32[24]{0:T(128)S(1)} %copy-done.3, s32[1]{0:T(128)} %bitcast.place, f32[2,128,128]{2,1,0:T(8,128)S(1)} %copy-done, ...), custom_call_target="tpu_custom_call" | custom-call | tf_op jit(solution)/shard_map/fields/pallas_call | solution.py:441
  34.4 0.1 collective-permute-start.2
  34.5 3.5 %collective-permute-start.3 = (f32[2,64,128]{2,1,0:T(8,128)S(1)}, f32[2,64,128]{2,1,0:T(8,128)S(1)}, u32[]{:S(2)}, u32[]{:S(2)}) collective-permute-start(f32[2,64,128]{2,1,0:T(8,128)S(1)} %get-tuple-element.9), channel_id=1, source_target_pairs={{1,2},{2,1},{3,4},{4,3},{5,6},{6,5},{7,8},{8,7},{9,10},{10,9},{11,... | collective-permute-start | bytes 196616 | tf_op jit(solution)/shard_map/ppermute | solution.py:468
  38.0 0.0 collective-permute-done.2.near
  38.0 2.9 %collective-permute-done.3.far = f32[2,64,128]{2,1,0:T(8,128)S(1)} collective-permute-done((f32[2,64,128]{2,1,0:T(8,128)S(1)}, f32[2,64,128]{2,1,0:T(8,128)S(1)}, u32[]{:S(2)}, u32[]{:S(2)}) %collective-permute-start.3) | collective-permute-done | bytes 65568 | tf_op jit(solution)/shard_map/ppermute | solution.py:468
  40.9 0.7 %join.1 = f32[2,128,128]{2,1,0:T(8,128)} custom-call(s32[1]{0:T(128)} %bitcast.place, f32[2,128,128]{2,1,0:T(8,128)S(1)} %get-tuple-element.7.own, f32[2,64,128]{2,1,0:T(8,128)S(1)} %collective-permute-done.2.near, f32[2,64,128]{2,1,0:T(8,128)S(1)} %collective-permute-done.3.far), custom_call_target="tpu_custom_call" | custom-call | tf_op jit(solution)/shard_map/join/pallas_call | solution.py:469
Async XLA Ops:
  0.6 14.1 %copy-start = (f32[2,128,128]{2,1,0:T(8,128)S(1)}, f32[2,128,128]{2,1,0:T(8,128)}, u32[]{:S(2)}) copy-start(f32[2,128,128]{2,1,0:T(8,128)} %own.1) | copy-start | bytes 393220
  0.6 14.1 %copy-start.3 = (f32[24]{0:T(128)S(1)}, f32[24]{0:T(128)}, u32[]{:S(2)}) copy-start(f32[24]{0:T(128)} %weight.1) | copy-start | bytes 292
  0.7 14.1 %copy-start.2 = (s32[24]{0:T(128)S(1)}, s32[24]{0:T(128)}, u32[]{:S(2)}) copy-start(s32[24]{0:T(128)} %group.1) | copy-start | bytes 292
  0.7 14.1 %copy-start.1 = (s32[128,128]{1,0:T(8,128)S(1)}, s32[128,128]{1,0:T(8,128)}, u32[]{:S(2)}) copy-start(s32[128,128]{1,0:T(8,128)} %target.1) | copy-start | bytes 196612
  0.7 14.1 %collective-permute-start = (f32[2,128,128]{2,1,0:T(8,128)}, f32[2,128,128]{2,1,0:T(8,128)S(1)}, u32[]{:S(2)}, u32[]{:S(2)}) collective-permute-start(f32[2,128,128]{2,1,0:T(8,128)} %own.1), channel_id=1, source_target_pairs={{0,1},{1,0},{2,3},{3,2},{4,5},{5,4},{6,7},{7,6},{8,9},{9,8},{10,11... | collective-permute-start | bytes 393224 | tf_op jit(solution)/shard_map/ppermute | solution.py:408
  1.4 13.3 %collective-permute-start.1 = (f32[2,128,128]{2,1,0:T(8,128)}, f32[2,128,128]{2,1,0:T(8,128)S(1)}, u32[]{:S(2)}, u32[]{:S(2)}) collective-permute-start(f32[2,128,128]{2,1,0:T(8,128)} %own.1), channel_id=1, source_target_pairs={{1,2},{2,1},{3,4},{4,3},{5,6},{6,5},{7,8},{8,7},{9,10},{10,9},{11,... | collective-permute-start | bytes 393224 | tf_op jit(solution)/shard_map/ppermute | solution.py:409
  34.4 3.6 %collective-permute-start.2 = (f32[2,64,128]{2,1,0:T(8,128)S(1)}, f32[2,64,128]{2,1,0:T(8,128)S(1)}, u32[]{:S(2)}, u32[]{:S(2)}) collective-permute-start(f32[2,64,128]{2,1,0:T(8,128)S(1)} %get-tuple-element.8), channel_id=1, source_target_pairs={{0,1},{1,0},{2,3},{3,2},{4,5},{5,4},{6,7},{7,6},{8,9},{9,8},{10,11... | collective-permute-start | bytes 196616 | tf_op jit(solution)/shard_map/ppermute | solution.py:467
  34.5 6.5 %collective-permute-start.3 = (f32[2,64,128]{2,1,0:T(8,128)S(1)}, f32[2,64,128]{2,1,0:T(8,128)S(1)}, u32[]{:S(2)}, u32[]{:S(2)}) collective-permute-start(f32[2,64,128]{2,1,0:T(8,128)S(1)} %get-tuple-element.9), channel_id=1, source_target_pairs={{1,2},{2,1},{3,4},{4,3},{5,6},{6,5},{7,8},{8,7},{9,10},{10,9},{11,... | collective-permute-start | bytes 196616 | tf_op jit(solution)/shard_map/ppermute | solution.py:468

commit v20 on v13

--- a/solution.py
+++ b/solution.py
@@ -181,30 +181,40 @@
     return pltpu.roll(x, x.shape[1] // 2, 1)
 
 
-def spectra_body(radii, taps_far, row_ref, head_ref, tail_ref, spec_far, taps, spec, in_sems, out_sems):
+def spectra_body(radii, taps_far, row_far, head_far, tail_far, spec_far, taps, spec, row_ref, head_ref, tail_ref, in_sems, out_sems, table_sems):
     kernels, _, span, _ = taps.shape
-    row_fwd, head, tail = row_ref[...], head_ref[...], tail_ref[...]
-    steps = in_sems.shape[0]
-    batch = kernels // steps
+    batch = BATCH
+    steps = kernels // batch
+    moves = [
+        pltpu.make_async_copy(far, here, table_sems.at[i])
+        for i, (far, here) in enumerate([(row_far, row_ref), (head_far, head_ref), (tail_far, tail_ref)])
+    ]
 
     def fetch(i):
-        here = pl.ds(i * batch, batch)
+        here = pl.ds(2 * i, 2)
         return pltpu.make_async_copy(taps_far.at[here], taps.at[here], in_sems.at[i])
 
     def put(i):
         here = pl.ds(2 * i, 2)
         return pltpu.make_async_copy(spec.at[here], spec_far.at[here], out_sems.at[i])
 
-    for i in range(steps):
+    moves[0].start()
+    fetch(0).start()
+    moves[1].start()
+    moves[2].start()
+    for i in range(1, kernels // 2):
         fetch(i).start()
     row_at = lax.broadcasted_iota(jnp.int32, (span, span), 0) - span // 2
     col_at = lax.broadcasted_iota(jnp.int32, (span, span), 1) - span // 2
     reach = jnp.maximum(jnp.maximum(row_at, -1 - row_at), jnp.maximum(col_at, -1 - col_at))
 
+    for move in moves:
+        move.wait()
+    row_fwd, head, tail = row_ref[...], head_ref[...], tail_ref[...]
+
     def step(i, carry):
-        fetch(i).wait()
-
         def rows_of(p):
+            fetch(i * (batch // 2) + p).wait()
             planes = [[], []]
             for j in range(2):
                 k = i * batch + 2 * p + j
@@ -232,9 +242,9 @@
 
 def main_body(
     group, weight, place,
-    own, near, far, target, spec_far, tables_far,
+    own, target, near_out, far_out, spec_far, tables_far,
     resist_far, grad_own, near_rim, far_rim,
-    spec, field, mask_spec, resist, slopes, grad_spec, tables, spec_sems, table_sems, out_sem,
+    spec, field, mask_spec, resist, slopes, grad_spec, tables, near, far, spec_sems, table_sems, halo_sems, out_sem,
     *, layout, sections,
 ):
     kernels, grid_rows, _ = spec.shape
@@ -256,11 +266,21 @@
         parts = [tables[start + b * rows:start + (b + 1) * rows] for b in range(blocks)]
         return jnp.concatenate(parts, axis=1)
 
+    halos = [
+        pltpu.make_async_copy(out, here, halo_sems.at[i])
+        for i, (out, here) in enumerate([(near_out, near), (far_out, far)])
+    ]
+    for halo in halos:
+        halo.start()
     fetch_table(0).start()
     fetch_table(1).start()
     for i in range(steps):
         fetch(i).start()
     fetch_table(2).start()
+    slopes[...] = jnp.zeros(slopes.shape, f32)
+    grad_spec[...] = jnp.zeros(grad_spec.shape, f32)
+    for halo in halos:
+        halo.wait()
     fetch_table(0).wait()
 
     odd = place[0] % 2 == 1
@@ -279,8 +299,6 @@
     mask_spec[:, 2 * width:3 * width] = jnp.where(real_half, m_rest, turned)
     mask_spec[:, 3 * width:] = jnp.where(real_half, -turned, m_rest)
 
-    slopes[...] = jnp.zeros(slopes.shape, f32)
-    grad_spec[...] = jnp.zeros(grad_spec.shape, f32)
     fetch_table(1).wait()
     col_inv, row_inv = table("col_inv"), table("row_inv")
 
@@ -438,13 +456,17 @@
     spectra = pl.pallas_call(
         spectra_body,
         out_shape=jax.ShapeDtypeStruct((kernels, grid_rows, 2 * grid_cols), f32),
-        in_specs=[smem, hbm, vmem, vmem, vmem],
+        in_specs=[smem] + [hbm] * 4,
         out_specs=hbm,
         scratch_shapes=[
             pltpu.VMEM(kernel_taps.shape, f32),
             pltpu.VMEM((kernels, grid_rows, 2 * grid_cols), f32),
-            pltpu.SemaphoreType.DMA((kernels // BATCH,)),
+            pltpu.VMEM(row_fwd.shape, bf16),
+            pltpu.VMEM(head.shape, bf16),
+            pltpu.VMEM(tail.shape, bf16),
             pltpu.SemaphoreType.DMA((kernels // 2,)),
+            pltpu.SemaphoreType.DMA((kernels // 2,)),
+            pltpu.SemaphoreType.DMA((3,)),
         ],
         compiler_params=pltpu.CompilerParams(vmem_limit_bytes=56 * MIB),
         cost_estimate=pl.CostEstimate(flops=18 * 10**9, bytes_accessed=14 * 10**6, transcendentals=0),
@@ -464,7 +486,7 @@
             jax.ShapeDtypeStruct((2, rim, width), f32),
             jax.ShapeDtypeStruct((2, rim, width), f32),
         ],
-        in_specs=[smem] * 3 + [vmem] * 4 + [hbm] * 2,
+        in_specs=[smem] * 3 + [vmem] * 2 + [hbm] * 4,
         out_specs=[hbm] + [vmem] * 3,
         scratch_shapes=[
             pltpu.VMEM((kernels, grid_rows, 2 * grid_cols), f32),
@@ -474,13 +496,16 @@
             pltpu.VMEM((GROUPS, count, width), f32),
             pltpu.VMEM((grid_rows, 4 * width), f32),
             pltpu.VMEM(tables.shape, bf16),
+            pltpu.VMEM(mask_field.shape, f32),
+            pltpu.VMEM(mask_field.shape, f32),
             pltpu.SemaphoreType.DMA((kernels // BATCH,)),
             pltpu.SemaphoreType.DMA((len(sections),)),
+            pltpu.SemaphoreType.DMA((2,)),
             pltpu.SemaphoreType.DMA,
         ],
         compiler_params=pltpu.CompilerParams(vmem_limit_bytes=LIMIT * MIB),
         name="fields",
-    )(kernel_group, kernel_weight, place, mask_field, near, far, target, spectra, jnp.asarray(tables))
+    )(kernel_group, kernel_weight, place, mask_field, target, near, far, spectra, jnp.asarray(tables))
 
     near_in = lax.ppermute(near_rim, "row", near_pairs)
     far_in = lax.ppermute(far_rim, "row", far_pairs)

time: 39.4 us -> 42 us (1.066)
  Pallas kernels: 28 us -> 30.6 us
    pallas_call x1, Pallas kernels: 9.81 us -> 12 us  [on_device(): pl.pallas_call(spectra_body, out_shape=jax.ShapeDtypeStruct((kernels, gri...]
  transfers between devices with their start and end apart: 4 -> 4, of which waited for: 1 -> 1; matrix products, arithmetic and copies ran while one was open for 0% -> 0% of each run, Pallas kernels for 25% -> 29%
where the time goes in v20:
time: 42 us; the launch traced here: 41.7 us
  Pallas kernels  30.6 us (73%)
  starting transfers between devices  7.38 us (18%)
  waiting for transfers between devices  2.95 us (7%)
  between operations  0.76 us (2%)
    pallas_call x1, Pallas kernels, on_device(): pl.pallas_call(functools.partial(main_body, layout=layout, sections=secti...  17.8 us
    pallas_call x1, Pallas kernels, on_device(): pl.pallas_call(spectra_body, out_shape=jax.ShapeDtypeStruct((kernels, gri...  12 us
    ppermute x1, starting transfers between devices, on_device(): far_in = lax.ppermute(far_rim, 'row', far_pairs)  3.52 us
    ppermute x1, starting transfers between devices, on_device(): far = lax.ppermute(mask_field, 'row', far_pairs)  3.05 us
    ppermute x1, waiting for transfers between devices, on_device(): far_in = lax.ppermute(far_rim, 'row', far_pairs)  2.95 us
  transfers between devices with their start and end apart: 4, of which 1 were waited for; matrix products, arithmetic and copies ran while one was open for 0% of the time, Pallas kernels for 29%

profile of v20, /device:TPU:21, one launch (start us, length us, event | category | flops | bytes accessed | tf_op | source)
XLA Modules:
  0.0 41.7 jit_solution(11535747717357451320)
XLA Ops:
  0.6 0.0 copy-start
  0.6 0.0 copy-start.3
  0.7 0.0 copy-start.2
  0.7 0.0 copy-start.1
  0.7 0.7 %collective-permute-start = (f32[2,128,128]{2,1,0:T(8,128)}, f32[2,128,128]{2,1,0:T(8,128)S(1)}, u32[]{:S(2)}, u32[]{:S(2)}) collective-permute-start(f32[2,128,128]{2,1,0:T(8,128)} %own.1), channel_id=1, source_target_pairs={{0,1},{1,0},{2,3},{3,2},{4,5},{5,4},{6,7},{7,6},{8,9},{9,8},{10,11... | collective-permute-start | bytes 393224 | tf_op jit(solution)/shard_map/ppermute | solution.py:433
  1.4 3.0 %collective-permute-start.1 = (f32[2,128,128]{2,1,0:T(8,128)}, f32[2,128,128]{2,1,0:T(8,128)S(1)}, u32[]{:S(2)}, u32[]{:S(2)}) collective-permute-start(f32[2,128,128]{2,1,0:T(8,128)} %own.1), channel_id=1, source_target_pairs={{1,2},{2,1},{3,4},{4,3},{5,6},{6,5},{7,8},{8,7},{9,10},{10,9},{11,... | collective-permute-start | bytes 393224 | tf_op jit(solution)/shard_map/ppermute | solution.py:434
  4.5 12.0 %spectra.1.spec_far = f32[24,256,384]{2,1,0:T(8,128)} custom-call(s32[24]{0:T(128)} %radii.1, f32[24,2,128,128]{3,2,1,0:T(8,128)} %taps_far.1, bf16[256,512]{1,0:T(8,128)(2,1)} %constant.12.clone.row_far, bf16[512,256]{1,0:T(8,128)(2,1)} %constant.13.clone.head_far, bf16[256,256]{1,0:T(8,128)(2,1)} %constant.14.clone.tail_far), custom_call_target="tpu_custom_call" | custom-call | flops 17999998976 | bytes 14000000 | tf_op jit(solution)/shard_map/spectra/pallas_call | solution.py:456
  16.5 0.0 collective-permute-done.near_out
  16.5 0.0 collective-permute-done.1.far_out
  16.5 0.0 copy-done
  16.6 0.0 copy-done.3
  16.6 0.0 copy-done.2
  16.6 0.0 copy-done.1
  16.6 17.8 %fields.1 = (f32[3,128,128]{2,1,0:T(8,128)}, f32[2,128,128]{2,1,0:T(8,128)S(1)}, f32[2,64,128]{2,1,0:T(8,128)S(1)}, f32[2,64,128]{2,1,0:T(8,128)S(1)}) custom-call(s32[24]{0:T(128)S(1)} %copy-done.2, f32[24]{0:T(128)S(1)} %copy-done.3, s32[1]{0:T(128)} %bitcast.place, f32[2,128,128]{2,1,0:T(8,128)S(1)} %copy-done, s32[128,128]{1,0:T(8,128)S(1)} %copy-done.1, ...), custom_call_target="tpu_custom_call" | custom-call | tf_op jit(solution)/shard_map/fields/pallas_call | solution.py:481
  34.4 0.1 collective-permute-start.2
  34.5 3.5 %collective-permute-start.3 = (f32[2,64,128]{2,1,0:T(8,128)S(1)}, f32[2,64,128]{2,1,0:T(8,128)S(1)}, u32[]{:S(2)}, u32[]{:S(2)}) collective-permute-start(f32[2,64,128]{2,1,0:T(8,128)S(1)} %get-tuple-element.9), channel_id=1, source_target_pairs={{1,2},{2,1},{3,4},{4,3},{5,6},{6,5},{7,8},{8,7},{9,10},{10,9},{11,... | collective-permute-start | bytes 196616 | tf_op jit(solution)/shard_map/ppermute | solution.py:511
  38.0 0.0 collective-permute-done.2.near
  38.0 2.9 %collective-permute-done.3.far = f32[2,64,128]{2,1,0:T(8,128)S(1)} collective-permute-done((f32[2,64,128]{2,1,0:T(8,128)S(1)}, f32[2,64,128]{2,1,0:T(8,128)S(1)}, u32[]{:S(2)}, u32[]{:S(2)}) %collective-permute-start.3) | collective-permute-done | bytes 65568 | tf_op jit(solution)/shard_map/ppermute | solution.py:511
  41.0 0.7 %join.1 = f32[2,128,128]{2,1,0:T(8,128)} custom-call(s32[1]{0:T(128)} %bitcast.place, f32[2,128,128]{2,1,0:T(8,128)S(1)} %get-tuple-element.7.own, f32[2,64,128]{2,1,0:T(8,128)S(1)} %collective-permute-done.2.near, f32[2,64,128]{2,1,0:T(8,128)S(1)} %collective-permute-done.3.far), custom_call_target="tpu_custom_call" | custom-call | tf_op jit(solution)/shard_map/join/pallas_call | solution.py:512
Async XLA Ops:
  0.6 15.9 %copy-start = (f32[2,128,128]{2,1,0:T(8,128)S(1)}, f32[2,128,128]{2,1,0:T(8,128)}, u32[]{:S(2)}) copy-start(f32[2,128,128]{2,1,0:T(8,128)} %own.1) | copy-start | bytes 393220
  0.6 15.9 %copy-start.3 = (f32[24]{0:T(128)S(1)}, f32[24]{0:T(128)}, u32[]{:S(2)}) copy-start(f32[24]{0:T(128)} %weight.1) | copy-start | bytes 292
  0.7 15.9 %copy-start.2 = (s32[24]{0:T(128)S(1)}, s32[24]{0:T(128)}, u32[]{:S(2)}) copy-start(s32[24]{0:T(128)} %group.1) | copy-start | bytes 292
  0.7 15.9 %copy-start.1 = (s32[128,128]{1,0:T(8,128)S(1)}, s32[128,128]{1,0:T(8,128)}, u32[]{:S(2)}) copy-start(s32[128,128]{1,0:T(8,128)} %target.1) | copy-start | bytes 196612
  0.7 15.9 %collective-permute-start = (f32[2,128,128]{2,1,0:T(8,128)}, f32[2,128,128]{2,1,0:T(8,128)S(1)}, u32[]{:S(2)}, u32[]{:S(2)}) collective-permute-start(f32[2,128,128]{2,1,0:T(8,128)} %own.1), channel_id=1, source_target_pairs={{0,1},{1,0},{2,3},{3,2},{4,5},{5,4},{6,7},{7,6},{8,9},{9,8},{10,11... | collective-permute-start | bytes 393224 | tf_op jit(solution)/shard_map/ppermute | solution.py:433
  1.4 15.1 %collective-permute-start.1 = (f32[2,128,128]{2,1,0:T(8,128)}, f32[2,128,128]{2,1,0:T(8,128)S(1)}, u32[]{:S(2)}, u32[]{:S(2)}) collective-permute-start(f32[2,128,128]{2,1,0:T(8,128)} %own.1), channel_id=1, source_target_pairs={{1,2},{2,1},{3,4},{4,3},{5,6},{6,5},{7,8},{8,7},{9,10},{10,9},{11,... | collective-permute-start | bytes 393224 | tf_op jit(solution)/shard_map/ppermute | solution.py:434
  34.4 3.6 %collective-permute-start.2 = (f32[2,64,128]{2,1,0:T(8,128)S(1)}, f32[2,64,128]{2,1,0:T(8,128)S(1)}, u32[]{:S(2)}, u32[]{:S(2)}) collective-permute-start(f32[2,64,128]{2,1,0:T(8,128)S(1)} %get-tuple-element.8), channel_id=1, source_target_pairs={{0,1},{1,0},{2,3},{3,2},{4,5},{5,4},{6,7},{7,6},{8,9},{9,8},{10,11... | collective-permute-start | bytes 196616 | tf_op jit(solution)/shard_map/ppermute | solution.py:510
  34.5 6.5 %collective-permute-start.3 = (f32[2,64,128]{2,1,0:T(8,128)S(1)}, f32[2,64,128]{2,1,0:T(8,128)S(1)}, u32[]{:S(2)}, u32[]{:S(2)}) collective-permute-start(f32[2,64,128]{2,1,0:T(8,128)S(1)} %get-tuple-element.9), channel_id=1, source_target_pairs={{1,2},{2,1},{3,4},{4,3},{5,6},{6,5},{7,8},{8,7},{9,10},{10,9},{11,... | collective-permute-start | bytes 196616 | tf_op jit(solution)/shard_map/ppermute | solution.py:511

commit v21 on v15

--- a/solution.py
+++ b/solution.py
@@ -15,7 +15,7 @@
 STEEPNESS = 1.0
 THRESHOLD = 2.0
 UNIT = 4
-SPECTRA_UNITS = 6
+SPECTRA_UNITS = 3
 UNITS = 3
 PIECE = 256
 TURN = math.sqrt(0.75)
@@ -219,7 +219,6 @@
     def step(i, carry):
         def cols_of(p):
             u = i * SPECTRA_UNITS + p
-            fetch(u).wait()
             planes = []
             for j in range(UNIT):
                 k = u * UNIT + j
@@ -232,9 +231,12 @@
             for c, found in enumerate(to_row_freqs(quarters_of(*both, quarter), row_fwd)):
                 for part in range(2):
                     spec[u, part, c * quarter:(c + 1) * quarter] = found[part]
-            put(u).start()
-
+
+        for p in range(SPECTRA_UNITS):
+            fetch(i * SPECTRA_UNITS + p).wait()
         staggered(SPECTRA_UNITS, cols_of, rows_of)
+        for p in range(SPECTRA_UNITS):
+            put(i * SPECTRA_UNITS + p).start()
         return carry
 
     loop(steps, step)
@@ -286,7 +288,6 @@
     def forward(i, carry):
         def rows_of(p):
             u = i * UNITS + p
-            fetch(u).wait()
             classes = []
             for c in range(4):
                 here = slice(c * rim, (c + 1) * rim)
@@ -306,6 +307,8 @@
                     field[k, side] = x
                     slopes[group[k], side] = slopes[group[k], side] + weight[k] * (x * x)
 
+        for p in range(UNITS):
+            fetch(i * UNITS + p).wait()
         staggered(UNITS, rows_of, cols_of)
         return carry
 

time: 39.9 us -> 40.1 us (level)
    pallas_call x1, Pallas kernels: 9.2 us -> 9.88 us  [on_device(): pl.pallas_call(spectra_body, out_shape=jax.ShapeDtypeStruct(spec_shape, f...]
    pallas_call x1, Pallas kernels: 18.6 us -> 18.1 us  [on_device(): pl.pallas_call(functools.partial(main_body, layout=layout), out_shape=[ja...]
  transfers between devices with their start and end apart: 4 -> 4, of which waited for: 1 -> 1; matrix products, arithmetic and copies ran while one was open for 0% -> 0% of each run, Pallas kernels for 23% -> 25%
where the time goes in v21:
time: 40.1 us; the launch traced here: 39.8 us
  Pallas kernels  28.7 us (72%)
  starting transfers between devices  7.37 us (18%)
  waiting for transfers between devices  2.96 us (7%)
  between operations  0.76 us (2%)
    pallas_call x1, Pallas kernels, on_device(): pl.pallas_call(functools.partial(main_body, layout=layout), out_shape=[ja...  18.1 us
    pallas_call x1, Pallas kernels, on_device(): pl.pallas_call(spectra_body, out_shape=jax.ShapeDtypeStruct(spec_shape, f...  9.88 us
    ppermute x1, starting transfers between devices, on_device(): far_in = lax.ppermute(far_rim, 'row', far_pairs)  3.51 us
    ppermute x1, starting transfers between devices, on_device(): far = lax.ppermute(mask_field, 'row', far_pairs)  3.05 us
    ppermute x1, waiting for transfers between devices, on_device(): far_in = lax.ppermute(far_rim, 'row', far_pairs)  2.95 us
  transfers between devices with their start and end apart: 4, of which 1 were waited for; matrix products, arithmetic and copies ran while one was open for 0% of the time, Pallas kernels for 25%

profile of v21, /device:TPU:21, one launch (start us, length us, event | category | flops | bytes accessed | tf_op | source)
XLA Modules:
  0.0 39.8 jit_solution(10883852458519679947)
XLA Ops:
  0.6 0.0 copy-start
  0.6 0.0 copy-start.3
  0.7 0.0 copy-start.2
  0.7 0.0 copy-start.1
  0.7 0.7 %collective-permute-start = (f32[2,128,128]{2,1,0:T(8,128)}, f32[2,128,128]{2,1,0:T(8,128)S(1)}, u32[]{:S(2)}, u32[]{:S(2)}) collective-permute-start(f32[2,128,128]{2,1,0:T(8,128)} %own.1), channel_id=1, source_target_pairs={{0,1},{1,0},{2,3},{3,2},{4,5},{5,4},{6,7},{7,6},{8,9},{9,8},{10,11... | collective-permute-start | bytes 393224 | tf_op jit(solution)/shard_map/ppermute | solution.py:401
  1.4 3.0 %collective-permute-start.1 = (f32[2,128,128]{2,1,0:T(8,128)}, f32[2,128,128]{2,1,0:T(8,128)S(1)}, u32[]{:S(2)}, u32[]{:S(2)}) collective-permute-start(f32[2,128,128]{2,1,0:T(8,128)} %own.1), channel_id=1, source_target_pairs={{1,2},{2,1},{3,4},{4,3},{5,6},{6,5},{7,8},{8,7},{9,10},{10,9},{11,... | collective-permute-start | bytes 393224 | tf_op jit(solution)/shard_map/ppermute | solution.py:402
  4.5 9.9 %spectra.1.spec_far = f32[6,2,256,768]{3,2,1,0:T(8,128)} custom-call(s32[24]{0:T(128)} %radii.1, f32[24,2,128,128]{3,2,1,0:T(8,128)} %taps_far.1, bf16[256,512]{1,0:T(8,128)(2,1)} %constant.10.clone.row_ref, bf16[384,256]{1,0:T(8,128)(2,1)} %constant.11.clone.col_ref), custom_call_target="tpu_custom_call" | custom-call | flops 17999998976 | bytes 14000000 | tf_op jit(solution)/shard_map/spectra/pallas_call | solution.py:418
  14.4 0.0 collective-permute-done.near
  14.4 0.0 collective-permute-done.1.far
  14.4 0.0 copy-done
  14.4 0.0 copy-done.3
  14.4 0.0 copy-done.2
  14.4 0.0 copy-done.1
  14.4 18.1 %fields.1 = (f32[3,128,128]{2,1,0:T(8,128)}, f32[2,128,128]{2,1,0:T(8,128)S(1)}, f32[2,64,128]{2,1,0:T(8,128)S(1)}, f32[2,64,128]{2,1,0:T(8,128)S(1)}) custom-call(s32[24]{0:T(128)S(1)} %copy-done.2, f32[24]{0:T(128)S(1)} %copy-done.3, s32[1]{0:T(128)} %bitcast.place, f32[2,128,128]{2,1,0:T(8,128)S(1)} %copy-done, ...), custom_call_target="tpu_custom_call" | custom-call | tf_op jit(solution)/shard_map/fields/pallas_call | solution.py:434
  32.6 0.1 collective-permute-start.2
  32.7 3.5 %collective-permute-start.3 = (f32[2,64,128]{2,1,0:T(8,128)S(1)}, f32[2,64,128]{2,1,0:T(8,128)S(1)}, u32[]{:S(2)}, u32[]{:S(2)}) collective-permute-start(f32[2,64,128]{2,1,0:T(8,128)S(1)} %get-tuple-element.9), channel_id=1, source_target_pairs={{1,2},{2,1},{3,4},{4,3},{5,6},{6,5},{7,8},{8,7},{9,10},{10,9},{11,... | collective-permute-start | bytes 196616 | tf_op jit(solution)/shard_map/ppermute | solution.py:461
  36.2 0.0 collective-permute-done.2.near
  36.2 3.0 %collective-permute-done.3.far = f32[2,64,128]{2,1,0:T(8,128)S(1)} collective-permute-done((f32[2,64,128]{2,1,0:T(8,128)S(1)}, f32[2,64,128]{2,1,0:T(8,128)S(1)}, u32[]{:S(2)}, u32[]{:S(2)}) %collective-permute-start.3) | collective-permute-done | bytes 65568 | tf_op jit(solution)/shard_map/ppermute | solution.py:461
  39.1 0.7 %join.1 = f32[2,128,128]{2,1,0:T(8,128)} custom-call(s32[1]{0:T(128)} %bitcast.place, f32[2,128,128]{2,1,0:T(8,128)S(1)} %get-tuple-element.7.own, f32[2,64,128]{2,1,0:T(8,128)S(1)} %collective-permute-done.2.near, f32[2,64,128]{2,1,0:T(8,128)S(1)} %collective-permute-done.3.far), custom_call_target="tpu_custom_call" | custom-call | tf_op jit(solution)/shard_map/join/pallas_call | solution.py:462
Async XLA Ops:
  0.6 13.7 %copy-start = (f32[2,128,128]{2,1,0:T(8,128)S(1)}, f32[2,128,128]{2,1,0:T(8,128)}, u32[]{:S(2)}) copy-start(f32[2,128,128]{2,1,0:T(8,128)} %own.1) | copy-start | bytes 393220
  0.6 13.7 %copy-start.3 = (f32[24]{0:T(128)S(1)}, f32[24]{0:T(128)}, u32[]{:S(2)}) copy-start(f32[24]{0:T(128)} %weight.1) | copy-start | bytes 292
  0.7 13.7 %copy-start.2 = (s32[24]{0:T(128)S(1)}, s32[24]{0:T(128)}, u32[]{:S(2)}) copy-start(s32[24]{0:T(128)} %group.1) | copy-start | bytes 292
  0.7 13.7 %copy-start.1 = (s32[128,128]{1,0:T(8,128)S(1)}, s32[128,128]{1,0:T(8,128)}, u32[]{:S(2)}) copy-start(s32[128,128]{1,0:T(8,128)} %target.1) | copy-start | bytes 196612
  0.7 13.7 %collective-permute-start = (f32[2,128,128]{2,1,0:T(8,128)}, f32[2,128,128]{2,1,0:T(8,128)S(1)}, u32[]{:S(2)}, u32[]{:S(2)}) collective-permute-start(f32[2,128,128]{2,1,0:T(8,128)} %own.1), channel_id=1, source_target_pairs={{0,1},{1,0},{2,3},{3,2},{4,5},{5,4},{6,7},{7,6},{8,9},{9,8},{10,11... | collective-permute-start | bytes 393224 | tf_op jit(solution)/shard_map/ppermute | solution.py:401
  1.4 13.0 %collective-permute-start.1 = (f32[2,128,128]{2,1,0:T(8,128)}, f32[2,128,128]{2,1,0:T(8,128)S(1)}, u32[]{:S(2)}, u32[]{:S(2)}) collective-permute-start(f32[2,128,128]{2,1,0:T(8,128)} %own.1), channel_id=1, source_target_pairs={{1,2},{2,1},{3,4},{4,3},{5,6},{6,5},{7,8},{8,7},{9,10},{10,9},{11,... | collective-permute-start | bytes 393224 | tf_op jit(solution)/shard_map/ppermute | solution.py:402
  32.6 3.6 %collective-permute-start.2 = (f32[2,64,128]{2,1,0:T(8,128)S(1)}, f32[2,64,128]{2,1,0:T(8,128)S(1)}, u32[]{:S(2)}, u32[]{:S(2)}) collective-permute-start(f32[2,64,128]{2,1,0:T(8,128)S(1)} %get-tuple-element.8), channel_id=1, source_target_pairs={{0,1},{1,0},{2,3},{3,2},{4,5},{5,4},{6,7},{7,6},{8,9},{9,8},{10,11... | collective-permute-start | bytes 196616 | tf_op jit(solution)/shard_map/ppermute | solution.py:460
  32.7 6.5 %collective-permute-start.3 = (f32[2,64,128]{2,1,0:T(8,128)S(1)}, f32[2,64,128]{2,1,0:T(8,128)S(1)}, u32[]{:S(2)}, u32[]{:S(2)}) collective-permute-start(f32[2,64,128]{2,1,0:T(8,128)S(1)} %get-tuple-element.9), channel_id=1, source_target_pairs={{1,2},{2,1},{3,4},{4,3},{5,6},{6,5},{7,8},{8,7},{9,10},{10,9},{11,... | collective-permute-start | bytes 196616 | tf_op jit(solution)/shard_map/ppermute | solution.py:461

commit v22 on v13

--- a/solution.py
+++ b/solution.py
@@ -20,7 +20,8 @@
 f32 = jnp.float32
 bf16 = jnp.bfloat16
 MIB = 1024 * 1024
-LIMIT = 53
+SPECTRA_LIMIT = 45
+LIMIT = 34
 
 
 def halves(table, axis):
@@ -181,7 +182,7 @@
     return pltpu.roll(x, x.shape[1] // 2, 1)
 
 
-def spectra_body(radii, taps_far, row_ref, head_ref, tail_ref, spec_far, taps, spec, in_sems, out_sems):
+def spectra_body(radii, taps_far, row_ref, head_ref, tail_ref, spec, taps, in_sems):
     kernels, _, span, _ = taps.shape
     row_fwd, head, tail = row_ref[...], head_ref[...], tail_ref[...]
     steps = in_sems.shape[0]
@@ -190,10 +191,6 @@
     def fetch(i):
         here = pl.ds(i * batch, batch)
         return pltpu.make_async_copy(taps_far.at[here], taps.at[here], in_sems.at[i])
-
-    def put(i):
-        here = pl.ds(2 * i, 2)
-        return pltpu.make_async_copy(spec.at[here], spec_far.at[here], out_sems.at[i])
 
     for i in range(steps):
         fetch(i).start()
@@ -220,32 +217,25 @@
                 a, b = to_freqs(tiles[j], head, tail)
                 spec[k, :, :a.shape[1]] = a
                 spec[k, :, a.shape[1]:] = b
-            put(i * (batch // 2) + p).start()
 
         staggered(batch // 2, rows_of, cols_of)
         return carry
 
     lax.fori_loop(0, steps, step, 0)
-    for i in range(kernels // 2):
-        put(i).wait()
 
 
 def main_body(
     group, weight, place,
-    own, near, far, target, spec_far, tables_far,
+    own, near, far, target, spec, tables_far,
     resist_far, grad_own, near_rim, far_rim,
-    spec, field, mask_spec, resist, slopes, grad_spec, tables, spec_sems, table_sems, out_sem,
+    field, mask_spec, resist, slopes, grad_spec, tables, table_sems, out_sem,
     *, layout, sections,
 ):
     kernels, grid_rows, _ = spec.shape
     count, width = target.shape
     rim = (grid_rows - count) // 2
-    steps = spec_sems.shape[0]
-    batch = kernels // steps
-
-    def fetch(i):
-        here = pl.ds(i * batch, batch)
-        return pltpu.make_async_copy(spec_far.at[here], spec.at[here], spec_sems.at[i])
+    batch = BATCH
+    steps = kernels // batch
 
     def fetch_table(i):
         here = pl.ds(sections[i][0], sections[i][1])
@@ -258,8 +248,6 @@
 
     fetch_table(0).start()
     fetch_table(1).start()
-    for i in range(steps):
-        fetch(i).start()
     fetch_table(2).start()
     fetch_table(0).wait()
 
@@ -285,7 +273,6 @@
     col_inv, row_inv = table("col_inv"), table("row_inv")
 
     def forward(i, carry):
-        fetch(i).wait()
         m_re, m_im = mask_spec[:, :width], mask_spec[:, width:2 * width]
         m_same, m_cross = mask_spec[:, 2 * width:3 * width], mask_spec[:, 3 * width:]
 
@@ -438,15 +425,13 @@
     spectra = pl.pallas_call(
         spectra_body,
         out_shape=jax.ShapeDtypeStruct((kernels, grid_rows, 2 * grid_cols), f32),
-        in_specs=[smem, hbm, vmem, vmem, vmem],
-        out_specs=hbm,
+        in_specs=[smem, hbm] + [vmem] * 3,
+        out_specs=vmem,
         scratch_shapes=[
             pltpu.VMEM(kernel_taps.shape, f32),
-            pltpu.VMEM((kernels, grid_rows, 2 * grid_cols), f32),
             pltpu.SemaphoreType.DMA((kernels // BATCH,)),
-            pltpu.SemaphoreType.DMA((kernels // 2,)),
         ],
-        compiler_params=pltpu.CompilerParams(vmem_limit_bytes=56 * MIB),
+        compiler_params=pltpu.CompilerParams(vmem_limit_bytes=SPECTRA_LIMIT * MIB),
         cost_estimate=pl.CostEstimate(flops=18 * 10**9, bytes_accessed=14 * 10**6, transcendentals=0),
         name="spectra",
     )(kernel_radii, kernel_taps, *map(jnp.asarray, (row_fwd, head, tail)))
@@ -464,17 +449,15 @@
             jax.ShapeDtypeStruct((2, rim, width), f32),
             jax.ShapeDtypeStruct((2, rim, width), f32),
         ],
-        in_specs=[smem] * 3 + [vmem] * 4 + [hbm] * 2,
+        in_specs=[smem] * 3 + [vmem] * 5 + [hbm],
         out_specs=[hbm] + [vmem] * 3,
         scratch_shapes=[
-            pltpu.VMEM((kernels, grid_rows, 2 * grid_cols), f32),
             pltpu.VMEM((kernels // 2, 2 * count, 2 * width), f32),
             pltpu.VMEM((grid_rows, 4 * width), f32),
             pltpu.VMEM((GROUPS, count, width), f32),
             pltpu.VMEM((GROUPS, count, width), f32),
             pltpu.VMEM((grid_rows, 4 * width), f32),
             pltpu.VMEM(tables.shape, bf16),
-            pltpu.SemaphoreType.DMA((kernels // BATCH,)),
             pltpu.SemaphoreType.DMA((len(sections),)),
             pltpu.SemaphoreType.DMA,
         ],

time: 39.4 us -> 48.5 us (1.23)
  local copies, waits for them, and re-layouts: 0.02 us -> 9.04 us
    unnamed x8 -> x22, local copies, waits for them, and re-layouts: 0.02 us -> 9.04 us
    pallas_call x1, Pallas kernels: 17.5 us -> 16.2 us  [on_device(): pl.pallas_call(functools.partial(main_body, layout=layout, sections=secti...]
    pallas_call x1, Pallas kernels: 9.81 us -> 10.9 us  [on_device(): pl.pallas_call(spectra_body, out_shape=jax.ShapeDtypeStruct((kernels, gri...]
  transfers between devices with their start and end apart: 4 -> 4, of which waited for: 1 -> 1; matrix products, arithmetic and copies ran while one was open for 0% -> 0% of each run, Pallas kernels for 25% -> 23%
where the time goes in v22:
time: 48.5 us; the launch traced here: 48.1 us
  Pallas kernels  27.8 us (57%)
  local copies, waits for them, and re-layouts  9.04 us (19%)
  starting transfers between devices  7.5 us (15%)
  waiting for transfers between devices  2.96 us (6%)
  between operations  0.8 us (2%)
    pallas_call x1, Pallas kernels, on_device(): pl.pallas_call(functools.partial(main_body, layout=layout, sections=secti...  16.2 us
    pallas_call x1, Pallas kernels, on_device(): pl.pallas_call(spectra_body, out_shape=jax.ShapeDtypeStruct((kernels, gri...  10.9 us
    unnamed x22, local copies, waits for them, and re-layouts  9.04 us
    ppermute x1, starting transfers between devices, on_device(): far_in = lax.ppermute(far_rim, 'row', far_pairs)  3.51 us
    ppermute x1, starting transfers between devices, on_device(): far = lax.ppermute(mask_field, 'row', far_pairs)  3.18 us
    ppermute x1, waiting for transfers between devices, on_device(): far_in = lax.ppermute(far_rim, 'row', far_pairs)  2.95 us
  transfers between devices with their start and end apart: 4, of which 1 were waited for; matrix products, arithmetic and copies ran while one was open for 0% of the time, Pallas kernels for 23%

profile of v22, /device:TPU:21, one launch (start us, length us, event | category | flops | bytes accessed | tf_op | source)
XLA Modules:
  0.0 48.1 jit_solution(5727297432954502405)
XLA Ops:
  0.6 0.0 copy-start.1
  0.7 0.7 %collective-permute-start = (f32[2,128,128]{2,1,0:T(8,128)}, f32[2,128,128]{2,1,0:T(8,128)S(1)}, u32[]{:S(2)}, u32[]{:S(2)}) collective-permute-start(f32[2,128,128]{2,1,0:T(8,128)} %own.1), channel_id=1, source_target_pairs={{0,1},{1,0},{2,3},{3,2},{4,5},{5,4},{6,7},{7,6},{8,9},{9,8},{10,11... | collective-permute-start | bytes 393224 | tf_op jit(solution)/shard_map/ppermute | solution.py:402
  1.4 3.2 %collective-permute-start.1 = (f32[2,128,128]{2,1,0:T(8,128)}, f32[2,128,128]{2,1,0:T(8,128)S(1)}, u32[]{:S(2)}, u32[]{:S(2)}) collective-permute-start(f32[2,128,128]{2,1,0:T(8,128)} %own.1), channel_id=1, source_target_pairs={{1,2},{2,1},{3,4},{4,3},{5,6},{6,5},{7,8},{8,7},{9,10},{10,9},{11,... | collective-permute-start | bytes 393224 | tf_op jit(solution)/shard_map/ppermute | solution.py:403
  4.6 0.0 copy-start.6
  4.6 1.9 %copy-done.6 = f32[24,2,128,128]{3,2,1,0:T(8,128)S(1)} copy-done((f32[24,2,128,128]{3,2,1,0:T(8,128)S(1)}, f32[24,2,128,128]{3,2,1,0:T(8,128)}, u32[]{:S(2)}) %copy-start.6) | copy-done | bytes 3145752
  6.5 0.7 %copy-done.7 = s32[24]{0:T(128)S(1)} copy-done((s32[24]{0:T(128)S(1)}, s32[24]{0:T(128)}, u32[]{:S(2)}) %copy-start.7) | copy-done | bytes 120
  7.2 0.9 %copy-done.8 = bf16[512,256]{1,0:T(8,128)(2,1)S(1)} copy-done((bf16[512,256]{1,0:T(8,128)(2,1)S(1)}, bf16[512,256]{1,0:T(8,128)(2,1)}, u32[]{:S(2)}) %copy-start.8) | copy-done | bytes 262168
  8.1 0.9 %copy-done.9 = bf16[256,512]{1,0:T(8,128)(2,1)S(1)} copy-done((bf16[256,512]{1,0:T(8,128)(2,1)S(1)}, bf16[256,512]{1,0:T(8,128)(2,1)}, u32[]{:S(2)}) %copy-start.9) | copy-done | bytes 262168
  9.1 0.9 %copy-done.10 = bf16[256,256]{1,0:T(8,128)(2,1)S(1)} copy-done((bf16[256,256]{1,0:T(8,128)(2,1)S(1)}, bf16[256,256]{1,0:T(8,128)(2,1)}, u32[]{:S(2)}) %copy-start.10) | copy-done | bytes 131096
  10.0 10.9 %spectra.1.spec = f32[24,256,384]{2,1,0:T(8,128)} custom-call(s32[24]{0:T(128)S(1)} %copy-done.7, f32[24,2,128,128]{3,2,1,0:T(8,128)S(1)} %copy-done.6, bf16[256,512]{1,0:T(8,128)(2,1)S(1)} %copy-done.9, bf16[512,256]{1,0:T(8,128)(2,1)S(1)} %copy-done.8, bf16[256,256]{1,0:T(8,128)(2,1)S(1)} %copy-done.10), custom_call_target="tpu_custom_call" | custom-call | flops 17999998976 | bytes 14000000 | tf_op jit(solution)/shard_map/spectra/pallas_call | solution.py:425
  20.9 0.0 collective-permute-done.near
  20.9 0.0 collective-permute-done.1.far
  20.9 0.0 copy-done.1
  20.9 0.0 copy-done.2
  20.9 0.0 copy-done.5
  20.9 0.0 copy-done.4
  20.9 0.0 copy-done.3
  21.0 3.7 %copy-done = f32[24,256,384]{2,1,0:T(8,128)S(1)} copy-done((f32[24,256,384]{2,1,0:T(8,128)S(1)}, f32[24,256,384]{2,1,0:T(8,128)}, u32[]{:S(2)}) %copy-start) | copy-done | bytes 9437208
  24.6 16.2 %fields.1 = (f32[3,128,128]{2,1,0:T(8,128)}, f32[2,128,128]{2,1,0:T(8,128)S(1)}, f32[2,64,128]{2,1,0:T(8,128)S(1)}, f32[2,64,128]{2,1,0:T(8,128)S(1)}) custom-call(s32[24]{0:T(128)S(1)} %copy-done.4, f32[24]{0:T(128)S(1)} %copy-done.5, s32[1]{0:T(128)} %bitcast.place, f32[2,128,128]{2,1,0:T(8,128)S(1)} %copy-done.2, ...), custom_call_target="tpu_custom_call" | custom-call | tf_op jit(solution)/shard_map/fields/pallas_call | solution.py:444
  40.8 0.1 collective-permute-start.2
  40.9 3.5 %collective-permute-start.3 = (f32[2,64,128]{2,1,0:T(8,128)S(1)}, f32[2,64,128]{2,1,0:T(8,128)S(1)}, u32[]{:S(2)}, u32[]{:S(2)}) collective-permute-start(f32[2,64,128]{2,1,0:T(8,128)S(1)} %get-tuple-element.9), channel_id=1, source_target_pairs={{1,2},{2,1},{3,4},{4,3},{5,6},{6,5},{7,8},{8,7},{9,10},{10,9},{11,... | collective-permute-start | bytes 196616 | tf_op jit(solution)/shard_map/ppermute | solution.py:469
  44.4 0.0 collective-permute-done.2.near
  44.4 3.0 %collective-permute-done.3.far = f32[2,64,128]{2,1,0:T(8,128)S(1)} collective-permute-done((f32[2,64,128]{2,1,0:T(8,128)S(1)}, f32[2,64,128]{2,1,0:T(8,128)S(1)}, u32[]{:S(2)}, u32[]{:S(2)}) %collective-permute-start.3) | collective-permute-done | bytes 65568 | tf_op jit(solution)/shard_map/ppermute | solution.py:469
  47.4 0.7 %join.1 = f32[2,128,128]{2,1,0:T(8,128)} custom-call(s32[1]{0:T(128)} %bitcast.place, f32[2,128,128]{2,1,0:T(8,128)S(1)} %get-tuple-element.7.own, f32[2,64,128]{2,1,0:T(8,128)S(1)} %collective-permute-done.2.near, f32[2,64,128]{2,1,0:T(8,128)S(1)} %collective-permute-done.3.far), custom_call_target="tpu_custom_call" | custom-call | tf_op jit(solution)/shard_map/join/pallas_call | solution.py:470
  (9 shorter events, 0.0 us)
Async XLA Ops:
  0.6 20.3 %copy-start.1 = (bf16[4096,256]{1,0:T(8,128)(2,1)S(1)}, bf16[4096,256]{1,0:T(8,128)(2,1)}, u32[]{:S(2)}) copy-start(bf16[4096,256]{1,0:T(8,128)(2,1)} %constant.15.clone.tables_far) | copy-start | bytes 6291460
  0.6 20.3 %copy-start.2 = (f32[2,128,128]{2,1,0:T(8,128)S(1)}, f32[2,128,128]{2,1,0:T(8,128)}, u32[]{:S(2)}) copy-start(f32[2,128,128]{2,1,0:T(8,128)} %own.1) | copy-start | bytes 393220
  0.7 20.3 %copy-start.5 = (f32[24]{0:T(128)S(1)}, f32[24]{0:T(128)}, u32[]{:S(2)}) copy-start(f32[24]{0:T(128)} %weight.1) | copy-start | bytes 292
  0.7 20.3 %copy-start.4 = (s32[24]{0:T(128)S(1)}, s32[24]{0:T(128)}, u32[]{:S(2)}) copy-start(s32[24]{0:T(128)} %group.1) | copy-start | bytes 292
  0.7 20.3 %copy-start.3 = (s32[128,128]{1,0:T(8,128)S(1)}, s32[128,128]{1,0:T(8,128)}, u32[]{:S(2)}) copy-start(s32[128,128]{1,0:T(8,128)} %target.1) | copy-start | bytes 196612
  0.7 20.2 %collective-permute-start = (f32[2,128,128]{2,1,0:T(8,128)}, f32[2,128,128]{2,1,0:T(8,128)S(1)}, u32[]{:S(2)}, u32[]{:S(2)}) collective-permute-start(f32[2,128,128]{2,1,0:T(8,128)} %own.1), channel_id=1, source_target_pairs={{0,1},{1,0},{2,3},{3,2},{4,5},{5,4},{6,7},{7,6},{8,9},{9,8},{10,11... | collective-permute-start | bytes 393224 | tf_op jit(solution)/shard_map/ppermute | solution.py:402
  1.4 19.5 %collective-permute-start.1 = (f32[2,128,128]{2,1,0:T(8,128)}, f32[2,128,128]{2,1,0:T(8,128)S(1)}, u32[]{:S(2)}, u32[]{:S(2)}) collective-permute-start(f32[2,128,128]{2,1,0:T(8,128)} %own.1), channel_id=1, source_target_pairs={{1,2},{2,1},{3,4},{4,3},{5,6},{6,5},{7,8},{8,7},{9,10},{10,9},{11,... | collective-permute-start | bytes 393224 | tf_op jit(solution)/shard_map/ppermute | solution.py:403
  4.6 1.9 %copy-start.6 = (f32[24,2,128,128]{3,2,1,0:T(8,128)S(1)}, f32[24,2,128,128]{3,2,1,0:T(8,128)}, u32[]{:S(2)}) copy-start(f32[24,2,128,128]{3,2,1,0:T(8,128)} %taps_far.1) | copy-start | bytes 9437188
  6.5 0.7 %copy-start.7 = (s32[24]{0:T(128)S(1)}, s32[24]{0:T(128)}, u32[]{:S(2)}) copy-start(s32[24]{0:T(128)} %radii.1) | copy-start | bytes 292
  7.2 0.9 %copy-start.8 = (bf16[512,256]{1,0:T(8,128)(2,1)S(1)}, bf16[512,256]{1,0:T(8,128)(2,1)}, u32[]{:S(2)}) copy-start(bf16[512,256]{1,0:T(8,128)(2,1)} %constant.13.clone.head_ref) | copy-start | bytes 786436
  8.1 0.9 %copy-start.9 = (bf16[256,512]{1,0:T(8,128)(2,1)S(1)}, bf16[256,512]{1,0:T(8,128)(2,1)}, u32[]{:S(2)}) copy-start(bf16[256,512]{1,0:T(8,128)(2,1)} %constant.12.clone.row_ref) | copy-start | bytes 786436
  9.1 0.9 %copy-start.10 = (bf16[256,256]{1,0:T(8,128)(2,1)S(1)}, bf16[256,256]{1,0:T(8,128)(2,1)}, u32[]{:S(2)}) copy-start(bf16[256,256]{1,0:T(8,128)(2,1)} %constant.14.clone.tail_ref) | copy-start | bytes 393220
  20.9 3.7 %copy-start = (f32[24,256,384]{2,1,0:T(8,128)S(1)}, f32[24,256,384]{2,1,0:T(8,128)}, u32[]{:S(2)}) copy-start(f32[24,256,384]{2,1,0:T(8,128)} %spectra.1.spec) | copy-start | bytes 28311556
  40.8 3.6 %collective-permute-start.2 = (f32[2,64,128]{2,1,0:T(8,128)S(1)}, f32[2,64,128]{2,1,0:T(8,128)S(1)}, u32[]{:S(2)}, u32[]{:S(2)}) collective-permute-start(f32[2,64,128]{2,1,0:T(8,128)S(1)} %get-tuple-element.8), channel_id=1, source_target_pairs={{0,1},{1,0},{2,3},{3,2},{4,5},{5,4},{6,7},{7,6},{8,9},{9,8},{10,11... | collective-permute-start | bytes 196616 | tf_op jit(solution)/shard_map/ppermute | solution.py:468
  40.9 6.5 %collective-permute-start.3 = (f32[2,64,128]{2,1,0:T(8,128)S(1)}, f32[2,64,128]{2,1,0:T(8,128)S(1)}, u32[]{:S(2)}, u32[]{:S(2)}) collective-permute-start(f32[2,64,128]{2,1,0:T(8,128)S(1)} %get-tuple-element.9), channel_id=1, source_target_pairs={{1,2},{2,1},{3,4},{4,3},{5,6},{6,5},{7,8},{8,7},{9,10},{10,9},{11,... | collective-permute-start | bytes 196616 | tf_op jit(solution)/shard_map/ppermute | solution.py:469

commit v23 on v13

--- a/solution.py
+++ b/solution.py
@@ -14,7 +14,7 @@
 GROUPS = 3
 STEEPNESS = 1.0
 THRESHOLD = 2.0
-BATCH = 8
+BATCH = 12
 PIECE = 256
 
 f32 = jnp.float32

time: 39.4 us -> 39.4 us (level)
  no operation moved by 1% of the time
where the time goes in v23:
time: 39.4 us; the launch traced here: 39.1 us
  Pallas kernels  28 us (71%)
  starting transfers between devices  7.38 us (19%)
  waiting for transfers between devices  2.95 us (7%)
  between operations  0.76 us (2%)
    pallas_call x1, Pallas kernels, on_device(): pl.pallas_call(functools.partial(main_body, layout=layout, sections=secti...  17.5 us
    pallas_call x1, Pallas kernels, on_device(): pl.pallas_call(spectra_body, out_shape=jax.ShapeDtypeStruct((kernels, gri...  9.77 us
    ppermute x1, starting transfers between devices, on_device(): far_in = lax.ppermute(far_rim, 'row', far_pairs)  3.52 us
    ppermute x1, starting transfers between devices, on_device(): far = lax.ppermute(mask_field, 'row', far_pairs)  3.05 us
    ppermute x1, waiting for transfers between devices, on_device(): far_in = lax.ppermute(far_rim, 'row', far_pairs)  2.95 us
  transfers between devices with their start and end apart: 4, of which 1 were waited for; matrix products, arithmetic and copies ran while one was open for 0% of the time, Pallas kernels for 25%

profile of v23, /device:TPU:21, one launch (start us, length us, event | category | flops | bytes accessed | tf_op | source)
XLA Modules:
  0.0 39.1 jit_solution(17743532751236229422)
XLA Ops:
  0.6 0.0 copy-start
  0.6 0.0 copy-start.3
  0.7 0.0 copy-start.2
  0.7 0.0 copy-start.1
  0.7 0.7 %collective-permute-start = (f32[2,128,128]{2,1,0:T(8,128)}, f32[2,128,128]{2,1,0:T(8,128)S(1)}, u32[]{:S(2)}, u32[]{:S(2)}) collective-permute-start(f32[2,128,128]{2,1,0:T(8,128)} %own.1), channel_id=1, source_target_pairs={{0,1},{1,0},{2,3},{3,2},{4,5},{5,4},{6,7},{7,6},{8,9},{9,8},{10,11... | collective-permute-start | bytes 393224 | tf_op jit(solution)/shard_map/ppermute | solution.py:415
  1.4 3.0 %collective-permute-start.1 = (f32[2,128,128]{2,1,0:T(8,128)}, f32[2,128,128]{2,1,0:T(8,128)S(1)}, u32[]{:S(2)}, u32[]{:S(2)}) collective-permute-start(f32[2,128,128]{2,1,0:T(8,128)} %own.1), channel_id=1, source_target_pairs={{1,2},{2,1},{3,4},{4,3},{5,6},{6,5},{7,8},{8,7},{9,10},{10,9},{11,... | collective-permute-start | bytes 393224 | tf_op jit(solution)/shard_map/ppermute | solution.py:416
  4.5 9.8 %spectra.1.spec_far = f32[24,256,384]{2,1,0:T(8,128)} custom-call(s32[24]{0:T(128)} %radii.1, f32[24,2,128,128]{3,2,1,0:T(8,128)} %taps_far.1, bf16[256,512]{1,0:T(8,128)(2,1)} %constant.12.clone.row_ref, bf16[512,256]{1,0:T(8,128)(2,1)} %constant.13.clone.head_ref, bf16[256,256]{1,0:T(8,128)(2,1)} %constant.14.clone.tail_ref), custom_call_target="tpu_custom_call" | custom-call | flops 17999998976 | bytes 14000000 | tf_op jit(solution)/shard_map/spectra/pallas_call | solution.py:438
  14.3 0.0 collective-permute-done.near
  14.3 0.0 collective-permute-done.1.far
  14.3 0.0 copy-done
  14.3 0.0 copy-done.3
  14.3 0.0 copy-done.2
  14.3 0.0 copy-done.1
  14.3 17.5 %fields.1 = (f32[3,128,128]{2,1,0:T(8,128)}, f32[2,128,128]{2,1,0:T(8,128)S(1)}, f32[2,64,128]{2,1,0:T(8,128)S(1)}, f32[2,64,128]{2,1,0:T(8,128)S(1)}) custom-call(s32[24]{0:T(128)S(1)} %copy-done.2, f32[24]{0:T(128)S(1)} %copy-done.3, s32[1]{0:T(128)} %bitcast.place, f32[2,128,128]{2,1,0:T(8,128)S(1)} %copy-done, ...), custom_call_target="tpu_custom_call" | custom-call | tf_op jit(solution)/shard_map/fields/pallas_call | solution.py:459
  31.8 0.1 collective-permute-start.2
  31.9 3.5 %collective-permute-start.3 = (f32[2,64,128]{2,1,0:T(8,128)S(1)}, f32[2,64,128]{2,1,0:T(8,128)S(1)}, u32[]{:S(2)}, u32[]{:S(2)}) collective-permute-start(f32[2,64,128]{2,1,0:T(8,128)S(1)} %get-tuple-element.9), channel_id=1, source_target_pairs={{1,2},{2,1},{3,4},{4,3},{5,6},{6,5},{7,8},{8,7},{9,10},{10,9},{11,... | collective-permute-start | bytes 196616 | tf_op jit(solution)/shard_map/ppermute | solution.py:486
  35.4 0.0 collective-permute-done.2.near
  35.5 2.9 %collective-permute-done.3.far = f32[2,64,128]{2,1,0:T(8,128)S(1)} collective-permute-done((f32[2,64,128]{2,1,0:T(8,128)S(1)}, f32[2,64,128]{2,1,0:T(8,128)S(1)}, u32[]{:S(2)}, u32[]{:S(2)}) %collective-permute-start.3) | collective-permute-done | bytes 65568 | tf_op jit(solution)/shard_map/ppermute | solution.py:486
  38.4 0.7 %join.1 = f32[2,128,128]{2,1,0:T(8,128)} custom-call(s32[1]{0:T(128)} %bitcast.place, f32[2,128,128]{2,1,0:T(8,128)S(1)} %get-tuple-element.7.own, f32[2,64,128]{2,1,0:T(8,128)S(1)} %collective-permute-done.2.near, f32[2,64,128]{2,1,0:T(8,128)S(1)} %collective-permute-done.3.far), custom_call_target="tpu_custom_call" | custom-call | tf_op jit(solution)/shard_map/join/pallas_call | solution.py:487
Async XLA Ops:
  0.6 13.6 %copy-start = (f32[2,128,128]{2,1,0:T(8,128)S(1)}, f32[2,128,128]{2,1,0:T(8,128)}, u32[]{:S(2)}) copy-start(f32[2,128,128]{2,1,0:T(8,128)} %own.1) | copy-start | bytes 393220
  0.6 13.6 %copy-start.3 = (f32[24]{0:T(128)S(1)}, f32[24]{0:T(128)}, u32[]{:S(2)}) copy-start(f32[24]{0:T(128)} %weight.1) | copy-start | bytes 292
  0.7 13.6 %copy-start.2 = (s32[24]{0:T(128)S(1)}, s32[24]{0:T(128)}, u32[]{:S(2)}) copy-start(s32[24]{0:T(128)} %group.1) | copy-start | bytes 292
  0.7 13.6 %copy-start.1 = (s32[128,128]{1,0:T(8,128)S(1)}, s32[128,128]{1,0:T(8,128)}, u32[]{:S(2)}) copy-start(s32[128,128]{1,0:T(8,128)} %target.1) | copy-start | bytes 196612
  0.7 13.6 %collective-permute-start = (f32[2,128,128]{2,1,0:T(8,128)}, f32[2,128,128]{2,1,0:T(8,128)S(1)}, u32[]{:S(2)}, u32[]{:S(2)}) collective-permute-start(f32[2,128,128]{2,1,0:T(8,128)} %own.1), channel_id=1, source_target_pairs={{0,1},{1,0},{2,3},{3,2},{4,5},{5,4},{6,7},{7,6},{8,9},{9,8},{10,11... | collective-permute-start | bytes 393224 | tf_op jit(solution)/shard_map/ppermute | solution.py:415
  1.4 12.9 %collective-permute-start.1 = (f32[2,128,128]{2,1,0:T(8,128)}, f32[2,128,128]{2,1,0:T(8,128)S(1)}, u32[]{:S(2)}, u32[]{:S(2)}) collective-permute-start(f32[2,128,128]{2,1,0:T(8,128)} %own.1), channel_id=1, source_target_pairs={{1,2},{2,1},{3,4},{4,3},{5,6},{6,5},{7,8},{8,7},{9,10},{10,9},{11,... | collective-permute-start | bytes 393224 | tf_op jit(solution)/shard_map/ppermute | solution.py:416
  31.8 3.6 %collective-permute-start.2 = (f32[2,64,128]{2,1,0:T(8,128)S(1)}, f32[2,64,128]{2,1,0:T(8,128)S(1)}, u32[]{:S(2)}, u32[]{:S(2)}) collective-permute-start(f32[2,64,128]{2,1,0:T(8,128)S(1)} %get-tuple-element.8), channel_id=1, source_target_pairs={{0,1},{1,0},{2,3},{3,2},{4,5},{5,4},{6,7},{7,6},{8,9},{9,8},{10,11... | collective-permute-start | bytes 196616 | tf_op jit(solution)/shard_map/ppermute | solution.py:485
  31.9 6.5 %collective-permute-start.3 = (f32[2,64,128]{2,1,0:T(8,128)S(1)}, f32[2,64,128]{2,1,0:T(8,128)S(1)}, u32[]{:S(2)}, u32[]{:S(2)}) collective-permute-start(f32[2,64,128]{2,1,0:T(8,128)S(1)} %get-tuple-element.9), channel_id=1, source_target_pairs={{1,2},{2,1},{3,4},{4,3},{5,6},{6,5},{7,8},{8,7},{9,10},{10,9},{11,... | collective-permute-start | bytes 196616 | tf_op jit(solution)/shard_map/ppermute | solution.py:486

commit v24 on v22

--- a/solution.py
+++ b/solution.py
@@ -14,14 +14,15 @@
 GROUPS = 3
 STEEPNESS = 1.0
 THRESHOLD = 2.0
-BATCH = 8
+BATCH = 12
+EARLY = 4
+LATE_BATCH = 10
 PIECE = 256
 
 f32 = jnp.float32
 bf16 = jnp.bfloat16
 MIB = 1024 * 1024
-SPECTRA_LIMIT = 45
-LIMIT = 34
+LIMIT = 53
 
 
 def halves(table, axis):
@@ -182,53 +183,48 @@
     return pltpu.roll(x, x.shape[1] // 2, 1)
 
 
-def spectra_body(radii, taps_far, row_ref, head_ref, tail_ref, spec, taps, in_sems):
-    kernels, _, span, _ = taps.shape
-    row_fwd, head, tail = row_ref[...], head_ref[...], tail_ref[...]
-    steps = in_sems.shape[0]
-    batch = kernels // steps
-
-    def fetch(i):
-        here = pl.ds(i * batch, batch)
-        return pltpu.make_async_copy(taps_far.at[here], taps.at[here], in_sems.at[i])
-
-    for i in range(steps):
-        fetch(i).start()
+def spectra_of(radii, taps, spec, first, batch, row_fwd, head, tail):
+    span = taps.shape[2]
     row_at = lax.broadcasted_iota(jnp.int32, (span, span), 0) - span // 2
     col_at = lax.broadcasted_iota(jnp.int32, (span, span), 1) - span // 2
     reach = jnp.maximum(jnp.maximum(row_at, -1 - row_at), jnp.maximum(col_at, -1 - col_at))
 
-    def step(i, carry):
-        fetch(i).wait()
-
-        def rows_of(p):
-            planes = [[], []]
-            for j in range(2):
-                k = i * batch + 2 * p + j
-                inside = reach < radii[k]
-                for c in range(2):
-                    planes[c].append(jnp.where(inside, taps[k, c], 0.0))
-            re, im = [jnp.concatenate(plane, axis=1) for plane in planes]
-            return row_stage(quarters_of(re, im, span // 2), row_fwd, span)
-
-        def cols_of(p, tiles):
-            for j in range(2):
-                k = i * batch + 2 * p + j
-                a, b = to_freqs(tiles[j], head, tail)
-                spec[k, :, :a.shape[1]] = a
-                spec[k, :, a.shape[1]:] = b
-
-        staggered(batch // 2, rows_of, cols_of)
-        return carry
-
-    lax.fori_loop(0, steps, step, 0)
+    def rows_of(p):
+        planes = [[], []]
+        for j in range(2):
+            k = first + 2 * p + j
+            inside = reach < radii[k]
+            for c in range(2):
+                planes[c].append(jnp.where(inside, taps[k, c], 0.0))
+        re, im = [jnp.concatenate(plane, axis=1) for plane in planes]
+        return row_stage(quarters_of(re, im, span // 2), row_fwd, span)
+
+    def cols_of(p, tiles):
+        for j in range(2):
+            k = first + 2 * p + j
+            a, b = to_freqs(tiles[j], head, tail)
+            spec[k, :, :a.shape[1]] = a
+            spec[k, :, a.shape[1]:] = b
+
+    staggered(batch // 2, rows_of, cols_of)
+
+
+def spectra_body(radii, taps_far, row_ref, head_ref, tail_ref, spec_far, taps, spec, in_sem, out_sem):
+    early = spec.shape[0]
+    fetch = pltpu.make_async_copy(taps_far.at[pl.ds(0, early)], taps, in_sem)
+    fetch.start()
+    fetch.wait()
+    spectra_of(radii, taps, spec, 0, early, row_ref[...], head_ref[...], tail_ref[...])
+    put = pltpu.make_async_copy(spec, spec_far, out_sem)
+    put.start()
+    put.wait()
 
 
 def main_body(
-    group, weight, place,
-    own, near, far, target, spec, tables_far,
+    group, weight, place, radii,
+    own, near, far, target, taps_far, spec_far, tables_far,
     resist_far, grad_own, near_rim, far_rim,
-    field, mask_spec, resist, slopes, grad_spec, tables, table_sems, out_sem,
+    spec, taps, field, mask_spec, resist, slopes, grad_spec, tables, spec_sem, taps_sems, table_sems, out_sem,
     *, layout, sections,
 ):
     kernels, grid_rows, _ = spec.shape
@@ -236,6 +232,15 @@
     rim = (grid_rows - count) // 2
     batch = BATCH
     steps = kernels // batch
+    early = spec_far.shape[0]
+    late_steps = taps_sems.shape[0]
+    late = (kernels - early) // late_steps
+
+    fetch_early = pltpu.make_async_copy(spec_far, spec.at[pl.ds(0, early)], spec_sem)
+
+    def fetch_taps(i):
+        here = pl.ds(early + i * late, late)
+        return pltpu.make_async_copy(taps_far.at[here], taps.at[here], taps_sems.at[i])
 
     def fetch_table(i):
         here = pl.ds(sections[i][0], sections[i][1])
@@ -247,12 +252,25 @@
         return jnp.concatenate(parts, axis=1)
 
     fetch_table(0).start()
+    for i in range(late_steps):
+        fetch_taps(i).start()
     fetch_table(1).start()
-    fetch_table(2).start()
+    fetch_early.start()
+    slopes[...] = jnp.zeros(slopes.shape, f32)
+    grad_spec[...] = jnp.zeros(grad_spec.shape, f32)
     fetch_table(0).wait()
+    row_fwd, head, tail = table("row_fwd"), table("head"), table("tail")
+
+    def spectra(i, carry):
+        fetch_taps(i).wait()
+        spectra_of(radii, taps, spec, early + i * late, late, row_fwd, head, tail)
+        return carry
+
+    lax.fori_loop(0, late_steps, spectra, 0)
+    fetch_table(1).wait()
+    fetch_early.wait()
 
     odd = place[0] % 2 == 1
-    row_fwd = table("row_fwd")
     above, below = [], []
     for c in range(2):
         above.append(jnp.where(odd, near[c, count - rim:], far[c, count - rim:]))
@@ -267,9 +285,6 @@
     mask_spec[:, 2 * width:3 * width] = jnp.where(real_half, m_rest, turned)
     mask_spec[:, 3 * width:] = jnp.where(real_half, -turned, m_rest)
 
-    slopes[...] = jnp.zeros(slopes.shape, f32)
-    grad_spec[...] = jnp.zeros(grad_spec.shape, f32)
-    fetch_table(1).wait()
     col_inv, row_inv = table("col_inv"), table("row_inv")
 
     def forward(i, carry):
@@ -314,8 +329,6 @@
         slopes[g] = 2.0 * (seen - wanted) * seen * (1.0 - seen) * STEEPNESS
     out = pltpu.make_async_copy(resist, resist_far, out_sem)
     out.start()
-    fetch_table(2).wait()
-    head, tail = table("head"), table("tail")
 
     def backward(i, carry):
         def rows_of(p):
@@ -392,7 +405,7 @@
     rim = span // 2
     grid_rows = count + 2 * rim
     grid_cols = width + rim
-    assert count == span and width == span and kernels % BATCH == 0 and BATCH % 2 == 0 and count == 2 * rim
+    assert count == span and width == span and kernels % BATCH == 0 and (kernels - EARLY) % LATE_BATCH == 0 and count == 2 * rim
 
     strips = lax.axis_size("row")
     assert strips % 2 == 0
@@ -424,22 +437,23 @@
     hbm = pl.BlockSpec(memory_space=pltpu.HBM)
     spectra = pl.pallas_call(
         spectra_body,
-        out_shape=jax.ShapeDtypeStruct((kernels, grid_rows, 2 * grid_cols), f32),
-        in_specs=[smem, hbm] + [vmem] * 3,
-        out_specs=vmem,
+        out_shape=jax.ShapeDtypeStruct((EARLY, grid_rows, 2 * grid_cols), f32),
+        in_specs=[smem, hbm, vmem, vmem, vmem],
+        out_specs=hbm,
         scratch_shapes=[
-            pltpu.VMEM(kernel_taps.shape, f32),
-            pltpu.SemaphoreType.DMA((kernels // BATCH,)),
+            pltpu.VMEM((EARLY,) + kernel_taps.shape[1:], f32),
+            pltpu.VMEM((EARLY, grid_rows, 2 * grid_cols), f32),
+            pltpu.SemaphoreType.DMA,
+            pltpu.SemaphoreType.DMA,
         ],
-        compiler_params=pltpu.CompilerParams(vmem_limit_bytes=SPECTRA_LIMIT * MIB),
-        cost_estimate=pl.CostEstimate(flops=18 * 10**9, bytes_accessed=14 * 10**6, transcendentals=0),
+        compiler_params=pltpu.CompilerParams(vmem_limit_bytes=56 * MIB),
+        cost_estimate=pl.CostEstimate(flops=3 * 10**9, bytes_accessed=3 * 10**6, transcendentals=0),
         name="spectra",
     )(kernel_radii, kernel_taps, *map(jnp.asarray, (row_fwd, head, tail)))
 
     tables, layout, sections = stacked([
-        {"row_fwd": row_fwd, "mask_head": mask_head, "mask_tail": mask_tail},
-        {"col_inv": col_inv, "row_inv": row_inv},
-        {"head": head, "tail": tail, "grad_col": grad_col},
+        {"row_fwd": row_fwd, "head": head, "tail": tail},
+        {"mask_head": mask_head, "mask_tail": mask_tail, "col_inv": col_inv, "row_inv": row_inv, "grad_col": grad_col},
     ])
     resist, own, near_rim, far_rim = pl.pallas_call(
         functools.partial(main_body, layout=layout, sections=sections),
@@ -449,21 +463,25 @@
             jax.ShapeDtypeStruct((2, rim, width), f32),
             jax.ShapeDtypeStruct((2, rim, width), f32),
         ],
-        in_specs=[smem] * 3 + [vmem] * 5 + [hbm],
+        in_specs=[smem] * 4 + [vmem] * 4 + [hbm] * 3,
         out_specs=[hbm] + [vmem] * 3,
         scratch_shapes=[
+            pltpu.VMEM((kernels, grid_rows, 2 * grid_cols), f32),
+            pltpu.VMEM(kernel_taps.shape, f32),
             pltpu.VMEM((kernels // 2, 2 * count, 2 * width), f32),
             pltpu.VMEM((grid_rows, 4 * width), f32),
             pltpu.VMEM((GROUPS, count, width), f32),
             pltpu.VMEM((GROUPS, count, width), f32),
             pltpu.VMEM((grid_rows, 4 * width), f32),
             pltpu.VMEM(tables.shape, bf16),
+            pltpu.SemaphoreType.DMA,
+            pltpu.SemaphoreType.DMA(((kernels - EARLY) // LATE_BATCH,)),
             pltpu.SemaphoreType.DMA((len(sections),)),
             pltpu.SemaphoreType.DMA,
         ],
         compiler_params=pltpu.CompilerParams(vmem_limit_bytes=LIMIT * MIB),
         name="fields",
-    )(kernel_group, kernel_weight, place, mask_field, near, far, target, spectra, jnp.asarray(tables))
+    )(kernel_group, kernel_weight, place, kernel_radii, mask_field, near, far, target, kernel_taps, spectra, jnp.asarray(tables))
 
     near_in = lax.ppermute(near_rim, "row", near_pairs)
     far_in = lax.ppermute(far_rim, "row", far_pairs)

time: 48.5 us -> 38.9 us (0.80)
  local copies, waits for them, and re-layouts: 9.04 us -> 0.02 us
    unnamed x22 -> x10, local copies, waits for them, and re-layouts: 9.04 us -> 0.02 us
    pallas_call x1, Pallas kernels: 10.9 us -> 4.45 us  [on_device(): pl.pallas_call(spectra_body, out_shape=jax.ShapeDtypeStruct((EARLY, grid_...]
    pallas_call x1, Pallas kernels: 16.2 us -> 22.3 us  [on_device(): pl.pallas_call(functools.partial(main_body, layout=layout, sections=secti...]
  transfers between devices with their start and end apart: 4 -> 4, of which waited for: 1 -> 1; matrix products, arithmetic and copies ran while one was open for 0% -> 0% of each run, Pallas kernels for 23% -> 12%
where the time goes in v24:
time: 38.9 us; the launch traced here: 38.6 us
  Pallas kernels  27.4 us (70%)
  starting transfers between devices  7.69 us (20%)
  waiting for transfers between devices  2.78 us (7%)
  between operations  0.78 us (2%)
    pallas_call x1, Pallas kernels, on_device(): pl.pallas_call(functools.partial(main_body, layout=layout, sections=secti...  22.3 us
    pallas_call x1, Pallas kernels, on_device(): pl.pallas_call(spectra_body, out_shape=jax.ShapeDtypeStruct((EARLY, grid_...  4.45 us
    ppermute x1, starting transfers between devices, on_device(): far_in = lax.ppermute(far_rim, 'row', far_pairs)  3.7 us
    ppermute x1, starting transfers between devices, on_device(): far = lax.ppermute(mask_field, 'row', far_pairs)  3.18 us
    ppermute x1, waiting for transfers between devices, on_device(): far_in = lax.ppermute(far_rim, 'row', far_pairs)  2.77 us
  transfers between devices with their start and end apart: 4, of which 1 were waited for; matrix products, arithmetic and copies ran while one was open for 0% of the time, Pallas kernels for 12%

profile of v24, /device:TPU:21, one launch (start us, length us, event | category | flops | bytes accessed | tf_op | source)
XLA Modules:
  0.0 38.6 jit_solution(7489279965068940025)
XLA Ops:
  0.6 0.0 copy-start
  0.6 0.0 copy-start.4
  0.7 0.0 copy-start.3
  0.7 0.0 copy-start.2
  0.7 0.0 copy-start.1
  0.7 0.7 %collective-permute-start = (f32[2,128,128]{2,1,0:T(8,128)}, f32[2,128,128]{2,1,0:T(8,128)S(1)}, u32[]{:S(2)}, u32[]{:S(2)}) collective-permute-start(f32[2,128,128]{2,1,0:T(8,128)} %own.1), channel_id=1, source_target_pairs={{0,1},{1,0},{2,3},{3,2},{4,5},{5,4},{6,7},{7,6},{8,9},{9,8},{10,11... | collective-permute-start | bytes 393224 | tf_op jit(solution)/shard_map/ppermute | solution.py:415
  1.4 3.2 %collective-permute-start.1 = (f32[2,128,128]{2,1,0:T(8,128)}, f32[2,128,128]{2,1,0:T(8,128)S(1)}, u32[]{:S(2)}, u32[]{:S(2)}) collective-permute-start(f32[2,128,128]{2,1,0:T(8,128)} %own.1), channel_id=1, source_target_pairs={{1,2},{2,1},{3,4},{4,3},{5,6},{6,5},{7,8},{8,7},{9,10},{10,9},{11,... | collective-permute-start | bytes 393224 | tf_op jit(solution)/shard_map/ppermute | solution.py:416
  4.6 4.5 %spectra.1.spec_far = f32[4,256,384]{2,1,0:T(8,128)} custom-call(s32[24]{0:T(128)} %radii.3, f32[24,2,128,128]{3,2,1,0:T(8,128)} %taps_far.3, bf16[256,512]{1,0:T(8,128)(2,1)} %constant.12.clone.row_ref, bf16[512,256]{1,0:T(8,128)(2,1)} %constant.13.clone.head_ref, bf16[256,256]{1,0:T(8,128)(2,1)} %constant.14.clone.tail_ref), custom_call_target="tpu_custom_call" | custom-call | flops 3000000000 | bytes 3000000 | tf_op jit(solution)/shard_map/spectra/pallas_call | solution.py:438
  9.1 0.0 collective-permute-done.near
  9.1 0.0 collective-permute-done.1.far
  9.1 0.0 copy-done
  9.1 0.0 copy-done.4
  9.1 0.0 copy-done.3
  9.1 0.0 copy-done.2
  9.1 0.0 copy-done.1
  9.1 22.3 %fields.1 = (f32[3,128,128]{2,1,0:T(8,128)}, f32[2,128,128]{2,1,0:T(8,128)S(1)}, f32[2,64,128]{2,1,0:T(8,128)S(1)}, f32[2,64,128]{2,1,0:T(8,128)S(1)}) custom-call(s32[24]{0:T(128)S(1)} %copy-done.2, f32[24]{0:T(128)S(1)} %copy-done.3, s32[1]{0:T(128)} %bitcast.place, s32[24]{0:T(128)S(1)} %copy-done.4, f32[2,128,128]{2,1,0:T(8,128)S(1)} %copy-done, ...), custom_call_target="tpu_custom_call" | custom-call | tf_op jit(solution)/shard_map/fields/pallas_call | solution.py:458
  31.4 0.1 collective-permute-start.2
  31.5 3.7 %collective-permute-start.3 = (f32[2,64,128]{2,1,0:T(8,128)S(1)}, f32[2,64,128]{2,1,0:T(8,128)S(1)}, u32[]{:S(2)}, u32[]{:S(2)}) collective-permute-start(f32[2,64,128]{2,1,0:T(8,128)S(1)} %get-tuple-element.9), channel_id=1, source_target_pairs={{1,2},{2,1},{3,4},{4,3},{5,6},{6,5},{7,8},{8,7},{9,10},{10,9},{11,... | collective-permute-start | bytes 196616 | tf_op jit(solution)/shard_map/ppermute | solution.py:487
  35.2 0.0 collective-permute-done.2.near
  35.2 2.8 %collective-permute-done.3.far = f32[2,64,128]{2,1,0:T(8,128)S(1)} collective-permute-done((f32[2,64,128]{2,1,0:T(8,128)S(1)}, f32[2,64,128]{2,1,0:T(8,128)S(1)}, u32[]{:S(2)}, u32[]{:S(2)}) %collective-permute-start.3) | collective-permute-done | bytes 65568 | tf_op jit(solution)/shard_map/ppermute | solution.py:487
  38.0 0.7 %join.1 = f32[2,128,128]{2,1,0:T(8,128)} custom-call(s32[1]{0:T(128)} %bitcast.place, f32[2,128,128]{2,1,0:T(8,128)S(1)} %get-tuple-element.7.own, f32[2,64,128]{2,1,0:T(8,128)S(1)} %collective-permute-done.2.near, f32[2,64,128]{2,1,0:T(8,128)S(1)} %collective-permute-done.3.far), custom_call_target="tpu_custom_call" | custom-call | tf_op jit(solution)/shard_map/join/pallas_call | solution.py:488
Async XLA Ops:
  0.6 8.5 %copy-start = (f32[2,128,128]{2,1,0:T(8,128)S(1)}, f32[2,128,128]{2,1,0:T(8,128)}, u32[]{:S(2)}) copy-start(f32[2,128,128]{2,1,0:T(8,128)} %own.1) | copy-start | bytes 393220
  0.6 8.5 %copy-start.4 = (s32[24]{0:T(128)S(1)}, s32[24]{0:T(128)}, u32[]{:S(2)}) copy-start(s32[24]{0:T(128)} %radii.3) | copy-start | bytes 292
  0.7 8.5 %copy-start.3 = (f32[24]{0:T(128)S(1)}, f32[24]{0:T(128)}, u32[]{:S(2)}) copy-start(f32[24]{0:T(128)} %weight.1) | copy-start | bytes 292
  0.7 8.5 %copy-start.2 = (s32[24]{0:T(128)S(1)}, s32[24]{0:T(128)}, u32[]{:S(2)}) copy-start(s32[24]{0:T(128)} %group.1) | copy-start | bytes 292
  0.7 8.5 %copy-start.1 = (s32[128,128]{1,0:T(8,128)S(1)}, s32[128,128]{1,0:T(8,128)}, u32[]{:S(2)}) copy-start(s32[128,128]{1,0:T(8,128)} %target.1) | copy-start | bytes 196612
  0.7 8.4 %collective-permute-start = (f32[2,128,128]{2,1,0:T(8,128)}, f32[2,128,128]{2,1,0:T(8,128)S(1)}, u32[]{:S(2)}, u32[]{:S(2)}) collective-permute-start(f32[2,128,128]{2,1,0:T(8,128)} %own.1), channel_id=1, source_target_pairs={{0,1},{1,0},{2,3},{3,2},{4,5},{5,4},{6,7},{7,6},{8,9},{9,8},{10,11... | collective-permute-start | bytes 393224 | tf_op jit(solution)/shard_map/ppermute | solution.py:415
  1.4 7.7 %collective-permute-start.1 = (f32[2,128,128]{2,1,0:T(8,128)}, f32[2,128,128]{2,1,0:T(8,128)S(1)}, u32[]{:S(2)}, u32[]{:S(2)}) collective-permute-start(f32[2,128,128]{2,1,0:T(8,128)} %own.1), channel_id=1, source_target_pairs={{1,2},{2,1},{3,4},{4,3},{5,6},{6,5},{7,8},{8,7},{9,10},{10,9},{11,... | collective-permute-start | bytes 393224 | tf_op jit(solution)/shard_map/ppermute | solution.py:416
  31.4 3.8 %collective-permute-start.2 = (f32[2,64,128]{2,1,0:T(8,128)S(1)}, f32[2,64,128]{2,1,0:T(8,128)S(1)}, u32[]{:S(2)}, u32[]{:S(2)}) collective-permute-start(f32[2,64,128]{2,1,0:T(8,128)S(1)} %get-tuple-element.8), channel_id=1, source_target_pairs={{0,1},{1,0},{2,3},{3,2},{4,5},{5,4},{6,7},{7,6},{8,9},{9,8},{10,11... | collective-permute-start | bytes 196616 | tf_op jit(solution)/shard_map/ppermute | solution.py:486
  31.5 6.5 %collective-permute-start.3 = (f32[2,64,128]{2,1,0:T(8,128)S(1)}, f32[2,64,128]{2,1,0:T(8,128)S(1)}, u32[]{:S(2)}, u32[]{:S(2)}) collective-permute-start(f32[2,64,128]{2,1,0:T(8,128)S(1)} %get-tuple-element.9), channel_id=1, source_target_pairs={{1,2},{2,1},{3,4},{4,3},{5,6},{6,5},{7,8},{8,7},{9,10},{10,9},{11,... | collective-permute-start | bytes 196616 | tf_op jit(solution)/shard_map/ppermute | solution.py:487

commit v25 on v24

--- a/solution.py
+++ b/solution.py
@@ -132,12 +132,10 @@
     high, low = parts
     rows, depth = high.shape
     lanes = tail.shape[1] // 2
-    stack = jnp.concatenate([high, low], axis=0)
-    both = jnp.dot(stack, head[:depth], preferred_element_type=f32)
-    third = jnp.dot(high, head[depth:], preferred_element_type=f32)
-    first = both[:rows] + (both[rows:] + third)
-    both = jnp.dot(stack, tail, preferred_element_type=f32)
-    return first, both[:rows, :lanes] + (both[:rows, lanes:] + both[rows:, :lanes])
+    right = jnp.concatenate([head, head[:depth]], axis=0)
+    first = dot(jnp.concatenate([high, high, low], axis=1), right)
+    rest = dot(jnp.concatenate([high, low], axis=1), jnp.concatenate([tail, tail], axis=0))
+    return first, rest[:, :lanes] + rest[:, lanes:]
 
 
 def beside(classes, at, width):

time: 38.9 us -> 38.8 us (level)
  no operation moved by 1% of the time
where the time goes in v25:
time: 38.8 us; the launch traced here: 38.6 us
  Pallas kernels  27.3 us (70%)
  starting transfers between devices  7.71 us (20%)
  waiting for transfers between devices  2.75 us (7%)
  between operations  0.78 us (2%)
    pallas_call x1, Pallas kernels, on_device(): pl.pallas_call(functools.partial(main_body, layout=layout, sections=secti...  22.2 us
    pallas_call x1, Pallas kernels, on_device(): pl.pallas_call(spectra_body, out_shape=jax.ShapeDtypeStruct((EARLY, grid_...  4.45 us
    ppermute x1, starting transfers between devices, on_device(): far_in = lax.ppermute(far_rim, 'row', far_pairs)  3.72 us
    ppermute x1, starting transfers between devices, on_device(): far = lax.ppermute(mask_field, 'row', far_pairs)  3.18 us
    ppermute x1, waiting for transfers between devices, on_device(): far_in = lax.ppermute(far_rim, 'row', far_pairs)  2.74 us
  transfers between devices with their start and end apart: 4, of which 1 were waited for; matrix products, arithmetic and copies ran while one was open for 0% of the time, Pallas kernels for 12%

profile of v25, /device:TPU:21, one launch (start us, length us, event | category | flops | bytes accessed | tf_op | source)
XLA Modules:
  0.0 38.6 jit_solution(15509957405431622469)
XLA Ops:
  0.6 0.0 copy-start
  0.6 0.0 copy-start.4
  0.7 0.0 copy-start.3
  0.7 0.0 copy-start.2
  0.7 0.0 copy-start.1
  0.7 0.7 %collective-permute-start = (f32[2,128,128]{2,1,0:T(8,128)}, f32[2,128,128]{2,1,0:T(8,128)S(1)}, u32[]{:S(2)}, u32[]{:S(2)}) collective-permute-start(f32[2,128,128]{2,1,0:T(8,128)} %own.1), channel_id=1, source_target_pairs={{0,1},{1,0},{2,3},{3,2},{4,5},{5,4},{6,7},{7,6},{8,9},{9,8},{10,11... | collective-permute-start | bytes 393224 | tf_op jit(solution)/shard_map/ppermute | solution.py:413
  1.4 3.2 %collective-permute-start.1 = (f32[2,128,128]{2,1,0:T(8,128)}, f32[2,128,128]{2,1,0:T(8,128)S(1)}, u32[]{:S(2)}, u32[]{:S(2)}) collective-permute-start(f32[2,128,128]{2,1,0:T(8,128)} %own.1), channel_id=1, source_target_pairs={{1,2},{2,1},{3,4},{4,3},{5,6},{6,5},{7,8},{8,7},{9,10},{10,9},{11,... | collective-permute-start | bytes 393224 | tf_op jit(solution)/shard_map/ppermute | solution.py:414
  4.6 4.4 %spectra.1.spec_far = f32[4,256,384]{2,1,0:T(8,128)} custom-call(s32[24]{0:T(128)} %radii.3, f32[24,2,128,128]{3,2,1,0:T(8,128)} %taps_far.3, bf16[256,512]{1,0:T(8,128)(2,1)} %constant.12.clone.row_ref, bf16[512,256]{1,0:T(8,128)(2,1)} %constant.13.clone.head_ref, bf16[256,256]{1,0:T(8,128)(2,1)} %constant.14.clone.tail_ref), custom_call_target="tpu_custom_call" | custom-call | flops 3000000000 | bytes 3000000 | tf_op jit(solution)/shard_map/spectra/pallas_call | solution.py:436
  9.1 0.0 collective-permute-done.near
  9.1 0.0 collective-permute-done.1.far
  9.1 0.0 copy-done
  9.1 0.0 copy-done.4
  9.1 0.0 copy-done.3
  9.1 0.0 copy-done.2
  9.1 0.0 copy-done.1
  9.1 22.2 %fields.1 = (f32[3,128,128]{2,1,0:T(8,128)}, f32[2,128,128]{2,1,0:T(8,128)S(1)}, f32[2,64,128]{2,1,0:T(8,128)S(1)}, f32[2,64,128]{2,1,0:T(8,128)S(1)}) custom-call(s32[24]{0:T(128)S(1)} %copy-done.2, f32[24]{0:T(128)S(1)} %copy-done.3, s32[1]{0:T(128)} %bitcast.place, s32[24]{0:T(128)S(1)} %copy-done.4, f32[2,128,128]{2,1,0:T(8,128)S(1)} %copy-done, ...), custom_call_target="tpu_custom_call" | custom-call | tf_op jit(solution)/shard_map/fields/pallas_call | solution.py:456
  31.3 0.1 collective-permute-start.2
  31.4 3.7 %collective-permute-start.3 = (f32[2,64,128]{2,1,0:T(8,128)S(1)}, f32[2,64,128]{2,1,0:T(8,128)S(1)}, u32[]{:S(2)}, u32[]{:S(2)}) collective-permute-start(f32[2,64,128]{2,1,0:T(8,128)S(1)} %get-tuple-element.9), channel_id=1, source_target_pairs={{1,2},{2,1},{3,4},{4,3},{5,6},{6,5},{7,8},{8,7},{9,10},{10,9},{11,... | collective-permute-start | bytes 196616 | tf_op jit(solution)/shard_map/ppermute | solution.py:485
  35.1 0.0 collective-permute-done.2.near
  35.1 2.7 %collective-permute-done.3.far = f32[2,64,128]{2,1,0:T(8,128)S(1)} collective-permute-done((f32[2,64,128]{2,1,0:T(8,128)S(1)}, f32[2,64,128]{2,1,0:T(8,128)S(1)}, u32[]{:S(2)}, u32[]{:S(2)}) %collective-permute-start.3) | collective-permute-done | bytes 65568 | tf_op jit(solution)/shard_map/ppermute | solution.py:485
  37.9 0.7 %join.1 = f32[2,128,128]{2,1,0:T(8,128)} custom-call(s32[1]{0:T(128)} %bitcast.place, f32[2,128,128]{2,1,0:T(8,128)S(1)} %get-tuple-element.7.own, f32[2,64,128]{2,1,0:T(8,128)S(1)} %collective-permute-done.2.near, f32[2,64,128]{2,1,0:T(8,128)S(1)} %collective-permute-done.3.far), custom_call_target="tpu_custom_call" | custom-call | tf_op jit(solution)/shard_map/join/pallas_call | solution.py:486
Async XLA Ops:
  0.6 8.5 %copy-start = (f32[2,128,128]{2,1,0:T(8,128)S(1)}, f32[2,128,128]{2,1,0:T(8,128)}, u32[]{:S(2)}) copy-start(f32[2,128,128]{2,1,0:T(8,128)} %own.1) | copy-start | bytes 393220
  0.6 8.5 %copy-start.4 = (s32[24]{0:T(128)S(1)}, s32[24]{0:T(128)}, u32[]{:S(2)}) copy-start(s32[24]{0:T(128)} %radii.3) | copy-start | bytes 292
  0.7 8.5 %copy-start.3 = (f32[24]{0:T(128)S(1)}, f32[24]{0:T(128)}, u32[]{:S(2)}) copy-start(f32[24]{0:T(128)} %weight.1) | copy-start | bytes 292
  0.7 8.5 %copy-start.2 = (s32[24]{0:T(128)S(1)}, s32[24]{0:T(128)}, u32[]{:S(2)}) copy-start(s32[24]{0:T(128)} %group.1) | copy-start | bytes 292
  0.7 8.5 %copy-start.1 = (s32[128,128]{1,0:T(8,128)S(1)}, s32[128,128]{1,0:T(8,128)}, u32[]{:S(2)}) copy-start(s32[128,128]{1,0:T(8,128)} %target.1) | copy-start | bytes 196612
  0.7 8.4 %collective-permute-start = (f32[2,128,128]{2,1,0:T(8,128)}, f32[2,128,128]{2,1,0:T(8,128)S(1)}, u32[]{:S(2)}, u32[]{:S(2)}) collective-permute-start(f32[2,128,128]{2,1,0:T(8,128)} %own.1), channel_id=1, source_target_pairs={{0,1},{1,0},{2,3},{3,2},{4,5},{5,4},{6,7},{7,6},{8,9},{9,8},{10,11... | collective-permute-start | bytes 393224 | tf_op jit(solution)/shard_map/ppermute | solution.py:413
  1.4 7.7 %collective-permute-start.1 = (f32[2,128,128]{2,1,0:T(8,128)}, f32[2,128,128]{2,1,0:T(8,128)S(1)}, u32[]{:S(2)}, u32[]{:S(2)}) collective-permute-start(f32[2,128,128]{2,1,0:T(8,128)} %own.1), channel_id=1, source_target_pairs={{1,2},{2,1},{3,4},{4,3},{5,6},{6,5},{7,8},{8,7},{9,10},{10,9},{11,... | collective-permute-start | bytes 393224 | tf_op jit(solution)/shard_map/ppermute | solution.py:414
  31.3 3.8 %collective-permute-start.2 = (f32[2,64,128]{2,1,0:T(8,128)S(1)}, f32[2,64,128]{2,1,0:T(8,128)S(1)}, u32[]{:S(2)}, u32[]{:S(2)}) collective-permute-start(f32[2,64,128]{2,1,0:T(8,128)S(1)} %get-tuple-element.8), channel_id=1, source_target_pairs={{0,1},{1,0},{2,3},{3,2},{4,5},{5,4},{6,7},{7,6},{8,9},{9,8},{10,11... | collective-permute-start | bytes 196616 | tf_op jit(solution)/shard_map/ppermute | solution.py:484
  31.4 6.5 %collective-permute-start.3 = (f32[2,64,128]{2,1,0:T(8,128)S(1)}, f32[2,64,128]{2,1,0:T(8,128)S(1)}, u32[]{:S(2)}, u32[]{:S(2)}) collective-permute-start(f32[2,64,128]{2,1,0:T(8,128)S(1)} %get-tuple-element.9), channel_id=1, source_target_pairs={{1,2},{2,1},{3,4},{4,3},{5,6},{6,5},{7,8},{8,7},{9,10},{10,9},{11,... | collective-permute-start | bytes 196616 | tf_op jit(solution)/shard_map/ppermute | solution.py:485

commit v26 on v25

--- a/solution.py
+++ b/solution.py
@@ -207,20 +207,13 @@
     staggered(batch // 2, rows_of, cols_of)
 
 
-def spectra_body(radii, taps_far, row_ref, head_ref, tail_ref, spec_far, taps, spec, in_sem, out_sem):
-    early = spec.shape[0]
-    fetch = pltpu.make_async_copy(taps_far.at[pl.ds(0, early)], taps, in_sem)
-    fetch.start()
-    fetch.wait()
-    spectra_of(radii, taps, spec, 0, early, row_ref[...], head_ref[...], tail_ref[...])
-    put = pltpu.make_async_copy(spec, spec_far, out_sem)
-    put.start()
-    put.wait()
+def spectra_body(radii, taps, row_ref, head_ref, tail_ref, spec):
+    spectra_of(radii, taps, spec, 0, spec.shape[0], row_ref[...], head_ref[...], tail_ref[...])
 
 
 def main_body(
     group, weight, place, radii,
-    own, near, far, target, taps_far, spec_far, tables_far,
+    own, near, far, target, row_ref, head_ref, tail_ref, taps_far, spec_far, tables_far,
     resist_far, grad_own, near_rim, far_rim,
     spec, taps, field, mask_spec, resist, slopes, grad_spec, tables, spec_sem, taps_sems, table_sems, out_sem,
     *, layout, sections,
@@ -249,15 +242,13 @@
         parts = [tables[start + b * rows:start + (b + 1) * rows] for b in range(blocks)]
         return jnp.concatenate(parts, axis=1)
 
-    fetch_table(0).start()
     for i in range(late_steps):
         fetch_taps(i).start()
-    fetch_table(1).start()
+    fetch_table(0).start()
     fetch_early.start()
     slopes[...] = jnp.zeros(slopes.shape, f32)
     grad_spec[...] = jnp.zeros(grad_spec.shape, f32)
-    fetch_table(0).wait()
-    row_fwd, head, tail = table("row_fwd"), table("head"), table("tail")
+    row_fwd, head, tail = row_ref[...], head_ref[...], tail_ref[...]
 
     def spectra(i, carry):
         fetch_taps(i).wait()
@@ -265,7 +256,7 @@
         return carry
 
     lax.fori_loop(0, late_steps, spectra, 0)
-    fetch_table(1).wait()
+    fetch_table(0).wait()
     fetch_early.wait()
 
     odd = place[0] % 2 == 1
@@ -433,24 +424,19 @@
     smem = pl.BlockSpec(memory_space=pltpu.SMEM)
     vmem = pl.BlockSpec(memory_space=pltpu.VMEM)
     hbm = pl.BlockSpec(memory_space=pltpu.HBM)
+    early_tables = [jnp.asarray(t) for t in (row_fwd, head, tail)]
     spectra = pl.pallas_call(
         spectra_body,
         out_shape=jax.ShapeDtypeStruct((EARLY, grid_rows, 2 * grid_cols), f32),
-        in_specs=[smem, hbm, vmem, vmem, vmem],
-        out_specs=hbm,
-        scratch_shapes=[
-            pltpu.VMEM((EARLY,) + kernel_taps.shape[1:], f32),
-            pltpu.VMEM((EARLY, grid_rows, 2 * grid_cols), f32),
-            pltpu.SemaphoreType.DMA,
-            pltpu.SemaphoreType.DMA,
-        ],
+        grid=(1,),
+        in_specs=[smem, pl.BlockSpec((EARLY, 2, span, span), lambda i: (0, 0, 0, 0)), vmem, vmem, vmem],
+        out_specs=pl.BlockSpec((EARLY, grid_rows, 2 * grid_cols), lambda i: (0, 0, 0)),
         compiler_params=pltpu.CompilerParams(vmem_limit_bytes=56 * MIB),
         cost_estimate=pl.CostEstimate(flops=3 * 10**9, bytes_accessed=3 * 10**6, transcendentals=0),
         name="spectra",
-    )(kernel_radii, kernel_taps, *map(jnp.asarray, (row_fwd, head, tail)))
+    )(kernel_radii, kernel_taps, *early_tables)
 
     tables, layout, sections = stacked([
-        {"row_fwd": row_fwd, "head": head, "tail": tail},
         {"mask_head": mask_head, "mask_tail": mask_tail, "col_inv": col_inv, "row_inv": row_inv, "grad_col": grad_col},
     ])
     resist, own, near_rim, far_rim = pl.pallas_call(
@@ -461,7 +447,7 @@
             jax.ShapeDtypeStruct((2, rim, width), f32),
             jax.ShapeDtypeStruct((2, rim, width), f32),
         ],
-        in_specs=[smem] * 4 + [vmem] * 4 + [hbm] * 3,
+        in_specs=[smem] * 4 + [vmem] * 7 + [hbm] * 3,
         out_specs=[hbm] + [vmem] * 3,
         scratch_shapes=[
             pltpu.VMEM((kernels, grid_rows, 2 * grid_cols), f32),
@@ -479,7 +465,7 @@
         ],
         compiler_params=pltpu.CompilerParams(vmem_limit_bytes=LIMIT * MIB),
         name="fields",
-    )(kernel_group, kernel_weight, place, kernel_radii, mask_field, near, far, target, kernel_taps, spectra, jnp.asarray(tables))
+    )(kernel_group, kernel_weight, place, kernel_radii, mask_field, near, far, target, *early_tables, kernel_taps, spectra, jnp.asarray(tables))
 
     near_in = lax.ppermute(near_rim, "row", near_pairs)
     far_in = lax.ppermute(far_rim, "row", far_pairs)

time: 38.8 us -> 39.1 us (level)
  Pallas kernels: 27.3 us -> 26.7 us
    pallas_call x1, Pallas kernels: 4.45 us -> 3.56 us  [on_device(): pl.pallas_call(spectra_body, out_shape=jax.ShapeDtypeStruct((EARLY, grid_...]
    ppermute x1, waiting for transfers between devices: 0.01 us -> 0.64 us  [on_device(): far = lax.ppermute(mask_field, 'row', far_pairs)]
  transfers between devices with their start and end apart: 4 -> 4, of which waited for: 1 -> 2; matrix products, arithmetic and copies ran while one was open for 0% -> 0% of each run, Pallas kernels for 12% -> 9%
where the time goes in v26:
time: 39.1 us; the launch traced here: 38.6 us
  Pallas kernels  26.7 us (68%)
  starting transfers between devices  8.01 us (20%)
  waiting for transfers between devices  3.09 us (8%)
  between operations  0.75 us (2%)
    pallas_call x1, Pallas kernels, on_device(): pl.pallas_call(functools.partial(main_body, layout=layout, sections=secti...  22.5 us
    ppermute x1, starting transfers between devices, on_device(): far_in = lax.ppermute(far_rim, 'row', far_pairs)  4.02 us
    pallas_call x1, Pallas kernels, on_device(): pl.pallas_call(spectra_body, out_shape=jax.ShapeDtypeStruct((EARLY, grid_...  3.56 us
    ppermute x1, starting transfers between devices, on_device(): far = lax.ppermute(mask_field, 'row', far_pairs)  3.18 us
    ppermute x1, waiting for transfers between devices, on_device(): far_in = lax.ppermute(far_rim, 'row', far_pairs)  2.45 us
  transfers between devices with their start and end apart: 4, of which 2 were waited for; matrix products, arithmetic and copies ran while one was open for 0% of the time, Pallas kernels for 9%

profile of v26, /device:TPU:21, one launch (start us, length us, event | category | flops | bytes accessed | tf_op | source)
XLA Modules:
  0.0 38.6 jit_solution(14170707227290877797)
XLA Ops:
  0.6 0.0 copy-start.1
  0.6 0.0 copy-start
  0.7 0.0 copy-start.5
  0.7 0.0 copy-start.4
  0.7 0.0 copy-start.3
  0.7 0.0 copy-start.2
  0.7 0.7 %collective-permute-start = (f32[2,128,128]{2,1,0:T(8,128)}, f32[2,128,128]{2,1,0:T(8,128)S(1)}, u32[]{:S(2)}, u32[]{:S(2)}) collective-permute-start(f32[2,128,128]{2,1,0:T(8,128)} %own.1), channel_id=1, source_target_pairs={{0,1},{1,0},{2,3},{3,2},{4,5},{5,4},{6,7},{7,6},{8,9},{9,8},{10,11... | collective-permute-start | bytes 393224 | tf_op jit(solution)/shard_map/ppermute | solution.py:404
  1.4 3.2 %collective-permute-start.1 = (f32[2,128,128]{2,1,0:T(8,128)}, f32[2,128,128]{2,1,0:T(8,128)S(1)}, u32[]{:S(2)}, u32[]{:S(2)}) collective-permute-start(f32[2,128,128]{2,1,0:T(8,128)} %own.1), channel_id=1, source_target_pairs={{1,2},{2,1},{3,4},{4,3},{5,6},{6,5},{7,8},{8,7},{9,10},{10,9},{11,... | collective-permute-start | bytes 393224 | tf_op jit(solution)/shard_map/ppermute | solution.py:405
  4.6 3.6 %spectra.1.spec_far = f32[4,256,384]{2,1,0:T(8,128)} custom-call(s32[24]{0:T(128)} %radii.3, f32[24,2,128,128]{3,2,1,0:T(8,128)} %taps_far.1, bf16[256,512]{1,0:T(8,128)(2,1)} %constant.12.clone.row_ref, bf16[512,256]{1,0:T(8,128)(2,1)} %constant.13.clone.head_ref, bf16[256,256]{1,0:T(8,128)(2,1)} %constant.14.clone.tail_ref), custom_call_target="tpu_custom_call" | custom-call | flops 3000000000 | bytes 3000000 | tf_op jit(solution)/shard_map/spectra/pallas_call | solution.py:428
  8.2 0.0 collective-permute-done.near
  8.2 0.6 %collective-permute-done.1.far = f32[2,128,128]{2,1,0:T(8,128)S(1)} collective-permute-done((f32[2,128,128]{2,1,0:T(8,128)}, f32[2,128,128]{2,1,0:T(8,128)S(1)}, u32[]{:S(2)}, u32[]{:S(2)}) %collective-permute-start.1) | collective-permute-done | bytes 131104 | tf_op jit(solution)/shard_map/ppermute | solution.py:405
  8.8 0.0 copy-done.1
  8.8 0.0 copy-done
  8.8 0.0 copy-done.5
  8.8 0.0 copy-done.4
  8.8 0.0 copy-done.3
  8.8 0.0 copy-done.2
  8.9 22.5 %fields.1 = (f32[3,128,128]{2,1,0:T(8,128)}, f32[2,128,128]{2,1,0:T(8,128)S(1)}, f32[2,64,128]{2,1,0:T(8,128)S(1)}, f32[2,64,128]{2,1,0:T(8,128)S(1)}) custom-call(s32[24]{0:T(128)S(1)} %copy-done.3, f32[24]{0:T(128)S(1)} %copy-done.4, s32[1]{0:T(128)} %bitcast.place, s32[24]{0:T(128)S(1)} %copy-done.5, f32[2,128,128]{2,1,0:T(8,128)S(1)} %copy-done, ...), custom_call_target="tpu_custom_call" | custom-call | tf_op jit(solution)/shard_map/fields/pallas_call | solution.py:442
  31.4 0.1 collective-permute-start.2
  31.4 4.0 %collective-permute-start.3 = (f32[2,64,128]{2,1,0:T(8,128)S(1)}, f32[2,64,128]{2,1,0:T(8,128)S(1)}, u32[]{:S(2)}, u32[]{:S(2)}) collective-permute-start(f32[2,64,128]{2,1,0:T(8,128)S(1)} %get-tuple-element.9), channel_id=1, source_target_pairs={{1,2},{2,1},{3,4},{4,3},{5,6},{6,5},{7,8},{8,7},{9,10},{10,9},{11,... | collective-permute-start | bytes 196616 | tf_op jit(solution)/shard_map/ppermute | solution.py:471
  35.5 0.0 collective-permute-done.2.near
  35.5 2.4 %collective-permute-done.3.far = f32[2,64,128]{2,1,0:T(8,128)S(1)} collective-permute-done((f32[2,64,128]{2,1,0:T(8,128)S(1)}, f32[2,64,128]{2,1,0:T(8,128)S(1)}, u32[]{:S(2)}, u32[]{:S(2)}) %collective-permute-start.3) | collective-permute-done | bytes 65568 | tf_op jit(solution)/shard_map/ppermute | solution.py:471
  37.9 0.7 %join.1 = f32[2,128,128]{2,1,0:T(8,128)} custom-call(s32[1]{0:T(128)} %bitcast.place, f32[2,128,128]{2,1,0:T(8,128)S(1)} %get-tuple-element.7.own, f32[2,64,128]{2,1,0:T(8,128)S(1)} %collective-permute-done.2.near, f32[2,64,128]{2,1,0:T(8,128)S(1)} %collective-permute-done.3.far), custom_call_target="tpu_custom_call" | custom-call | tf_op jit(solution)/shard_map/join/pallas_call | solution.py:472
Async XLA Ops:
  0.6 8.2 %copy-start.1 = (bf16[256,256]{1,0:T(8,128)(2,1)S(1)}, bf16[256,256]{1,0:T(8,128)(2,1)}, u32[]{:S(2)}) copy-start(bf16[256,256]{1,0:T(8,128)(2,1)} %constant.14.clone.tail_ref) | copy-start | bytes 393220
  0.6 8.2 %copy-start = (f32[2,128,128]{2,1,0:T(8,128)S(1)}, f32[2,128,128]{2,1,0:T(8,128)}, u32[]{:S(2)}) copy-start(f32[2,128,128]{2,1,0:T(8,128)} %own.1) | copy-start | bytes 393220
  0.7 8.2 %copy-start.5 = (s32[24]{0:T(128)S(1)}, s32[24]{0:T(128)}, u32[]{:S(2)}) copy-start(s32[24]{0:T(128)} %radii.3) | copy-start | bytes 292
  0.7 8.2 %copy-start.4 = (f32[24]{0:T(128)S(1)}, f32[24]{0:T(128)}, u32[]{:S(2)}) copy-start(f32[24]{0:T(128)} %weight.1) | copy-start | bytes 292
  0.7 8.2 %copy-start.3 = (s32[24]{0:T(128)S(1)}, s32[24]{0:T(128)}, u32[]{:S(2)}) copy-start(s32[24]{0:T(128)} %group.1) | copy-start | bytes 292
  0.7 8.2 %copy-start.2 = (s32[128,128]{1,0:T(8,128)S(1)}, s32[128,128]{1,0:T(8,128)}, u32[]{:S(2)}) copy-start(s32[128,128]{1,0:T(8,128)} %target.1) | copy-start | bytes 196612
  0.7 7.5 %collective-permute-start = (f32[2,128,128]{2,1,0:T(8,128)}, f32[2,128,128]{2,1,0:T(8,128)S(1)}, u32[]{:S(2)}, u32[]{:S(2)}) collective-permute-start(f32[2,128,128]{2,1,0:T(8,128)} %own.1), channel_id=1, source_target_pairs={{0,1},{1,0},{2,3},{3,2},{4,5},{5,4},{6,7},{7,6},{8,9},{9,8},{10,11... | collective-permute-start | bytes 393224 | tf_op jit(solution)/shard_map/ppermute | solution.py:404
  1.4 7.4 %collective-permute-start.1 = (f32[2,128,128]{2,1,0:T(8,128)}, f32[2,128,128]{2,1,0:T(8,128)S(1)}, u32[]{:S(2)}, u32[]{:S(2)}) collective-permute-start(f32[2,128,128]{2,1,0:T(8,128)} %own.1), channel_id=1, source_target_pairs={{1,2},{2,1},{3,4},{4,3},{5,6},{6,5},{7,8},{8,7},{9,10},{10,9},{11,... | collective-permute-start | bytes 393224 | tf_op jit(solution)/shard_map/ppermute | solution.py:405
  31.4 4.1 %collective-permute-start.2 = (f32[2,64,128]{2,1,0:T(8,128)S(1)}, f32[2,64,128]{2,1,0:T(8,128)S(1)}, u32[]{:S(2)}, u32[]{:S(2)}) collective-permute-start(f32[2,64,128]{2,1,0:T(8,128)S(1)} %get-tuple-element.8), channel_id=1, source_target_pairs={{0,1},{1,0},{2,3},{3,2},{4,5},{5,4},{6,7},{7,6},{8,9},{9,8},{10,11... | collective-permute-start | bytes 196616 | tf_op jit(solution)/shard_map/ppermute | solution.py:470
  31.4 6.5 %collective-permute-start.3 = (f32[2,64,128]{2,1,0:T(8,128)S(1)}, f32[2,64,128]{2,1,0:T(8,128)S(1)}, u32[]{:S(2)}, u32[]{:S(2)}) collective-permute-start(f32[2,64,128]{2,1,0:T(8,128)S(1)} %get-tuple-element.9), channel_id=1, source_target_pairs={{1,2},{2,1},{3,4},{4,3},{5,6},{6,5},{7,8},{8,7},{9,10},{10,9},{11,... | collective-permute-start | bytes 196616 | tf_op jit(solution)/shard_map/ppermute | solution.py:471

commit v27 on v26

--- a/solution.py
+++ b/solution.py
@@ -15,8 +15,8 @@
 STEEPNESS = 1.0
 THRESHOLD = 2.0
 BATCH = 12
-EARLY = 4
-LATE_BATCH = 10
+EARLY = 8
+LATE_BATCH = 8
 PIECE = 256
 
 f32 = jnp.float32
@@ -213,7 +213,7 @@
 
 def main_body(
     group, weight, place, radii,
-    own, near, far, target, row_ref, head_ref, tail_ref, taps_far, spec_far, tables_far,
+    own, near, far, target, taps_far, spec_far, tables_far,
     resist_far, grad_own, near_rim, far_rim,
     spec, taps, field, mask_spec, resist, slopes, grad_spec, tables, spec_sem, taps_sems, table_sems, out_sem,
     *, layout, sections,
@@ -242,13 +242,15 @@
         parts = [tables[start + b * rows:start + (b + 1) * rows] for b in range(blocks)]
         return jnp.concatenate(parts, axis=1)
 
+    fetch_table(0).start()
     for i in range(late_steps):
         fetch_taps(i).start()
-    fetch_table(0).start()
+    fetch_table(1).start()
     fetch_early.start()
     slopes[...] = jnp.zeros(slopes.shape, f32)
     grad_spec[...] = jnp.zeros(grad_spec.shape, f32)
-    row_fwd, head, tail = row_ref[...], head_ref[...], tail_ref[...]
+    fetch_table(0).wait()
+    row_fwd, head, tail = table("row_fwd"), table("head"), table("tail")
 
     def spectra(i, carry):
         fetch_taps(i).wait()
@@ -256,7 +258,7 @@
         return carry
 
     lax.fori_loop(0, late_steps, spectra, 0)
-    fetch_table(0).wait()
+    fetch_table(1).wait()
     fetch_early.wait()
 
     odd = place[0] % 2 == 1
@@ -424,7 +426,6 @@
     smem = pl.BlockSpec(memory_space=pltpu.SMEM)
     vmem = pl.BlockSpec(memory_space=pltpu.VMEM)
     hbm = pl.BlockSpec(memory_space=pltpu.HBM)
-    early_tables = [jnp.asarray(t) for t in (row_fwd, head, tail)]
     spectra = pl.pallas_call(
         spectra_body,
         out_shape=jax.ShapeDtypeStruct((EARLY, grid_rows, 2 * grid_cols), f32),
@@ -434,9 +435,10 @@
         compiler_params=pltpu.CompilerParams(vmem_limit_bytes=56 * MIB),
         cost_estimate=pl.CostEstimate(flops=3 * 10**9, bytes_accessed=3 * 10**6, transcendentals=0),
         name="spectra",
-    )(kernel_radii, kernel_taps, *early_tables)
+    )(kernel_radii, kernel_taps, *map(jnp.asarray, (row_fwd, head, tail)))
 
     tables, layout, sections = stacked([
+        {"row_fwd": row_fwd, "head": head, "tail": tail},
         {"mask_head": mask_head, "mask_tail": mask_tail, "col_inv": col_inv, "row_inv": row_inv, "grad_col": grad_col},
     ])
     resist, own, near_rim, far_rim = pl.pallas_call(
@@ -447,7 +449,7 @@
             jax.ShapeDtypeStruct((2, rim, width), f32),
             jax.ShapeDtypeStruct((2, rim, width), f32),
         ],
-        in_specs=[smem] * 4 + [vmem] * 7 + [hbm] * 3,
+        in_specs=[smem] * 4 + [vmem] * 4 + [hbm] * 3,
         out_specs=[hbm] + [vmem] * 3,
         scratch_shapes=[
             pltpu.VMEM((kernels, grid_rows, 2 * grid_cols), f32),
@@ -465,7 +467,7 @@
         ],
         compiler_params=pltpu.CompilerParams(vmem_limit_bytes=LIMIT * MIB),
         name="fields",
-    )(kernel_group, kernel_weight, place, kernel_radii, mask_field, near, far, target, *early_tables, kernel_taps, spectra, jnp.asarray(tables))
+    )(kernel_group, kernel_weight, place, kernel_radii, mask_field, near, far, target, kernel_taps, spectra, jnp.asarray(tables))
 
     near_in = lax.ppermute(near_rim, "row", near_pairs)
     far_in = lax.ppermute(far_rim, "row", far_pairs)

time: 39.1 us -> 38.5 us (0.985)
  starting transfers between devices: 8.01 us -> 7.51 us
    pallas_call x1, Pallas kernels: 3.56 us -> 5.16 us  [on_device(): pl.pallas_call(spectra_body, out_shape=jax.ShapeDtypeStruct((EARLY, grid_...]
    pallas_call x1, Pallas kernels: 22.5 us -> 21.1 us  [on_device(): pl.pallas_call(functools.partial(main_body, layout=layout, sections=secti...]
    ppermute x1, waiting for transfers between devices: 0.64 us -> 0.01 us  [on_device(): far = lax.ppermute(mask_field, 'row', far_pairs)]
    ppermute x1, waiting for transfers between devices: 2.45 us -> 2.95 us  [on_device(): far_in = lax.ppermute(far_rim, 'row', far_pairs)]
    ppermute x1, starting transfers between devices: 4.02 us -> 3.52 us  [on_device(): far_in = lax.ppermute(far_rim, 'row', far_pairs)]
  transfers between devices with their start and end apart: 4 -> 4, of which waited for: 2 -> 1; matrix products, arithmetic and copies ran while one was open for 0% -> 0% of each run, Pallas kernels for 9% -> 14%
where the time goes in v27:
time: 38.5 us; the launch traced here: 38.2 us
  Pallas kernels  27 us (70%)
  starting transfers between devices  7.51 us (20%)
  waiting for transfers between devices  2.95 us (8%)
  between operations  0.75 us (2%)
    pallas_call x1, Pallas kernels, on_device(): pl.pallas_call(functools.partial(main_body, layout=layout, sections=secti...  21.1 us
    pallas_call x1, Pallas kernels, on_device(): pl.pallas_call(spectra_body, out_shape=jax.ShapeDtypeStruct((EARLY, grid_...  5.16 us
    ppermute x1, starting transfers between devices, on_device(): far_in = lax.ppermute(far_rim, 'row', far_pairs)  3.52 us
    ppermute x1, starting transfers between devices, on_device(): far = lax.ppermute(mask_field, 'row', far_pairs)  3.18 us
    ppermute x1, waiting for transfers between devices, on_device(): far_in = lax.ppermute(far_rim, 'row', far_pairs)  2.95 us
  transfers between devices with their start and end apart: 4, of which 1 were waited for; matrix products, arithmetic and copies ran while one was open for 0% of the time, Pallas kernels for 14%

profile of v27, /device:TPU:21, one launch (start us, length us, event | category | flops | bytes accessed | tf_op | source)
XLA Modules:
  0.0 38.2 jit_solution(9780674384884300822)
XLA Ops:
  0.6 0.0 copy-start
  0.6 0.0 copy-start.4
  0.7 0.0 copy-start.3
  0.7 0.0 copy-start.2
  0.7 0.0 copy-start.1
  0.7 0.7 %collective-permute-start = (f32[2,128,128]{2,1,0:T(8,128)}, f32[2,128,128]{2,1,0:T(8,128)S(1)}, u32[]{:S(2)}, u32[]{:S(2)}) collective-permute-start(f32[2,128,128]{2,1,0:T(8,128)} %own.1), channel_id=1, source_target_pairs={{0,1},{1,0},{2,3},{3,2},{4,5},{5,4},{6,7},{7,6},{8,9},{9,8},{10,11... | collective-permute-start | bytes 393224 | tf_op jit(solution)/shard_map/ppermute | solution.py:406
  1.4 3.2 %collective-permute-start.1 = (f32[2,128,128]{2,1,0:T(8,128)}, f32[2,128,128]{2,1,0:T(8,128)S(1)}, u32[]{:S(2)}, u32[]{:S(2)}) collective-permute-start(f32[2,128,128]{2,1,0:T(8,128)} %own.1), channel_id=1, source_target_pairs={{1,2},{2,1},{3,4},{4,3},{5,6},{6,5},{7,8},{8,7},{9,10},{10,9},{11,... | collective-permute-start | bytes 393224 | tf_op jit(solution)/shard_map/ppermute | solution.py:407
  4.6 5.2 %spectra.1.spec_far = f32[8,256,384]{2,1,0:T(8,128)} custom-call(s32[24]{0:T(128)} %radii.3, f32[24,2,128,128]{3,2,1,0:T(8,128)} %taps_far.1, bf16[256,512]{1,0:T(8,128)(2,1)} %constant.12.clone.row_ref, bf16[512,256]{1,0:T(8,128)(2,1)} %constant.13.clone.head_ref, bf16[256,256]{1,0:T(8,128)(2,1)} %constant.14.clone.tail_ref), custom_call_target="tpu_custom_call" | custom-call | flops 3000000000 | bytes 3000000 | tf_op jit(solution)/shard_map/spectra/pallas_call | solution.py:429
  9.8 0.0 collective-permute-done.near
  9.8 0.0 collective-permute-done.1.far
  9.8 0.0 copy-done
  9.8 0.0 copy-done.4
  9.8 0.0 copy-done.3
  9.8 0.0 copy-done.2
  9.8 0.0 copy-done.1
  9.8 21.1 %fields.1 = (f32[3,128,128]{2,1,0:T(8,128)}, f32[2,128,128]{2,1,0:T(8,128)S(1)}, f32[2,64,128]{2,1,0:T(8,128)S(1)}, f32[2,64,128]{2,1,0:T(8,128)S(1)}) custom-call(s32[24]{0:T(128)S(1)} %copy-done.2, f32[24]{0:T(128)S(1)} %copy-done.3, s32[1]{0:T(128)} %bitcast.place, s32[24]{0:T(128)S(1)} %copy-done.4, f32[2,128,128]{2,1,0:T(8,128)S(1)} %copy-done, ...), custom_call_target="tpu_custom_call" | custom-call | tf_op jit(solution)/shard_map/fields/pallas_call | solution.py:444
  31.0 0.1 collective-permute-start.2
  31.0 3.5 %collective-permute-start.3 = (f32[2,64,128]{2,1,0:T(8,128)S(1)}, f32[2,64,128]{2,1,0:T(8,128)S(1)}, u32[]{:S(2)}, u32[]{:S(2)}) collective-permute-start(f32[2,64,128]{2,1,0:T(8,128)S(1)} %get-tuple-element.9), channel_id=1, source_target_pairs={{1,2},{2,1},{3,4},{4,3},{5,6},{6,5},{7,8},{8,7},{9,10},{10,9},{11,... | collective-permute-start | bytes 196616 | tf_op jit(solution)/shard_map/ppermute | solution.py:473
  34.6 0.0 collective-permute-done.2.near
  34.6 2.9 %collective-permute-done.3.far = f32[2,64,128]{2,1,0:T(8,128)S(1)} collective-permute-done((f32[2,64,128]{2,1,0:T(8,128)S(1)}, f32[2,64,128]{2,1,0:T(8,128)S(1)}, u32[]{:S(2)}, u32[]{:S(2)}) %collective-permute-start.3) | collective-permute-done | bytes 65568 | tf_op jit(solution)/shard_map/ppermute | solution.py:473
  37.5 0.7 %join.1 = f32[2,128,128]{2,1,0:T(8,128)} custom-call(s32[1]{0:T(128)} %bitcast.place, f32[2,128,128]{2,1,0:T(8,128)S(1)} %get-tuple-element.7.own, f32[2,64,128]{2,1,0:T(8,128)S(1)} %collective-permute-done.2.near, f32[2,64,128]{2,1,0:T(8,128)S(1)} %collective-permute-done.3.far), custom_call_target="tpu_custom_call" | custom-call | tf_op jit(solution)/shard_map/join/pallas_call | solution.py:474
Async XLA Ops:
  0.6 9.1 %copy-start = (f32[2,128,128]{2,1,0:T(8,128)S(1)}, f32[2,128,128]{2,1,0:T(8,128)}, u32[]{:S(2)}) copy-start(f32[2,128,128]{2,1,0:T(8,128)} %own.1) | copy-start | bytes 393220
  0.6 9.1 %copy-start.4 = (s32[24]{0:T(128)S(1)}, s32[24]{0:T(128)}, u32[]{:S(2)}) copy-start(s32[24]{0:T(128)} %radii.3) | copy-start | bytes 292
  0.7 9.1 %copy-start.3 = (f32[24]{0:T(128)S(1)}, f32[24]{0:T(128)}, u32[]{:S(2)}) copy-start(f32[24]{0:T(128)} %weight.1) | copy-start | bytes 292
  0.7 9.1 %copy-start.2 = (s32[24]{0:T(128)S(1)}, s32[24]{0:T(128)}, u32[]{:S(2)}) copy-start(s32[24]{0:T(128)} %group.1) | copy-start | bytes 292
  0.7 9.1 %copy-start.1 = (s32[128,128]{1,0:T(8,128)S(1)}, s32[128,128]{1,0:T(8,128)}, u32[]{:S(2)}) copy-start(s32[128,128]{1,0:T(8,128)} %target.1) | copy-start | bytes 196612
  0.7 9.1 %collective-permute-start = (f32[2,128,128]{2,1,0:T(8,128)}, f32[2,128,128]{2,1,0:T(8,128)S(1)}, u32[]{:S(2)}, u32[]{:S(2)}) collective-permute-start(f32[2,128,128]{2,1,0:T(8,128)} %own.1), channel_id=1, source_target_pairs={{0,1},{1,0},{2,3},{3,2},{4,5},{5,4},{6,7},{7,6},{8,9},{9,8},{10,11... | collective-permute-start | bytes 393224 | tf_op jit(solution)/shard_map/ppermute | solution.py:406
  1.4 8.3 %collective-permute-start.1 = (f32[2,128,128]{2,1,0:T(8,128)}, f32[2,128,128]{2,1,0:T(8,128)S(1)}, u32[]{:S(2)}, u32[]{:S(2)}) collective-permute-start(f32[2,128,128]{2,1,0:T(8,128)} %own.1), channel_id=1, source_target_pairs={{1,2},{2,1},{3,4},{4,3},{5,6},{6,5},{7,8},{8,7},{9,10},{10,9},{11,... | collective-permute-start | bytes 393224 | tf_op jit(solution)/shard_map/ppermute | solution.py:407
  31.0 3.6 %collective-permute-start.2 = (f32[2,64,128]{2,1,0:T(8,128)S(1)}, f32[2,64,128]{2,1,0:T(8,128)S(1)}, u32[]{:S(2)}, u32[]{:S(2)}) collective-permute-start(f32[2,64,128]{2,1,0:T(8,128)S(1)} %get-tuple-element.8), channel_id=1, source_target_pairs={{0,1},{1,0},{2,3},{3,2},{4,5},{5,4},{6,7},{7,6},{8,9},{9,8},{10,11... | collective-permute-start | bytes 196616 | tf_op jit(solution)/shard_map/ppermute | solution.py:472
  31.0 6.5 %collective-permute-start.3 = (f32[2,64,128]{2,1,0:T(8,128)S(1)}, f32[2,64,128]{2,1,0:T(8,128)S(1)}, u32[]{:S(2)}, u32[]{:S(2)}) collective-permute-start(f32[2,64,128]{2,1,0:T(8,128)S(1)} %get-tuple-element.9), channel_id=1, source_target_pairs={{1,2},{2,1},{3,4},{4,3},{5,6},{6,5},{7,8},{8,7},{9,10},{10,9},{11,... | collective-permute-start | bytes 196616 | tf_op jit(solution)/shard_map/ppermute | solution.py:473

commit v28 on v27

--- a/solution.py
+++ b/solution.py
@@ -469,8 +469,8 @@
         name="fields",
     )(kernel_group, kernel_weight, place, kernel_radii, mask_field, near, far, target, kernel_taps, spectra, jnp.asarray(tables))
 
+    far_in = lax.ppermute(far_rim, "row", far_pairs)
     near_in = lax.ppermute(near_rim, "row", near_pairs)
-    far_in = lax.ppermute(far_rim, "row", far_pairs)
     gradient = pl.pallas_call(
         join_body,
         out_shape=jax.ShapeDtypeStruct((2, count, width), f32),

time: 38.5 us -> 38.5 us (level)
  no operation moved by 1% of the time
where the time goes in v28:
time: 38.5 us; the launch traced here: 38.2 us
  Pallas kernels  27 us (70%)
  starting transfers between devices  7.51 us (20%)
  waiting for transfers between devices  2.95 us (8%)
  between operations  0.75 us (2%)
    pallas_call x1, Pallas kernels, on_device(): pl.pallas_call(functools.partial(main_body, layout=layout, sections=secti...  21.1 us
    pallas_call x1, Pallas kernels, on_device(): pl.pallas_call(spectra_body, out_shape=jax.ShapeDtypeStruct((EARLY, grid_...  5.16 us
    ppermute x1, starting transfers between devices, on_device(): far_in = lax.ppermute(far_rim, 'row', far_pairs)  3.52 us
    ppermute x1, starting transfers between devices, on_device(): far = lax.ppermute(mask_field, 'row', far_pairs)  3.18 us
    ppermute x1, waiting for transfers between devices, on_device(): far_in = lax.ppermute(far_rim, 'row', far_pairs)  2.95 us
  transfers between devices with their start and end apart: 4, of which 1 were waited for; matrix products, arithmetic and copies ran while one was open for 0% of the time, Pallas kernels for 14%

profile of v28, /device:TPU:21, one launch (start us, length us, event | category | flops | bytes accessed | tf_op | source)
XLA Modules:
  0.0 38.2 jit_solution(9780674384884300822)
XLA Ops:
  0.6 0.0 copy-start
  0.6 0.0 copy-start.4
  0.7 0.0 copy-start.3
  0.7 0.0 copy-start.2
  0.7 0.0 copy-start.1
  0.7 0.7 %collective-permute-start = (f32[2,128,128]{2,1,0:T(8,128)}, f32[2,128,128]{2,1,0:T(8,128)S(1)}, u32[]{:S(2)}, u32[]{:S(2)}) collective-permute-start(f32[2,128,128]{2,1,0:T(8,128)} %own.1), channel_id=1, source_target_pairs={{0,1},{1,0},{2,3},{3,2},{4,5},{5,4},{6,7},{7,6},{8,9},{9,8},{10,11... | collective-permute-start | bytes 393224 | tf_op jit(solution)/shard_map/ppermute | solution.py:406
  1.4 3.2 %collective-permute-start.1 = (f32[2,128,128]{2,1,0:T(8,128)}, f32[2,128,128]{2,1,0:T(8,128)S(1)}, u32[]{:S(2)}, u32[]{:S(2)}) collective-permute-start(f32[2,128,128]{2,1,0:T(8,128)} %own.1), channel_id=1, source_target_pairs={{1,2},{2,1},{3,4},{4,3},{5,6},{6,5},{7,8},{8,7},{9,10},{10,9},{11,... | collective-permute-start | bytes 393224 | tf_op jit(solution)/shard_map/ppermute | solution.py:407
  4.6 5.2 %spectra.1.spec_far = f32[8,256,384]{2,1,0:T(8,128)} custom-call(s32[24]{0:T(128)} %radii.3, f32[24,2,128,128]{3,2,1,0:T(8,128)} %taps_far.1, bf16[256,512]{1,0:T(8,128)(2,1)} %constant.12.clone.row_ref, bf16[512,256]{1,0:T(8,128)(2,1)} %constant.13.clone.head_ref, bf16[256,256]{1,0:T(8,128)(2,1)} %constant.14.clone.tail_ref), custom_call_target="tpu_custom_call" | custom-call | flops 3000000000 | bytes 3000000 | tf_op jit(solution)/shard_map/spectra/pallas_call | solution.py:429
  9.8 0.0 collective-permute-done.near
  9.8 0.0 collective-permute-done.1.far
  9.8 0.0 copy-done
  9.8 0.0 copy-done.4
  9.8 0.0 copy-done.3
  9.8 0.0 copy-done.2
  9.8 0.0 copy-done.1
  9.8 21.1 %fields.1 = (f32[3,128,128]{2,1,0:T(8,128)}, f32[2,128,128]{2,1,0:T(8,128)S(1)}, f32[2,64,128]{2,1,0:T(8,128)S(1)}, f32[2,64,128]{2,1,0:T(8,128)S(1)}) custom-call(s32[24]{0:T(128)S(1)} %copy-done.2, f32[24]{0:T(128)S(1)} %copy-done.3, s32[1]{0:T(128)} %bitcast.place, s32[24]{0:T(128)S(1)} %copy-done.4, f32[2,128,128]{2,1,0:T(8,128)S(1)} %copy-done, ...), custom_call_target="tpu_custom_call" | custom-call | tf_op jit(solution)/shard_map/fields/pallas_call | solution.py:444
  31.0 0.1 collective-permute-start.2
  31.0 3.5 %collective-permute-start.3 = (f32[2,64,128]{2,1,0:T(8,128)S(1)}, f32[2,64,128]{2,1,0:T(8,128)S(1)}, u32[]{:S(2)}, u32[]{:S(2)}) collective-permute-start(f32[2,64,128]{2,1,0:T(8,128)S(1)} %get-tuple-element.9), channel_id=1, source_target_pairs={{1,2},{2,1},{3,4},{4,3},{5,6},{6,5},{7,8},{8,7},{9,10},{10,9},{11,... | collective-permute-start | bytes 196616 | tf_op jit(solution)/shard_map/ppermute | solution.py:472
  34.6 0.0 collective-permute-done.2.near
  34.6 2.9 %collective-permute-done.3.far = f32[2,64,128]{2,1,0:T(8,128)S(1)} collective-permute-done((f32[2,64,128]{2,1,0:T(8,128)S(1)}, f32[2,64,128]{2,1,0:T(8,128)S(1)}, u32[]{:S(2)}, u32[]{:S(2)}) %collective-permute-start.3) | collective-permute-done | bytes 65568 | tf_op jit(solution)/shard_map/ppermute | solution.py:472
  37.5 0.7 %join.1 = f32[2,128,128]{2,1,0:T(8,128)} custom-call(s32[1]{0:T(128)} %bitcast.place, f32[2,128,128]{2,1,0:T(8,128)S(1)} %get-tuple-element.7.own, f32[2,64,128]{2,1,0:T(8,128)S(1)} %collective-permute-done.2.near, f32[2,64,128]{2,1,0:T(8,128)S(1)} %collective-permute-done.3.far), custom_call_target="tpu_custom_call" | custom-call | tf_op jit(solution)/shard_map/join/pallas_call | solution.py:474
Async XLA Ops:
  0.6 9.1 %copy-start = (f32[2,128,128]{2,1,0:T(8,128)S(1)}, f32[2,128,128]{2,1,0:T(8,128)}, u32[]{:S(2)}) copy-start(f32[2,128,128]{2,1,0:T(8,128)} %own.1) | copy-start | bytes 393220
  0.6 9.1 %copy-start.4 = (s32[24]{0:T(128)S(1)}, s32[24]{0:T(128)}, u32[]{:S(2)}) copy-start(s32[24]{0:T(128)} %radii.3) | copy-start | bytes 292
  0.7 9.1 %copy-start.3 = (f32[24]{0:T(128)S(1)}, f32[24]{0:T(128)}, u32[]{:S(2)}) copy-start(f32[24]{0:T(128)} %weight.1) | copy-start | bytes 292
  0.7 9.1 %copy-start.2 = (s32[24]{0:T(128)S(1)}, s32[24]{0:T(128)}, u32[]{:S(2)}) copy-start(s32[24]{0:T(128)} %group.1) | copy-start | bytes 292
  0.7 9.1 %copy-start.1 = (s32[128,128]{1,0:T(8,128)S(1)}, s32[128,128]{1,0:T(8,128)}, u32[]{:S(2)}) copy-start(s32[128,128]{1,0:T(8,128)} %target.1) | copy-start | bytes 196612
  0.7 9.1 %collective-permute-start = (f32[2,128,128]{2,1,0:T(8,128)}, f32[2,128,128]{2,1,0:T(8,128)S(1)}, u32[]{:S(2)}, u32[]{:S(2)}) collective-permute-start(f32[2,128,128]{2,1,0:T(8,128)} %own.1), channel_id=1, source_target_pairs={{0,1},{1,0},{2,3},{3,2},{4,5},{5,4},{6,7},{7,6},{8,9},{9,8},{10,11... | collective-permute-start | bytes 393224 | tf_op jit(solution)/shard_map/ppermute | solution.py:406
  1.4 8.3 %collective-permute-start.1 = (f32[2,128,128]{2,1,0:T(8,128)}, f32[2,128,128]{2,1,0:T(8,128)S(1)}, u32[]{:S(2)}, u32[]{:S(2)}) collective-permute-start(f32[2,128,128]{2,1,0:T(8,128)} %own.1), channel_id=1, source_target_pairs={{1,2},{2,1},{3,4},{4,3},{5,6},{6,5},{7,8},{8,7},{9,10},{10,9},{11,... | collective-permute-start | bytes 393224 | tf_op jit(solution)/shard_map/ppermute | solution.py:407
  31.0 3.6 %collective-permute-start.2 = (f32[2,64,128]{2,1,0:T(8,128)S(1)}, f32[2,64,128]{2,1,0:T(8,128)S(1)}, u32[]{:S(2)}, u32[]{:S(2)}) collective-permute-start(f32[2,64,128]{2,1,0:T(8,128)S(1)} %get-tuple-element.8), channel_id=1, source_target_pairs={{0,1},{1,0},{2,3},{3,2},{4,5},{5,4},{6,7},{7,6},{8,9},{9,8},{10,11... | collective-permute-start | bytes 196616 | tf_op jit(solution)/shard_map/ppermute | solution.py:473
  31.0 6.5 %collective-permute-start.3 = (f32[2,64,128]{2,1,0:T(8,128)S(1)}, f32[2,64,128]{2,1,0:T(8,128)S(1)}, u32[]{:S(2)}, u32[]{:S(2)}) collective-permute-start(f32[2,64,128]{2,1,0:T(8,128)S(1)} %get-tuple-element.9), channel_id=1, source_target_pairs={{1,2},{2,1},{3,4},{4,3},{5,6},{6,5},{7,8},{8,7},{9,10},{10,9},{11,... | collective-permute-start | bytes 196616 | tf_op jit(solution)/shard_map/ppermute | solution.py:472

commit v29 on v28

--- a/solution.py
+++ b/solution.py
@@ -243,23 +243,15 @@
         return jnp.concatenate(parts, axis=1)
 
     fetch_table(0).start()
+    fetch_table(1).start()
     for i in range(late_steps):
         fetch_taps(i).start()
-    fetch_table(1).start()
     fetch_early.start()
     slopes[...] = jnp.zeros(slopes.shape, f32)
     grad_spec[...] = jnp.zeros(grad_spec.shape, f32)
     fetch_table(0).wait()
+    fetch_table(1).wait()
     row_fwd, head, tail = table("row_fwd"), table("head"), table("tail")
-
-    def spectra(i, carry):
-        fetch_taps(i).wait()
-        spectra_of(radii, taps, spec, early + i * late, late, row_fwd, head, tail)
-        return carry
-
-    lax.fori_loop(0, late_steps, spectra, 0)
-    fetch_table(1).wait()
-    fetch_early.wait()
 
     odd = place[0] % 2 == 1
     above, below = [], []
@@ -275,6 +267,14 @@
     mask_spec[:, :2 * width] = m_first
     mask_spec[:, 2 * width:3 * width] = jnp.where(real_half, m_rest, turned)
     mask_spec[:, 3 * width:] = jnp.where(real_half, -turned, m_rest)
+
+    def spectra(i, carry):
+        fetch_taps(i).wait()
+        spectra_of(radii, taps, spec, early + i * late, late, row_fwd, head, tail)
+        return carry
+
+    lax.fori_loop(0, late_steps, spectra, 0)
+    fetch_early.wait()
 
     col_inv, row_inv = table("col_inv"), table("row_inv")
 

time: 38.5 us -> 38.9 us (1.010)
  Pallas kernels: 27 us -> 27.4 us
    pallas_call x1, Pallas kernels: 21.1 us -> 21.6 us  [on_device(): pl.pallas_call(functools.partial(main_body, layout=layout, sections=secti...]
  transfers between devices with their start and end apart: 4 -> 4, of which waited for: 1 -> 1; matrix products, arithmetic and copies ran while one was open for 0% -> 0% of each run, Pallas kernels for 14% -> 13%
where the time goes in v29:
time: 38.9 us; the launch traced here: 38.7 us
  Pallas kernels  27.4 us (70%)
  starting transfers between devices  7.51 us (19%)
  waiting for transfers between devices  2.95 us (8%)
  between operations  0.75 us (2%)
    pallas_call x1, Pallas kernels, on_device(): pl.pallas_call(functools.partial(main_body, layout=layout, sections=secti...  21.6 us
    pallas_call x1, Pallas kernels, on_device(): pl.pallas_call(spectra_body, out_shape=jax.ShapeDtypeStruct((EARLY, grid_...  5.16 us
    ppermute x1, starting transfers between devices, on_device(): far_in = lax.ppermute(far_rim, 'row', far_pairs)  3.52 us
    ppermute x1, starting transfers between devices, on_device(): far = lax.ppermute(mask_field, 'row', far_pairs)  3.18 us
    ppermute x1, waiting for transfers between devices, on_device(): far_in = lax.ppermute(far_rim, 'row', far_pairs)  2.95 us
  transfers between devices with their start and end apart: 4, of which 1 were waited for; matrix products, arithmetic and copies ran while one was open for 0% of the time, Pallas kernels for 13%

profile of v29, /device:TPU:21, one launch (start us, length us, event | category | flops | bytes accessed | tf_op | source)
XLA Modules:
  0.0 38.7 jit_solution(9938699641308571827)
XLA Ops:
  0.6 0.0 copy-start
  0.6 0.0 copy-start.4
  0.7 0.0 copy-start.3
  0.7 0.0 copy-start.2
  0.7 0.0 copy-start.1
  0.7 0.7 %collective-permute-start = (f32[2,128,128]{2,1,0:T(8,128)}, f32[2,128,128]{2,1,0:T(8,128)S(1)}, u32[]{:S(2)}, u32[]{:S(2)}) collective-permute-start(f32[2,128,128]{2,1,0:T(8,128)} %own.1), channel_id=1, source_target_pairs={{0,1},{1,0},{2,3},{3,2},{4,5},{5,4},{6,7},{7,6},{8,9},{9,8},{10,11... | collective-permute-start | bytes 393224 | tf_op jit(solution)/shard_map/ppermute | solution.py:406
  1.4 3.2 %collective-permute-start.1 = (f32[2,128,128]{2,1,0:T(8,128)}, f32[2,128,128]{2,1,0:T(8,128)S(1)}, u32[]{:S(2)}, u32[]{:S(2)}) collective-permute-start(f32[2,128,128]{2,1,0:T(8,128)} %own.1), channel_id=1, source_target_pairs={{1,2},{2,1},{3,4},{4,3},{5,6},{6,5},{7,8},{8,7},{9,10},{10,9},{11,... | collective-permute-start | bytes 393224 | tf_op jit(solution)/shard_map/ppermute | solution.py:407
  4.6 5.2 %spectra.1.spec_far = f32[8,256,384]{2,1,0:T(8,128)} custom-call(s32[24]{0:T(128)} %radii.3, f32[24,2,128,128]{3,2,1,0:T(8,128)} %taps_far.1, bf16[256,512]{1,0:T(8,128)(2,1)} %constant.12.clone.row_ref, bf16[512,256]{1,0:T(8,128)(2,1)} %constant.13.clone.head_ref, bf16[256,256]{1,0:T(8,128)(2,1)} %constant.14.clone.tail_ref), custom_call_target="tpu_custom_call" | custom-call | flops 3000000000 | bytes 3000000 | tf_op jit(solution)/shard_map/spectra/pallas_call | solution.py:429
  9.8 0.0 collective-permute-done.near
  9.8 0.0 collective-permute-done.1.far
  9.8 0.0 copy-done
  9.8 0.0 copy-done.4
  9.8 0.0 copy-done.3
  9.8 0.0 copy-done.2
  9.8 0.0 copy-done.1
  9.8 21.6 %fields.1 = (f32[3,128,128]{2,1,0:T(8,128)}, f32[2,128,128]{2,1,0:T(8,128)S(1)}, f32[2,64,128]{2,1,0:T(8,128)S(1)}, f32[2,64,128]{2,1,0:T(8,128)S(1)}) custom-call(s32[24]{0:T(128)S(1)} %copy-done.2, f32[24]{0:T(128)S(1)} %copy-done.3, s32[1]{0:T(128)} %bitcast.place, s32[24]{0:T(128)S(1)} %copy-done.4, f32[2,128,128]{2,1,0:T(8,128)S(1)} %copy-done, ...), custom_call_target="tpu_custom_call" | custom-call | tf_op jit(solution)/shard_map/fields/pallas_call | solution.py:444
  31.4 0.1 collective-permute-start.2
  31.5 3.5 %collective-permute-start.3 = (f32[2,64,128]{2,1,0:T(8,128)S(1)}, f32[2,64,128]{2,1,0:T(8,128)S(1)}, u32[]{:S(2)}, u32[]{:S(2)}) collective-permute-start(f32[2,64,128]{2,1,0:T(8,128)S(1)} %get-tuple-element.9), channel_id=1, source_target_pairs={{1,2},{2,1},{3,4},{4,3},{5,6},{6,5},{7,8},{8,7},{9,10},{10,9},{11,... | collective-permute-start | bytes 196616 | tf_op jit(solution)/shard_map/ppermute | solution.py:472
  35.1 0.0 collective-permute-done.2.near
  35.1 2.9 %collective-permute-done.3.far = f32[2,64,128]{2,1,0:T(8,128)S(1)} collective-permute-done((f32[2,64,128]{2,1,0:T(8,128)S(1)}, f32[2,64,128]{2,1,0:T(8,128)S(1)}, u32[]{:S(2)}, u32[]{:S(2)}) %collective-permute-start.3) | collective-permute-done | bytes 65568 | tf_op jit(solution)/shard_map/ppermute | solution.py:472
  38.0 0.7 %join.1 = f32[2,128,128]{2,1,0:T(8,128)} custom-call(s32[1]{0:T(128)} %bitcast.place, f32[2,128,128]{2,1,0:T(8,128)S(1)} %get-tuple-element.7.own, f32[2,64,128]{2,1,0:T(8,128)S(1)} %collective-permute-done.2.near, f32[2,64,128]{2,1,0:T(8,128)S(1)} %collective-permute-done.3.far), custom_call_target="tpu_custom_call" | custom-call | tf_op jit(solution)/shard_map/join/pallas_call | solution.py:474
Async XLA Ops:
  0.6 9.1 %copy-start = (f32[2,128,128]{2,1,0:T(8,128)S(1)}, f32[2,128,128]{2,1,0:T(8,128)}, u32[]{:S(2)}) copy-start(f32[2,128,128]{2,1,0:T(8,128)} %own.1) | copy-start | bytes 393220
  0.6 9.1 %copy-start.4 = (s32[24]{0:T(128)S(1)}, s32[24]{0:T(128)}, u32[]{:S(2)}) copy-start(s32[24]{0:T(128)} %radii.3) | copy-start | bytes 292
  0.7 9.1 %copy-start.3 = (f32[24]{0:T(128)S(1)}, f32[24]{0:T(128)}, u32[]{:S(2)}) copy-start(f32[24]{0:T(128)} %weight.1) | copy-start | bytes 292
  0.7 9.1 %copy-start.2 = (s32[24]{0:T(128)S(1)}, s32[24]{0:T(128)}, u32[]{:S(2)}) copy-start(s32[24]{0:T(128)} %group.1) | copy-start | bytes 292
  0.7 9.1 %copy-start.1 = (s32[128,128]{1,0:T(8,128)S(1)}, s32[128,128]{1,0:T(8,128)}, u32[]{:S(2)}) copy-start(s32[128,128]{1,0:T(8,128)} %target.1) | copy-start | bytes 196612
  0.7 9.1 %collective-permute-start = (f32[2,128,128]{2,1,0:T(8,128)}, f32[2,128,128]{2,1,0:T(8,128)S(1)}, u32[]{:S(2)}, u32[]{:S(2)}) collective-permute-start(f32[2,128,128]{2,1,0:T(8,128)} %own.1), channel_id=1, source_target_pairs={{0,1},{1,0},{2,3},{3,2},{4,5},{5,4},{6,7},{7,6},{8,9},{9,8},{10,11... | collective-permute-start | bytes 393224 | tf_op jit(solution)/shard_map/ppermute | solution.py:406
  1.4 8.3 %collective-permute-start.1 = (f32[2,128,128]{2,1,0:T(8,128)}, f32[2,128,128]{2,1,0:T(8,128)S(1)}, u32[]{:S(2)}, u32[]{:S(2)}) collective-permute-start(f32[2,128,128]{2,1,0:T(8,128)} %own.1), channel_id=1, source_target_pairs={{1,2},{2,1},{3,4},{4,3},{5,6},{6,5},{7,8},{8,7},{9,10},{10,9},{11,... | collective-permute-start | bytes 393224 | tf_op jit(solution)/shard_map/ppermute | solution.py:407
  31.4 3.6 %collective-permute-start.2 = (f32[2,64,128]{2,1,0:T(8,128)S(1)}, f32[2,64,128]{2,1,0:T(8,128)S(1)}, u32[]{:S(2)}, u32[]{:S(2)}) collective-permute-start(f32[2,64,128]{2,1,0:T(8,128)S(1)} %get-tuple-element.8), channel_id=1, source_target_pairs={{0,1},{1,0},{2,3},{3,2},{4,5},{5,4},{6,7},{7,6},{8,9},{9,8},{10,11... | collective-permute-start | bytes 196616 | tf_op jit(solution)/shard_map/ppermute | solution.py:473
  31.5 6.5 %collective-permute-start.3 = (f32[2,64,128]{2,1,0:T(8,128)S(1)}, f32[2,64,128]{2,1,0:T(8,128)S(1)}, u32[]{:S(2)}, u32[]{:S(2)}) collective-permute-start(f32[2,64,128]{2,1,0:T(8,128)S(1)} %get-tuple-element.9), channel_id=1, source_target_pairs={{1,2},{2,1},{3,4},{4,3},{5,6},{6,5},{7,8},{8,7},{9,10},{10,9},{11,... | collective-permute-start | bytes 196616 | tf_op jit(solution)/shard_map/ppermute | solution.py:472

commit v30 on v28

--- a/solution.py
+++ b/solution.py
@@ -16,7 +16,7 @@
 THRESHOLD = 2.0
 BATCH = 12
 EARLY = 8
-LATE_BATCH = 8
+LATE_BATCH = 16
 PIECE = 256
 
 f32 = jnp.float32

time: 38.5 us -> 38.8 us (level)
  transfers between devices with their start and end apart: 4 -> 4, of which waited for: 1 -> 1; matrix products, arithmetic and copies ran while one was open for 0% -> 0% of each run, Pallas kernels for 14% -> 13%
where the time goes in v30:
time: 38.8 us; the launch traced here: 38.6 us
  Pallas kernels  27.3 us (70%)
  starting transfers between devices  7.51 us (19%)
  waiting for transfers between devices  2.95 us (8%)
  between operations  0.76 us (2%)
    pallas_call x1, Pallas kernels, on_device(): pl.pallas_call(functools.partial(main_body, layout=layout, sections=secti...  21.5 us
    pallas_call x1, Pallas kernels, on_device(): pl.pallas_call(spectra_body, out_shape=jax.ShapeDtypeStruct((EARLY, grid_...  5.16 us
    ppermute x1, starting transfers between devices, on_device(): far_in = lax.ppermute(far_rim, 'row', far_pairs)  3.52 us
    ppermute x1, starting transfers between devices, on_device(): far = lax.ppermute(mask_field, 'row', far_pairs)  3.18 us
    ppermute x1, waiting for transfers between devices, on_device(): far_in = lax.ppermute(far_rim, 'row', far_pairs)  2.95 us
  transfers between devices with their start and end apart: 4, of which 1 were waited for; matrix products, arithmetic and copies ran while one was open for 0% of the time, Pallas kernels for 13%

profile of v30, /device:TPU:21, one launch (start us, length us, event | category | flops | bytes accessed | tf_op | source)
XLA Modules:
  0.0 38.6 jit_solution(14543500999635418171)
XLA Ops:
  0.6 0.0 copy-start
  0.6 0.0 copy-start.4
  0.7 0.0 copy-start.3
  0.7 0.0 copy-start.2
  0.7 0.0 copy-start.1
  0.7 0.7 %collective-permute-start = (f32[2,128,128]{2,1,0:T(8,128)}, f32[2,128,128]{2,1,0:T(8,128)S(1)}, u32[]{:S(2)}, u32[]{:S(2)}) collective-permute-start(f32[2,128,128]{2,1,0:T(8,128)} %own.1), channel_id=1, source_target_pairs={{0,1},{1,0},{2,3},{3,2},{4,5},{5,4},{6,7},{7,6},{8,9},{9,8},{10,11... | collective-permute-start | bytes 393224 | tf_op jit(solution)/shard_map/ppermute | solution.py:406
  1.4 3.2 %collective-permute-start.1 = (f32[2,128,128]{2,1,0:T(8,128)}, f32[2,128,128]{2,1,0:T(8,128)S(1)}, u32[]{:S(2)}, u32[]{:S(2)}) collective-permute-start(f32[2,128,128]{2,1,0:T(8,128)} %own.1), channel_id=1, source_target_pairs={{1,2},{2,1},{3,4},{4,3},{5,6},{6,5},{7,8},{8,7},{9,10},{10,9},{11,... | collective-permute-start | bytes 393224 | tf_op jit(solution)/shard_map/ppermute | solution.py:407
  4.6 5.2 %spectra.1.spec_far = f32[8,256,384]{2,1,0:T(8,128)} custom-call(s32[24]{0:T(128)} %radii.3, f32[24,2,128,128]{3,2,1,0:T(8,128)} %taps_far.1, bf16[256,512]{1,0:T(8,128)(2,1)} %constant.12.clone.row_ref, bf16[512,256]{1,0:T(8,128)(2,1)} %constant.13.clone.head_ref, bf16[256,256]{1,0:T(8,128)(2,1)} %constant.14.clone.tail_ref), custom_call_target="tpu_custom_call" | custom-call | flops 3000000000 | bytes 3000000 | tf_op jit(solution)/shard_map/spectra/pallas_call | solution.py:429
  9.8 0.0 collective-permute-done.near
  9.8 0.0 collective-permute-done.1.far
  9.8 0.0 copy-done
  9.8 0.0 copy-done.4
  9.8 0.0 copy-done.3
  9.8 0.0 copy-done.2
  9.8 0.0 copy-done.1
  9.8 21.5 %fields.1 = (f32[3,128,128]{2,1,0:T(8,128)}, f32[2,128,128]{2,1,0:T(8,128)S(1)}, f32[2,64,128]{2,1,0:T(8,128)S(1)}, f32[2,64,128]{2,1,0:T(8,128)S(1)}) custom-call(s32[24]{0:T(128)S(1)} %copy-done.2, f32[24]{0:T(128)S(1)} %copy-done.3, s32[1]{0:T(128)} %bitcast.place, s32[24]{0:T(128)S(1)} %copy-done.4, f32[2,128,128]{2,1,0:T(8,128)S(1)} %copy-done, ...), custom_call_target="tpu_custom_call" | custom-call | tf_op jit(solution)/shard_map/fields/pallas_call | solution.py:444
  31.3 0.1 collective-permute-start.2
  31.4 3.5 %collective-permute-start.3 = (f32[2,64,128]{2,1,0:T(8,128)S(1)}, f32[2,64,128]{2,1,0:T(8,128)S(1)}, u32[]{:S(2)}, u32[]{:S(2)}) collective-permute-start(f32[2,64,128]{2,1,0:T(8,128)S(1)} %get-tuple-element.9), channel_id=1, source_target_pairs={{1,2},{2,1},{3,4},{4,3},{5,6},{6,5},{7,8},{8,7},{9,10},{10,9},{11,... | collective-permute-start | bytes 196616 | tf_op jit(solution)/shard_map/ppermute | solution.py:472
  34.9 0.0 collective-permute-done.2.near
  34.9 2.9 %collective-permute-done.3.far = f32[2,64,128]{2,1,0:T(8,128)S(1)} collective-permute-done((f32[2,64,128]{2,1,0:T(8,128)S(1)}, f32[2,64,128]{2,1,0:T(8,128)S(1)}, u32[]{:S(2)}, u32[]{:S(2)}) %collective-permute-start.3) | collective-permute-done | bytes 65568 | tf_op jit(solution)/shard_map/ppermute | solution.py:472
  37.9 0.7 %join.1 = f32[2,128,128]{2,1,0:T(8,128)} custom-call(s32[1]{0:T(128)} %bitcast.place, f32[2,128,128]{2,1,0:T(8,128)S(1)} %get-tuple-element.7.own, f32[2,64,128]{2,1,0:T(8,128)S(1)} %collective-permute-done.2.near, f32[2,64,128]{2,1,0:T(8,128)S(1)} %collective-permute-done.3.far), custom_call_target="tpu_custom_call" | custom-call | tf_op jit(solution)/shard_map/join/pallas_call | solution.py:474
Async XLA Ops:
  0.6 9.1 %copy-start = (f32[2,128,128]{2,1,0:T(8,128)S(1)}, f32[2,128,128]{2,1,0:T(8,128)}, u32[]{:S(2)}) copy-start(f32[2,128,128]{2,1,0:T(8,128)} %own.1) | copy-start | bytes 393220
  0.6 9.1 %copy-start.4 = (s32[24]{0:T(128)S(1)}, s32[24]{0:T(128)}, u32[]{:S(2)}) copy-start(s32[24]{0:T(128)} %radii.3) | copy-start | bytes 292
  0.7 9.1 %copy-start.3 = (f32[24]{0:T(128)S(1)}, f32[24]{0:T(128)}, u32[]{:S(2)}) copy-start(f32[24]{0:T(128)} %weight.1) | copy-start | bytes 292
  0.7 9.1 %copy-start.2 = (s32[24]{0:T(128)S(1)}, s32[24]{0:T(128)}, u32[]{:S(2)}) copy-start(s32[24]{0:T(128)} %group.1) | copy-start | bytes 292
  0.7 9.1 %copy-start.1 = (s32[128,128]{1,0:T(8,128)S(1)}, s32[128,128]{1,0:T(8,128)}, u32[]{:S(2)}) copy-start(s32[128,128]{1,0:T(8,128)} %target.1) | copy-start | bytes 196612
  0.7 9.1 %collective-permute-start = (f32[2,128,128]{2,1,0:T(8,128)}, f32[2,128,128]{2,1,0:T(8,128)S(1)}, u32[]{:S(2)}, u32[]{:S(2)}) collective-permute-start(f32[2,128,128]{2,1,0:T(8,128)} %own.1), channel_id=1, source_target_pairs={{0,1},{1,0},{2,3},{3,2},{4,5},{5,4},{6,7},{7,6},{8,9},{9,8},{10,11... | collective-permute-start | bytes 393224 | tf_op jit(solution)/shard_map/ppermute | solution.py:406
  1.4 8.3 %collective-permute-start.1 = (f32[2,128,128]{2,1,0:T(8,128)}, f32[2,128,128]{2,1,0:T(8,128)S(1)}, u32[]{:S(2)}, u32[]{:S(2)}) collective-permute-start(f32[2,128,128]{2,1,0:T(8,128)} %own.1), channel_id=1, source_target_pairs={{1,2},{2,1},{3,4},{4,3},{5,6},{6,5},{7,8},{8,7},{9,10},{10,9},{11,... | collective-permute-start | bytes 393224 | tf_op jit(solution)/shard_map/ppermute | solution.py:407
  31.3 3.6 %collective-permute-start.2 = (f32[2,64,128]{2,1,0:T(8,128)S(1)}, f32[2,64,128]{2,1,0:T(8,128)S(1)}, u32[]{:S(2)}, u32[]{:S(2)}) collective-permute-start(f32[2,64,128]{2,1,0:T(8,128)S(1)} %get-tuple-element.8), channel_id=1, source_target_pairs={{0,1},{1,0},{2,3},{3,2},{4,5},{5,4},{6,7},{7,6},{8,9},{9,8},{10,11... | collective-permute-start | bytes 196616 | tf_op jit(solution)/shard_map/ppermute | solution.py:473
  31.4 6.5 %collective-permute-start.3 = (f32[2,64,128]{2,1,0:T(8,128)S(1)}, f32[2,64,128]{2,1,0:T(8,128)S(1)}, u32[]{:S(2)}, u32[]{:S(2)}) collective-permute-start(f32[2,64,128]{2,1,0:T(8,128)S(1)} %get-tuple-element.9), channel_id=1, source_target_pairs={{1,2},{2,1},{3,4},{4,3},{5,6},{6,5},{7,8},{8,7},{9,10},{10,9},{11,... | collective-permute-start | bytes 196616 | tf_op jit(solution)/shard_map/ppermute | solution.py:472
